TPU v7x, 32 devices: a whole 2x2x4 slice. The times are simulated.
32 devices in a mesh: groups: 2 (over y), hid: 4 (over z), rows: 2 (over x), mp: 2 (over core).
Axes of the slice: x: 2, y: 2, z: 4, core: 2. Of those that a mesh axis runs over, the one named last changes fastest.
Arguments:
- tokens: bfloat16 [1024, 4096], P(('groups', 'rows'), 'hid'), parts along dimension 0, may hold values from -6 to 6
- norm_gain: float32 [2, 4096], P('mp'), may hold values from 0.1 to 1.9
- gate_weight: bfloat16 [2, 4096, 14336], P('mp', 'rows', 'hid'), may hold values from -0.09375 to 0.09375
- up_weight: bfloat16 [2, 4096, 14336], P('mp', 'rows', 'hid'), may hold values from -0.09375 to 0.09375
- down_weight: bfloat16 [2, 14336, 4096], P('mp', 'hid', 'rows'), may hold values from -0.046875 to 0.046875
- enc_weight: bfloat16 [2, 4096, 16384], P('mp', 'rows', 'hid'), may hold values from -0.0625 to 0.0625
- enc_bias: float32 [16384], P('hid'), may hold values from -3 to 3
- adjoint: bfloat16 [1024, 16384], P(('groups', 'rows', 'mp'), 'hid'), parts along dimension 0, may hold values from -6 to 6
Outputs:
- gated: bfloat16 [1024, 16384], P(('groups', 'rows', 'mp'), 'hid'), parts along dimension 0
There are 2 independent parts, one for each index of `groups`. A program takes and returns all parts, laid end to end along the dimension named above; an argument that names none is the same for every part. Nothing has to cross between parts.
All inputs are finite; a program needn't handle non-finite values.
Results may differ from a plain program's by a relative error of at most 0.0058.
Values may be sent and summed in bfloat16 or wider, within the bound.
No kernel may reach another device: no remote copies, remote signals or barrier semaphores. Data moves between devices by JAX's collectives and lax.ppermute only.
A program may use at most 128 MiB of HBM per device.

v0:
```python
import jax
import jax.numpy as jnp
from jax import lax
from jax.sharding import PartitionSpec as P


def on_device(
    tokens, norm_gain, gate_weight, up_weight, down_weight, enc_weight, enc_bias, adjoint
):
    gathered = lax.all_gather(tokens, "hid", axis=1, tiled=True)
    tokens_float = gathered.astype(jnp.float32)
    inverse_rms = lax.rsqrt(jnp.mean(tokens_float * tokens_float, axis=-1, keepdims=True) + 1e-05)
    normed = (tokens_float * inverse_rms * norm_gain[0][None, :]).astype(jnp.bfloat16)
    gate_local = gate_weight[0]
    up_local = up_weight[0]
    hidden_width = gate_local.shape[1]
    all_normed = lax.all_gather(normed, "rows", axis=0, tiled=True)
    width_rows = gate_local.shape[0]
    column_start = lax.axis_index("rows") * width_rows
    own_columns = lax.dynamic_slice_in_dim(all_normed, column_start, width_rows, 1)
    both_local = jnp.concatenate((gate_local, up_local), axis=1)
    selected = own_columns
    summed = lax.psum_scatter(
        jnp.dot(selected, both_local, preferred_element_type=jnp.float32),
        "rows",
        scatter_dimension=0,
        tiled=True,
    )
    gate_acts = summed[:, :hidden_width]
    up_acts = summed[:, hidden_width:]
    hidden = (jax.nn.silu(gate_acts) * up_acts).astype(jnp.bfloat16)
    down_local = down_weight[0]
    partial_out = jnp.dot(
        lax.all_gather(hidden, "rows", axis=0, tiled=True),
        down_local,
        preferred_element_type=jnp.float32,
    )
    block_out = lax.psum(partial_out, "hid").astype(jnp.bfloat16)
    enc_local = enc_weight[0]
    selected = block_out
    pre_rows = lax.psum_scatter(
        jnp.dot(selected, enc_local, preferred_element_type=jnp.float32),
        ("rows", "mp"),
        scatter_dimension=0,
        tiled=True,
    )
    pre_rows = pre_rows + enc_bias[None, :]
    return (jnp.maximum(pre_rows, 0.0) * adjoint.astype(jnp.float32)).astype(jnp.bfloat16)


def solution(mesh):
    placed = (
        P(("groups", "rows"), "hid"),
        P("mp", None),
        P("mp", "rows", "hid"),
        P("mp", "rows", "hid"),
        P("mp", "hid", "rows"),
        P("mp", "rows", "hid"),
        P("hid"),
        P(("groups", "rows", "mp"), "hid"),
    )
    return jax.shard_map(
        on_device,
        mesh=mesh,
        in_specs=placed,
        out_specs=P(("groups", "rows", "mp"), "hid"),
        check_vma=False,
    )
```

profile of v0, /device:TPU:0, one launch (start us, length us, event | category | flops | bytes accessed | tf_op | source)
XLA Modules:
  0.0 619.1 jit_solution(2788526948449439029)
XLA Ops:
  6.5 0.0 all-gather.4.cloned.1.call-start
  6.5 0.7 all-gather.4.cloned.1.call-update
  7.3 0.0 all-gather.6.cloned.1.call-start
  7.3 50.3 %all-gather.4.cloned.1.call-done = bf16[256,4096]{1,0:T(8,128)(2,1)} async-done(((bf16[256,1024]{1,0:T(8,128)(2,1)}), bf16[256,4096]{1,0:T(8,128)(2,1)}) %all-gather.4.cloned.1.call-update) | async-done | bytes 2097168 | tf_op jit(solution)/shard_map/all_gather | solution.py:10
  57.6 2.1 fusion.8
  59.7 3.6 fusion.10
  63.3 0.0 all-gather.6.cloned.1.call-update
  63.3 0.0 reduce-scatter.3.cloned.1.call-start
  63.3 55.6 %all-gather.6.cloned.1.call-done = bf16[512,4096]{1,0:T(8,128)(2,1)} async-done(((bf16[256,4096]{1,0:T(8,128)(2,1)}), bf16[512,4096]{1,0:T(8,128)(2,1)}) %all-gather.6.cloned.1.call-update) | async-done | bytes 4194320 | tf_op jit(solution)/shard_map/all_gather | solution.py:17
  118.9 22.1 %fusion = f32[512,7168]{1,0:T(8,128)} fusion(bf16[2048,3584]{1,0:T(8,128)(2,1)} %bitcast.12, bf16[2048,3584]{1,0:T(8,128)(2,1)} %bitcast.13, bf16[512,4096]{1,0:T(8,128)(2,1)} %all-gather.6.cloned.1.call-done, s32[]{:T(128)S(6)} %select_n.3), kind=kOutput, calls=%fused_computation | convolution fusion | flops 15091105792 | bytes 46137348 | tf_op jit(solution)/shard_map/dot_general | solution.py:24
  141.0 0.0 reduce-scatter.3.cloned.1.call-update
  141.1 0.0 all-gather.8.cloned.1.call-start
  141.1 167.2 %reduce-scatter.3.cloned.1.call-done = f32[256,7168]{1,0:T(8,128)} async-done(((f32[512,7168]{1,0:T(8,128)}), f32[256,7168]{1,0:T(8,128)}) %reduce-scatter.3.cloned.1.call-update) | async-done | bytes 7340048 | tf_op jit(solution)/shard_map/reduce_scatter | solution.py:23
  308.3 5.5 fusion.11
  313.8 0.0 all-gather.8.cloned.1.call-update
  313.8 0.0 reduce-scatter.5.cloned.1.call-start
  313.8 50.9 %all-gather.8.cloned.1.call-done = bf16[512,3584]{1,0:T(8,128)(2,1)} async-done(((bf16[256,3584]{1,0:T(8,128)(2,1)}), bf16[512,3584]{1,0:T(8,128)(2,1)}) %all-gather.8.cloned.1.call-update) | async-done | bytes 3670032 | tf_op jit(solution)/shard_map/all_gather | solution.py:34
  364.8 13.4 %fusion.6 = f32[512,2048]{1,0:T(8,128)} fusion(bf16[512,3584]{1,0:T(8,128)(2,1)} %all-gather.8.cloned.1.call-done, bf16[1,3584,2048]{2,1,0:T(8,128)(2,1)} %param.12), kind=kOutput, calls=%fused_computation.6 | convolution fusion | flops 7516192768 | bytes 22544384 | tf_op jit(solution)/shard_map/dot_general | solution.py:33
  378.2 147.3 %all-reduce.1 = bf16[512,2048]{1,0:T(8,128)(2,1)S(1)} all-reduce(f32[512,2048]{1,0:T(8,128)} %fusion.6), channel_id=1, replica_groups=mesh['groups'=2,'hid'=4,'rows'=2,'mp'=2] {'hid'}, use_global_device_ids=true, to_apply=%region_2.3 | all-reduce | flops 1048576 | bytes 6291456 | tf_op jit(solution)/shard_map/psum | solution.py:38
  525.5 14.4 %fusion.4 = f32[512,4096]{1,0:T(8,128)} fusion(bf16[1,2048,4096]{2,1,0:T(8,128)(2,1)} %param.13, bf16[512,2048]{1,0:T(8,128)(2,1)S(1)} %all-reduce.1), kind=kOutput, calls=%fused_computation.4 | convolution fusion | flops 8589934592 | bytes 27262976 | tf_op jit(solution)/shard_map/dot_general | solution.py:42
  539.8 0.0 reduce-scatter.5.cloned.1.call-update
  539.9 69.8 %reduce-scatter.5.cloned.1.call-done = f32[128,4096]{1,0:T(8,128)} async-done(((f32[512,4096]{1,0:T(8,128)}), f32[128,4096]{1,0:T(8,128)}) %reduce-scatter.5.cloned.1.call-update) | async-done | bytes 2097168 | tf_op jit(solution)/shard_map/reduce_scatter | solution.py:41
  609.6 0.0 copy-done.1
  609.6 2.9 multiply_convert_fusion
  (4 shorter events, 0.0 us)
Async XLA Ops:
  6.5 51.1 %all-gather.4.cloned.1.call-start = ((), (), s32[]{:S(2)}) async-start(), calls=%async_computation.2 | async-start | bytes 2621440 | tf_op jit(solution)/shard_map/all_gather | solution.py:10
  7.3 111.6 %all-gather.6.cloned.1.call-start = ((), (), s32[]{:S(2)}) async-start(), calls=%async_computation.3 | async-start | bytes 6291456 | tf_op jit(solution)/shard_map/all_gather | solution.py:17
  63.3 245.0 %reduce-scatter.3.cloned.1.call-start = ((), (), s32[]{:S(2)}) async-start(), calls=%async_computation.4 | async-start | bytes 22020096 | tf_op jit(solution)/shard_map/reduce_scatter | solution.py:23
  141.1 223.7 %all-gather.8.cloned.1.call-start = ((), (), s32[]{:S(2)}) async-start(), calls=%async_computation.5 | async-start | bytes 5505024 | tf_op jit(solution)/shard_map/all_gather | solution.py:34
  313.8 295.8 %reduce-scatter.5.cloned.1.call-start = ((), (), s32[]{:S(2)}) async-start(), calls=%async_computation.6 | async-start | bytes 10485760 | tf_op jit(solution)/shard_map/reduce_scatter | solution.py:41
  539.8 69.8 %copy-start = (bf16[128,4096]{1,0:T(8,128)(2,1)S(1)}, bf16[128,4096]{1,0:T(8,128)(2,1)}, u32[]{:S(2)}) copy-start(bf16[128,4096]{1,0:T(8,128)(2,1)} %param.15) | copy-start | bytes 3145732
  539.8 69.8 %copy-start.1 = (f32[4096]{0:T(1024)S(1)}, f32[4096]{0:T(1024)}, u32[]{:S(2)}) copy-start(f32[4096]{0:T(1024)} %param.14) | copy-start | bytes 49156
Sparse Core Ops, SparseCore 0:
  8.9 48.6 all-gather.3
  63.4 55.4 all-gather.5
  141.2 167.0 reduce-scatter.2
  313.9 50.8 all-gather.7
  540.0 69.6 reduce-scatter.4
where the time goes:
time: 619 us
  waiting for transfers between devices  395 us (64%)
  blocking collectives  147 us (24%)
  matrix products  49.9 us (8%)
  other arithmetic  14 us (2%)
  between operations  13.2 us (2%)
    reduce_scatter x1, waiting for transfers between devices, on_device(): lax.psum_scatter(jnp.dot(selected, both_local, preferred_element_type=jnp...  167 us
    psum x1, blocking collectives, on_device(): block_out = lax.psum(partial_out, 'hid').astype(jnp.bfloat16)  147 us
    reduce_scatter x1, waiting for transfers between devices, on_device(): lax.psum_scatter(jnp.dot(selected, enc_local, preferred_element_type=jnp....  69.8 us
    all_gather x1, waiting for transfers between devices, on_device(): all_normed = lax.all_gather(normed, 'rows', axis=0, tiled=True)  55.6 us
    all_gather x1, waiting for transfers between devices, on_device(): lax.all_gather(hidden, 'rows', axis=0, tiled=True)  50.9 us
    all_gather x1, waiting for transfers between devices, on_device(): gathered = lax.all_gather(tokens, 'hid', axis=1, tiled=True)  50.3 us
    dot_general x1, matrix products, on_device(): jnp.dot(selected, both_local, preferred_element_type=jnp.float32)  22.1 us
    dot_general x1, matrix products, on_device(): jnp.dot(selected, enc_local, preferred_element_type=jnp.float32)  14.4 us
  transfers between devices with their start and end apart: 5, of which 5 were waited for; matrix products, arithmetic and copies ran while one was open for 0% of the time, Pallas kernels for 0%

commit v1 on v0

v1 whole, which is shorter than its diff:
```python
import functools

import jax
import jax.numpy as jnp
from jax import lax
from jax.experimental import pallas as pl
from jax.experimental.pallas import tpu as pltpu
from jax.sharding import PartitionSpec as P

BF16 = jnp.bfloat16
F32 = jnp.float32
VMEM_BYTES = 40 * 1024 * 1024


def shift(value, axis, size, hop):
    return lax.ppermute(value, axis, [((d + hop) % size, d) for d in range(size)])


def send(value, axis, size, hop):
    return lax.ppermute(value, axis, [(d, (d + hop) % size) for d in range(size)])


def tile_of(width, most):
    tile = most
    while tile > 128 and width % tile:
        tile //= 2
    return tile if width % tile == 0 else width


def whole(shape):
    return pl.BlockSpec(shape, lambda j, *_: (0,) * len(shape))


def params():
    return pltpu.CompilerParams(
        dimension_semantics=("arbitrary",), vmem_limit_bytes=VMEM_BYTES
    )


def cost(rows, depth, width):
    return pl.CostEstimate(
        flops=2 * rows * depth * width,
        bytes_accessed=2 * (rows * depth + depth * width + rows * width),
        transcendentals=0,
    )


def gate_up_body(owners, x_ref, gate_ref, up_ref, own_ref, *send_refs):
    rows = x_ref.shape[0] // owners
    x = x_ref[...]
    for at, weight_ref in enumerate((gate_ref, up_ref)):
        acts = jnp.dot(x, weight_ref[0], preferred_element_type=F32)
        own_ref[at] = acts[:rows]
        for hop in range(1, owners):
            send_refs[hop - 1][at] = acts[hop * rows : (hop + 1) * rows].astype(BF16)


def gate_up(x, gate_weight, up_weight, owners, piece, pieces):
    rows, depth = x.shape
    width = gate_weight.shape[2] // pieces
    tile = tile_of(width, 256)
    tiles = width // tile
    own_rows = rows // owners
    weight_spec = pl.BlockSpec((1, depth, tile), lambda j: (0, 0, j + piece * tiles))
    out_spec = pl.BlockSpec((2, own_rows, tile), lambda j: (0, 0, j))
    return pl.pallas_call(
        functools.partial(gate_up_body, owners),
        grid=(tiles,),
        in_specs=[whole((rows, depth)), weight_spec, weight_spec],
        out_specs=[out_spec] * owners,
        out_shape=[jax.ShapeDtypeStruct((2, own_rows, width), F32)]
        + [jax.ShapeDtypeStruct((2, own_rows, width), BF16)] * (owners - 1),
        compiler_params=params(),
        cost_estimate=cost(rows, depth, 2 * width),
    )(x, gate_weight, up_weight)


def down_body(owners, members, pieces, ranks, rank_ref, *refs):
    hidden_refs = refs[: owners * pieces]
    weight_ref = refs[owners * pieces]
    out_refs = refs[owners * pieces + 1 : -2]
    lhs_ref, acc_ref = refs[-2:]
    q = hidden_refs[0].shape[0] // members
    part = hidden_refs[0].shape[1]
    block = acc_ref.shape[0] // ranks

    @pl.when(pl.program_id(0) == 0)
    def _():
        for owner in range(owners):
            for piece in range(pieces):
                for member in range(members):
                    row = (member * owners + owner) * q
                    lhs_ref[row : row + q, piece * part : (piece + 1) * part] = hidden_refs[
                        owner * pieces + piece
                    ][member * q : (member + 1) * q]

    acc_ref[...] = jnp.dot(lhs_ref[...], weight_ref[0], preferred_element_type=F32)
    for hop in range(ranks):
        at = lax.rem(rank_ref[0] + hop, ranks) * block
        taken = acc_ref[pl.ds(pl.multiple_of(at, block), block), :]
        out_refs[hop][...] = taken.astype(out_refs[hop].dtype)


def down(rank, hidden, down_weight, members, ranks):
    owners, pieces = len(hidden), len(hidden[0])
    rows_each, part = hidden[0][0].shape
    rows, depth, width = owners * rows_each, pieces * part, down_weight.shape[2]
    tile = tile_of(width, 256)
    block = rows // ranks
    out_spec = pl.BlockSpec((block, tile), lambda j, *_: (0, j))
    return pl.pallas_call(
        functools.partial(down_body, owners, members, pieces, ranks),
        grid_spec=pltpu.PrefetchScalarGridSpec(
            num_scalar_prefetch=1,
            grid=(width // tile,),
            in_specs=[whole((rows_each, part))] * (owners * pieces)
            + [pl.BlockSpec((1, depth, tile), lambda j, *_: (0, 0, j))],
            out_specs=[out_spec] * ranks,
            scratch_shapes=[pltpu.VMEM((rows, depth), BF16), pltpu.VMEM((rows, tile), F32)],
        ),
        out_shape=[jax.ShapeDtypeStruct((block, width), F32)]
        + [jax.ShapeDtypeStruct((block, width), BF16)] * (ranks - 1),
        compiler_params=params(),
        cost_estimate=cost(rows, depth, width),
    )(rank, *[piece for of_owner in hidden for piece in of_owner], down_weight)


def encode_body(members, ranks, rank_ref, *refs):
    block_refs = refs[:ranks]
    weight_ref = refs[ranks]
    out_refs = refs[ranks + 1 : -1]
    lhs_ref = refs[-1]
    block = block_refs[0].shape[0]

    @pl.when(pl.program_id(0) == 0)
    def _():
        for hop in range(ranks):
            at = lax.rem(rank_ref[0] + hop, ranks) * block
            lhs_ref[pl.ds(pl.multiple_of(at, block), block), :] = block_refs[hop][...]

    pre = jnp.dot(lhs_ref[...], weight_ref[0], preferred_element_type=F32)
    rows = pre.shape[0] // members
    for member in range(members):
        taken = pre[member * rows : (member + 1) * rows]
        out_refs[member][...] = taken.astype(out_refs[member].dtype)


def encode(rank, blocks, enc_weight, members):
    ranks = len(blocks)
    block, depth = blocks[0].shape
    width = enc_weight.shape[2]
    rows = block * ranks
    rows_each = rows // members
    tile = tile_of(width, 512)
    out_spec = pl.BlockSpec((rows_each, tile), lambda j, *_: (0, j))
    return pl.pallas_call(
        functools.partial(encode_body, members, ranks),
        grid_spec=pltpu.PrefetchScalarGridSpec(
            num_scalar_prefetch=1,
            grid=(width // tile,),
            in_specs=[whole((block, depth))] * ranks
            + [pl.BlockSpec((1, depth, tile), lambda j, *_: (0, 0, j))],
            out_specs=[out_spec] * members,
            scratch_shapes=[pltpu.VMEM((rows, depth), BF16)],
        ),
        out_shape=[jax.ShapeDtypeStruct((rows_each, width), F32)] * members,
        compiler_params=params(),
        cost_estimate=cost(rows, depth, width),
    )(rank, *blocks, enc_weight)


def on_device(
    owners, members, ranks, tokens, norm_gain, gate_weight, up_weight, down_weight, enc_weight,
    enc_bias, adjoint,
):
    row_at = lax.axis_index("rows")
    member_at = lax.axis_index("mp")
    rank_at = lax.axis_index("hid")
    rank = rank_at.astype(jnp.int32).reshape(1)
    per_device = adjoint.shape[0]
    cut = tokens.shape[1]
    half_cuts = ranks // owners
    model_width = cut * ranks

    tokens_float = tokens.astype(F32)
    local_squares = jnp.sum(tokens_float * tokens_float, axis=1)
    squares = local_squares
    for hop in range(1, ranks):
        squares = squares + shift(local_squares, "hid", ranks, hop)
    inverse = lax.rsqrt(squares / model_width + 1e-05).reshape(members, per_device)
    inverses = [inverse] + [shift(inverse, "rows", owners, hop) for hop in range(1, owners)]
    inverses = jnp.stack(inverses)
    turned = jnp.concatenate((inverses, inverses), axis=1)
    inverses = lax.dynamic_slice_in_dim(turned, member_at, members, 1)
    gain = lax.dynamic_slice_in_dim(
        norm_gain[0], row_at * (model_width // owners), model_width // owners, 0
    )

    own_tokens = lax.dynamic_slice_in_dim(tokens, member_at * per_device, per_device, 0)

    chunks = max(1, 16 // ranks)
    pieces = 1
    q = per_device // chunks

    def normed_rows(start, q):
        mine = own_tokens[start : start + q]
        gathered = jnp.zeros((ranks, q, cut), BF16)
        gathered = lax.dynamic_update_slice(gathered, mine[None], (rank_at, 0, 0))
        for hop in range(1, ranks):
            there = lax.rem(rank_at + hop, ranks)
            gathered = lax.dynamic_update_slice(
                gathered, shift(mine, "hid", ranks, hop)[None], (there, 0, 0)
            )
        columns = []
        for hop in range(owners):
            target = lax.rem(row_at + owners - hop, owners)
            half = lax.dynamic_slice_in_dim(gathered, target * half_cuts, half_cuts, 0)
            columns.append(half if hop == 0 else shift(half, "rows", owners, hop))
        columns = jnp.stack(columns)
        columns = [columns] + [shift(columns, "mp", members, hop) for hop in range(1, members)]
        columns = jnp.stack(columns, axis=1).astype(F32)
        scale = inverses[:, :, None, start : start + q, None]
        normed = (columns * scale * gain.reshape(half_cuts, 1, cut)).astype(BF16)
        return normed.transpose(0, 1, 3, 2, 4).reshape(owners * members * q, half_cuts * cut)

    def layer(x):
        hidden = [[] for _ in range(owners)]
        for piece in range(pieces):
            own, *sends = gate_up(x, gate_weight, up_weight, owners, piece, pieces)
            acts = own
            for hop in range(1, owners):
                acts = acts + send(sends[hop - 1], "rows", owners, hop).astype(F32)
            mine = (jax.nn.silu(acts[0]) * acts[1]).astype(BF16)
            hidden[0].append(mine)
            for hop in range(1, owners):
                hidden[hop].append(shift(mine, "rows", owners, hop))
        own, *sends = down(rank, hidden, down_weight, members, ranks)
        total = own
        for hop in range(1, ranks):
            total = total + send(sends[hop - 1], "hid", ranks, hop).astype(F32)
        block = total.astype(BF16)
        return [block] + [shift(block, "hid", ranks, hop) for hop in range(1, ranks)]

    def features(blocks, start, q):
        own, *sends = encode(rank, blocks, enc_weight, members)
        total = own
        for hop in range(1, members):
            total = total + send(sends[hop - 1], "mp", members, hop)
        pre = total[:q]
        for hop in range(1, owners):
            going = total[hop * q : (hop + 1) * q].astype(BF16)
            pre = pre + send(going, "rows", owners, hop).astype(F32)
        pre = pre + enc_bias[None, :]
        factor = adjoint[start : start + q].astype(F32)
        return (jnp.maximum(pre, 0.0) * factor).astype(BF16)

    outs = []
    for chunk in range(chunks):
        x = normed_rows(chunk * q, q)
        blocks = layer(x)
        outs.append(features(blocks, chunk * q, q))
    return jnp.concatenate(outs, axis=0)


def solution(mesh):
    placed = (
        P(("groups", "rows"), "hid"),
        P("mp", None),
        P("mp", "rows", "hid"),
        P("mp", "rows", "hid"),
        P("mp", "hid", "rows"),
        P("mp", "rows", "hid"),
        P("hid"),
        P(("groups", "rows", "mp"), "hid"),
    )
    sizes = (mesh.shape["rows"], mesh.shape["mp"], mesh.shape["hid"])
    return jax.shard_map(
        functools.partial(on_device, *sizes),
        mesh=mesh,
        in_specs=placed,
        out_specs=P(("groups", "rows", "mp"), "hid"),
        check_vma=False,
    )
```

time: 619 us -> 334 us (0.54)
  waiting for transfers between devices: 395 us -> 80.6 us
  blocking collectives: 147 us -> 0 us
  Pallas kernels: 0 us -> 136 us
  starting transfers between devices: 0.17 us -> 103 us
  matrix products: 49.9 us -> 0 us
  between operations: 13.2 us -> 0.71 us
  other arithmetic: 14 us -> 5.98 us
  local copies, waits for them, and re-layouts: 0.01 us -> 6.57 us
    reduce_scatter x2 -> x0, waiting for transfers between devices: 237 us -> none  [the longest x1 167 us: on_device(): lax.psum_scatter(jnp.dot(selected, both_local, preferred_element_type=jnp...]
    all_gather x3 -> x0, waiting for transfers between devices: 157 us -> none  [the longest x1 55.6 us: on_device(): all_normed = lax.all_gather(normed, 'rows', axis=0, tiled=True)]
    psum x1 -> x0, blocking collectives: 147 us -> none  [on_device(): block_out = lax.psum(partial_out, 'hid').astype(jnp.bfloat16)]
    pallas_call x0 -> x12, Pallas kernels: none -> 136 us  [the longest x4 62.9 us: gate_up(): pl.pallas_call(functools.partial(gate_up_body, owners), grid=(tiles,), in...]
    ppermute x0 -> x64, starting transfers between devices: none -> 103 us  [the longest x40 70.1 us: shift(): lax.ppermute(value, axis, [((d + hop) % size, d) for d in range(size)])]
    ppermute x0 -> x64, waiting for transfers between devices: none -> 80.6 us  [the longest x24 55.1 us: send(): lax.ppermute(value, axis, [(d, (d + hop) % size) for d in range(size)])]
    dot_general x3 -> x0, matrix products: 49.9 us -> none  [the longest x1 22.1 us: on_device(): jnp.dot(selected, both_local, preferred_element_type=jnp.float32)]
    convert_element_type x3 -> x9, other arithmetic: 11.9 us -> 1.72 us  [the longest x4 1 us: layer(): mine = (jax.nn.silu(acts[0]) * acts[1]).astype(BF16)]
  transfers between devices with their start and end apart: 5 -> 64, of which waited for: 5 -> 20; matrix products, arithmetic and copies ran while one was open for 0% -> 2% of each run, Pallas kernels for 0% -> 36%
where the time goes in v1:
time: 334 us; the launch traced here: 333 us
  Pallas kernels  136 us (41%)
  starting transfers between devices  103 us (31%)
  waiting for transfers between devices  80.6 us (24%)
  local copies, waits for them, and re-layouts  6.57 us (2%)
  other arithmetic  5.98 us (2%)
    ppermute x40, starting transfers between devices, shift(): lax.ppermute(value, axis, [((d + hop) % size, d) for d in range(size)])  70.1 us
    pallas_call x4, Pallas kernels, gate_up(): pl.pallas_call(functools.partial(gate_up_body, owners), grid=(tiles,), in...  62.9 us
    ppermute x24, waiting for transfers between devices, send(): lax.ppermute(value, axis, [(d, (d + hop) % size) for d in range(size)])  55.1 us
    pallas_call x4, Pallas kernels, encode(): pl.pallas_call(functools.partial(encode_body, members, ranks), grid_spec=...  37.6 us
    pallas_call x4, Pallas kernels, down(): pl.pallas_call(functools.partial(down_body, owners, members, pieces, rank...  35.4 us
    ppermute x24, starting transfers between devices, send(): lax.ppermute(value, axis, [(d, (d + hop) % size) for d in range(size)])  32.8 us
    ppermute x40, waiting for transfers between devices, shift(): lax.ppermute(value, axis, [((d + hop) % size, d) for d in range(size)])  25.5 us
  transfers between devices with their start and end apart: 64, of which 20 were waited for; matrix products, arithmetic and copies ran while one was open for 2% of the time, Pallas kernels for 36%

profile of v1, /device:TPU:0, one launch (start us, length us, event | category | flops | bytes accessed | tf_op | source)
XLA Modules:
  0.0 332.7 jit_solution(4168573619806518264)
XLA Ops:
  36.9 4.0 %collective-permute-start = (bf16[32,1024]{1,0:T(8,128)(2,1)S(1)}, bf16[32,1024]{1,0:T(8,128)(2,1)S(1)}, u32[]{:S(2)}, u32[]{:S(2)}) collective-permute-start(bf16[32,1024]{1,0:T(8,128)(2,1)S(1)} %get-tuple-element.70), channel_id=1, source_target_pairs={{4,0},{8,4},{12,8},{0,12},{5,1},{9,5},{13,9},{1,13},{6,2},{10,6},{... | collective-permute-start | bytes 196616 | tf_op jit(solution)/shard_map/ppermute | solution.py:16
  59.9 15.7 %shard_map.88 = (f32[2,64,3584]{2,1,0:T(8,128)S(1)}, bf16[2,64,3584]{2,1,0:T(8,128)(2,1)S(1)}) custom-call(bf16[128,2048]{1,0:T(8,128)(2,1)S(1)} %bitcast.125, bf16[1,2048,3584]{2,1,0:T(8,128)(2,1)} %gate_ref.7, bf16[1,2048,3584]{2,1,0:T(8,128)(2,1)} %up_ref.7), custom_call_target="tpu_custom_call" | custom-call | flops 3758096384 | bytes 31719424 | tf_op jit(solution)/shard_map/pallas_call | solution.py:66
  77.1 15.7 %shard_map.91 = (f32[2,64,3584]{2,1,0:T(8,128)S(1)}, bf16[2,64,3584]{2,1,0:T(8,128)(2,1)S(1)}) custom-call(bf16[128,2048]{1,0:T(8,128)(2,1)S(1)} %bitcast.124, bf16[1,2048,3584]{2,1,0:T(8,128)(2,1)} %gate_ref.7, bf16[1,2048,3584]{2,1,0:T(8,128)(2,1)} %up_ref.7), custom_call_target="tpu_custom_call" | custom-call | flops 3758096384 | bytes 31719424 | tf_op jit(solution)/shard_map/pallas_call | solution.py:66
  93.6 15.7 %shard_map.85 = (f32[2,64,3584]{2,1,0:T(8,128)S(1)}, bf16[2,64,3584]{2,1,0:T(8,128)(2,1)S(1)}) custom-call(bf16[128,2048]{1,0:T(8,128)(2,1)S(1)} %bitcast.123, bf16[1,2048,3584]{2,1,0:T(8,128)(2,1)} %gate_ref.7, bf16[1,2048,3584]{2,1,0:T(8,128)(2,1)} %up_ref.7), custom_call_target="tpu_custom_call" | custom-call | flops 3758096384 | bytes 31719424 | tf_op jit(solution)/shard_map/pallas_call | solution.py:66
  110.7 15.7 %shard_map.82 = (f32[2,64,3584]{2,1,0:T(8,128)S(1)}, bf16[2,64,3584]{2,1,0:T(8,128)(2,1)S(1)}) custom-call(bf16[128,2048]{1,0:T(8,128)(2,1)S(1)} %bitcast.122, bf16[1,2048,3584]{2,1,0:T(8,128)(2,1)} %gate_ref.7, bf16[1,2048,3584]{2,1,0:T(8,128)(2,1)} %up_ref.7), custom_call_target="tpu_custom_call" | custom-call | flops 3758096384 | bytes 31719424 | tf_op jit(solution)/shard_map/pallas_call | solution.py:66
  130.3 8.0 %collective-permute-done.24 = bf16[2,64,3584]{2,1,0:T(8,128)(2,1)S(1)} collective-permute-done((bf16[2,64,3584]{2,1,0:T(8,128)(2,1)S(1)}, bf16[2,64,3584]{2,1,0:T(8,128)(2,1)S(1)}, u32[]{:S(2)}, u32[]{:S(2)}) %collective-permute-start.24) | collective-permute-done | bytes 917536 | tf_op jit(solution)/shard_map/ppermute | solution.py:20
  140.1 17.8 %collective-permute-done.9 = bf16[2,64,3584]{2,1,0:T(8,128)(2,1)S(1)} collective-permute-done((bf16[2,64,3584]{2,1,0:T(8,128)(2,1)S(1)}, bf16[2,64,3584]{2,1,0:T(8,128)(2,1)S(1)}, u32[]{:S(2)}, u32[]{:S(2)}) %collective-permute-start.9) | collective-permute-done | bytes 917536 | tf_op jit(solution)/shard_map/ppermute | solution.py:20
  159.8 8.0 %collective-permute-done.40.refs_1_ = bf16[64,3584]{1,0:T(8,128)(2,1)S(1)} collective-permute-done((bf16[64,3584]{1,0:T(8,128)(2,1)S(1)}, bf16[64,3584]{1,0:T(8,128)(2,1)S(1)}, u32[]{:S(2)}, u32[]{:S(2)}) %collective-permute-start.40) | collective-permute-done | bytes 458784 | tf_op jit(solution)/shard_map/ppermute | solution.py:16
  167.8 8.9 %shard_map.89 = (f32[32,2048]{1,0:T(8,128)S(1)}, bf16[32,2048]{1,0:T(8,128)(2,1)S(1)}, bf16[32,2048]{1,0:T(8,128)(2,1)S(1)}, bf16[32,2048]{1,0:T(8,128)(2,1)S(1)}) custom-call(s32[1]{0:T(128)} %bitcast.rank_ref, bf16[64,3584]{1,0:T(8,128)(2,1)S(1)} %fusion.5.refs_0_, bf16[64,3584]{1,0:T(8,128)(2,1)S(1)} %collective-permute-done.40.refs_1_, ...), custom_call_target="tpu_custom_call" | custom-call | flops 1879048192 | bytes 16121856 | tf_op jit(solution)/shard_map/pallas_call | solution.py:111
  180.5 8.9 %shard_map.92 = (f32[32,2048]{1,0:T(8,128)S(1)}, bf16[32,2048]{1,0:T(8,128)(2,1)S(1)}, bf16[32,2048]{1,0:T(8,128)(2,1)S(1)}, bf16[32,2048]{1,0:T(8,128)(2,1)S(1)}) custom-call(s32[1]{0:T(128)} %bitcast.rank_ref, bf16[64,3584]{1,0:T(8,128)(2,1)S(1)} %fusion.3.refs_0_, bf16[64,3584]{1,0:T(8,128)(2,1)S(1)} %collective-permute-done.55.refs_1_, ...), custom_call_target="tpu_custom_call" | custom-call | flops 1879048192 | bytes 16121856 | tf_op jit(solution)/shard_map/pallas_call | solution.py:111
  190.2 8.9 %shard_map.86 = (f32[32,2048]{1,0:T(8,128)S(1)}, bf16[32,2048]{1,0:T(8,128)(2,1)S(1)}, bf16[32,2048]{1,0:T(8,128)(2,1)S(1)}, bf16[32,2048]{1,0:T(8,128)(2,1)S(1)}) custom-call(s32[1]{0:T(128)} %bitcast.rank_ref, bf16[64,3584]{1,0:T(8,128)(2,1)S(1)} %fusion.7.refs_0_, bf16[64,3584]{1,0:T(8,128)(2,1)S(1)} %collective-permute-done.25.refs_1_, ...), custom_call_target="tpu_custom_call" | custom-call | flops 1879048192 | bytes 16121856 | tf_op jit(solution)/shard_map/pallas_call | solution.py:111
  200.6 8.9 %shard_map.83 = (f32[32,2048]{1,0:T(8,128)S(1)}, bf16[32,2048]{1,0:T(8,128)(2,1)S(1)}, bf16[32,2048]{1,0:T(8,128)(2,1)S(1)}, bf16[32,2048]{1,0:T(8,128)(2,1)S(1)}) custom-call(s32[1]{0:T(128)} %bitcast.rank_ref, bf16[64,3584]{1,0:T(8,128)(2,1)S(1)} %fusion.9.refs_0_, bf16[64,3584]{1,0:T(8,128)(2,1)S(1)} %collective-permute-done.10.refs_1_, ...), custom_call_target="tpu_custom_call" | custom-call | flops 1879048192 | bytes 16121856 | tf_op jit(solution)/shard_map/pallas_call | solution.py:111
  218.9 4.7 %collective-permute-start.12 = (bf16[32,2048]{1,0:T(8,128)(2,1)S(1)}, bf16[32,2048]{1,0:T(8,128)(2,1)S(1)}, u32[]{:S(2)}, u32[]{:S(2)}) collective-permute-start(bf16[32,2048]{1,0:T(8,128)(2,1)S(1)} %get-tuple-element.41), channel_id=1, source_target_pairs={{0,8},{4,12},{8,0},{12,4},{1,9},{5,13},{9,1},{13,5},{2,10},{6,14},... | collective-permute-start | bytes 393224 | tf_op jit(solution)/shard_map/ppermute | solution.py:20
  227.6 5.4 %collective-permute-done.27 = bf16[32,2048]{1,0:T(8,128)(2,1)S(1)} collective-permute-done((bf16[32,2048]{1,0:T(8,128)(2,1)S(1)}, bf16[32,2048]{1,0:T(8,128)(2,1)S(1)}, u32[]{:S(2)}, u32[]{:S(2)}) %collective-permute-start.27) | collective-permute-done | bytes 131104 | tf_op jit(solution)/shard_map/ppermute | solution.py:20
  242.4 6.3 %collective-permute-start.60 = (bf16[32,2048]{1,0:T(8,128)(2,1)S(1)}, bf16[32,2048]{1,0:T(8,128)(2,1)S(1)}, u32[]{:S(2)}, u32[]{:S(2)}) collective-permute-start(bf16[32,2048]{1,0:T(8,128)(2,1)S(1)} %add_convert_fusion.refs_0_), channel_id=1, source_target_pairs={{8,0},{12,4},{0,8},{4,12},{9,1},{13,5},{1,9},{5,13},{10,2},{14,6},... | collective-permute-start | bytes 393224 | tf_op jit(solution)/shard_map/ppermute | solution.py:16
  252.6 7.2 %collective-permute-start.30 = (bf16[32,2048]{1,0:T(8,128)(2,1)S(1)}, bf16[32,2048]{1,0:T(8,128)(2,1)S(1)}, u32[]{:S(2)}, u32[]{:S(2)}) collective-permute-start(bf16[32,2048]{1,0:T(8,128)(2,1)S(1)} %add_convert_fusion.2.refs_0_), channel_id=1, source_target_pairs={{8,0},{12,4},{0,8},{4,12},{9,1},{13,5},{1,9},{5,13},{10,2},{14,6},... | collective-permute-start | bytes 393224 | tf_op jit(solution)/shard_map/ppermute | solution.py:16
  259.7 9.4 %shard_map.90 = (f32[64,4096]{1,0:T(8,128)S(1)}, f32[64,4096]{1,0:T(8,128)S(1)}) custom-call(s32[1]{0:T(128)} %bitcast.rank_ref, bf16[32,2048]{1,0:T(8,128)(2,1)S(1)} %add_convert_fusion.1.refs_0_, bf16[32,2048]{1,0:T(8,128)(2,1)S(1)} %collective-permute-done.44.refs_1_, bf16[32,2048]{1,0:T(8,128)(2,1)S(1)} %collective-permute-done.45.refs_2_, ...), custom_call_target="tpu_custom_call" | custom-call | flops 2147483648 | bytes 18350080 | tf_op jit(solution)/shard_map/pallas_call | solution.py:156
  272.2 9.4 %shard_map.93 = (f32[64,4096]{1,0:T(8,128)S(1)}, f32[64,4096]{1,0:T(8,128)S(1)}) custom-call(s32[1]{0:T(128)} %bitcast.rank_ref, bf16[32,2048]{1,0:T(8,128)(2,1)S(1)} %add_convert_fusion.refs_0_, bf16[32,2048]{1,0:T(8,128)(2,1)S(1)} %collective-permute-done.59.refs_1_, bf16[32,2048]{1,0:T(8,128)(2,1)S(1)} %collective-permute-done.60.refs_2_, ...), custom_call_target="tpu_custom_call" | custom-call | flops 2147483648 | bytes 18350080 | tf_op jit(solution)/shard_map/pallas_call | solution.py:156
  285.4 9.4 %shard_map.87 = (f32[64,4096]{1,0:T(8,128)S(1)}, f32[64,4096]{1,0:T(8,128)S(1)}) custom-call(s32[1]{0:T(128)} %bitcast.rank_ref, bf16[32,2048]{1,0:T(8,128)(2,1)S(1)} %add_convert_fusion.2.refs_0_, bf16[32,2048]{1,0:T(8,128)(2,1)S(1)} %collective-permute-done.29.refs_1_, bf16[32,2048]{1,0:T(8,128)(2,1)S(1)} %collective-permute-done.30.refs_2_, ...), custom_call_target="tpu_custom_call" | custom-call | flops 2147483648 | bytes 18350080 | tf_op jit(solution)/shard_map/pallas_call | solution.py:156
  294.9 9.4 %shard_map.84 = (f32[64,4096]{1,0:T(8,128)S(1)}, f32[64,4096]{1,0:T(8,128)S(1)}) custom-call(s32[1]{0:T(128)} %bitcast.rank_ref, bf16[32,2048]{1,0:T(8,128)(2,1)S(1)} %add_convert_fusion.3.refs_0_, bf16[32,2048]{1,0:T(8,128)(2,1)S(1)} %collective-permute-done.14.refs_1_, bf16[32,2048]{1,0:T(8,128)(2,1)S(1)} %collective-permute-done.15.refs_2_, ...), custom_call_target="tpu_custom_call" | custom-call | flops 2147483648 | bytes 18350080 | tf_op jit(solution)/shard_map/pallas_call | solution.py:156
  310.6 4.3 %collective-permute-done.48 = bf16[32,4096]{1,0:T(8,128)(2,1)S(1)} collective-permute-done((bf16[32,4096]{1,0:T(8,128)(2,1)S(1)}, bf16[32,4096]{1,0:T(8,128)(2,1)S(1)}, u32[]{:S(2)}, u32[]{:S(2)}) %collective-permute-start.48) | collective-permute-done | bytes 262176 | tf_op jit(solution)/shard_map/ppermute | solution.py:20
  314.9 5.6 %collective-permute-done.63 = bf16[32,4096]{1,0:T(8,128)(2,1)S(1)} collective-permute-done((bf16[32,4096]{1,0:T(8,128)(2,1)S(1)}, bf16[32,4096]{1,0:T(8,128)(2,1)S(1)}, u32[]{:S(2)}, u32[]{:S(2)}) %collective-permute-start.63) | collective-permute-done | bytes 262176 | tf_op jit(solution)/shard_map/ppermute | solution.py:20
  320.5 5.6 %collective-permute-done.33 = bf16[32,4096]{1,0:T(8,128)(2,1)S(1)} collective-permute-done((bf16[32,4096]{1,0:T(8,128)(2,1)S(1)}, bf16[32,4096]{1,0:T(8,128)(2,1)S(1)}, u32[]{:S(2)}, u32[]{:S(2)}) %collective-permute-start.33) | collective-permute-done | bytes 262176 | tf_op jit(solution)/shard_map/ppermute | solution.py:20
  326.1 5.1 %collective-permute-done.18 = bf16[32,4096]{1,0:T(8,128)(2,1)S(1)} collective-permute-done((bf16[32,4096]{1,0:T(8,128)(2,1)S(1)}, bf16[32,4096]{1,0:T(8,128)(2,1)S(1)}, u32[]{:S(2)}, u32[]{:S(2)}) %collective-permute-start.18) | collective-permute-done | bytes 262176 | tf_op jit(solution)/shard_map/ppermute | solution.py:20
  (189 shorter events, 114.0 us)
Async XLA Ops:
  9.1 32.4 %collective-permute-start.20 = (bf16[32,1024]{1,0:T(8,128)(2,1)S(1)}, bf16[32,1024]{1,0:T(8,128)(2,1)S(1)}, u32[]{:S(2)}, u32[]{:S(2)}) collective-permute-start(bf16[32,1024]{1,0:T(8,128)(2,1)S(1)} %get-tuple-element.72), channel_id=1, source_target_pairs={{8,0},{12,4},{0,8},{4,12},{9,1},{13,5},{1,9},{5,13},{10,2},{14,6},... | collective-permute-start | bytes 196616 | tf_op jit(solution)/shard_map/ppermute | solution.py:16
  14.9 28.8 %collective-permute-start.21 = (bf16[32,1024]{1,0:T(8,128)(2,1)S(1)}, bf16[32,1024]{1,0:T(8,128)(2,1)S(1)}, u32[]{:S(2)}, u32[]{:S(2)}) collective-permute-start(bf16[32,1024]{1,0:T(8,128)(2,1)S(1)} %get-tuple-element.72), channel_id=1, source_target_pairs={{12,0},{0,4},{4,8},{8,12},{13,1},{1,5},{5,9},{9,13},{14,2},{2,6},{... | collective-permute-start | bytes 196616 | tf_op jit(solution)/shard_map/ppermute | solution.py:16
  75.7 51.5 %collective-permute-start.39 = (bf16[2,64,3584]{2,1,0:T(8,128)(2,1)S(1)}, bf16[2,64,3584]{2,1,0:T(8,128)(2,1)S(1)}, u32[]{:S(2)}, u32[]{:S(2)}) collective-permute-start(bf16[2,64,3584]{2,1,0:T(8,128)(2,1)S(1)} %get-tuple-element.54), channel_id=1, source_target_pairs={{0,2},{2,0},{1,3},{3,1},{4,6},{6,4},{5,7},{7,5},{8,10},{10,8},{9,1... | collective-permute-start | bytes 2752520 | tf_op jit(solution)/shard_map/ppermute | solution.py:20
  92.8 36.2 %collective-permute-start.54 = (bf16[2,64,3584]{2,1,0:T(8,128)(2,1)S(1)}, bf16[2,64,3584]{2,1,0:T(8,128)(2,1)S(1)}, u32[]{:S(2)}, u32[]{:S(2)}) collective-permute-start(bf16[2,64,3584]{2,1,0:T(8,128)(2,1)S(1)} %get-tuple-element.62), channel_id=1, source_target_pairs={{0,2},{2,0},{1,3},{3,1},{4,6},{6,4},{5,7},{7,5},{8,10},{10,8},{9,1... | collective-permute-start | bytes 2752520 | tf_op jit(solution)/shard_map/ppermute | solution.py:20
  109.3 28.9 %collective-permute-start.24 = (bf16[2,64,3584]{2,1,0:T(8,128)(2,1)S(1)}, bf16[2,64,3584]{2,1,0:T(8,128)(2,1)S(1)}, u32[]{:S(2)}, u32[]{:S(2)}) collective-permute-start(bf16[2,64,3584]{2,1,0:T(8,128)(2,1)S(1)} %get-tuple-element.46), channel_id=1, source_target_pairs={{0,2},{2,0},{1,3},{3,1},{4,6},{6,4},{5,7},{7,5},{8,10},{10,8},{9,1... | collective-permute-start | bytes 2752520 | tf_op jit(solution)/shard_map/ppermute | solution.py:20
  126.4 31.5 %collective-permute-start.9 = (bf16[2,64,3584]{2,1,0:T(8,128)(2,1)S(1)}, bf16[2,64,3584]{2,1,0:T(8,128)(2,1)S(1)}, u32[]{:S(2)}, u32[]{:S(2)}) collective-permute-start(bf16[2,64,3584]{2,1,0:T(8,128)(2,1)S(1)} %get-tuple-element.38), channel_id=1, source_target_pairs={{0,2},{2,0},{1,3},{3,1},{4,6},{6,4},{5,7},{7,5},{8,10},{10,8},{9,1... | collective-permute-start | bytes 2752520 | tf_op jit(solution)/shard_map/ppermute | solution.py:20
  127.7 40.1 %collective-permute-start.40 = (bf16[64,3584]{1,0:T(8,128)(2,1)S(1)}, bf16[64,3584]{1,0:T(8,128)(2,1)S(1)}, u32[]{:S(2)}, u32[]{:S(2)}) collective-permute-start(bf16[64,3584]{1,0:T(8,128)(2,1)S(1)} %fusion.5.refs_0_), channel_id=1, source_target_pairs={{2,0},{0,2},{3,1},{1,3},{6,4},{4,6},{7,5},{5,7},{10,8},{8,10},{11,... | collective-permute-start | bytes 1376264 | tf_op jit(solution)/shard_map/ppermute | solution.py:16
  129.5 48.2 %collective-permute-start.55 = (bf16[64,3584]{1,0:T(8,128)(2,1)S(1)}, bf16[64,3584]{1,0:T(8,128)(2,1)S(1)}, u32[]{:S(2)}, u32[]{:S(2)}) collective-permute-start(bf16[64,3584]{1,0:T(8,128)(2,1)S(1)} %fusion.3.refs_0_), channel_id=1, source_target_pairs={{2,0},{0,2},{3,1},{1,3},{6,4},{4,6},{7,5},{5,7},{10,8},{8,10},{11,... | collective-permute-start | bytes 1376264 | tf_op jit(solution)/shard_map/ppermute | solution.py:16
  138.7 50.7 %collective-permute-start.25 = (bf16[64,3584]{1,0:T(8,128)(2,1)S(1)}, bf16[64,3584]{1,0:T(8,128)(2,1)S(1)}, u32[]{:S(2)}, u32[]{:S(2)}) collective-permute-start(bf16[64,3584]{1,0:T(8,128)(2,1)S(1)} %fusion.7.refs_0_), channel_id=1, source_target_pairs={{2,0},{0,2},{3,1},{1,3},{6,4},{4,6},{7,5},{5,7},{10,8},{8,10},{11,... | collective-permute-start | bytes 1376264 | tf_op jit(solution)/shard_map/ppermute | solution.py:16
  158.4 40.7 %collective-permute-start.10 = (bf16[64,3584]{1,0:T(8,128)(2,1)S(1)}, bf16[64,3584]{1,0:T(8,128)(2,1)S(1)}, u32[]{:S(2)}, u32[]{:S(2)}) collective-permute-start(bf16[64,3584]{1,0:T(8,128)(2,1)S(1)} %fusion.9.refs_0_), channel_id=1, source_target_pairs={{2,0},{0,2},{3,1},{1,3},{6,4},{4,6},{7,5},{5,7},{10,8},{8,10},{11,... | collective-permute-start | bytes 1376264 | tf_op jit(solution)/shard_map/ppermute | solution.py:16
  176.6 32.9 %collective-permute-start.41 = (bf16[32,2048]{1,0:T(8,128)(2,1)S(1)}, bf16[32,2048]{1,0:T(8,128)(2,1)S(1)}, u32[]{:S(2)}, u32[]{:S(2)}) collective-permute-start(bf16[32,2048]{1,0:T(8,128)(2,1)S(1)} %get-tuple-element.56), channel_id=1, source_target_pairs={{0,4},{4,8},{8,12},{12,0},{1,5},{5,9},{9,13},{13,1},{2,6},{6,10},{... | collective-permute-start | bytes 393224 | tf_op jit(solution)/shard_map/ppermute | solution.py:20
  176.7 35.7 %collective-permute-start.42 = (bf16[32,2048]{1,0:T(8,128)(2,1)S(1)}, bf16[32,2048]{1,0:T(8,128)(2,1)S(1)}, u32[]{:S(2)}, u32[]{:S(2)}) collective-permute-start(bf16[32,2048]{1,0:T(8,128)(2,1)S(1)} %get-tuple-element.57), channel_id=1, source_target_pairs={{0,8},{4,12},{8,0},{12,4},{1,9},{5,13},{9,1},{13,5},{2,10},{6,14},... | collective-permute-start | bytes 393224 | tf_op jit(solution)/shard_map/ppermute | solution.py:20
  177.7 34.8 %collective-permute-start.43 = (bf16[32,2048]{1,0:T(8,128)(2,1)S(1)}, bf16[32,2048]{1,0:T(8,128)(2,1)S(1)}, u32[]{:S(2)}, u32[]{:S(2)}) collective-permute-start(bf16[32,2048]{1,0:T(8,128)(2,1)S(1)} %get-tuple-element.58), channel_id=1, source_target_pairs={{0,12},{4,0},{8,4},{12,8},{1,13},{5,1},{9,5},{13,9},{2,14},{6,2},{... | collective-permute-start | bytes 393224 | tf_op jit(solution)/shard_map/ppermute | solution.py:20
  189.4 24.1 %collective-permute-start.56 = (bf16[32,2048]{1,0:T(8,128)(2,1)S(1)}, bf16[32,2048]{1,0:T(8,128)(2,1)S(1)}, u32[]{:S(2)}, u32[]{:S(2)}) collective-permute-start(bf16[32,2048]{1,0:T(8,128)(2,1)S(1)} %get-tuple-element.64), channel_id=1, source_target_pairs={{0,4},{4,8},{8,12},{12,0},{1,5},{5,9},{9,13},{13,1},{2,6},{6,10},{... | collective-permute-start | bytes 393224 | tf_op jit(solution)/shard_map/ppermute | solution.py:20
  218.9 22.1 %collective-permute-start.12 = (bf16[32,2048]{1,0:T(8,128)(2,1)S(1)}, bf16[32,2048]{1,0:T(8,128)(2,1)S(1)}, u32[]{:S(2)}, u32[]{:S(2)}) collective-permute-start(bf16[32,2048]{1,0:T(8,128)(2,1)S(1)} %get-tuple-element.41), channel_id=1, source_target_pairs={{0,8},{4,12},{8,0},{12,4},{1,9},{5,13},{9,1},{13,5},{2,10},{6,14},... | collective-permute-start | bytes 393224 | tf_op jit(solution)/shard_map/ppermute | solution.py:20
  241.0 28.2 %collective-permute-start.61 = (bf16[32,2048]{1,0:T(8,128)(2,1)S(1)}, bf16[32,2048]{1,0:T(8,128)(2,1)S(1)}, u32[]{:S(2)}, u32[]{:S(2)}) collective-permute-start(bf16[32,2048]{1,0:T(8,128)(2,1)S(1)} %add_convert_fusion.refs_0_), channel_id=1, source_target_pairs={{12,0},{0,4},{4,8},{8,12},{13,1},{1,5},{5,9},{9,13},{14,2},{2,6},{... | collective-permute-start | bytes 393224 | tf_op jit(solution)/shard_map/ppermute | solution.py:16
  242.4 29.2 %collective-permute-start.60 = (bf16[32,2048]{1,0:T(8,128)(2,1)S(1)}, bf16[32,2048]{1,0:T(8,128)(2,1)S(1)}, u32[]{:S(2)}, u32[]{:S(2)}) collective-permute-start(bf16[32,2048]{1,0:T(8,128)(2,1)S(1)} %add_convert_fusion.refs_0_), channel_id=1, source_target_pairs={{8,0},{12,4},{0,8},{4,12},{9,1},{13,5},{1,9},{5,13},{10,2},{14,6},... | collective-permute-start | bytes 393224 | tf_op jit(solution)/shard_map/ppermute | solution.py:16
  248.8 22.8 %collective-permute-start.59 = (bf16[32,2048]{1,0:T(8,128)(2,1)S(1)}, bf16[32,2048]{1,0:T(8,128)(2,1)S(1)}, u32[]{:S(2)}, u32[]{:S(2)}) collective-permute-start(bf16[32,2048]{1,0:T(8,128)(2,1)S(1)} %add_convert_fusion.refs_0_), channel_id=1, source_target_pairs={{4,0},{8,4},{12,8},{0,12},{5,1},{9,5},{13,9},{1,13},{6,2},{10,6},{... | collective-permute-start | bytes 393224 | tf_op jit(solution)/shard_map/ppermute | solution.py:16
  252.1 29.5 %collective-permute-start.31 = (bf16[32,2048]{1,0:T(8,128)(2,1)S(1)}, bf16[32,2048]{1,0:T(8,128)(2,1)S(1)}, u32[]{:S(2)}, u32[]{:S(2)}) collective-permute-start(bf16[32,2048]{1,0:T(8,128)(2,1)S(1)} %add_convert_fusion.2.refs_0_), channel_id=1, source_target_pairs={{12,0},{0,4},{4,8},{8,12},{13,1},{1,5},{5,9},{9,13},{14,2},{2,6},{... | collective-permute-start | bytes 393224 | tf_op jit(solution)/shard_map/ppermute | solution.py:16
  252.6 32.3 %collective-permute-start.30 = (bf16[32,2048]{1,0:T(8,128)(2,1)S(1)}, bf16[32,2048]{1,0:T(8,128)(2,1)S(1)}, u32[]{:S(2)}, u32[]{:S(2)}) collective-permute-start(bf16[32,2048]{1,0:T(8,128)(2,1)S(1)} %add_convert_fusion.2.refs_0_), channel_id=1, source_target_pairs={{8,0},{12,4},{0,8},{4,12},{9,1},{13,5},{1,9},{5,13},{10,2},{14,6},... | collective-permute-start | bytes 393224 | tf_op jit(solution)/shard_map/ppermute | solution.py:16
  271.5 23.2 %collective-permute-start.16 = (bf16[32,2048]{1,0:T(8,128)(2,1)S(1)}, bf16[32,2048]{1,0:T(8,128)(2,1)S(1)}, u32[]{:S(2)}, u32[]{:S(2)}) collective-permute-start(bf16[32,2048]{1,0:T(8,128)(2,1)S(1)} %add_convert_fusion.3.refs_0_), channel_id=1, source_target_pairs={{12,0},{0,4},{4,8},{8,12},{13,1},{1,5},{5,9},{9,13},{14,2},{2,6},{... | collective-permute-start | bytes 393224 | tf_op jit(solution)/shard_map/ppermute | solution.py:16
  271.6 23.4 %collective-permute-start.15 = (bf16[32,2048]{1,0:T(8,128)(2,1)S(1)}, bf16[32,2048]{1,0:T(8,128)(2,1)S(1)}, u32[]{:S(2)}, u32[]{:S(2)}) collective-permute-start(bf16[32,2048]{1,0:T(8,128)(2,1)S(1)} %add_convert_fusion.3.refs_0_), channel_id=1, source_target_pairs={{8,0},{12,4},{0,8},{4,12},{9,1},{13,5},{1,9},{5,13},{10,2},{14,6},... | collective-permute-start | bytes 393224 | tf_op jit(solution)/shard_map/ppermute | solution.py:16
  284.9 22.9 %collective-permute-start.62 = (f32[64,4096]{1,0:T(8,128)S(1)}, f32[64,4096]{1,0:T(8,128)S(1)}, u32[]{:S(2)}, u32[]{:S(2)}) collective-permute-start(f32[64,4096]{1,0:T(8,128)S(1)} %get-tuple-element.68), channel_id=1, source_target_pairs={{0,1},{1,0},{2,3},{3,2},{4,5},{5,4},{6,7},{7,6},{8,9},{9,8},{10,11... | collective-permute-start | bytes 3145736 | tf_op jit(solution)/shard_map/ppermute | solution.py:20
  310.5 20.7 %collective-permute-start.18 = (bf16[32,4096]{1,0:T(8,128)(2,1)S(1)}, bf16[32,4096]{1,0:T(8,128)(2,1)S(1)}, u32[]{:S(2)}, u32[]{:S(2)}) collective-permute-start(bf16[32,4096]{1,0:T(8,128)(2,1)S(1)} %slice.215), channel_id=1, source_target_pairs={{0,2},{2,0},{1,3},{3,1},{4,6},{6,4},{5,7},{7,5},{8,10},{10,8},{9,1... | collective-permute-start | bytes 786440 | tf_op jit(solution)/shard_map/ppermute | solution.py:20
  (44 other events, 505.1 us)

commit v2 on v1

v2 whole, which is shorter than its diff:
```python
import functools

import jax
import jax.numpy as jnp
from jax import lax
from jax.experimental import pallas as pl
from jax.experimental.pallas import tpu as pltpu
from jax.sharding import PartitionSpec as P

BF16 = jnp.bfloat16
F32 = jnp.float32
VMEM_BYTES = 28 * 1024 * 1024
BUFFERS = 4


def shift(value, axis, size, hop):
    return lax.ppermute(value, axis, [((d + hop) % size, d) for d in range(size)])


def send(value, axis, size, hop):
    return lax.ppermute(value, axis, [(d, (d + hop) % size) for d in range(size)])


def tile_of(width, most):
    tile = most
    while tile > 128 and width % tile:
        tile //= 2
    return tile if width % tile == 0 else width


def whole(shape):
    return pl.BlockSpec(shape, lambda j, *_: (0,) * len(shape))


def slots_of(tiles):
    return min(BUFFERS, tiles)


def slots(depth, tile, tiles):
    count = slots_of(tiles)
    return [pltpu.VMEM((count, depth, tile), BF16), pltpu.SemaphoreType.DMA((count,))]


def next_block(weight_ref, slot_ref, slot_sems, tiles, first=0):
    step = pl.program_id(0)
    count, _, tile = slot_ref.shape

    def copy(block, slot):
        columns = pl.ds(pl.multiple_of((first + block) * tile, 128), tile)
        return pltpu.make_async_copy(
            weight_ref.at[0, :, columns], slot_ref.at[slot], slot_sems.at[slot]
        )

    @pl.when(step == 0)
    def _():
        for block in range(count - 1):
            copy(block, block).start()

    ahead = step + count - 1

    @pl.when(ahead < tiles)
    def _():
        copy(ahead, lax.rem(ahead, count)).start()

    slot = lax.rem(step, count)
    copy(step, slot).wait()
    return slot_ref.at[slot]


def in_place(count):
    return [pl.BlockSpec(memory_space=pl.ANY)] * count


def params():
    return pltpu.CompilerParams(
        dimension_semantics=("arbitrary",), vmem_limit_bytes=VMEM_BYTES
    )


def cost(rows, depth, width):
    return pl.CostEstimate(
        flops=2 * rows * depth * width,
        bytes_accessed=2 * (rows * depth + depth * width + rows * width),
        transcendentals=0,
    )


def gate_up_body(owners, tiles, first, x_ref, gate_ref, up_ref, *refs):
    out_refs = refs[-4 - owners : -4]
    rows = x_ref.shape[0] // owners
    blocks = [
        next_block(gate_ref, refs[-4], refs[-3], tiles, first),
        next_block(up_ref, refs[-2], refs[-1], tiles, first),
    ]
    x = x_ref[...]
    for at, block_ref in enumerate(blocks):
        acts = jnp.dot(x, block_ref[...], preferred_element_type=F32)
        for hop in range(owners):
            taken = acts[hop * rows : (hop + 1) * rows]
            out_refs[hop][at] = taken.astype(out_refs[hop].dtype)


def gate_up(x, gate_weight, up_weight, owners, piece, pieces, after):
    rows, depth = x.shape
    width = gate_weight.shape[2] // pieces
    tile = tile_of(width, 256)
    tiles = width // tile
    own_rows = rows // owners
    return pl.pallas_call(
        functools.partial(gate_up_body, owners, tiles, piece * tiles),
        grid=(tiles,),
        in_specs=[whole((rows, depth))] + in_place(2 + len(after)),
        out_specs=[pl.BlockSpec((2, own_rows, tile), lambda j: (0, 0, j))] * owners,
        out_shape=[jax.ShapeDtypeStruct((2, own_rows, width), F32)]
        + [jax.ShapeDtypeStruct((2, own_rows, width), BF16)] * (owners - 1),
        scratch_shapes=slots(depth, tile, tiles) * 2,
        compiler_params=params(),
        cost_estimate=cost(rows, depth, 2 * width),
    )(x, gate_weight, up_weight, *after)


def down_body(owners, members, pieces, ranks, tiles, rank_ref, *refs):
    hidden_refs = refs[: owners * pieces]
    weight_ref = refs[owners * pieces]
    out_refs = refs[-4 - ranks : -4]
    lhs_ref, acc_ref, slot_ref, slot_sems = refs[-4:]
    block_ref = next_block(weight_ref, slot_ref, slot_sems, tiles)
    q = hidden_refs[0].shape[0] // members
    part = hidden_refs[0].shape[1]
    block = acc_ref.shape[0] // ranks

    @pl.when(pl.program_id(0) == 0)
    def _():
        for owner in range(owners):
            for piece in range(pieces):
                for member in range(members):
                    row = (member * owners + owner) * q
                    lhs_ref[row : row + q, piece * part : (piece + 1) * part] = hidden_refs[
                        owner * pieces + piece
                    ][member * q : (member + 1) * q]

    acc_ref[...] = jnp.dot(lhs_ref[...], block_ref[...], preferred_element_type=F32)
    for hop in range(ranks):
        at = lax.rem(rank_ref[0] + hop, ranks) * block
        taken = acc_ref[pl.ds(pl.multiple_of(at, block), block), :]
        out_refs[hop][...] = taken.astype(out_refs[hop].dtype)


def down(rank, hidden, down_weight, members, ranks, after):
    owners, pieces = len(hidden), len(hidden[0])
    rows_each, part = hidden[0][0].shape
    rows, depth, width = owners * rows_each, pieces * part, down_weight.shape[2]
    tile = tile_of(width, 256)
    block = rows // ranks
    return pl.pallas_call(
        functools.partial(down_body, owners, members, pieces, ranks, width // tile),
        grid_spec=pltpu.PrefetchScalarGridSpec(
            num_scalar_prefetch=1,
            grid=(width // tile,),
            in_specs=[whole((rows_each, part))] * (owners * pieces)
            + in_place(1 + len(after)),
            out_specs=[pl.BlockSpec((block, tile), lambda j, *_: (0, j))] * ranks,
            scratch_shapes=[pltpu.VMEM((rows, depth), BF16), pltpu.VMEM((rows, tile), F32)]
            + slots(depth, tile, width // tile),
        ),
        out_shape=[jax.ShapeDtypeStruct((block, width), F32)]
        + [jax.ShapeDtypeStruct((block, width), BF16)] * (ranks - 1),
        compiler_params=params(),
        cost_estimate=cost(rows, depth, width),
    )(rank, *[piece for of_owner in hidden for piece in of_owner], down_weight, *after)


def encode_body(members, ranks, tiles, rank_ref, *refs):
    block_refs = refs[:ranks]
    weight_ref = refs[ranks]
    out_refs = refs[-3 - members : -3]
    lhs_ref, slot_ref, slot_sems = refs[-3:]
    weight_block = next_block(weight_ref, slot_ref, slot_sems, tiles)
    block = block_refs[0].shape[0]

    @pl.when(pl.program_id(0) == 0)
    def _():
        for hop in range(ranks):
            at = lax.rem(rank_ref[0] + hop, ranks) * block
            lhs_ref[pl.ds(pl.multiple_of(at, block), block), :] = block_refs[hop][...]

    pre = jnp.dot(lhs_ref[...], weight_block[...], preferred_element_type=F32)
    rows = pre.shape[0] // members
    for member in range(members):
        taken = pre[member * rows : (member + 1) * rows]
        out_refs[member][...] = taken.astype(out_refs[member].dtype)


def encode(rank, blocks, enc_weight, members, after):
    ranks = len(blocks)
    block, depth = blocks[0].shape
    width = enc_weight.shape[2]
    rows = block * ranks
    rows_each = rows // members
    tile = tile_of(width, 512)
    return pl.pallas_call(
        functools.partial(encode_body, members, ranks, width // tile),
        grid_spec=pltpu.PrefetchScalarGridSpec(
            num_scalar_prefetch=1,
            grid=(width // tile,),
            in_specs=[whole((block, depth))] * ranks
            + in_place(1 + len(after)),
            out_specs=[pl.BlockSpec((rows_each, tile), lambda j, *_: (0, j))] * members,
            scratch_shapes=[pltpu.VMEM((rows, depth), BF16)] + slots(depth, tile, width // tile),
        ),
        out_shape=[jax.ShapeDtypeStruct((rows_each, width), F32)]
        + [jax.ShapeDtypeStruct((rows_each, width), BF16)] * (members - 1),
        compiler_params=params(),
        cost_estimate=cost(rows, depth, width),
    )(rank, *blocks, enc_weight, *after)


def chunk_rows(total, unit):
    units = total // unit
    if units < 8:
        return [total]
    eighth = units // 8
    sizes = [2 * eighth, 3 * eighth, 2 * eighth]
    return [size * unit for size in sizes + [units - sum(sizes)]]


def on_device(
    owners, members, ranks, tokens, norm_gain, gate_weight, up_weight, down_weight, enc_weight,
    enc_bias, adjoint,
):
    row_at = lax.axis_index("rows")
    member_at = lax.axis_index("mp")
    rank_at = lax.axis_index("hid")
    rank = rank_at.astype(jnp.int32).reshape(1)
    per_device = adjoint.shape[0]
    cut = tokens.shape[1]
    half_cuts = ranks // owners
    model_width = cut * ranks

    gain = lax.dynamic_slice_in_dim(
        norm_gain[0], row_at * (model_width // owners), model_width // owners, 0
    ).reshape(half_cuts, 1, cut)
    own_tokens = lax.dynamic_slice_in_dim(tokens, member_at * per_device, per_device, 0)

    def from_all(value, axis, size):
        return jnp.stack([value] + [shift(value, axis, size, hop) for hop in range(1, size)])

    def normed_rows(gathered, first, q):
        wide = gathered.astype(F32)
        squares = jnp.sum(wide * wide, axis=(0, 2))
        inverse = lax.rsqrt(squares / model_width + 1e-05)
        doubled = jnp.concatenate((gathered, gathered))
        columns = []
        for hop in range(owners):
            target = lax.rem(row_at + owners - hop, owners)
            start = lax.rem(target * half_cuts + ranks - first, ranks)
            half = lax.dynamic_slice_in_dim(doubled, start, half_cuts, 0)
            columns.append(half if hop == 0 else shift(half, "rows", owners, hop))
        inverses = from_all(from_all(inverse, "rows", owners), "mp", members)
        columns = from_all(jnp.stack(columns), "mp", members)
        return columns, inverses

    def normed(columns, inverses):
        scaled = columns.astype(F32) * inverses[:, :, None, :, None] * gain
        ordered = scaled.astype(BF16).transpose(1, 0, 3, 2, 4)
        return ordered.reshape(-1, half_cuts * cut)

    sizes = chunk_rows(per_device, 16 * max(1, ranks // (owners * members)))
    starts = [sum(sizes[:at]) for at in range(len(sizes))]
    chunks = len(sizes)
    head = sizes[0]

    xs = []
    first_columns, first_inverses = normed_rows(
        from_all(own_tokens[:head], "hid", ranks), rank_at, head
    )
    xs.append(normed(first_columns, first_inverses))
    if chunks > 1:
        rest = lax.all_gather(own_tokens[head:], "hid", axis=0)
        rest_columns, rest_inverses = normed_rows(rest, 0, per_device - head)
        for start, q in zip(starts[1:], sizes[1:]):
            rows = slice(start - head, start - head + q)
            xs.append(normed(rest_columns[:, :, :, rows], rest_inverses[:, :, rows]))

    sums, mine, hidden, layer, blocks, outs = ({} for _ in range(6))
    last = []

    def gate_up_of(t):
        pieces = 2 if t == 0 and gate_weight.shape[2] % 512 == 0 else 1
        sums[t] = []
        for piece in range(pieces):
            own, *sends = gate_up(
                xs[t], gate_weight, up_weight, owners, piece, pieces, list(last)
            )
            last[:] = [own]
            others = [send(sends[hop - 1], "rows", owners, hop) for hop in range(1, owners)]
            sums[t].append((own, others))

    def hidden_of(t):
        hidden[t] = [[] for _ in range(owners)]
        for own, others in sums[t]:
            acts = own
            for other in others:
                acts = acts + other.astype(F32)
            units = (jax.nn.silu(acts[0]) * acts[1]).astype(BF16)
            hidden[t][0].append(units)
            for hop in range(1, owners):
                hidden[t][hop].append(shift(units, "rows", owners, hop))
        last[:] = [hidden[t][0][-1]]

    def down_of(t):
        own, *sends = down(rank, hidden[t], down_weight, members, ranks, list(last))
        last[:] = [own]
        layer[t] = (own, [send(sends[hop - 1], "hid", ranks, hop) for hop in range(1, ranks)])

    def blocks_of(t):
        total, others = layer[t]
        for other in others:
            total = total + other.astype(F32)
        block = total.astype(BF16)
        blocks[t] = [block] + [shift(block, "hid", ranks, hop) for hop in range(1, ranks)]
        last[:] = [block]

    def features_of(t):
        own, *sends = encode(rank, blocks[t], enc_weight, members, list(last))
        last[:] = [own]
        start, q = starts[t], sizes[t]
        total = own
        for hop in range(1, members):
            total = total + send(sends[hop - 1], "mp", members, hop).astype(F32)
        pre = total[:q]
        for hop in range(1, owners):
            going = total[hop * q : (hop + 1) * q].astype(BF16)
            pre = pre + send(going, "rows", owners, hop).astype(F32)
        pre = pre + enc_bias[None, :]
        factor = adjoint[start : start + q].astype(F32)
        outs[t] = (jnp.maximum(pre, 0.0) * factor).astype(BF16)

    gate_up_of(0)
    if chunks > 1:
        gate_up_of(1)
    for step in range(chunks + 3):
        for stage, ahead in (
            (hidden_of, 0), (gate_up_of, 2), (down_of, -1), (blocks_of, -2), (features_of, -3)
        ):
            if 0 <= step + ahead < chunks:
                stage(step + ahead)
    return jnp.concatenate([outs[t] for t in range(chunks)], axis=0)


def solution(mesh):
    placed = (
        P(("groups", "rows"), "hid"),
        P("mp", None),
        P("mp", "rows", "hid"),
        P("mp", "rows", "hid"),
        P("mp", "hid", "rows"),
        P("mp", "rows", "hid"),
        P("hid"),
        P(("groups", "rows", "mp"), "hid"),
    )
    sizes = (mesh.shape["rows"], mesh.shape["mp"], mesh.shape["hid"])
    return jax.shard_map(
        functools.partial(on_device, *sizes),
        mesh=mesh,
        in_specs=placed,
        out_specs=P(("groups", "rows", "mp"), "hid"),
        check_vma=False,
    )
```

time: 334 us -> 314 us (0.940)
  Pallas kernels: 136 us -> 90.9 us
  local copies, waits for them, and re-layouts: 6.57 us -> 27.1 us
  starting transfers between devices: 103 us -> 83.1 us
  blocking collectives: 0 us -> 17.8 us
  waiting for transfers between devices: 80.6 us -> 86.8 us
    pallas_call x8 -> x9, Pallas kernels: 101 us -> 65.8 us  [the longest x5 40 us: gate_up(): pl.pallas_call(functools.partial(gate_up_body, owners, tiles, piece * til...]
    ppermute x40 -> x28, starting transfers between devices: 70.1 us -> 44.2 us  [shift(): lax.ppermute(value, axis, [((d + hop) % size, d) for d in range(size)])]
    unnamed x12 -> x37, local copies, waits for them, and re-layouts: 0.48 us -> 23.8 us
    all_gather x0 -> x1, blocking collectives: none -> 17.8 us  [on_device(): rest = lax.all_gather(own_tokens[head:], 'hid', axis=0)]
    ppermute x24 -> x25, waiting for transfers between devices: 55.1 us -> 72.1 us  [send(): lax.ppermute(value, axis, [(d, (d + hop) % size) for d in range(size)])]
    ppermute x40 -> x28, waiting for transfers between devices: 25.5 us -> 14.7 us  [shift(): lax.ppermute(value, axis, [((d + hop) % size, d) for d in range(size)])]
    pallas_call x4, Pallas kernels: 35.4 us -> 25.1 us  [down(): pl.pallas_call(functools.partial(down_body, owners, members, pieces, rank...]
    ppermute x24 -> x25, starting transfers between devices: 32.8 us -> 38.9 us  [send(): lax.ppermute(value, axis, [(d, (d + hop) % size) for d in range(size)])]
  transfers between devices with their start and end apart: 64 -> 53, of which waited for: 20 -> 17; matrix products, arithmetic and copies ran while one was open for 2% -> 3% of each run, Pallas kernels for 36% -> 27%
where the time goes in v2:
time: 314 us; the launch traced here: 313 us
  Pallas kernels  90.9 us (29%)
  waiting for transfers between devices  86.8 us (28%)
  starting transfers between devices  83.1 us (26%)
  local copies, waits for them, and re-layouts  27.1 us (9%)
  blocking collectives  17.8 us (6%)
  other arithmetic  6.89 us (2%)
    ppermute x25, waiting for transfers between devices, send(): lax.ppermute(value, axis, [(d, (d + hop) % size) for d in range(size)])  72.1 us
    ppermute x28, starting transfers between devices, shift(): lax.ppermute(value, axis, [((d + hop) % size, d) for d in range(size)])  44.2 us
    pallas_call x5, Pallas kernels, gate_up(): pl.pallas_call(functools.partial(gate_up_body, owners, tiles, piece * til...  40 us
    ppermute x25, starting transfers between devices, send(): lax.ppermute(value, axis, [(d, (d + hop) % size) for d in range(size)])  38.9 us
    pallas_call x4, Pallas kernels, encode(): pl.pallas_call(functools.partial(encode_body, members, ranks, width // ti...  25.8 us
    pallas_call x4, Pallas kernels, down(): pl.pallas_call(functools.partial(down_body, owners, members, pieces, rank...  25.1 us
    unnamed x37, local copies, waits for them, and re-layouts  23.8 us
    all_gather x1, blocking collectives, on_device(): rest = lax.all_gather(own_tokens[head:], 'hid', axis=0)  17.8 us
  transfers between devices with their start and end apart: 53, of which 17 were waited for; matrix products, arithmetic and copies ran while one was open for 3% of the time, Pallas kernels for 27%

profile of v2, /device:TPU:0, one launch (start us, length us, event | category | flops | bytes accessed | tf_op | source)
XLA Modules:
  0.0 313.3 jit_solution(1587678017282018114)
XLA Ops:
  8.8 17.8 %all-gather = bf16[384,1024]{1,0:T(8,128)(2,1)S(1)} all-gather(bf16[96,1024]{1,0:T(8,128)(2,1)S(1)} %constant_dynamic-slice_fusion.2), channel_id=2, replica_groups=mesh['groups'=2,'hid'=4,'rows'=2,'mp'=2] {'hid'}, dimensions={0}, use_global_device_ids=true | all-gather | bytes 983040 | tf_op jit(solution)/shard_map/all_gather | solution.py:279
  48.1 5.2 %shard_map.82 = (f32[2,64,1792]{2,1,0:T(8,128)S(1)}, bf16[2,64,1792]{2,1,0:T(8,128)(2,1)S(1)}) custom-call(bf16[128,2048]{1,0:T(8,128)(2,1)S(1)} %bitcast.110, bf16[1,2048,3584]{2,1,0:T(8,128)(2,1)S(1)} %copy-done.2, bf16[1,2048,3584]{2,1,0:T(8,128)(2,1)} %up_ref.9), custom_call_target="tpu_custom_call" | custom-call | flops 1879048192 | bytes 16121856 | tf_op jit(solution)/shard_map/pallas_call | solution.py:109
  53.8 5.2 %shard_map.83 = (f32[2,64,1792]{2,1,0:T(8,128)S(1)}, bf16[2,64,1792]{2,1,0:T(8,128)(2,1)S(1)}) custom-call(bf16[128,2048]{1,0:T(8,128)(2,1)S(1)} %bitcast.111, bf16[1,2048,3584]{2,1,0:T(8,128)(2,1)S(1)} %copy-done.2, bf16[1,2048,3584]{2,1,0:T(8,128)(2,1)} %up_ref.9, f32[2,64,1792]{2,1,0:T(8,128)S(1)} %get-tuple-element.39.refs_0_), custom_call_target="tpu_custom_call" | custom-call | flops 1879048192 | bytes 16121856 | tf_op jit(solution)/shard_map/pallas_call | solution.py:109
  60.6 11.0 %shard_map.84 = (f32[2,96,3584]{2,1,0:T(8,128)S(1)}, bf16[2,96,3584]{2,1,0:T(8,128)(2,1)S(1)}) custom-call(bf16[192,2048]{1,0:T(8,128)(2,1)S(1)} %bitcast.112, bf16[1,2048,3584]{2,1,0:T(8,128)(2,1)S(1)} %copy-done.2, bf16[1,2048,3584]{2,1,0:T(8,128)(2,1)} %up_ref.9, f32[2,64,1792]{2,1,0:T(8,128)S(1)} %get-tuple-element.41.refs_0_), custom_call_target="tpu_custom_call" | custom-call | flops 5637144576 | bytes 32899072 | tf_op jit(solution)/shard_map/pallas_call | solution.py:109
  77.3 9.1 %shard_map.87 = (f32[2,64,3584]{2,1,0:T(8,128)S(1)}, bf16[2,64,3584]{2,1,0:T(8,128)(2,1)S(1)}) custom-call(bf16[128,2048]{1,0:T(8,128)(2,1)S(1)} %bitcast.113, bf16[1,2048,3584]{2,1,0:T(8,128)(2,1)S(1)} %copy-done.2, bf16[1,2048,3584]{2,1,0:T(8,128)(2,1)} %up_ref.9, bf16[64,1792]{1,0:T(8,128)(2,1)S(1)} %fusion.23.refs_1_.refs_0_), custom_call_target="tpu_custom_call" | custom-call | flops 3758096384 | bytes 31719424 | tf_op jit(solution)/shard_map/pallas_call | solution.py:109
  87.9 18.0 %collective-permute-done.15 = bf16[2,96,3584]{2,1,0:T(8,128)(2,1)S(1)} collective-permute-done((bf16[2,96,3584]{2,1,0:T(8,128)(2,1)S(1)}, bf16[2,96,3584]{2,1,0:T(8,128)(2,1)S(1)}, u32[]{:S(2)}, u32[]{:S(2)}) %collective-permute-start.15) | collective-permute-done | bytes 1376288 | tf_op jit(solution)/shard_map/ppermute | solution.py:21
  107.2 9.6 %shard_map.85 = (f32[2,32,3584]{2,1,0:T(8,128)S(1)}, bf16[2,32,3584]{2,1,0:T(8,128)(2,1)S(1)}) custom-call(bf16[64,2048]{1,0:T(8,128)(2,1)S(1)} %bitcast.114, bf16[1,2048,3584]{2,1,0:T(8,128)(2,1)S(1)} %copy-done.2, bf16[1,2048,3584]{2,1,0:T(8,128)(2,1)} %up_ref.9, bf16[96,3584]{1,0:T(8,128)(2,1)S(1)} %fusion.1.refs_0_), custom_call_target="tpu_custom_call" | custom-call | flops 1879048192 | bytes 30539776 | tf_op jit(solution)/shard_map/pallas_call | solution.py:109
  116.8 5.2 %copy-done.3 = bf16[1,3584,2048]{2,1,0:T(8,128)(2,1)S(1)} copy-done((bf16[1,3584,2048]{2,1,0:T(8,128)(2,1)S(1)}, bf16[1,3584,2048]{2,1,0:T(8,128)(2,1)}, u32[]{:S(2)}) %copy-start.3) | copy-done | bytes 14680088
  122.0 6.0 %shard_map.86 = (f32[32,2048]{1,0:T(8,128)S(1)}, bf16[32,2048]{1,0:T(8,128)(2,1)S(1)}, bf16[32,2048]{1,0:T(8,128)(2,1)S(1)}, bf16[32,2048]{1,0:T(8,128)(2,1)S(1)}) custom-call(s32[1]{0:T(128)} %bitcast.rank_ref, bf16[64,1792]{1,0:T(8,128)(2,1)S(1)} %fusion.25.refs_0_, bf16[64,1792]{1,0:T(8,128)(2,1)S(1)} %fusion.23.refs_1_.refs_0_, ...), custom_call_target="tpu_custom_call" | custom-call | flops 1879048192 | bytes 16121856 | tf_op jit(solution)/shard_map/pallas_call | solution.py:155
  142.6 26.8 %collective-permute-done.33 = bf16[2,32,3584]{2,1,0:T(8,128)(2,1)S(1)} collective-permute-done((bf16[2,32,3584]{2,1,0:T(8,128)(2,1)S(1)}, bf16[2,32,3584]{2,1,0:T(8,128)(2,1)S(1)}, u32[]{:S(2)}, u32[]{:S(2)}) %collective-permute-start.33) | collective-permute-done | bytes 458784 | tf_op jit(solution)/shard_map/ppermute | solution.py:21
  169.6 5.2 %copy-done.4 = bf16[1,3584,2048]{2,1,0:T(8,128)(2,1)S(1)} copy-done((bf16[1,3584,2048]{2,1,0:T(8,128)(2,1)S(1)}, bf16[1,3584,2048]{2,1,0:T(8,128)(2,1)}, u32[]{:S(2)}) %copy-start.4) | copy-done | bytes 14680088
  174.8 7.1 %shard_map.88 = (f32[48,2048]{1,0:T(8,128)S(1)}, bf16[48,2048]{1,0:T(8,128)(2,1)S(1)}, bf16[48,2048]{1,0:T(8,128)(2,1)S(1)}, bf16[48,2048]{1,0:T(8,128)(2,1)S(1)}) custom-call(s32[1]{0:T(128)} %bitcast.rank_ref, bf16[96,3584]{1,0:T(8,128)(2,1)S(1)} %fusion.1.refs_0_, bf16[96,3584]{1,0:T(8,128)(2,1)S(1)} %collective-permute-done.22.refs_1_, ...), custom_call_target="tpu_custom_call" | custom-call | flops 2818572288 | bytes 16842752 | tf_op jit(solution)/shard_map/pallas_call | solution.py:155
  188.0 5.2 %copy-done.5 = bf16[1,3584,2048]{2,1,0:T(8,128)(2,1)S(1)} copy-done((bf16[1,3584,2048]{2,1,0:T(8,128)(2,1)S(1)}, bf16[1,3584,2048]{2,1,0:T(8,128)(2,1)}, u32[]{:S(2)}) %copy-start.5) | copy-done | bytes 14680088
  193.2 6.0 %shard_map.90 = (f32[32,2048]{1,0:T(8,128)S(1)}, bf16[32,2048]{1,0:T(8,128)(2,1)S(1)}, bf16[32,2048]{1,0:T(8,128)(2,1)S(1)}, bf16[32,2048]{1,0:T(8,128)(2,1)S(1)}) custom-call(s32[1]{0:T(128)} %bitcast.rank_ref, bf16[64,3584]{1,0:T(8,128)(2,1)S(1)} %fusion.3.refs_3_.refs_0_, bf16[64,3584]{1,0:T(8,128)(2,1)S(1)} %collective-permute-done.32.refs_1_, ...), custom_call_target="tpu_custom_call" | custom-call | flops 1879048192 | bytes 16121856 | tf_op jit(solution)/shard_map/pallas_call | solution.py:155
  200.7 7.1 %collective-permute-start.34 = (bf16[32,2048]{1,0:T(8,128)(2,1)S(1)}, bf16[32,2048]{1,0:T(8,128)(2,1)S(1)}, u32[]{:S(2)}, u32[]{:S(2)}) collective-permute-start(bf16[32,2048]{1,0:T(8,128)(2,1)S(1)} %get-tuple-element.60), channel_id=1, source_target_pairs={{0,4},{4,8},{8,12},{12,0},{1,5},{5,9},{9,13},{13,1},{2,6},{6,10},{... | collective-permute-start | bytes 393224 | tf_op jit(solution)/shard_map/ppermute | solution.py:21
  213.5 6.1 %shard_map.89 = (f32[64,4096]{1,0:T(8,128)S(1)}, bf16[64,4096]{1,0:T(8,128)(2,1)S(1)}) custom-call(s32[1]{0:T(128)} %bitcast.rank_ref, bf16[32,2048]{1,0:T(8,128)(2,1)S(1)} %add_convert_fusion.2.refs_0_, bf16[32,2048]{1,0:T(8,128)(2,1)S(1)} %collective-permute-done.19.refs_1_, bf16[32,2048]{1,0:T(8,128)(2,1)S(1)} %collective-permute-done.20.refs_2_, ...), custom_call_target="tpu_custom_call" | custom-call | flops 2147483648 | bytes 18350080 | tf_op jit(solution)/shard_map/pallas_call | solution.py:201
  219.6 5.2 %copy-done.6 = bf16[1,3584,2048]{2,1,0:T(8,128)(2,1)S(1)} copy-done((bf16[1,3584,2048]{2,1,0:T(8,128)(2,1)S(1)}, bf16[1,3584,2048]{2,1,0:T(8,128)(2,1)}, u32[]{:S(2)}) %copy-start.6) | copy-done | bytes 14680088
  224.8 6.0 %shard_map.92 = (f32[16,2048]{1,0:T(8,128)S(1)}, bf16[16,2048]{1,0:T(8,128)(2,1)S(1)}, bf16[16,2048]{1,0:T(8,128)(2,1)S(1)}, bf16[16,2048]{1,0:T(8,128)(2,1)S(1)}) custom-call(s32[1]{0:T(128)} %bitcast.rank_ref, bf16[32,3584]{1,0:T(8,128)(2,1)S(1)} %fusion.21.refs_3_.refs_0_, bf16[32,3584]{1,0:T(8,128)(2,1)S(1)} %collective-permute-done.42.refs_1_, ...), custom_call_target="tpu_custom_call" | custom-call | flops 939524096 | bytes 15400960 | tf_op jit(solution)/shard_map/pallas_call | solution.py:155
  242.0 8.8 %collective-permute-start.50 = (bf16[16,2048]{1,0:T(8,128)(2,1)S(1)}, bf16[16,2048]{1,0:T(8,128)(2,1)S(1)}, u32[]{:S(2)}, u32[]{:S(2)}) collective-permute-start(bf16[16,2048]{1,0:T(8,128)(2,1)S(1)} %add_convert_fusion.3.refs_5_.refs_0_), channel_id=1, source_target_pairs={{12,0},{0,4},{4,8},{8,12},{13,1},{1,5},{5,9},{9,13},{14,2},{2,6},{... | collective-permute-start | bytes 196616 | tf_op jit(solution)/shard_map/ppermute | solution.py:17
  265.3 6.1 %shard_map.93 = (f32[64,4096]{1,0:T(8,128)S(1)}, bf16[64,4096]{1,0:T(8,128)(2,1)S(1)}) custom-call(s32[1]{0:T(128)} %bitcast.rank_ref, bf16[32,2048]{1,0:T(8,128)(2,1)S(1)} %add_convert_fusion.1.refs_5_.refs_0_, bf16[32,2048]{1,0:T(8,128)(2,1)S(1)} %collective-permute-done.39.refs_1_, bf16[32,2048]{1,0:T(8,128)(2,1)S(1)} %collective-permute-done.40.refs_2_, ...), custom_call_target="tpu_custom_call" | custom-call | flops 2147483648 | bytes 18350080 | tf_op jit(solution)/shard_map/pallas_call | solution.py:201
  272.6 6.3 %shard_map.94 = (f32[32,4096]{1,0:T(8,128)S(1)}, bf16[32,4096]{1,0:T(8,128)(2,1)S(1)}) custom-call(s32[1]{0:T(128)} %bitcast.rank_ref, bf16[16,2048]{1,0:T(8,128)(2,1)S(1)} %add_convert_fusion.3.refs_5_.refs_0_, bf16[16,2048]{1,0:T(8,128)(2,1)S(1)} %collective-permute-done.48.refs_1_, bf16[16,2048]{1,0:T(8,128)(2,1)S(1)} %collective-permute-done.49.refs_2_, ...), custom_call_target="tpu_custom_call" | custom-call | flops 1073741824 | bytes 17563648 | tf_op jit(solution)/shard_map/pallas_call | solution.py:201
  279.0 7.2 %shard_map.91 = (f32[96,4096]{1,0:T(8,128)S(1)}, bf16[96,4096]{1,0:T(8,128)(2,1)S(1)}) custom-call(s32[1]{0:T(128)} %bitcast.rank_ref, bf16[48,2048]{1,0:T(8,128)(2,1)S(1)} %add_convert_fusion.refs_5_.refs_0_, bf16[48,2048]{1,0:T(8,128)(2,1)S(1)} %collective-permute-done.29.refs_1_, bf16[48,2048]{1,0:T(8,128)(2,1)S(1)} %collective-permute-done.30.refs_2_, ...), custom_call_target="tpu_custom_call" | custom-call | flops 3221225472 | bytes 19136512 | tf_op jit(solution)/shard_map/pallas_call | solution.py:201
  298.9 5.6 %collective-permute-done.47 = bf16[32,4096]{1,0:T(8,128)(2,1)S(1)} collective-permute-done((bf16[32,4096]{1,0:T(8,128)(2,1)S(1)}, bf16[32,4096]{1,0:T(8,128)(2,1)S(1)}, u32[]{:S(2)}, u32[]{:S(2)}) %collective-permute-start.47) | collective-permute-done | bytes 262176 | tf_op jit(solution)/shard_map/ppermute | solution.py:21
  304.8 7.3 %collective-permute-done.38 = bf16[48,4096]{1,0:T(8,128)(2,1)S(1)} collective-permute-done((bf16[48,4096]{1,0:T(8,128)(2,1)S(1)}, bf16[48,4096]{1,0:T(8,128)(2,1)S(1)}, u32[]{:S(2)}, u32[]{:S(2)}) %collective-permute-start.38) | collective-permute-done | bytes 393248 | tf_op jit(solution)/shard_map/ppermute | solution.py:21
  (185 shorter events, 109.6 us)
Async XLA Ops:
  0.9 31.1 %collective-permute-start.2 = (bf16[32,1024]{1,0:T(8,128)(2,1)S(1)}, bf16[32,1024]{1,0:T(8,128)(2,1)S(1)}, u32[]{:S(2)}, u32[]{:S(2)}) collective-permute-start(bf16[32,1024]{1,0:T(8,128)(2,1)S(1)} %get-tuple-element.74), channel_id=1, source_target_pairs={{12,0},{0,4},{4,8},{8,12},{13,1},{1,5},{5,9},{9,13},{14,2},{2,6},{... | collective-permute-start | bytes 196616 | tf_op jit(solution)/shard_map/ppermute | solution.py:17
  3.9 28.0 %collective-permute-start.1 = (bf16[32,1024]{1,0:T(8,128)(2,1)S(1)}, bf16[32,1024]{1,0:T(8,128)(2,1)S(1)}, u32[]{:S(2)}, u32[]{:S(2)}) collective-permute-start(bf16[32,1024]{1,0:T(8,128)(2,1)S(1)} %get-tuple-element.74), channel_id=1, source_target_pairs={{8,0},{12,4},{0,8},{4,12},{9,1},{13,5},{1,9},{5,13},{10,2},{14,6},... | collective-permute-start | bytes 196616 | tf_op jit(solution)/shard_map/ppermute | solution.py:17
  6.5 25.4 %collective-permute-start = (bf16[32,1024]{1,0:T(8,128)(2,1)S(1)}, bf16[32,1024]{1,0:T(8,128)(2,1)S(1)}, u32[]{:S(2)}, u32[]{:S(2)}) collective-permute-start(bf16[32,1024]{1,0:T(8,128)(2,1)S(1)} %get-tuple-element.74), channel_id=1, source_target_pairs={{4,0},{8,4},{12,8},{0,12},{5,1},{9,5},{13,9},{1,13},{6,2},{10,6},{... | collective-permute-start | bytes 196616 | tf_op jit(solution)/shard_map/ppermute | solution.py:17
  53.2 19.0 %collective-permute-start.7 = (bf16[2,64,1792]{2,1,0:T(8,128)(2,1)S(1)}, bf16[2,64,1792]{2,1,0:T(8,128)(2,1)S(1)}, u32[]{:S(2)}, u32[]{:S(2)}) collective-permute-start(bf16[2,64,1792]{2,1,0:T(8,128)(2,1)S(1)} %get-tuple-element.40), channel_id=1, source_target_pairs={{0,2},{2,0},{1,3},{3,1},{4,6},{6,4},{5,7},{7,5},{8,10},{10,8},{9,1... | collective-permute-start | bytes 1376264 | tf_op jit(solution)/shard_map/ppermute | solution.py:21
  71.6 34.3 %collective-permute-start.15 = (bf16[2,96,3584]{2,1,0:T(8,128)(2,1)S(1)}, bf16[2,96,3584]{2,1,0:T(8,128)(2,1)S(1)}, u32[]{:S(2)}, u32[]{:S(2)}) collective-permute-start(bf16[2,96,3584]{2,1,0:T(8,128)(2,1)S(1)} %get-tuple-element.44), channel_id=1, source_target_pairs={{0,2},{2,0},{1,3},{3,1},{4,6},{6,4},{5,7},{7,5},{8,10},{10,8},{9,1... | collective-permute-start | bytes 4128776 | tf_op jit(solution)/shard_map/ppermute | solution.py:21
  72.4 44.4 %collective-permute-start.9 = (bf16[64,1792]{1,0:T(8,128)(2,1)S(1)}, bf16[64,1792]{1,0:T(8,128)(2,1)S(1)}, u32[]{:S(2)}, u32[]{:S(2)}) collective-permute-start(bf16[64,1792]{1,0:T(8,128)(2,1)S(1)} %fusion.25.refs_0_), channel_id=1, source_target_pairs={{2,0},{0,2},{3,1},{1,3},{6,4},{4,6},{7,5},{5,7},{10,8},{8,10},{11,... | collective-permute-start | bytes 688136 | tf_op jit(solution)/shard_map/ppermute | solution.py:17
  76.7 40.1 %collective-permute-start.10 = (bf16[64,1792]{1,0:T(8,128)(2,1)S(1)}, bf16[64,1792]{1,0:T(8,128)(2,1)S(1)}, u32[]{:S(2)}, u32[]{:S(2)}) collective-permute-start(bf16[64,1792]{1,0:T(8,128)(2,1)S(1)} %fusion.23.refs_1_.refs_0_), channel_id=1, source_target_pairs={{2,0},{0,2},{3,1},{1,3},{6,4},{4,6},{7,5},{5,7},{10,8},{8,10},{11,... | collective-permute-start | bytes 688136 | tf_op jit(solution)/shard_map/ppermute | solution.py:17
  86.4 49.2 %collective-permute-start.23 = (bf16[2,64,3584]{2,1,0:T(8,128)(2,1)S(1)}, bf16[2,64,3584]{2,1,0:T(8,128)(2,1)}, u32[]{:S(2)}, u32[]{:S(2)}) collective-permute-start(bf16[2,64,3584]{2,1,0:T(8,128)(2,1)S(1)} %get-tuple-element.51), channel_id=1, source_target_pairs={{0,2},{2,0},{1,3},{3,1},{4,6},{6,4},{5,7},{7,5},{8,10},{10,8},{9,1... | collective-permute-start | bytes 2752520 | tf_op jit(solution)/shard_map/ppermute | solution.py:21
  106.6 62.9 %collective-permute-start.22 = (bf16[96,3584]{1,0:T(8,128)(2,1)S(1)}, bf16[96,3584]{1,0:T(8,128)(2,1)S(1)}, u32[]{:S(2)}, u32[]{:S(2)}) collective-permute-start(bf16[96,3584]{1,0:T(8,128)(2,1)S(1)} %fusion.1.refs_0_), channel_id=1, source_target_pairs={{2,0},{0,2},{3,1},{1,3},{6,4},{4,6},{7,5},{5,7},{10,8},{8,10},{11,... | collective-permute-start | bytes 2064392 | tf_op jit(solution)/shard_map/ppermute | solution.py:17
  137.2 49.0 %collective-permute-start.32 = (bf16[64,3584]{1,0:T(8,128)(2,1)S(1)}, bf16[64,3584]{1,0:T(8,128)(2,1)S(1)}, u32[]{:S(2)}, u32[]{:S(2)}) collective-permute-start(bf16[64,3584]{1,0:T(8,128)(2,1)S(1)} %fusion.3.refs_3_.refs_0_), channel_id=1, source_target_pairs={{2,0},{0,2},{3,1},{1,3},{6,4},{4,6},{7,5},{5,7},{10,8},{8,10},{11,... | collective-permute-start | bytes 1376264 | tf_op jit(solution)/shard_map/ppermute | solution.py:17
  137.8 31.7 %collective-permute-start.33 = (bf16[2,32,3584]{2,1,0:T(8,128)(2,1)S(1)}, bf16[2,32,3584]{2,1,0:T(8,128)(2,1)S(1)}, u32[]{:S(2)}, u32[]{:S(2)}) collective-permute-start(bf16[2,32,3584]{2,1,0:T(8,128)(2,1)S(1)} %get-tuple-element.58), channel_id=1, source_target_pairs={{0,2},{2,0},{1,3},{3,1},{4,6},{6,4},{5,7},{7,5},{8,10},{10,8},{9,1... | collective-permute-start | bytes 1376264 | tf_op jit(solution)/shard_map/ppermute | solution.py:21
  140.2 67.7 %collective-permute-start.21 = (bf16[32,2048]{1,0:T(8,128)(2,1)S(1)}, bf16[32,2048]{1,0:T(8,128)(2,1)S(1)}, u32[]{:S(2)}, u32[]{:S(2)}) collective-permute-start(bf16[32,2048]{1,0:T(8,128)(2,1)S(1)} %add_convert_fusion.2.refs_0_), channel_id=1, source_target_pairs={{12,0},{0,4},{4,8},{8,12},{13,1},{1,5},{5,9},{9,13},{14,2},{2,6},{... | collective-permute-start | bytes 393224 | tf_op jit(solution)/shard_map/ppermute | solution.py:17
  182.0 18.2 %collective-permute-start.25 = (bf16[48,2048]{1,0:T(8,128)(2,1)S(1)}, bf16[48,2048]{1,0:T(8,128)(2,1)S(1)}, u32[]{:S(2)}, u32[]{:S(2)}) collective-permute-start(bf16[48,2048]{1,0:T(8,128)(2,1)S(1)} %get-tuple-element.54), channel_id=1, source_target_pairs={{0,8},{4,12},{8,0},{12,4},{1,9},{5,13},{9,1},{13,5},{2,10},{6,14},... | collective-permute-start | bytes 589832 | tf_op jit(solution)/shard_map/ppermute | solution.py:21
  186.2 25.2 %collective-permute-start.20 = (bf16[32,2048]{1,0:T(8,128)(2,1)S(1)}, bf16[32,2048]{1,0:T(8,128)(2,1)S(1)}, u32[]{:S(2)}, u32[]{:S(2)}) collective-permute-start(bf16[32,2048]{1,0:T(8,128)(2,1)S(1)} %add_convert_fusion.2.refs_0_), channel_id=1, source_target_pairs={{8,0},{12,4},{0,8},{4,12},{9,1},{13,5},{1,9},{5,13},{10,2},{14,6},... | collective-permute-start | bytes 393224 | tf_op jit(solution)/shard_map/ppermute | solution.py:17
  200.1 19.5 %collective-permute-start.42 = (bf16[32,3584]{1,0:T(8,128)(2,1)S(1)}, bf16[32,3584]{1,0:T(8,128)(2,1)S(1)}, u32[]{:S(2)}, u32[]{:S(2)}) collective-permute-start(bf16[32,3584]{1,0:T(8,128)(2,1)S(1)} %fusion.21.refs_3_.refs_0_), channel_id=1, source_target_pairs={{2,0},{0,2},{3,1},{1,3},{6,4},{4,6},{7,5},{5,7},{10,8},{8,10},{11,... | collective-permute-start | bytes 688136 | tf_op jit(solution)/shard_map/ppermute | solution.py:17
  200.7 34.4 %collective-permute-start.34 = (bf16[32,2048]{1,0:T(8,128)(2,1)S(1)}, bf16[32,2048]{1,0:T(8,128)(2,1)S(1)}, u32[]{:S(2)}, u32[]{:S(2)}) collective-permute-start(bf16[32,2048]{1,0:T(8,128)(2,1)S(1)} %get-tuple-element.60), channel_id=1, source_target_pairs={{0,4},{4,8},{8,12},{12,0},{1,5},{5,9},{9,13},{13,1},{2,6},{6,10},{... | collective-permute-start | bytes 393224 | tf_op jit(solution)/shard_map/ppermute | solution.py:21
  207.9 29.7 %collective-permute-start.35 = (bf16[32,2048]{1,0:T(8,128)(2,1)S(1)}, bf16[32,2048]{1,0:T(8,128)(2,1)S(1)}, u32[]{:S(2)}, u32[]{:S(2)}) collective-permute-start(bf16[32,2048]{1,0:T(8,128)(2,1)S(1)} %get-tuple-element.61), channel_id=1, source_target_pairs={{0,8},{4,12},{8,0},{12,4},{1,9},{5,13},{9,1},{13,5},{2,10},{6,14},... | collective-permute-start | bytes 393224 | tf_op jit(solution)/shard_map/ppermute | solution.py:21
  211.3 26.2 %collective-permute-start.36 = (bf16[32,2048]{1,0:T(8,128)(2,1)S(1)}, bf16[32,2048]{1,0:T(8,128)(2,1)S(1)}, u32[]{:S(2)}, u32[]{:S(2)}) collective-permute-start(bf16[32,2048]{1,0:T(8,128)(2,1)S(1)} %get-tuple-element.62), channel_id=1, source_target_pairs={{0,12},{4,0},{8,4},{12,8},{1,13},{5,1},{9,5},{13,9},{2,14},{6,2},{... | collective-permute-start | bytes 393224 | tf_op jit(solution)/shard_map/ppermute | solution.py:21
  242.0 19.8 %collective-permute-start.50 = (bf16[16,2048]{1,0:T(8,128)(2,1)S(1)}, bf16[16,2048]{1,0:T(8,128)(2,1)S(1)}, u32[]{:S(2)}, u32[]{:S(2)}) collective-permute-start(bf16[16,2048]{1,0:T(8,128)(2,1)S(1)} %add_convert_fusion.3.refs_5_.refs_0_), channel_id=1, source_target_pairs={{12,0},{0,4},{4,8},{8,12},{13,1},{1,5},{5,9},{9,13},{14,2},{2,6},{... | collective-permute-start | bytes 196616 | tf_op jit(solution)/shard_map/ppermute | solution.py:17
  250.8 28.1 %collective-permute-start.31 = (bf16[48,2048]{1,0:T(8,128)(2,1)S(1)}, bf16[48,2048]{1,0:T(8,128)(2,1)S(1)}, u32[]{:S(2)}, u32[]{:S(2)}) collective-permute-start(bf16[48,2048]{1,0:T(8,128)(2,1)S(1)} %add_convert_fusion.refs_5_.refs_0_), channel_id=1, source_target_pairs={{12,0},{0,4},{4,8},{8,12},{13,1},{1,5},{5,9},{9,13},{14,2},{2,6},{... | collective-permute-start | bytes 589832 | tf_op jit(solution)/shard_map/ppermute | solution.py:17
  250.9 28.2 %collective-permute-start.30 = (bf16[48,2048]{1,0:T(8,128)(2,1)S(1)}, bf16[48,2048]{1,0:T(8,128)(2,1)S(1)}, u32[]{:S(2)}, u32[]{:S(2)}) collective-permute-start(bf16[48,2048]{1,0:T(8,128)(2,1)S(1)} %add_convert_fusion.refs_5_.refs_0_), channel_id=1, source_target_pairs={{8,0},{12,4},{0,8},{4,12},{9,1},{13,5},{1,9},{5,13},{10,2},{14,6},... | collective-permute-start | bytes 589832 | tf_op jit(solution)/shard_map/ppermute | solution.py:17
  254.7 24.3 %collective-permute-start.29 = (bf16[48,2048]{1,0:T(8,128)(2,1)S(1)}, bf16[48,2048]{1,0:T(8,128)(2,1)S(1)}, u32[]{:S(2)}, u32[]{:S(2)}) collective-permute-start(bf16[48,2048]{1,0:T(8,128)(2,1)S(1)} %add_convert_fusion.refs_5_.refs_0_), channel_id=1, source_target_pairs={{4,0},{8,4},{12,8},{0,12},{5,1},{9,5},{13,9},{1,13},{6,2},{10,6},{... | collective-permute-start | bytes 589832 | tf_op jit(solution)/shard_map/ppermute | solution.py:17
  272.1 21.3 %collective-permute-start.46 = (bf16[64,4096]{1,0:T(8,128)(2,1)S(1)}, bf16[64,4096]{1,0:T(8,128)(2,1)S(1)}, u32[]{:S(2)}, u32[]{:S(2)}) collective-permute-start(bf16[64,4096]{1,0:T(8,128)(2,1)S(1)} %get-tuple-element.70), channel_id=1, source_target_pairs={{0,1},{1,0},{2,3},{3,2},{4,5},{5,4},{6,7},{7,6},{8,9},{9,8},{10,11... | collective-permute-start | bytes 1572872 | tf_op jit(solution)/shard_map/ppermute | solution.py:21
  293.9 18.2 %collective-permute-start.38 = (bf16[48,4096]{1,0:T(8,128)(2,1)S(1)}, bf16[48,4096]{1,0:T(8,128)(2,1)S(1)}, u32[]{:S(2)}, u32[]{:S(2)}) collective-permute-start(bf16[48,4096]{1,0:T(8,128)(2,1)S(1)} %slice.252), channel_id=1, source_target_pairs={{0,2},{2,0},{1,3},{3,1},{4,6},{6,4},{5,7},{7,5},{8,10},{10,8},{9,1... | collective-permute-start | bytes 1179656 | tf_op jit(solution)/shard_map/ppermute | solution.py:21
  (42 other events, 497.5 us)

commit v3 on v2

v3 whole, which is shorter than its diff:
```python
import functools

import jax
import jax.numpy as jnp
from jax import lax
from jax.experimental import pallas as pl
from jax.experimental.pallas import tpu as pltpu
from jax.sharding import PartitionSpec as P

BF16 = jnp.bfloat16
F32 = jnp.float32
VMEM_BYTES = 52 * 1024 * 1024
BUFFERS = 4


def shift(value, axis, size, hop):
    return lax.ppermute(value, axis, [((d + hop) % size, d) for d in range(size)])


def send(value, axis, size, hop):
    return lax.ppermute(value, axis, [(d, (d + hop) % size) for d in range(size)])


def swap(value, axis, size, bit):
    return lax.ppermute(value, axis, [(d, d ^ bit) for d in range(size)])


def doubling(size):
    bits = [1 << at for at in reversed(range(size.bit_length() - 1))]
    order = [0]
    for bit in bits:
        order = order + [offset ^ bit for offset in order]
    return bits, order


def tile_of(width, most):
    tile = most
    while tile > 128 and width % tile:
        tile //= 2
    return tile if width % tile == 0 else width


def whole(shape):
    return pl.BlockSpec(shape, lambda j, *_: (0,) * len(shape))


def slots_of(tiles):
    return min(BUFFERS, tiles)


def slots(depth, tile, tiles):
    count = slots_of(tiles)
    return [pltpu.VMEM((count, depth, tile), BF16), pltpu.SemaphoreType.DMA((count,))]


def next_block(weight_ref, slot_ref, slot_sems, tiles, first=0):
    step = pl.program_id(0)
    count, _, tile = slot_ref.shape

    def copy(block, slot):
        columns = pl.ds(pl.multiple_of((first + block) * tile, 128), tile)
        return pltpu.make_async_copy(
            weight_ref.at[0, :, columns], slot_ref.at[slot], slot_sems.at[slot]
        )

    @pl.when(step == 0)
    def _():
        for block in range(count - 1):
            copy(block, block).start()

    ahead = step + count - 1

    @pl.when(ahead < tiles)
    def _():
        copy(ahead, lax.rem(ahead, count)).start()

    slot = lax.rem(step, count)
    copy(step, slot).wait()
    return slot_ref.at[slot]


def in_hbm(count):
    return [pl.BlockSpec(memory_space=pltpu.HBM)] * count


def unread(after):
    return [pl.BlockSpec(memory_space=pl.ANY)] * len(after)


def params():
    return pltpu.CompilerParams(
        dimension_semantics=("arbitrary",), vmem_limit_bytes=VMEM_BYTES
    )


def cost(rows, depth, width):
    return pl.CostEstimate(
        flops=2 * rows * depth * width,
        bytes_accessed=2 * (rows * depth + depth * width + rows * width),
        transcendentals=0,
    )


def gate_up_body(tiles, first, x_ref, gate_ref, up_ref, *refs):
    members, owners, cuts, q, cut = x_ref.shape
    out_refs = refs[-5 - owners : -5]
    lhs_ref = refs[-5]
    blocks = [
        next_block(gate_ref, refs[-4], refs[-3], tiles, first),
        next_block(up_ref, refs[-2], refs[-1], tiles, first),
    ]

    @pl.when(pl.program_id(0) == 0)
    def _():
        for owner in range(owners):
            for member in range(members):
                row = (owner * members + member) * q
                for at in range(cuts):
                    lhs_ref[row : row + q, at * cut : (at + 1) * cut] = x_ref[member, owner, at]

    rows = members * q
    for at, block_ref in enumerate(blocks):
        acts = jnp.dot(lhs_ref[...], block_ref[...], preferred_element_type=F32)
        for hop in range(owners):
            taken = acts[hop * rows : (hop + 1) * rows]
            out_refs[hop][at] = taken.astype(out_refs[hop].dtype)


def gate_up(x, gate_weight, up_weight, piece, pieces, after):
    members, owners, cuts, q, cut = x.shape
    rows, depth, own_rows = members * owners * q, cuts * cut, members * q
    width = gate_weight.shape[2] // pieces
    tile = tile_of(width, 256)
    tiles = width // tile
    return pl.pallas_call(
        functools.partial(gate_up_body, tiles, piece * tiles),
        grid=(tiles,),
        in_specs=[whole(x.shape)] + in_hbm(2) + unread(after),
        out_specs=[pl.BlockSpec((2, own_rows, tile), lambda j: (0, 0, j))] * owners,
        out_shape=[jax.ShapeDtypeStruct((2, own_rows, width), F32)]
        + [jax.ShapeDtypeStruct((2, own_rows, width), BF16)] * (owners - 1),
        scratch_shapes=[pltpu.VMEM((rows, depth), BF16)] + slots(depth, tile, tiles) * 2,
        compiler_params=params(),
        cost_estimate=cost(rows, depth, 2 * width),
    )(x, gate_weight, up_weight, *after)


def down_body(owners, members, pieces, order, tiles, rank_ref, *refs):
    hidden_refs = refs[: owners * pieces]
    weight_ref = refs[owners * pieces]
    out_refs = refs[-6:-4]
    lhs_ref, acc_ref, slot_ref, slot_sems = refs[-4:]
    block_ref = next_block(weight_ref, slot_ref, slot_sems, tiles)
    q = hidden_refs[0].shape[0] // members
    part = hidden_refs[0].shape[1]
    block = acc_ref.shape[0] // len(order)

    @pl.when(pl.program_id(0) == 0)
    def _():
        for owner in range(owners):
            for piece in range(pieces):
                for member in range(members):
                    row = (member * owners + owner) * q
                    lhs_ref[row : row + q, piece * part : (piece + 1) * part] = hidden_refs[
                        owner * pieces + piece
                    ][member * q : (member + 1) * q]

    acc_ref[...] = jnp.dot(lhs_ref[...], block_ref[...], preferred_element_type=F32)
    half = len(order) // 2
    for slot, offset in enumerate(order):
        at = (rank_ref[0] ^ offset) * block
        taken = acc_ref[pl.ds(pl.multiple_of(at, block), block), :]
        out_ref = out_refs[slot // half]
        row = (slot % half) * block
        out_ref[row : row + block] = taken.astype(out_ref.dtype)


def down(rank, hidden, down_weight, members, order, after):
    owners, pieces = len(hidden), len(hidden[0])
    rows_each, part = hidden[0][0].shape
    rows, depth, width = owners * rows_each, pieces * part, down_weight.shape[2]
    tile = tile_of(width, 256)
    return pl.pallas_call(
        functools.partial(down_body, owners, members, pieces, order, width // tile),
        grid_spec=pltpu.PrefetchScalarGridSpec(
            num_scalar_prefetch=1,
            grid=(width // tile,),
            in_specs=[whole((rows_each, part))] * (owners * pieces)
            + in_hbm(1)
            + unread(after),
            out_specs=[pl.BlockSpec((rows // 2, tile), lambda j, *_: (0, j))] * 2,
            scratch_shapes=[pltpu.VMEM((rows, depth), BF16), pltpu.VMEM((rows, tile), F32)]
            + slots(depth, tile, width // tile),
        ),
        out_shape=[jax.ShapeDtypeStruct((rows // 2, width), kind) for kind in (F32, BF16)],
        compiler_params=params(),
        cost_estimate=cost(rows, depth, width),
    )(rank, *[piece for of_owner in hidden for piece in of_owner], down_weight, *after)


def encode_body(members, order, tiles, rank_ref, near_ref, far_ref, weight_ref, *refs):
    out_refs = refs[-3 - members : -3]
    lhs_ref, slot_ref, slot_sems = refs[-3:]
    weight_block = next_block(weight_ref, slot_ref, slot_sems, tiles)
    block = lhs_ref.shape[0] // len(order)
    half = len(order) // 2

    @pl.when(pl.program_id(0) == 0)
    def _():
        for slot, offset in enumerate(order):
            at = (rank_ref[0] ^ offset) * block
            row = (slot % half) * block
            from_ref = far_ref if slot >= half else near_ref
            lhs_ref[pl.ds(pl.multiple_of(at, block), block), :] = from_ref[row : row + block]

    pre = jnp.dot(lhs_ref[...], weight_block[...], preferred_element_type=F32)
    rows = pre.shape[0] // members
    for member in range(members):
        taken = pre[member * rows : (member + 1) * rows]
        out_refs[member][...] = taken.astype(out_refs[member].dtype)


def encode(rank, near, far, enc_weight, members, order, after):
    rows, depth = 2 * near.shape[0], near.shape[1]
    width = enc_weight.shape[2]
    rows_each = rows // members
    tile = tile_of(width, 512)
    return pl.pallas_call(
        functools.partial(encode_body, members, order, width // tile),
        grid_spec=pltpu.PrefetchScalarGridSpec(
            num_scalar_prefetch=1,
            grid=(width // tile,),
            in_specs=[whole(near.shape)] * 2 + in_hbm(1) + unread(after),
            out_specs=[pl.BlockSpec((rows_each, tile), lambda j, *_: (0, j))] * members,
            scratch_shapes=[pltpu.VMEM((rows, depth), BF16)] + slots(depth, tile, width // tile),
        ),
        out_shape=[jax.ShapeDtypeStruct((rows_each, width), F32)]
        + [jax.ShapeDtypeStruct((rows_each, width), BF16)] * (members - 1),
        compiler_params=params(),
        cost_estimate=cost(rows, depth, width),
    )(rank, near, far, enc_weight, *after)


def chunk_rows(total, unit):
    units = total // unit
    if units < 8:
        return [total]
    eighth = units // 8
    sizes = [2 * eighth, 3 * eighth, 2 * eighth]
    return [size * unit for size in sizes + [units - sum(sizes)]]


def on_device(
    owners, members, ranks, tokens, norm_gain, gate_weight, up_weight, down_weight, enc_weight,
    enc_bias, adjoint,
):
    row_at = lax.axis_index("rows")
    member_at = lax.axis_index("mp")
    rank_at = lax.axis_index("hid")
    rank = rank_at.astype(jnp.int32).reshape(1)
    per_device = adjoint.shape[0]
    cut = tokens.shape[1]
    half_cuts = ranks // owners
    model_width = cut * ranks

    gain = lax.dynamic_slice_in_dim(
        norm_gain[0], row_at * (model_width // owners), model_width // owners, 0
    ).reshape(half_cuts, 1, cut)
    own_tokens = lax.dynamic_slice_in_dim(tokens, member_at * per_device, per_device, 0)

    bits, order = doubling(ranks)

    def from_all(value, axis, size):
        return jnp.stack([value] + [shift(value, axis, size, hop) for hop in range(1, size)])

    def place_of(offset):
        place = 0
        for at in range(len(bits)):
            place = place + ((offset >> at) & 1) * bits[at]
        return place

    def gathered_rows(mine, after=None):
        gathered = mine[None]
        for bit in bits:
            gathered = jnp.concatenate((gathered, swap(gathered, "hid", ranks, bit)))
        if after is not None:
            gathered, _ = lax.optimization_barrier((gathered, after))
        wide = gathered.astype(F32)
        squares = jnp.sum(wide * wide, axis=(0, 2))
        inverse = lax.rsqrt(squares / model_width + 1e-05)
        columns = []
        for hop in range(owners):
            target = lax.rem(row_at + owners - hop, owners)
            half = jnp.concatenate(
                [
                    lax.dynamic_slice_in_dim(
                        gathered, place_of(rank_at ^ (target * half_cuts + at)), 1, 0
                    )
                    for at in range(half_cuts)
                ]
            )
            columns.append(half if hop == 0 else shift(half, "rows", owners, hop))
        inverses = from_all(from_all(inverse, "rows", owners), "mp", members)
        return from_all(jnp.stack(columns), "mp", members), inverses

    def normed(columns, inverses):
        return (columns.astype(F32) * inverses[:, :, None, :, None] * gain).astype(BF16)

    sizes = chunk_rows(per_device, 16 * max(1, ranks // (owners * members)))
    starts = [sum(sizes[:at]) for at in range(len(sizes))]
    chunks = len(sizes)
    head = sizes[0]

    xs = [normed(*gathered_rows(own_tokens[:head]))]
    if chunks > 1:
        columns, inverses = gathered_rows(own_tokens[head:], xs[0])
        for start, q in zip(starts[1:], sizes[1:]):
            rows = slice(start - head, start - head + q)
            xs.append(normed(columns[:, :, :, rows], inverses[:, :, rows]))

    sums, hidden, layer, blocks, outs = ({} for _ in range(5))
    last = []

    def gate_up_of(t):
        pieces = 2 if t == 0 and gate_weight.shape[2] % 512 == 0 else 1
        sums[t] = []
        for piece in range(pieces):
            own, *sends = gate_up(
                xs[t], gate_weight, up_weight, piece, pieces, list(last)
            )
            last[:] = [own]
            others = [send(sends[hop - 1], "rows", owners, hop) for hop in range(1, owners)]
            sums[t].append((own, others))

    def hidden_of(t):
        hidden[t] = [[] for _ in range(owners)]
        for own, others in sums[t]:
            acts = own
            for other in others:
                acts = acts + other.astype(F32)
            units = (jax.nn.silu(acts[0]) * acts[1]).astype(BF16)
            hidden[t][0].append(units)
            for hop in range(1, owners):
                hidden[t][hop].append(shift(units, "rows", owners, hop))
        last.append(hidden[t][0][-1])

    def down_of(t):
        total, going = down(rank, hidden[t], down_weight, members, order, list(last))
        last[:] = [total]
        layer[t] = (total, swap(going, "hid", ranks, 1))

    def halve_of(t):
        total, arrived = layer[t]
        for bit in reversed(bits[:-1]):
            total = total + arrived.astype(F32)
            kept = total.shape[0] // 2
            going = total[kept:].astype(BF16)
            last.append(going)
            total, arrived = total[:kept], swap(going, "hid", ranks, bit)
        layer[t] = (total, arrived)

    def settle_of(t):
        total, arrived = layer[t]
        block = (total + arrived.astype(F32)).astype(BF16)
        last.append(block)
        layer[t] = (block, swap(block, "hid", ranks, bits[0]))

    def double_of(t):
        near, far = layer[t]
        for bit in bits[1:]:
            near = jnp.concatenate((near, far))
            last.append(near)
            far = swap(near, "hid", ranks, bit)
        blocks[t] = (near, far)

    def features_of(t):
        own, *sends = encode(rank, *blocks[t], enc_weight, members, order, list(last))
        last[:] = [own]
        sums[t] = (own, [send(sends[hop - 1], "mp", members, hop) for hop in range(1, members)])

    def share_of(t):
        total, others = sums[t]
        for other in others:
            total = total + other.astype(F32)
        start, q = starts[t], sizes[t]
        pre = total[:q]
        for hop in range(1, owners):
            going = total[hop * q : (hop + 1) * q].astype(BF16)
            last.append(going)
            pre = pre + send(going, "rows", owners, hop).astype(F32)
        pre = pre + enc_bias[None, :]
        factor = adjoint[start : start + q].astype(F32)
        outs[t] = (jnp.maximum(pre, 0.0) * factor).astype(BF16)

    end = chunks
    stages = [(gate_up_of, 0), (gate_up_of, 1)]
    for step in range(end):
        stages += [
            (hidden_of, step), (gate_up_of, step + 2), (double_of, step - 3), (halve_of, step - 2),
            (down_of, step - 1), (settle_of, step - 2),
        ]
    stages += [(double_of, end - 3), (down_of, end - 1), (halve_of, end - 2)]
    for t in range(end - 3):
        stages += [(features_of, t), (share_of, t)]
    stages += [
        (settle_of, end - 2), (halve_of, end - 1), (features_of, end - 3),
        (share_of, end - 3), (double_of, end - 2), (settle_of, end - 1), (features_of, end - 2),
        (share_of, end - 2), (double_of, end - 1), (features_of, end - 1), (share_of, end - 1),
    ]
    for stage, t in stages:
        if 0 <= t < chunks:
            stage(t)
    return jnp.concatenate([outs[t] for t in range(chunks)], axis=0)


def solution(mesh):
    placed = (
        P(("groups", "rows"), "hid"),
        P("mp", None),
        P("mp", "rows", "hid"),
        P("mp", "rows", "hid"),
        P("mp", "hid", "rows"),
        P("mp", "rows", "hid"),
        P("hid"),
        P(("groups", "rows", "mp"), "hid"),
    )
    sizes = (mesh.shape["rows"], mesh.shape["mp"], mesh.shape["hid"])
    return jax.shard_map(
        functools.partial(on_device, *sizes),
        mesh=mesh,
        in_specs=placed,
        out_specs=P(("groups", "rows", "mp"), "hid"),
        check_vma=False,
    )
```

time: 314 us -> 295 us (0.939)
  waiting for transfers between devices: 86.8 us -> 124 us
  starting transfers between devices: 83.1 us -> 47.1 us
  local copies, waits for them, and re-layouts: 27.1 us -> 3.86 us
  Pallas kernels: 90.9 us -> 110 us
  blocking collectives: 17.8 us -> 0 us
    ppermute x0 -> x20, waiting for transfers between devices: none -> 41.1 us  [swap(): return lax.ppermute(value, axis, [(d, d ^ bit) for d in range(size)])]
    ppermute x28 -> x13, starting transfers between devices: 44.2 us -> 10.4 us  [shift(): lax.ppermute(value, axis, [((d + hop) % size, d) for d in range(size)])]
    ppermute x25 -> x13, starting transfers between devices: 38.9 us -> 11.9 us  [send(): lax.ppermute(value, axis, [(d, (d + hop) % size) for d in range(size)])]
    ppermute x0 -> x20, starting transfers between devices: none -> 24.7 us  [swap(): return lax.ppermute(value, axis, [(d, d ^ bit) for d in range(size)])]
    unnamed x37 -> x28, local copies, waits for them, and re-layouts: 23.8 us -> 2.85 us
    pallas_call x13, Pallas kernels: 90.9 us -> 110 us  [the longest x5 52.4 us: gate_up(): pl.pallas_call(functools.partial(gate_up_body, tiles, piece * tiles), gri...]
    all_gather x1 -> x0, blocking collectives: 17.8 us -> none  [on_device(): rest = lax.all_gather(own_tokens[head:], 'hid', axis=0)]
    ppermute x25 -> x13, waiting for transfers between devices: 72.1 us -> 59.5 us  [send(): lax.ppermute(value, axis, [(d, (d + hop) % size) for d in range(size)])]
  transfers between devices with their start and end apart: 53 -> 46, of which waited for: 17 -> 26; matrix products, arithmetic and copies ran while one was open for 3% -> 3% of each run, Pallas kernels for 27% -> 35%
where the time goes in v3:
time: 295 us
  waiting for transfers between devices  124 us (42%)
  Pallas kernels  110 us (37%)
  starting transfers between devices  47.1 us (16%)
  other arithmetic  9.55 us (3%)
  local copies, waits for them, and re-layouts  3.86 us (1%)
    ppermute x13, waiting for transfers between devices, send(): lax.ppermute(value, axis, [(d, (d + hop) % size) for d in range(size)])  59.5 us
    pallas_call x5, Pallas kernels, gate_up(): pl.pallas_call(functools.partial(gate_up_body, tiles, piece * tiles), gri...  52.4 us
    ppermute x20, waiting for transfers between devices, swap(): return lax.ppermute(value, axis, [(d, d ^ bit) for d in range(size)])  41.1 us
    pallas_call x4, Pallas kernels, encode(): pl.pallas_call(functools.partial(encode_body, members, order, width // ti...  29.9 us
    pallas_call x4, Pallas kernels, down(): pl.pallas_call(functools.partial(down_body, owners, members, pieces, orde...  27.4 us
    ppermute x20, starting transfers between devices, swap(): return lax.ppermute(value, axis, [(d, d ^ bit) for d in range(size)])  24.7 us
    ppermute x13, waiting for transfers between devices, shift(): lax.ppermute(value, axis, [((d + hop) % size, d) for d in range(size)])  23.5 us
    ppermute x13, starting transfers between devices, send(): lax.ppermute(value, axis, [(d, (d + hop) % size) for d in range(size)])  11.9 us
  transfers between devices with their start and end apart: 46, of which 26 were waited for; matrix products, arithmetic and copies ran while one was open for 3% of the time, Pallas kernels for 35%

profile of v3, /device:TPU:0, one launch (start us, length us, event | category | flops | bytes accessed | tf_op | source)
XLA Modules:
  0.0 295.0 jit_solution(2935606307555393754)
XLA Ops:
  1.0 4.0 %collective-permute-start = (bf16[1,32,1024]{2,1,0:T(8,128)(2,1)S(1)}, bf16[1,32,1024]{2,1,0:T(8,128)(2,1)S(1)}, u32[]{:S(2)}, u32[]{:S(2)}) collective-permute-start(bf16[1,32,1024]{2,1,0:T(8,128)(2,1)S(1)} %dynamic-slice_bitcast_fusion.1), channel_id=1, source_target_pairs={{0,8},{4,12},{8,0},{12,4},{1,9},{5,13},{9,1},{13,5},{2,10},{6,14},... | collective-permute-start | bytes 196616 | tf_op jit(solution)/shard_map/ppermute | solution.py:25
  23.0 6.9 %shard_map.82 = (f32[2,64,1792]{2,1,0:T(8,128)S(1)}, bf16[2,64,1792]{2,1,0:T(8,128)(2,1)S(1)}) custom-call(bf16[2,2,2,32,1024]{4,3,2,1,0:T(8,128)(2,1)S(1)} %multiply_convert_fusion.2.x_ref, bf16[1,2048,3584]{2,1,0:T(8,128)(2,1)} %gate_ref.9, bf16[1,2048,3584]{2,1,0:T(8,128)(2,1)} %up_ref.9), custom_call_target="tpu_custom_call" | custom-call | flops 1879048192 | bytes 16121856 | tf_op jit(solution)/shard_map/pallas_call | solution.py:135
  32.7 6.9 %shard_map.83 = (f32[2,64,1792]{2,1,0:T(8,128)S(1)}, bf16[2,64,1792]{2,1,0:T(8,128)(2,1)S(1)}) custom-call(bf16[2,2,2,32,1024]{4,3,2,1,0:T(8,128)(2,1)S(1)} %multiply_convert_fusion.2.x_ref, bf16[1,2048,3584]{2,1,0:T(8,128)(2,1)} %gate_ref.9, bf16[1,2048,3584]{2,1,0:T(8,128)(2,1)} %up_ref.9, f32[2,64,1792]{2,1,0:T(8,128)} %copy-done.3), custom_call_target="tpu_custom_call" | custom-call | flops 1879048192 | bytes 16121856 | tf_op jit(solution)/shard_map/pallas_call | solution.py:135
  42.4 11.6 %collective-permute-done.14 = f32[96]{0:T(128)S(1)} collective-permute-done((f32[96]{0:T(128)S(1)}, f32[96]{0:T(128)S(1)}, u32[]{:S(2)}, u32[]{:S(2)}) %collective-permute-start.14) | collective-permute-done | bytes 416 | tf_op jit(solution)/shard_map/ppermute | solution.py:17
  55.4 6.4 %collective-permute-done.12 = bf16[2,96,1024]{2,1,0:T(8,128)(2,1)S(1)} collective-permute-done((bf16[2,96,1024]{2,1,0:T(8,128)(2,1)S(1)}, bf16[2,96,1024]{2,1,0:T(8,128)(2,1)S(1)}, u32[]{:S(2)}, u32[]{:S(2)}) %collective-permute-start.12) | collective-permute-done | bytes 393248 | tf_op jit(solution)/shard_map/ppermute | solution.py:17
  64.5 13.5 %shard_map.84 = (f32[2,96,3584]{2,1,0:T(8,128)}, bf16[2,96,3584]{2,1,0:T(8,128)(2,1)}) custom-call(bf16[2,2,2,48,1024]{4,3,2,1,0:T(8,128)(2,1)S(1)} %multiply_convert_fusion.x_ref, bf16[1,2048,3584]{2,1,0:T(8,128)(2,1)} %gate_ref.9, bf16[1,2048,3584]{2,1,0:T(8,128)(2,1)} %up_ref.9, f32[2,64,1792]{2,1,0:T(8,128)S(1)} %get-tuple-element.34.refs_0_), custom_call_target="tpu_custom_call" | custom-call | flops 5637144576 | bytes 32899072 | tf_op jit(solution)/shard_map/pallas_call | solution.py:135
  80.6 12.6 %shard_map.85 = (f32[2,64,3584]{2,1,0:T(8,128)}, bf16[2,64,3584]{2,1,0:T(8,128)(2,1)S(1)}) custom-call(bf16[2,2,2,32,1024]{4,3,2,1,0:T(8,128)(2,1)S(1)} %multiply_convert_fusion.1.x_ref, bf16[1,2048,3584]{2,1,0:T(8,128)(2,1)} %gate_ref.9, bf16[1,2048,3584]{2,1,0:T(8,128)(2,1)} %up_ref.9, f32[2,96,3584]{2,1,0:T(8,128)} %get-tuple-element.37.refs_0_, ...), custom_call_target="tpu_custom_call" | custom-call | flops 3758096384 | bytes 31719424 | tf_op jit(solution)/shard_map/pallas_call | solution.py:135
  95.2 16.1 %collective-permute-done.16 = bf16[2,96,3584]{2,1,0:T(8,128)(2,1)S(1)} collective-permute-done((bf16[2,96,3584]{2,1,0:T(8,128)(2,1)}, bf16[2,96,3584]{2,1,0:T(8,128)(2,1)S(1)}, u32[]{:S(2)}, u32[]{:S(2)}) %collective-permute-start.16) | collective-permute-done | bytes 1376288 | tf_op jit(solution)/shard_map/ppermute | solution.py:21
  112.0 12.5 %shard_map.86 = (f32[2,32,3584]{2,1,0:T(8,128)}, bf16[2,32,3584]{2,1,0:T(8,128)(2,1)S(1)}) custom-call(bf16[2,2,2,16,1024]{4,3,2,1,0:T(8,128)(2,1)S(1)} %multiply_convert_fusion.3.x_ref, bf16[1,2048,3584]{2,1,0:T(8,128)(2,1)} %gate_ref.9, bf16[1,2048,3584]{2,1,0:T(8,128)(2,1)} %up_ref.9, f32[2,64,3584]{2,1,0:T(8,128)} %get-tuple-element.38.refs_0_, ...), custom_call_target="tpu_custom_call" | custom-call | flops 1879048192 | bytes 30539776 | tf_op jit(solution)/shard_map/pallas_call | solution.py:135
  124.5 6.2 %shard_map.87 = (f32[64,2048]{1,0:T(8,128)S(1)}, bf16[64,2048]{1,0:T(8,128)(2,1)S(1)}) custom-call(s32[1]{0:T(128)} %bitcast.rank_ref, bf16[64,1792]{1,0:T(8,128)(2,1)S(1)} %fusion.21.refs_0_, bf16[64,1792]{1,0:T(8,128)(2,1)S(1)} %fusion.19.refs_1_, bf16[64,1792]{1,0:T(8,128)(2,1)S(1)} %collective-permute-done.8.refs_2_, ...), custom_call_target="tpu_custom_call" | custom-call | flops 1879048192 | bytes 16121856 | tf_op jit(solution)/shard_map/pallas_call | solution.py:183
  146.5 27.6 %collective-permute-done.21 = bf16[2,32,3584]{2,1,0:T(8,128)(2,1)S(1)} collective-permute-done((bf16[2,32,3584]{2,1,0:T(8,128)(2,1)S(1)}, bf16[2,32,3584]{2,1,0:T(8,128)(2,1)S(1)}, u32[]{:S(2)}, u32[]{:S(2)}) %collective-permute-start.21) | collective-permute-done | bytes 458784 | tf_op jit(solution)/shard_map/ppermute | solution.py:21
  175.1 8.3 %shard_map.88 = (f32[96,2048]{1,0:T(8,128)}, bf16[96,2048]{1,0:T(8,128)(2,1)S(1)}) custom-call(s32[1]{0:T(128)} %bitcast.rank_ref, bf16[96,3584]{1,0:T(8,128)(2,1)} %copy-done.2, bf16[96,3584]{1,0:T(8,128)(2,1)} %copy-done.12, bf16[1,3584,2048]{2,1,0:T(8,128)(2,1)} %refs_2_.5, f32[64,2048]{1,0:T(8,128)S(1)} %get-tuple-element.41.refs_3_, ...), custom_call_target="tpu_custom_call" | custom-call | flops 2818572288 | bytes 16842752 | tf_op jit(solution)/shard_map/pallas_call | solution.py:183
  186.4 7.6 %collective-permute-done.26 = bf16[96,2048]{1,0:T(8,128)(2,1)S(1)} collective-permute-done((bf16[96,2048]{1,0:T(8,128)(2,1)S(1)}, bf16[96,2048]{1,0:T(8,128)(2,1)S(1)}, u32[]{:S(2)}, u32[]{:S(2)}) %collective-permute-start.26) | collective-permute-done | bytes 393248 | tf_op jit(solution)/shard_map/ppermute | solution.py:25
  196.5 6.8 %shard_map.89 = (f32[64,2048]{1,0:T(8,128)}, bf16[64,2048]{1,0:T(8,128)(2,1)S(1)}) custom-call(s32[1]{0:T(128)} %bitcast.rank_ref, bf16[64,3584]{1,0:T(8,128)(2,1)S(1)} %fusion.3.refs_4_.refs_0_, bf16[64,3584]{1,0:T(8,128)(2,1)S(1)} %collective-permute-done.24.refs_1_, bf16[1,3584,2048]{2,1,0:T(8,128)(2,1)} %refs_2_.5, ...), custom_call_target="tpu_custom_call" | custom-call | flops 1879048192 | bytes 16121856 | tf_op jit(solution)/shard_map/pallas_call | solution.py:183
  206.2 6.3 %collective-permute-done.29 = bf16[64,2048]{1,0:T(8,128)(2,1)S(1)} collective-permute-done((bf16[64,2048]{1,0:T(8,128)(2,1)S(1)}, bf16[64,2048]{1,0:T(8,128)(2,1)S(1)}, u32[]{:S(2)}, u32[]{:S(2)}) %collective-permute-start.29) | collective-permute-done | bytes 262176 | tf_op jit(solution)/shard_map/ppermute | solution.py:25
  216.7 6.1 %shard_map.90 = (f32[32,2048]{1,0:T(8,128)S(1)}, bf16[32,2048]{1,0:T(8,128)(2,1)S(1)}) custom-call(s32[1]{0:T(128)} %bitcast.rank_ref, bf16[32,3584]{1,0:T(8,128)(2,1)S(1)} %fusion.17.refs_5_.refs_0_, bf16[32,3584]{1,0:T(8,128)(2,1)S(1)} %collective-permute-done.22.refs_1_, bf16[1,3584,2048]{2,1,0:T(8,128)(2,1)} %refs_2_.5, f32[64,2048]{1,0:T(8,128)S(1)} %copy-done.5, ...), custom_call_target="tpu_custom_call" | custom-call | flops 939524096 | bytes 15400960 | tf_op jit(solution)/shard_map/pallas_call | solution.py:183
  223.5 7.5 %shard_map.91 = (f32[64,4096]{1,0:T(8,128)}, bf16[64,4096]{1,0:T(8,128)(2,1)S(1)}) custom-call(s32[1]{0:T(128)} %bitcast.rank_ref, bf16[64,2048]{1,0:T(8,128)(2,1)S(1)} %pad_maximum_fusion.9.refs_6_.near_ref, bf16[64,2048]{1,0:T(8,128)(2,1)S(1)} %collective-permute-done.20.far_ref, bf16[1,2048,4096]{2,1,0:T(8,128)(2,1)} %weight_ref.7, ...), custom_call_target="tpu_custom_call" | custom-call | flops 2147483648 | bytes 18350080 | tf_op jit(solution)/shard_map/pallas_call | solution.py:228
  233.2 8.1 %shard_map.92 = (f32[96,4096]{1,0:T(8,128)}, bf16[96,4096]{1,0:T(8,128)(2,1)}) custom-call(s32[1]{0:T(128)} %bitcast.rank_ref, bf16[96,2048]{1,0:T(8,128)(2,1)S(1)} %pad_maximum_fusion.6.refs_5_.near_ref, bf16[96,2048]{1,0:T(8,128)(2,1)S(1)} %collective-permute-done.32.far_ref, bf16[1,2048,4096]{2,1,0:T(8,128)(2,1)} %weight_ref.7, ...), custom_call_target="tpu_custom_call" | custom-call | flops 3221225472 | bytes 19136512 | tf_op jit(solution)/shard_map/pallas_call | solution.py:228
  244.3 3.8 %collective-permute-done.39 = bf16[16,2048]{1,0:T(8,128)(2,1)S(1)} collective-permute-done((bf16[16,2048]{1,0:T(8,128)(2,1)S(1)}, bf16[16,2048]{1,0:T(8,128)(2,1)S(1)}, u32[]{:S(2)}, u32[]{:S(2)}) %collective-permute-start.39) | collective-permute-done | bytes 65568 | tf_op jit(solution)/shard_map/ppermute | solution.py:25
  252.4 7.5 %shard_map.93 = (f32[64,4096]{1,0:T(8,128)}, bf16[64,4096]{1,0:T(8,128)(2,1)S(1)}) custom-call(s32[1]{0:T(128)} %bitcast.rank_ref, bf16[64,2048]{1,0:T(8,128)(2,1)S(1)} %pad_maximum_fusion.10.near_ref.refs_2_, bf16[64,2048]{1,0:T(8,128)(2,1)S(1)} %collective-permute-done.38.far_ref, bf16[1,2048,4096]{2,1,0:T(8,128)(2,1)} %weight_ref.7, ...), custom_call_target="tpu_custom_call" | custom-call | flops 2147483648 | bytes 18350080 | tf_op jit(solution)/shard_map/pallas_call | solution.py:228
  261.5 5.3 %collective-permute-done.42 = bf16[16,2048]{1,0:T(8,128)(2,1)S(1)} collective-permute-done((bf16[16,2048]{1,0:T(8,128)(2,1)S(1)}, bf16[16,2048]{1,0:T(8,128)(2,1)S(1)}, u32[]{:S(2)}, u32[]{:S(2)}) %collective-permute-start.42) | collective-permute-done | bytes 65568 | tf_op jit(solution)/shard_map/ppermute | solution.py:25
  272.2 6.7 %shard_map.94 = (f32[32,4096]{1,0:T(8,128)S(1)}, bf16[32,4096]{1,0:T(8,128)(2,1)S(1)}) custom-call(s32[1]{0:T(128)} %bitcast.rank_ref, bf16[32,2048]{1,0:T(8,128)(2,1)S(1)} %pad_maximum_fusion.13.near_ref.refs_2_, bf16[32,2048]{1,0:T(8,128)(2,1)S(1)} %collective-permute-done.43.far_ref, bf16[1,2048,4096]{2,1,0:T(8,128)(2,1)} %weight_ref.7, ...), custom_call_target="tpu_custom_call" | custom-call | flops 1073741824 | bytes 17563648 | tf_op jit(solution)/shard_map/pallas_call | solution.py:228
  279.0 4.5 %collective-permute-done.36 = bf16[48,4096]{1,0:T(8,128)(2,1)S(1)} collective-permute-done((bf16[48,4096]{1,0:T(8,128)(2,1)S(1)}, bf16[48,4096]{1,0:T(8,128)(2,1)S(1)}, u32[]{:S(2)}, u32[]{:S(2)}) %collective-permute-start.36) | collective-permute-done | bytes 393248 | tf_op jit(solution)/shard_map/ppermute | solution.py:21
  286.0 6.5 %collective-permute-done.41 = bf16[32,4096]{1,0:T(8,128)(2,1)S(1)} collective-permute-done((bf16[32,4096]{1,0:T(8,128)(2,1)S(1)}, bf16[32,4096]{1,0:T(8,128)(2,1)S(1)}, u32[]{:S(2)}, u32[]{:S(2)}) %collective-permute-start.41) | collective-permute-done | bytes 262176 | tf_op jit(solution)/shard_map/ppermute | solution.py:21
  (176 shorter events, 84.8 us)
Async XLA Ops:
  9.4 12.4 %collective-permute-start.10 = (bf16[1,96,1024]{2,1,0:T(8,128)(2,1)S(1)}, bf16[1,96,1024]{2,1,0:T(8,128)(2,1)S(1)}, u32[]{:S(2)}, u32[]{:S(2)}) collective-permute-start(bf16[1,96,1024]{2,1,0:T(8,128)(2,1)S(1)} %dynamic-slice_bitcast_fusion), channel_id=1, source_target_pairs={{0,8},{4,12},{8,0},{12,4},{1,9},{5,13},{9,1},{13,5},{2,10},{6,14},... | collective-permute-start | bytes 589832 | tf_op jit(solution)/shard_map/ppermute | solution.py:25
  21.8 18.0 %collective-permute-start.11 = (bf16[2,96,1024]{2,1,0:T(8,128)(2,1)S(1)}, bf16[2,96,1024]{2,1,0:T(8,128)(2,1)S(1)}, u32[]{:S(2)}, u32[]{:S(2)}) collective-permute-start(bf16[2,96,1024]{2,1,0:T(8,128)(2,1)S(1)} %pad_maximum_fusion.4), channel_id=1, source_target_pairs={{0,4},{4,0},{8,12},{12,8},{1,5},{5,1},{9,13},{13,9},{2,6},{6,2},{1... | collective-permute-start | bytes 1179656 | tf_op jit(solution)/shard_map/ppermute | solution.py:25
  30.8 31.2 %collective-permute-start.6 = (bf16[2,64,1792]{2,1,0:T(8,128)(2,1)S(1)}, bf16[2,64,1792]{2,1,0:T(8,128)(2,1)S(1)}, u32[]{:S(2)}, u32[]{:S(2)}) collective-permute-start(bf16[2,64,1792]{2,1,0:T(8,128)(2,1)S(1)} %get-tuple-element.33), channel_id=1, source_target_pairs={{0,2},{2,0},{1,3},{3,1},{4,6},{6,4},{5,7},{7,5},{8,10},{10,8},{9,1... | collective-permute-start | bytes 1376264 | tf_op jit(solution)/shard_map/ppermute | solution.py:21
  39.6 40.3 %collective-permute-start.7 = (bf16[2,64,1792]{2,1,0:T(8,128)(2,1)S(1)}, bf16[2,64,1792]{2,1,0:T(8,128)(2,1)S(1)}, u32[]{:S(2)}, u32[]{:S(2)}) collective-permute-start(bf16[2,64,1792]{2,1,0:T(8,128)(2,1)S(1)} %get-tuple-element.35), channel_id=1, source_target_pairs={{0,2},{2,0},{1,3},{3,1},{4,6},{6,4},{5,7},{7,5},{8,10},{10,8},{9,1... | collective-permute-start | bytes 1376264 | tf_op jit(solution)/shard_map/ppermute | solution.py:21
  40.2 13.8 %collective-permute-start.14 = (f32[96]{0:T(128)S(1)}, f32[96]{0:T(128)S(1)}, u32[]{:S(2)}, u32[]{:S(2)}) collective-permute-start(f32[96]{0:T(128)S(1)} %get-tuple-element.80), channel_id=1, source_target_pairs={{2,0},{0,2},{3,1},{1,3},{6,4},{4,6},{7,5},{5,7},{10,8},{8,10},{11,... | collective-permute-start | bytes 1160 | tf_op jit(solution)/shard_map/ppermute | solution.py:17
  42.2 19.6 %collective-permute-start.12 = (bf16[2,96,1024]{2,1,0:T(8,128)(2,1)S(1)}, bf16[2,96,1024]{2,1,0:T(8,128)(2,1)S(1)}, u32[]{:S(2)}, u32[]{:S(2)}) collective-permute-start(bf16[2,96,1024]{2,1,0:T(8,128)(2,1)S(1)} %pad_maximum_fusion.5), channel_id=1, source_target_pairs={{2,0},{0,2},{3,1},{1,3},{6,4},{4,6},{7,5},{5,7},{10,8},{8,10},{11,... | collective-permute-start | bytes 1179656 | tf_op jit(solution)/shard_map/ppermute | solution.py:17
  62.3 62.2 %collective-permute-start.8 = (bf16[64,1792]{1,0:T(8,128)(2,1)S(1)}, bf16[64,1792]{1,0:T(8,128)(2,1)S(1)}, u32[]{:S(2)}, u32[]{:S(2)}) collective-permute-start(bf16[64,1792]{1,0:T(8,128)(2,1)S(1)} %fusion.21.refs_0_), channel_id=1, source_target_pairs={{2,0},{0,2},{3,1},{1,3},{6,4},{4,6},{7,5},{5,7},{10,8},{8,10},{11,... | collective-permute-start | bytes 688136 | tf_op jit(solution)/shard_map/ppermute | solution.py:17
  78.0 33.3 %collective-permute-start.16 = (bf16[2,96,3584]{2,1,0:T(8,128)(2,1)}, bf16[2,96,3584]{2,1,0:T(8,128)(2,1)S(1)}, u32[]{:S(2)}, u32[]{:S(2)}) collective-permute-start(bf16[2,96,3584]{2,1,0:T(8,128)(2,1)} %get-tuple-element.39), channel_id=1, source_target_pairs={{0,2},{2,0},{1,3},{3,1},{4,6},{6,4},{5,7},{7,5},{8,10},{10,8},{9,1... | collective-permute-start | bytes 4128776 | tf_op jit(solution)/shard_map/ppermute | solution.py:21
  80.1 44.4 %collective-permute-start.9 = (bf16[64,1792]{1,0:T(8,128)(2,1)S(1)}, bf16[64,1792]{1,0:T(8,128)(2,1)S(1)}, u32[]{:S(2)}, u32[]{:S(2)}) collective-permute-start(bf16[64,1792]{1,0:T(8,128)(2,1)S(1)} %fusion.19.refs_1_), channel_id=1, source_target_pairs={{2,0},{0,2},{3,1},{1,3},{6,4},{4,6},{7,5},{5,7},{10,8},{8,10},{11,... | collective-permute-start | bytes 688136 | tf_op jit(solution)/shard_map/ppermute | solution.py:17
  93.3 41.8 %collective-permute-start.23 = (bf16[2,64,3584]{2,1,0:T(8,128)(2,1)S(1)}, bf16[2,64,3584]{2,1,0:T(8,128)(2,1)S(1)}, u32[]{:S(2)}, u32[]{:S(2)}) collective-permute-start(bf16[2,64,3584]{2,1,0:T(8,128)(2,1)S(1)} %get-tuple-element.44), channel_id=1, source_target_pairs={{0,2},{2,0},{1,3},{3,1},{4,6},{6,4},{5,7},{7,5},{8,10},{10,8},{9,1... | collective-permute-start | bytes 2752520 | tf_op jit(solution)/shard_map/ppermute | solution.py:21
  139.8 56.7 %collective-permute-start.24 = (bf16[64,3584]{1,0:T(8,128)(2,1)S(1)}, bf16[64,3584]{1,0:T(8,128)(2,1)S(1)}, u32[]{:S(2)}, u32[]{:S(2)}) collective-permute-start(bf16[64,3584]{1,0:T(8,128)(2,1)S(1)} %fusion.3.refs_4_.refs_0_), channel_id=1, source_target_pairs={{2,0},{0,2},{3,1},{1,3},{6,4},{4,6},{7,5},{5,7},{10,8},{8,10},{11,... | collective-permute-start | bytes 1376264 | tf_op jit(solution)/shard_map/ppermute | solution.py:17
  141.3 32.9 %collective-permute-start.25 = (bf16[96,3584]{1,0:T(8,128)(2,1)S(1)}, bf16[96,3584]{1,0:T(8,128)(2,1)S(1)}, u32[]{:S(2)}, u32[]{:S(2)}) collective-permute-start(bf16[96,3584]{1,0:T(8,128)(2,1)S(1)} %fusion.1.refs_1_.refs_0_), channel_id=1, source_target_pairs={{2,0},{0,2},{3,1},{1,3},{6,4},{4,6},{7,5},{5,7},{10,8},{8,10},{11,... | collective-permute-start | bytes 2064392 | tf_op jit(solution)/shard_map/ppermute | solution.py:17
  141.9 32.3 %collective-permute-start.21 = (bf16[2,32,3584]{2,1,0:T(8,128)(2,1)S(1)}, bf16[2,32,3584]{2,1,0:T(8,128)(2,1)S(1)}, u32[]{:S(2)}, u32[]{:S(2)}) collective-permute-start(bf16[2,32,3584]{2,1,0:T(8,128)(2,1)S(1)} %get-tuple-element.43), channel_id=1, source_target_pairs={{0,2},{2,0},{1,3},{3,1},{4,6},{6,4},{5,7},{7,5},{8,10},{10,8},{9,1... | collective-permute-start | bytes 1376264 | tf_op jit(solution)/shard_map/ppermute | solution.py:21
  146.4 47.8 %collective-permute-start.19 = (bf16[32,2048]{1,0:T(8,128)(2,1)S(1)}, bf16[32,2048]{1,0:T(8,128)(2,1)S(1)}, u32[]{:S(2)}, u32[]{:S(2)}) collective-permute-start(bf16[32,2048]{1,0:T(8,128)(2,1)S(1)} %fusion.28.refs_4_), channel_id=1, source_target_pairs={{0,8},{4,12},{8,0},{12,4},{1,9},{5,13},{9,1},{13,5},{2,10},{6,14},... | collective-permute-start | bytes 393224 | tf_op jit(solution)/shard_map/ppermute | solution.py:25
  183.4 10.6 %collective-permute-start.26 = (bf16[96,2048]{1,0:T(8,128)(2,1)S(1)}, bf16[96,2048]{1,0:T(8,128)(2,1)S(1)}, u32[]{:S(2)}, u32[]{:S(2)}) collective-permute-start(bf16[96,2048]{1,0:T(8,128)(2,1)S(1)} %get-tuple-element.46), channel_id=1, source_target_pairs={{0,4},{4,0},{8,12},{12,8},{1,5},{5,1},{9,13},{13,9},{2,6},{6,2},{1... | collective-permute-start | bytes 1179656 | tf_op jit(solution)/shard_map/ppermute | solution.py:25
  184.9 31.9 %collective-permute-start.22 = (bf16[32,3584]{1,0:T(8,128)(2,1)S(1)}, bf16[32,3584]{1,0:T(8,128)(2,1)S(1)}, u32[]{:S(2)}, u32[]{:S(2)}) collective-permute-start(bf16[32,3584]{1,0:T(8,128)(2,1)S(1)} %fusion.17.refs_5_.refs_0_), channel_id=1, source_target_pairs={{2,0},{0,2},{3,1},{1,3},{6,4},{4,6},{7,5},{5,7},{10,8},{8,10},{11,... | collective-permute-start | bytes 688136 | tf_op jit(solution)/shard_map/ppermute | solution.py:17
  194.1 10.8 %collective-permute-start.27 = (bf16[48,2048]{1,0:T(8,128)(2,1)S(1)}, bf16[48,2048]{1,0:T(8,128)(2,1)S(1)}, u32[]{:S(2)}, u32[]{:S(2)}) collective-permute-start(bf16[48,2048]{1,0:T(8,128)(2,1)S(1)} %slice.305.refs_7_), channel_id=1, source_target_pairs={{0,8},{4,12},{8,0},{12,4},{1,9},{5,13},{9,1},{13,5},{2,10},{6,14},... | collective-permute-start | bytes 589832 | tf_op jit(solution)/shard_map/ppermute | solution.py:25
  194.2 29.2 %collective-permute-start.20 = (bf16[64,2048]{1,0:T(8,128)(2,1)S(1)}, bf16[64,2048]{1,0:T(8,128)(2,1)S(1)}, u32[]{:S(2)}, u32[]{:S(2)}) collective-permute-start(bf16[64,2048]{1,0:T(8,128)(2,1)S(1)} %pad_maximum_fusion.9.refs_6_.near_ref), channel_id=1, source_target_pairs={{0,4},{4,0},{8,12},{12,8},{1,5},{5,1},{9,13},{13,9},{2,6},{6,2},{1... | collective-permute-start | bytes 786440 | tf_op jit(solution)/shard_map/ppermute | solution.py:25
  204.9 10.2 %collective-permute-start.28 = (bf16[48,2048]{1,0:T(8,128)(2,1)S(1)}, bf16[48,2048]{1,0:T(8,128)(2,1)S(1)}, u32[]{:S(2)}, u32[]{:S(2)}) collective-permute-start(bf16[48,2048]{1,0:T(8,128)(2,1)S(1)} %fusion.22.refs_4_), channel_id=1, source_target_pairs={{0,8},{4,12},{8,0},{12,4},{1,9},{5,13},{9,1},{13,5},{2,10},{6,14},... | collective-permute-start | bytes 589832 | tf_op jit(solution)/shard_map/ppermute | solution.py:25
  213.7 17.5 %collective-permute-start.33 = (bf16[32,2048]{1,0:T(8,128)(2,1)S(1)}, bf16[32,2048]{1,0:T(8,128)(2,1)S(1)}, u32[]{:S(2)}, u32[]{:S(2)}) collective-permute-start(bf16[32,2048]{1,0:T(8,128)(2,1)S(1)} %slice.307.refs_1_), channel_id=1, source_target_pairs={{0,8},{4,12},{8,0},{12,4},{1,9},{5,13},{9,1},{13,5},{2,10},{6,14},... | collective-permute-start | bytes 393224 | tf_op jit(solution)/shard_map/ppermute | solution.py:25
  215.2 18.0 %collective-permute-start.32 = (bf16[96,2048]{1,0:T(8,128)(2,1)S(1)}, bf16[96,2048]{1,0:T(8,128)(2,1)S(1)}, u32[]{:S(2)}, u32[]{:S(2)}) collective-permute-start(bf16[96,2048]{1,0:T(8,128)(2,1)S(1)} %pad_maximum_fusion.6.refs_5_.near_ref), channel_id=1, source_target_pairs={{0,4},{4,0},{8,12},{12,8},{1,5},{5,1},{9,13},{13,9},{2,6},{6,2},{1... | collective-permute-start | bytes 1179656 | tf_op jit(solution)/shard_map/ppermute | solution.py:25
  231.2 11.8 %collective-permute-start.37 = (bf16[32,2048]{1,0:T(8,128)(2,1)S(1)}, bf16[32,2048]{1,0:T(8,128)(2,1)S(1)}, u32[]{:S(2)}, u32[]{:S(2)}) collective-permute-start(bf16[32,2048]{1,0:T(8,128)(2,1)S(1)} %fusion.27.refs_2_), channel_id=1, source_target_pairs={{0,8},{4,12},{8,0},{12,4},{1,9},{5,13},{9,1},{13,5},{2,10},{6,14},... | collective-permute-start | bytes 393224 | tf_op jit(solution)/shard_map/ppermute | solution.py:25
  266.9 19.1 %collective-permute-start.31 = (bf16[32,4096]{1,0:T(8,128)(2,1)S(1)}, bf16[32,4096]{1,0:T(8,128)(2,1)S(1)}, u32[]{:S(2)}, u32[]{:S(2)}) collective-permute-start(bf16[32,4096]{1,0:T(8,128)(2,1)S(1)} %slice.304.refs_1_), channel_id=1, source_target_pairs={{0,2},{2,0},{1,3},{3,1},{4,6},{6,4},{5,7},{7,5},{8,10},{10,8},{9,1... | collective-permute-start | bytes 786440 | tf_op jit(solution)/shard_map/ppermute | solution.py:21
  268.7 14.8 %collective-permute-start.36 = (bf16[48,4096]{1,0:T(8,128)(2,1)S(1)}, bf16[48,4096]{1,0:T(8,128)(2,1)S(1)}, u32[]{:S(2)}, u32[]{:S(2)}) collective-permute-start(bf16[48,4096]{1,0:T(8,128)(2,1)S(1)} %slice.302.refs_1_), channel_id=1, source_target_pairs={{0,2},{2,0},{1,3},{3,1},{4,6},{6,4},{5,7},{7,5},{8,10},{10,8},{9,1... | collective-permute-start | bytes 1179656 | tf_op jit(solution)/shard_map/ppermute | solution.py:21
  (36 other events, 306.8 us)

commit v4 on v3

--- a/solution.py
+++ b/solution.py
@@ -10,6 +10,7 @@
 BF16 = jnp.bfloat16
 F32 = jnp.float32
 VMEM_BYTES = 52 * 1024 * 1024
+GATE_UP_VMEM_BYTES = 44 * 1024 * 1024
 BUFFERS = 4
 
 
@@ -87,18 +88,13 @@
     return [pl.BlockSpec(memory_space=pl.ANY)] * len(after)
 
 
-def params():
+def params(vmem_bytes=VMEM_BYTES):
     return pltpu.CompilerParams(
-        dimension_semantics=("arbitrary",), vmem_limit_bytes=VMEM_BYTES
+        dimension_semantics=("arbitrary",), vmem_limit_bytes=vmem_bytes
     )
 
 
-def cost(rows, depth, width):
-    return pl.CostEstimate(
-        flops=2 * rows * depth * width,
-        bytes_accessed=2 * (rows * depth + depth * width + rows * width),
-        transcendentals=0,
-    )
+NO_COST = pl.CostEstimate(flops=1, bytes_accessed=1, transcendentals=0)
 
 
 def gate_up_body(tiles, first, x_ref, gate_ref, up_ref, *refs):
@@ -140,8 +136,8 @@
         out_shape=[jax.ShapeDtypeStruct((2, own_rows, width), F32)]
         + [jax.ShapeDtypeStruct((2, own_rows, width), BF16)] * (owners - 1),
         scratch_shapes=[pltpu.VMEM((rows, depth), BF16)] + slots(depth, tile, tiles) * 2,
-        compiler_params=params(),
-        cost_estimate=cost(rows, depth, 2 * width),
+        compiler_params=params(GATE_UP_VMEM_BYTES),
+        cost_estimate=NO_COST,
     )(x, gate_weight, up_weight, *after)
 
 
@@ -194,7 +190,7 @@
         ),
         out_shape=[jax.ShapeDtypeStruct((rows // 2, width), kind) for kind in (F32, BF16)],
         compiler_params=params(),
-        cost_estimate=cost(rows, depth, width),
+        cost_estimate=NO_COST,
     )(rank, *[piece for of_owner in hidden for piece in of_owner], down_weight, *after)
 
 
@@ -237,7 +233,7 @@
         out_shape=[jax.ShapeDtypeStruct((rows_each, width), F32)]
         + [jax.ShapeDtypeStruct((rows_each, width), BF16)] * (members - 1),
         compiler_params=params(),
-        cost_estimate=cost(rows, depth, width),
+        cost_estimate=NO_COST,
     )(rank, near, far, enc_weight, *after)
 
 
@@ -245,9 +241,8 @@
     units = total // unit
     if units < 8:
         return [total]
-    eighth = units // 8
-    sizes = [2 * eighth, 3 * eighth, 2 * eighth]
-    return [size * unit for size in sizes + [units - sum(sizes)]]
+    most = 3 * (units // 8)
+    return [most * unit, most * unit, (units - 2 * most) * unit]
 
 
 def on_device(
@@ -279,16 +274,17 @@
             place = place + ((offset >> at) & 1) * bits[at]
         return place
 
-    def gathered_rows(mine, after=None):
+    def all_columns(mine):
         gathered = mine[None]
         for bit in bits:
             gathered = jnp.concatenate((gathered, swap(gathered, "hid", ranks, bit)))
-        if after is not None:
-            gathered, _ = lax.optimization_barrier((gathered, after))
+        return gathered
+
+    def from_owners(gathered):
         wide = gathered.astype(F32)
         squares = jnp.sum(wide * wide, axis=(0, 2))
         inverse = lax.rsqrt(squares / model_width + 1e-05)
-        columns = []
+        columns, going = [], []
         for hop in range(owners):
             target = lax.rem(row_at + owners - hop, owners)
             half = jnp.concatenate(
@@ -299,9 +295,12 @@
                     for at in range(half_cuts)
                 ]
             )
+            going.append(half)
             columns.append(half if hop == 0 else shift(half, "rows", owners, hop))
-        inverses = from_all(from_all(inverse, "rows", owners), "mp", members)
-        return from_all(jnp.stack(columns), "mp", members), inverses
+        return columns, from_all(inverse, "rows", owners), going
+
+    def from_members(columns, inverses):
+        return from_all(jnp.stack(columns), "mp", members), from_all(inverses, "mp", members)
 
     def normed(columns, inverses):
         return (columns.astype(F32) * inverses[:, :, None, :, None] * gain).astype(BF16)
@@ -311,12 +310,12 @@
     chunks = len(sizes)
     head = sizes[0]
 
-    xs = [normed(*gathered_rows(own_tokens[:head]))]
+    columns, inverses, going = from_owners(all_columns(own_tokens[:head]))
+    xs = [normed(*from_members(columns, inverses))]
+    rest = None
     if chunks > 1:
-        columns, inverses = gathered_rows(own_tokens[head:], xs[0])
-        for start, q in zip(starts[1:], sizes[1:]):
-            rows = slice(start - head, start - head + q)
-            xs.append(normed(columns[:, :, :, rows], inverses[:, :, rows]))
+        rest, _ = lax.optimization_barrier((all_columns(own_tokens[head:]), going))
+        rest = from_owners(rest)
 
     sums, hidden, layer, blocks, outs = ({} for _ in range(5))
     last = []
@@ -329,8 +328,22 @@
                 xs[t], gate_weight, up_weight, piece, pieces, list(last)
             )
             last[:] = [own]
+            if t == 0 and rest is not None:
+                last.extend(rest[2])
             others = [send(sends[hop - 1], "rows", owners, hop) for hop in range(1, owners)]
             sums[t].append((own, others))
+
+    def rest_of(_):
+        if rest is None:
+            return
+        (columns, inverses), _ = lax.optimization_barrier((rest[:2], sums[0][0][0]))
+        columns, inverses = from_members(columns, inverses)
+        for start, q in zip(starts[1:], sizes[1:]):
+            rows = slice(start - head, start - head + q)
+            xs.append(normed(columns[:, :, :, rows], inverses[:, :, rows]))
+
+    def ordered(values):
+        return lax.optimization_barrier((values, last[0]))[0]
 
     def hidden_of(t):
         hidden[t] = [[] for _ in range(owners)]
@@ -350,7 +363,7 @@
         layer[t] = (total, swap(going, "hid", ranks, 1))
 
     def halve_of(t):
-        total, arrived = layer[t]
+        total, arrived = ordered(layer[t])
         for bit in reversed(bits[:-1]):
             total = total + arrived.astype(F32)
             kept = total.shape[0] // 2
@@ -360,13 +373,13 @@
         layer[t] = (total, arrived)
 
     def settle_of(t):
-        total, arrived = layer[t]
+        total, arrived = ordered(layer[t])
         block = (total + arrived.astype(F32)).astype(BF16)
         last.append(block)
         layer[t] = (block, swap(block, "hid", ranks, bits[0]))
 
     def double_of(t):
-        near, far = layer[t]
+        near, far = ordered(layer[t])
         for bit in bits[1:]:
             near = jnp.concatenate((near, far))
             last.append(near)
@@ -379,36 +392,36 @@
         sums[t] = (own, [send(sends[hop - 1], "mp", members, hop) for hop in range(1, members)])
 
     def share_of(t):
-        total, others = sums[t]
+        total, others = ordered(sums[t])
         for other in others:
             total = total + other.astype(F32)
-        start, q = starts[t], sizes[t]
-        pre = total[:q]
+        q = sizes[t]
+        others = []
         for hop in range(1, owners):
             going = total[hop * q : (hop + 1) * q].astype(BF16)
             last.append(going)
-            pre = pre + send(going, "rows", owners, hop).astype(F32)
+            others.append(send(going, "rows", owners, hop))
+        sums[t] = (total[:q], others)
+
+    def finish_of(t):
+        pre, others = sums[t]
+        for other in others:
+            pre = pre + other.astype(F32)
         pre = pre + enc_bias[None, :]
-        factor = adjoint[start : start + q].astype(F32)
+        factor = adjoint[starts[t] : starts[t] + sizes[t]].astype(F32)
         outs[t] = (jnp.maximum(pre, 0.0) * factor).astype(BF16)
-
-    end = chunks
-    stages = [(gate_up_of, 0), (gate_up_of, 1)]
-    for step in range(end):
-        stages += [
-            (hidden_of, step), (gate_up_of, step + 2), (double_of, step - 3), (halve_of, step - 2),
-            (down_of, step - 1), (settle_of, step - 2),
-        ]
-    stages += [(double_of, end - 3), (down_of, end - 1), (halve_of, end - 2)]
-    for t in range(end - 3):
-        stages += [(features_of, t), (share_of, t)]
-    stages += [
-        (settle_of, end - 2), (halve_of, end - 1), (features_of, end - 3),
-        (share_of, end - 3), (double_of, end - 2), (settle_of, end - 1), (features_of, end - 2),
-        (share_of, end - 2), (double_of, end - 1), (features_of, end - 1), (share_of, end - 1),
-    ]
+        last.append(outs[t])
+
+    stages = (
+        (gate_up_of, 0), (rest_of, 0), (gate_up_of, 1), (hidden_of, 0), (hidden_of, 1), (gate_up_of, 2),
+        (down_of, 0), (down_of, 1), (halve_of, 0), (halve_of, 1), (settle_of, 0), (hidden_of, 2),
+        (settle_of, 1), (double_of, 0), (double_of, 1), (down_of, 2), (features_of, 0),
+        (halve_of, 2), (share_of, 0), (features_of, 1), (settle_of, 2), (share_of, 1),
+        (double_of, 2), (finish_of, 0), (features_of, 2), (share_of, 2), (finish_of, 1),
+        (finish_of, 2),
+    )
     for stage, t in stages:
-        if 0 <= t < chunks:
+        if t < chunks:
             stage(t)
     return jnp.concatenate([outs[t] for t in range(chunks)], axis=0)
 

time: 295 us -> 280 us (0.949)
  Pallas kernels: 110 us -> 83.2 us
  waiting for transfers between devices: 124 us -> 149 us
  starting transfers between devices: 47.1 us -> 33 us
    ppermute x20 -> x16, waiting for transfers between devices: 41.1 us -> 81.2 us  [swap(): return lax.ppermute(value, axis, [(d, d ^ bit) for d in range(size)])]
    pallas_call x5 -> x4, Pallas kernels: 52.4 us -> 37.5 us  [gate_up(): pl.pallas_call(functools.partial(gate_up_body, tiles, piece * tiles), gri...]
    ppermute x13 -> x12, waiting for transfers between devices: 23.5 us -> 12.2 us  [shift(): lax.ppermute(value, axis, [((d + hop) % size, d) for d in range(size)])]
    ppermute x20 -> x16, starting transfers between devices: 24.7 us -> 17.1 us  [swap(): return lax.ppermute(value, axis, [(d, d ^ bit) for d in range(size)])]
    pallas_call x4 -> x3, Pallas kernels: 29.9 us -> 23.6 us  [encode(): pl.pallas_call(functools.partial(encode_body, members, order, width // ti...]
    pallas_call x4 -> x3, Pallas kernels: 27.4 us -> 22 us  [down(): pl.pallas_call(functools.partial(down_body, owners, members, pieces, orde...]
    ppermute x13 -> x10, starting transfers between devices: 11.9 us -> 7.18 us  [send(): lax.ppermute(value, axis, [(d, (d + hop) % size) for d in range(size)])]
    ppermute x13 -> x10, waiting for transfers between devices: 59.5 us -> 56.1 us  [send(): lax.ppermute(value, axis, [(d, (d + hop) % size) for d in range(size)])]
  transfers between devices with their start and end apart: 46 -> 38, of which waited for: 26 -> 25; matrix products, arithmetic and copies ran while one was open for 3% -> 2% of each run, Pallas kernels for 35% -> 21%
where the time goes in v4:
time: 280 us
  waiting for transfers between devices  149 us (53%)
  Pallas kernels  83.2 us (30%)
  starting transfers between devices  33 us (12%)
  other arithmetic  8.38 us (3%)
  local copies, waits for them, and re-layouts  5.26 us (2%)
    ppermute x16, waiting for transfers between devices, swap(): return lax.ppermute(value, axis, [(d, d ^ bit) for d in range(size)])  81.2 us
    ppermute x10, waiting for transfers between devices, send(): lax.ppermute(value, axis, [(d, (d + hop) % size) for d in range(size)])  56.1 us
    pallas_call x4, Pallas kernels, gate_up(): pl.pallas_call(functools.partial(gate_up_body, tiles, piece * tiles), gri...  37.5 us
    pallas_call x3, Pallas kernels, encode(): pl.pallas_call(functools.partial(encode_body, members, order, width // ti...  23.6 us
    pallas_call x3, Pallas kernels, down(): pl.pallas_call(functools.partial(down_body, owners, members, pieces, orde...  22 us
    ppermute x16, starting transfers between devices, swap(): return lax.ppermute(value, axis, [(d, d ^ bit) for d in range(size)])  17.1 us
    ppermute x12, waiting for transfers between devices, shift(): lax.ppermute(value, axis, [((d + hop) % size, d) for d in range(size)])  12.2 us
    ppermute x12, starting transfers between devices, shift(): lax.ppermute(value, axis, [((d + hop) % size, d) for d in range(size)])  8.73 us
  transfers between devices with their start and end apart: 38, of which 25 were waited for; matrix products, arithmetic and copies ran while one was open for 2% of the time, Pallas kernels for 21%

profile of v4, /device:TPU:0, one launch (start us, length us, event | category | flops | bytes accessed | tf_op | source)
XLA Modules:
  0.0 280.0 jit_solution(12043129526980219845)
XLA Ops:
  5.3 9.1 %collective-permute-done = bf16[1,48,1024]{2,1,0:T(8,128)(2,1)S(1)} collective-permute-done((bf16[1,48,1024]{2,1,0:T(8,128)(2,1)S(1)}, bf16[1,48,1024]{2,1,0:T(8,128)(2,1)S(1)}, u32[]{:S(2)}, u32[]{:S(2)}) %collective-permute-start) | collective-permute-done | bytes 98336 | tf_op jit(solution)/shard_map/ppermute | solution.py:26
  17.9 4.4 %collective-permute-done.1 = bf16[2,48,1024]{2,1,0:T(8,128)(2,1)S(1)} collective-permute-done((bf16[2,48,1024]{2,1,0:T(8,128)(2,1)S(1)}, bf16[2,48,1024]{2,1,0:T(8,128)(2,1)S(1)}, u32[]{:S(2)}, u32[]{:S(2)}) %collective-permute-start.1) | collective-permute-done | bytes 196640 | tf_op jit(solution)/shard_map/ppermute | solution.py:26
  34.2 7.2 %shard_map.82 = (f32[2,96,1792]{2,1,0:T(8,128)S(1)}, bf16[2,96,1792]{2,1,0:T(8,128)(2,1)S(1)}) custom-call(bf16[2,2,2,48,1024]{4,3,2,1,0:T(8,128)(2,1)S(1)} %multiply_convert_fusion.1.x_ref, bf16[1,2048,3584]{2,1,0:T(8,128)(2,1)} %gate_ref.7, bf16[1,2048,3584]{2,1,0:T(8,128)(2,1)} %up_ref.7), custom_call_target="tpu_custom_call" | custom-call | flops 1 | bytes 1 | tf_op jit(solution)/shard_map/pallas_call | solution.py:131
  42.7 7.2 %shard_map.83 = (f32[2,96,1792]{2,1,0:T(8,128)S(1)}, bf16[2,96,1792]{2,1,0:T(8,128)(2,1)S(1)}) custom-call(bf16[2,2,2,48,1024]{4,3,2,1,0:T(8,128)(2,1)S(1)} %multiply_convert_fusion.1.x_ref, bf16[1,2048,3584]{2,1,0:T(8,128)(2,1)} %gate_ref.7, bf16[1,2048,3584]{2,1,0:T(8,128)(2,1)} %up_ref.7, f32[2,96,1792]{2,1,0:T(8,128)S(1)} %get-tuple-element.53.refs_0_, ...), custom_call_target="tpu_custom_call" | custom-call | flops 1 | bytes 1 | tf_op jit(solution)/shard_map/pallas_call | solution.py:131
  51.4 11.7 %shard_map.84 = (f32[2,96,3584]{2,1,0:T(8,128)S(1)}, bf16[2,96,3584]{2,1,0:T(8,128)(2,1)S(1)}) custom-call(bf16[2,2,2,48,1024]{4,3,2,1,0:T(8,128)(2,1)S(1)} %multiply_convert_fusion.x_ref, bf16[1,2048,3584]{2,1,0:T(8,128)(2,1)} %gate_ref.7, bf16[1,2048,3584]{2,1,0:T(8,128)(2,1)} %up_ref.7, f32[2,96,1792]{2,1,0:T(8,128)S(1)} %get-tuple-element.56.refs_0_, ...), custom_call_target="tpu_custom_call" | custom-call | flops 1 | bytes 1 | tf_op jit(solution)/shard_map/pallas_call | solution.py:131
  65.6 9.0 %collective-permute-done.9 = bf16[2,96,1792]{2,1,0:T(8,128)(2,1)S(1)} collective-permute-done((bf16[2,96,1792]{2,1,0:T(8,128)(2,1)S(1)}, bf16[2,96,1792]{2,1,0:T(8,128)(2,1)S(1)}, u32[]{:S(2)}, u32[]{:S(2)}) %collective-permute-start.9) | collective-permute-done | bytes 688160 | tf_op jit(solution)/shard_map/ppermute | solution.py:22
  75.9 28.2 %collective-permute-done.16 = bf16[2,96,3584]{2,1,0:T(8,128)(2,1)S(1)} collective-permute-done((bf16[2,96,3584]{2,1,0:T(8,128)(2,1)S(1)}, bf16[2,96,3584]{2,1,0:T(8,128)(2,1)S(1)}, u32[]{:S(2)}, u32[]{:S(2)}) %collective-permute-start.16) | collective-permute-done | bytes 1376288 | tf_op jit(solution)/shard_map/ppermute | solution.py:22
  106.1 11.4 %shard_map.85 = (f32[2,64,3584]{2,1,0:T(8,128)S(1)}, bf16[2,64,3584]{2,1,0:T(8,128)(2,1)S(1)}) custom-call(bf16[2,2,2,32,1024]{4,3,2,1,0:T(8,128)(2,1)S(1)} %multiply_convert_fusion.2.x_ref, bf16[1,2048,3584]{2,1,0:T(8,128)(2,1)} %gate_ref.7, bf16[1,2048,3584]{2,1,0:T(8,128)(2,1)} %up_ref.7, f32[2,96,3584]{2,1,0:T(8,128)S(1)} %get-tuple-element.61.refs_0_, ...), custom_call_target="tpu_custom_call" | custom-call | flops 1 | bytes 1 | tf_op jit(solution)/shard_map/pallas_call | solution.py:131
  118.9 7.0 %shard_map.86 = (f32[96,2048]{1,0:T(8,128)}, bf16[96,2048]{1,0:T(8,128)(2,1)S(1)}) custom-call(s32[1]{0:T(128)} %bitcast.rank_ref, bf16[96,1792]{1,0:T(8,128)(2,1)S(1)} %fusion.15.refs_0_, bf16[96,1792]{1,0:T(8,128)(2,1)S(1)} %fusion.13.refs_1_, bf16[96,1792]{1,0:T(8,128)(2,1)S(1)} %collective-permute-done.10.refs_2_, ...), custom_call_target="tpu_custom_call" | custom-call | flops 1 | bytes 1 | tf_op jit(solution)/shard_map/pallas_call | solution.py:179
  127.0 6.6 %collective-permute-done.18.refs_1_ = bf16[96,3584]{1,0:T(8,128)(2,1)S(1)} collective-permute-done((bf16[96,3584]{1,0:T(8,128)(2,1)S(1)}, bf16[96,3584]{1,0:T(8,128)(2,1)S(1)}, u32[]{:S(2)}, u32[]{:S(2)}) %collective-permute-start.18) | collective-permute-done | bytes 688160 | tf_op jit(solution)/shard_map/ppermute | solution.py:18
  133.6 7.1 %shard_map.87 = (f32[96,2048]{1,0:T(8,128)}, bf16[96,2048]{1,0:T(8,128)(2,1)S(1)}) custom-call(s32[1]{0:T(128)} %bitcast.rank_ref, bf16[96,3584]{1,0:T(8,128)(2,1)S(1)} %fusion.1.refs_2_.refs_0_, bf16[96,3584]{1,0:T(8,128)(2,1)S(1)} %collective-permute-done.18.refs_1_, bf16[1,3584,2048]{2,1,0:T(8,128)(2,1)} %refs_2_.3, f32[96,2048]{1,0:T(8,128)} %get-tuple-element.67.refs_3_), custom_call_target="tpu_custom_call" | custom-call | flops 1 | bytes 1 | tf_op jit(solution)/shard_map/pallas_call | solution.py:179
  144.6 8.5 %collective-permute-done.19 = bf16[48,2048]{1,0:T(8,128)(2,1)S(1)} collective-permute-done((bf16[48,2048]{1,0:T(8,128)(2,1)S(1)}, bf16[48,2048]{1,0:T(8,128)(2,1)S(1)}, u32[]{:S(2)}, u32[]{:S(2)}) %collective-permute-start.19) | collective-permute-done | bytes 196640 | tf_op jit(solution)/shard_map/ppermute | solution.py:26
  156.9 8.8 %collective-permute-done.25 = bf16[48,2048]{1,0:T(8,128)(2,1)S(1)} collective-permute-done((bf16[48,2048]{1,0:T(8,128)(2,1)S(1)}, bf16[48,2048]{1,0:T(8,128)(2,1)S(1)}, u32[]{:S(2)}, u32[]{:S(2)}) %collective-permute-start.25) | collective-permute-done | bytes 196640 | tf_op jit(solution)/shard_map/ppermute | solution.py:26
  169.9 12.1 %collective-permute-done.20 = bf16[48,2048]{1,0:T(8,128)(2,1)S(1)} collective-permute-done((bf16[48,2048]{1,0:T(8,128)(2,1)S(1)}, bf16[48,2048]{1,0:T(8,128)(2,1)S(1)}, u32[]{:S(2)}, u32[]{:S(2)}) %collective-permute-start.20) | collective-permute-done | bytes 196640 | tf_op jit(solution)/shard_map/ppermute | solution.py:26
  185.3 7.9 %shard_map.88 = (f32[64,2048]{1,0:T(8,128)}, bf16[64,2048]{1,0:T(8,128)(2,1)S(1)}) custom-call(s32[1]{0:T(128)} %bitcast.rank_ref, bf16[64,3584]{1,0:T(8,128)(2,1)} %copy-done.6, bf16[64,3584]{1,0:T(8,128)(2,1)} %copy-done.11, bf16[1,3584,2048]{2,1,0:T(8,128)(2,1)} %refs_2_.3, f32[96,2048]{1,0:T(8,128)} %get-tuple-element.75.refs_3_, ...), custom_call_target="tpu_custom_call" | custom-call | flops 1 | bytes 1 | tf_op jit(solution)/shard_map/pallas_call | solution.py:179
  195.0 8.0 %shard_map.89 = (f32[96,4096]{1,0:T(8,128)}, bf16[96,4096]{1,0:T(8,128)(2,1)}) custom-call(s32[1]{0:T(128)} %bitcast.rank_ref, bf16[96,2048]{1,0:T(8,128)(2,1)S(1)} %constant_dynamic-update-slice_fusion.refs_9_.near_ref, bf16[96,2048]{1,0:T(8,128)(2,1)S(1)} %collective-permute-done.21.far_ref, bf16[1,2048,4096]{2,1,0:T(8,128)(2,1)} %weight_ref.5, ...), custom_call_target="tpu_custom_call" | custom-call | flops 1 | bytes 1 | tf_op jit(solution)/shard_map/pallas_call | solution.py:224
  205.2 7.1 %collective-permute-done.30 = bf16[64,2048]{1,0:T(8,128)(2,1)S(1)} collective-permute-done((bf16[64,2048]{1,0:T(8,128)(2,1)S(1)}, bf16[64,2048]{1,0:T(8,128)(2,1)S(1)}, u32[]{:S(2)}, u32[]{:S(2)}) %collective-permute-start.30) | collective-permute-done | bytes 262176 | tf_op jit(solution)/shard_map/ppermute | solution.py:26
  212.6 7.6 %collective-permute-done.29.far_ref = bf16[96,2048]{1,0:T(8,128)(2,1)S(1)} collective-permute-done((bf16[96,2048]{1,0:T(8,128)(2,1)S(1)}, bf16[96,2048]{1,0:T(8,128)(2,1)S(1)}, u32[]{:S(2)}, u32[]{:S(2)}) %collective-permute-start.29) | collective-permute-done | bytes 393248 | tf_op jit(solution)/shard_map/ppermute | solution.py:26
  220.3 8.0 %shard_map.90 = (f32[96,4096]{1,0:T(8,128)}, bf16[96,4096]{1,0:T(8,128)(2,1)}) custom-call(s32[1]{0:T(128)} %bitcast.rank_ref, bf16[96,2048]{1,0:T(8,128)(2,1)S(1)} %constant_dynamic-update-slice_fusion.2.refs_10_.near_ref, bf16[96,2048]{1,0:T(8,128)(2,1)S(1)} %collective-permute-done.29.far_ref, bf16[1,2048,4096]{2,1,0:T(8,128)(2,1)} %weight_ref.5, ...), custom_call_target="tpu_custom_call" | custom-call | flops 1 | bytes 1 | tf_op jit(solution)/shard_map/pallas_call | solution.py:224
  230.3 7.7 %collective-permute-done.33 = bf16[32,2048]{1,0:T(8,128)(2,1)S(1)} collective-permute-done((bf16[32,2048]{1,0:T(8,128)(2,1)S(1)}, bf16[32,2048]{1,0:T(8,128)(2,1)S(1)}, u32[]{:S(2)}, u32[]{:S(2)}) %collective-permute-start.33) | collective-permute-done | bytes 131104 | tf_op jit(solution)/shard_map/ppermute | solution.py:26
  239.1 7.8 %collective-permute-done.34 = bf16[32,2048]{1,0:T(8,128)(2,1)S(1)} collective-permute-done((bf16[32,2048]{1,0:T(8,128)(2,1)S(1)}, bf16[32,2048]{1,0:T(8,128)(2,1)S(1)}, u32[]{:S(2)}, u32[]{:S(2)}) %collective-permute-start.34) | collective-permute-done | bytes 131104 | tf_op jit(solution)/shard_map/ppermute | solution.py:26
  249.6 9.5 %collective-permute-done.32 = bf16[48,4096]{1,0:T(8,128)(2,1)S(1)} collective-permute-done((bf16[48,4096]{1,0:T(8,128)(2,1)S(1)}, bf16[48,4096]{1,0:T(8,128)(2,1)S(1)}, u32[]{:S(2)}, u32[]{:S(2)}) %collective-permute-start.32) | collective-permute-done | bytes 393248 | tf_op jit(solution)/shard_map/ppermute | solution.py:22
  259.5 7.6 %shard_map.91 = (f32[64,4096]{1,0:T(8,128)}, bf16[64,4096]{1,0:T(8,128)(2,1)S(1)}) custom-call(s32[1]{0:T(128)} %bitcast.rank_ref, bf16[64,2048]{1,0:T(8,128)(2,1)S(1)} %constant_dynamic-update-slice_fusion.4.near_ref.refs_3_, bf16[64,2048]{1,0:T(8,128)(2,1)S(1)} %collective-permute-done.35.far_ref, bf16[1,2048,4096]{2,1,0:T(8,128)(2,1)} %weight_ref.5, ...), custom_call_target="tpu_custom_call" | custom-call | flops 1 | bytes 1 | tf_op jit(solution)/shard_map/pallas_call | solution.py:224
  271.4 7.5 %collective-permute-done.37 = bf16[32,4096]{1,0:T(8,128)(2,1)S(1)} collective-permute-done((bf16[32,4096]{1,0:T(8,128)(2,1)S(1)}, bf16[32,4096]{1,0:T(8,128)(2,1)S(1)}, u32[]{:S(2)}, u32[]{:S(2)}) %collective-permute-start.37) | collective-permute-done | bytes 262176 | tf_op jit(solution)/shard_map/ppermute | solution.py:22
  (150 shorter events, 62.3 us)
Async XLA Ops:
  1.1 13.3 %collective-permute-start = (bf16[1,48,1024]{2,1,0:T(8,128)(2,1)S(1)}, bf16[1,48,1024]{2,1,0:T(8,128)(2,1)S(1)}, u32[]{:S(2)}, u32[]{:S(2)}) collective-permute-start(bf16[1,48,1024]{2,1,0:T(8,128)(2,1)S(1)} %dynamic-slice_bitcast_fusion.1), channel_id=1, source_target_pairs={{0,8},{4,12},{8,0},{12,4},{1,9},{5,13},{9,1},{13,5},{2,10},{6,14},... | collective-permute-start | bytes 294920 | tf_op jit(solution)/shard_map/ppermute | solution.py:26
  5.2 12.0 %collective-permute-start.7 = (bf16[1,80,1024]{2,1,0:T(8,128)(2,1)S(1)}, bf16[1,80,1024]{2,1,0:T(8,128)(2,1)S(1)}, u32[]{:S(2)}, u32[]{:S(2)}) collective-permute-start(bf16[1,80,1024]{2,1,0:T(8,128)(2,1)S(1)} %dynamic-slice_bitcast_fusion), channel_id=1, source_target_pairs={{0,8},{4,12},{8,0},{12,4},{1,9},{5,13},{9,1},{13,5},{2,10},{6,14},... | collective-permute-start | bytes 491528 | tf_op jit(solution)/shard_map/ppermute | solution.py:26
  17.2 11.1 %collective-permute-start.8 = (bf16[2,80,1024]{2,1,0:T(8,128)(2,1)S(1)}, bf16[2,80,1024]{2,1,0:T(8,128)(2,1)S(1)}, u32[]{:S(2)}, u32[]{:S(2)}) collective-permute-start(bf16[2,80,1024]{2,1,0:T(8,128)(2,1)S(1)} %pad_maximum_fusion.6), channel_id=1, source_target_pairs={{0,4},{4,0},{8,12},{12,8},{1,5},{5,1},{9,13},{13,9},{2,6},{6,2},{1... | collective-permute-start | bytes 983048 | tf_op jit(solution)/shard_map/ppermute | solution.py:26
  30.7 10.7 %collective-permute-start.12 = (bf16[2,80,1024]{2,1,0:T(8,128)(2,1)S(1)}, bf16[2,80,1024]{2,1,0:T(8,128)(2,1)S(1)}, u32[]{:S(2)}, u32[]{:S(2)}) collective-permute-start(bf16[2,80,1024]{2,1,0:T(8,128)(2,1)S(1)} %pad_maximum_fusion.8.refs_2_), channel_id=1, source_target_pairs={{2,0},{0,2},{3,1},{1,3},{6,4},{4,6},{7,5},{5,7},{10,8},{8,10},{11,... | collective-permute-start | bytes 983048 | tf_op jit(solution)/shard_map/ppermute | solution.py:18
  41.6 22.5 %collective-permute-start.6 = (bf16[2,96,1792]{2,1,0:T(8,128)(2,1)S(1)}, bf16[2,96,1792]{2,1,0:T(8,128)(2,1)S(1)}, u32[]{:S(2)}, u32[]{:S(2)}) collective-permute-start(bf16[2,96,1792]{2,1,0:T(8,128)(2,1)S(1)} %get-tuple-element.54), channel_id=1, source_target_pairs={{0,2},{2,0},{1,3},{3,1},{4,6},{6,4},{5,7},{7,5},{8,10},{10,8},{9,1... | collective-permute-start | bytes 2064392 | tf_op jit(solution)/shard_map/ppermute | solution.py:22
  49.9 24.7 %collective-permute-start.9 = (bf16[2,96,1792]{2,1,0:T(8,128)(2,1)S(1)}, bf16[2,96,1792]{2,1,0:T(8,128)(2,1)S(1)}, u32[]{:S(2)}, u32[]{:S(2)}) collective-permute-start(bf16[2,96,1792]{2,1,0:T(8,128)(2,1)S(1)} %get-tuple-element.57), channel_id=1, source_target_pairs={{0,2},{2,0},{1,3},{3,1},{4,6},{6,4},{5,7},{7,5},{8,10},{10,8},{9,1... | collective-permute-start | bytes 2064392 | tf_op jit(solution)/shard_map/ppermute | solution.py:22
  63.1 41.0 %collective-permute-start.16 = (bf16[2,96,3584]{2,1,0:T(8,128)(2,1)S(1)}, bf16[2,96,3584]{2,1,0:T(8,128)(2,1)S(1)}, u32[]{:S(2)}, u32[]{:S(2)}) collective-permute-start(bf16[2,96,3584]{2,1,0:T(8,128)(2,1)S(1)} %get-tuple-element.62), channel_id=1, source_target_pairs={{0,2},{2,0},{1,3},{3,1},{4,6},{6,4},{5,7},{7,5},{8,10},{10,8},{9,1... | collective-permute-start | bytes 4128776 | tf_op jit(solution)/shard_map/ppermute | solution.py:22
  64.4 54.3 %collective-permute-start.10 = (bf16[96,1792]{1,0:T(8,128)(2,1)S(1)}, bf16[96,1792]{1,0:T(8,128)(2,1)S(1)}, u32[]{:S(2)}, u32[]{:S(2)}) collective-permute-start(bf16[96,1792]{1,0:T(8,128)(2,1)S(1)} %fusion.15.refs_0_), channel_id=1, source_target_pairs={{2,0},{0,2},{3,1},{1,3},{6,4},{4,6},{7,5},{5,7},{10,8},{8,10},{11,... | collective-permute-start | bytes 1032200 | tf_op jit(solution)/shard_map/ppermute | solution.py:18
  75.0 43.9 %collective-permute-start.11 = (bf16[96,1792]{1,0:T(8,128)(2,1)S(1)}, bf16[96,1792]{1,0:T(8,128)(2,1)S(1)}, u32[]{:S(2)}, u32[]{:S(2)}) collective-permute-start(bf16[96,1792]{1,0:T(8,128)(2,1)S(1)} %fusion.13.refs_1_), channel_id=1, source_target_pairs={{2,0},{0,2},{3,1},{1,3},{6,4},{4,6},{7,5},{5,7},{10,8},{8,10},{11,... | collective-permute-start | bytes 1032200 | tf_op jit(solution)/shard_map/ppermute | solution.py:18
  104.8 28.8 %collective-permute-start.18 = (bf16[96,3584]{1,0:T(8,128)(2,1)S(1)}, bf16[96,3584]{1,0:T(8,128)(2,1)S(1)}, u32[]{:S(2)}, u32[]{:S(2)}) collective-permute-start(bf16[96,3584]{1,0:T(8,128)(2,1)S(1)} %fusion.1.refs_2_.refs_0_), channel_id=1, source_target_pairs={{2,0},{0,2},{3,1},{1,3},{6,4},{4,6},{7,5},{5,7},{10,8},{8,10},{11,... | collective-permute-start | bytes 2064392 | tf_op jit(solution)/shard_map/ppermute | solution.py:18
  125.9 14.8 %collective-permute-start.17 = (bf16[96,2048]{1,0:T(8,128)(2,1)S(1)}, bf16[96,2048]{1,0:T(8,128)(2,1)S(1)}, u32[]{:S(2)}, u32[]{:S(2)}) collective-permute-start(bf16[96,2048]{1,0:T(8,128)(2,1)S(1)} %get-tuple-element.65), channel_id=1, source_target_pairs={{0,4},{4,0},{8,12},{12,8},{1,5},{5,1},{9,13},{13,9},{2,6},{6,2},{1... | collective-permute-start | bytes 1179656 | tf_op jit(solution)/shard_map/ppermute | solution.py:26
  126.0 30.7 %collective-permute-start.22 = (bf16[2,64,3584]{2,1,0:T(8,128)(2,1)S(1)}, bf16[2,64,3584]{2,1,0:T(8,128)(2,1)S(1)}, u32[]{:S(2)}, u32[]{:S(2)}) collective-permute-start(bf16[2,64,3584]{2,1,0:T(8,128)(2,1)S(1)} %get-tuple-element.73), channel_id=1, source_target_pairs={{0,2},{2,0},{1,3},{3,1},{4,6},{6,4},{5,7},{7,5},{8,10},{10,8},{9,1... | collective-permute-start | bytes 2752520 | tf_op jit(solution)/shard_map/ppermute | solution.py:22
  140.7 14.5 %collective-permute-start.24 = (bf16[96,2048]{1,0:T(8,128)(2,1)S(1)}, bf16[96,2048]{1,0:T(8,128)(2,1)S(1)}, u32[]{:S(2)}, u32[]{:S(2)}) collective-permute-start(bf16[96,2048]{1,0:T(8,128)(2,1)S(1)} %get-tuple-element.74), channel_id=1, source_target_pairs={{0,4},{4,0},{8,12},{12,8},{1,5},{5,1},{9,13},{13,9},{2,6},{6,2},{1... | collective-permute-start | bytes 1179656 | tf_op jit(solution)/shard_map/ppermute | solution.py:26
  141.0 12.1 %collective-permute-start.19 = (bf16[48,2048]{1,0:T(8,128)(2,1)S(1)}, bf16[48,2048]{1,0:T(8,128)(2,1)S(1)}, u32[]{:S(2)}, u32[]{:S(2)}) collective-permute-start(bf16[48,2048]{1,0:T(8,128)(2,1)S(1)} %slice.218.refs_4_), channel_id=1, source_target_pairs={{0,8},{4,12},{8,0},{12,4},{1,9},{5,13},{9,1},{13,5},{2,10},{6,14},... | collective-permute-start | bytes 589832 | tf_op jit(solution)/shard_map/ppermute | solution.py:26
  155.4 10.3 %collective-permute-start.25 = (bf16[48,2048]{1,0:T(8,128)(2,1)S(1)}, bf16[48,2048]{1,0:T(8,128)(2,1)S(1)}, u32[]{:S(2)}, u32[]{:S(2)}) collective-permute-start(bf16[48,2048]{1,0:T(8,128)(2,1)S(1)} %slice.217.refs_5_), channel_id=1, source_target_pairs={{0,8},{4,12},{8,0},{12,4},{1,9},{5,13},{9,1},{13,5},{2,10},{6,14},... | collective-permute-start | bytes 589832 | tf_op jit(solution)/shard_map/ppermute | solution.py:26
  165.7 16.3 %collective-permute-start.20 = (bf16[48,2048]{1,0:T(8,128)(2,1)S(1)}, bf16[48,2048]{1,0:T(8,128)(2,1)S(1)}, u32[]{:S(2)}, u32[]{:S(2)}) collective-permute-start(bf16[48,2048]{1,0:T(8,128)(2,1)S(1)} %get-tuple-element.71.refs_6_), channel_id=1, source_target_pairs={{0,8},{4,12},{8,0},{12,4},{1,9},{5,13},{9,1},{13,5},{2,10},{6,14},... | collective-permute-start | bytes 589832 | tf_op jit(solution)/shard_map/ppermute | solution.py:26
  166.1 18.5 %collective-permute-start.23 = (bf16[64,3584]{1,0:T(8,128)(2,1)S(1)}, bf16[64,3584]{1,0:T(8,128)(2,1)S(1)}, u32[]{:S(2)}, u32[]{:S(2)}) collective-permute-start(bf16[64,3584]{1,0:T(8,128)(2,1)S(1)} %fusion.3.refs_0_.refs_7_), channel_id=1, source_target_pairs={{2,0},{0,2},{3,1},{1,3},{6,4},{4,6},{7,5},{5,7},{10,8},{8,10},{11,... | collective-permute-start | bytes 1376264 | tf_op jit(solution)/shard_map/ppermute | solution.py:18
  167.0 17.5 %collective-permute-start.26 = (bf16[48,2048]{1,0:T(8,128)(2,1)S(1)}, bf16[48,2048]{1,0:T(8,128)(2,1)S(1)}, u32[]{:S(2)}, u32[]{:S(2)}) collective-permute-start(bf16[48,2048]{1,0:T(8,128)(2,1)S(1)} %get-tuple-element.79.refs_8_), channel_id=1, source_target_pairs={{0,8},{4,12},{8,0},{12,4},{1,9},{5,13},{9,1},{13,5},{2,10},{6,14},... | collective-permute-start | bytes 589832 | tf_op jit(solution)/shard_map/ppermute | solution.py:26
  204.6 15.7 %collective-permute-start.29 = (bf16[96,2048]{1,0:T(8,128)(2,1)S(1)}, bf16[96,2048]{1,0:T(8,128)(2,1)S(1)}, u32[]{:S(2)}, u32[]{:S(2)}) collective-permute-start(bf16[96,2048]{1,0:T(8,128)(2,1)S(1)} %constant_dynamic-update-slice_fusion.2.refs_10_.near_ref), channel_id=1, source_target_pairs={{0,4},{4,0},{8,12},{12,8},{1,5},{5,1},{9,13},{13,9},{2,6},{6,2},{1... | collective-permute-start | bytes 1179656 | tf_op jit(solution)/shard_map/ppermute | solution.py:26
  228.3 18.6 %collective-permute-start.31 = (bf16[96,4096]{1,0:T(8,128)(2,1)}, bf16[96,4096]{1,0:T(8,128)(2,1)S(1)}, u32[]{:S(2)}, u32[]{:S(2)}) collective-permute-start(bf16[96,4096]{1,0:T(8,128)(2,1)} %get-tuple-element.90), channel_id=1, source_target_pairs={{0,1},{1,0},{2,3},{3,2},{4,5},{5,4},{6,7},{7,6},{8,9},{9,8},{10,11... | collective-permute-start | bytes 2359304 | tf_op jit(solution)/shard_map/ppermute | solution.py:22
  228.4 9.6 %collective-permute-start.33 = (bf16[32,2048]{1,0:T(8,128)(2,1)S(1)}, bf16[32,2048]{1,0:T(8,128)(2,1)S(1)}, u32[]{:S(2)}, u32[]{:S(2)}) collective-permute-start(bf16[32,2048]{1,0:T(8,128)(2,1)S(1)} %slice.219.refs_1_), channel_id=1, source_target_pairs={{0,8},{4,12},{8,0},{12,4},{1,9},{5,13},{9,1},{13,5},{2,10},{6,14},... | collective-permute-start | bytes 393224 | tf_op jit(solution)/shard_map/ppermute | solution.py:26
  238.1 11.5 %collective-permute-start.28 = (bf16[48,4096]{1,0:T(8,128)(2,1)S(1)}, bf16[48,4096]{1,0:T(8,128)(2,1)S(1)}, u32[]{:S(2)}, u32[]{:S(2)}) collective-permute-start(bf16[48,4096]{1,0:T(8,128)(2,1)S(1)} %slice.215.refs_2_), channel_id=1, source_target_pairs={{0,2},{2,0},{1,3},{3,1},{4,6},{6,4},{5,7},{7,5},{8,10},{10,8},{9,1... | collective-permute-start | bytes 1179656 | tf_op jit(solution)/shard_map/ppermute | solution.py:22
  248.5 10.5 %collective-permute-start.32 = (bf16[48,4096]{1,0:T(8,128)(2,1)S(1)}, bf16[48,4096]{1,0:T(8,128)(2,1)S(1)}, u32[]{:S(2)}, u32[]{:S(2)}) collective-permute-start(bf16[48,4096]{1,0:T(8,128)(2,1)S(1)} %slice.214.refs_2_), channel_id=1, source_target_pairs={{0,2},{2,0},{1,3},{3,1},{4,6},{6,4},{5,7},{7,5},{8,10},{10,8},{9,1... | collective-permute-start | bytes 1179656 | tf_op jit(solution)/shard_map/ppermute | solution.py:22
  249.5 9.9 %collective-permute-start.35 = (bf16[64,2048]{1,0:T(8,128)(2,1)S(1)}, bf16[64,2048]{1,0:T(8,128)(2,1)S(1)}, u32[]{:S(2)}, u32[]{:S(2)}) collective-permute-start(bf16[64,2048]{1,0:T(8,128)(2,1)S(1)} %constant_dynamic-update-slice_fusion.4.near_ref.refs_3_), channel_id=1, source_target_pairs={{0,4},{4,0},{8,12},{12,8},{1,5},{5,1},{9,13},{13,9},{2,6},{6,2},{1... | collective-permute-start | bytes 786440 | tf_op jit(solution)/shard_map/ppermute | solution.py:26
  (28 other events, 225.4 us)

commit v5 on v4

--- a/solution.py
+++ b/solution.py
@@ -274,17 +274,17 @@
             place = place + ((offset >> at) & 1) * bits[at]
         return place
 
-    def all_columns(mine):
-        gathered = mine[None]
-        for bit in bits:
-            gathered = jnp.concatenate((gathered, swap(gathered, "hid", ranks, bit)))
-        return gathered
+    def after(values, others):
+        return lax.optimization_barrier((values, others))[0]
+
+    def doubled(gathered, bit):
+        return jnp.concatenate((gathered, swap(gathered, "hid", ranks, bit)))
 
     def from_owners(gathered):
         wide = gathered.astype(F32)
         squares = jnp.sum(wide * wide, axis=(0, 2))
         inverse = lax.rsqrt(squares / model_width + 1e-05)
-        columns, going = [], []
+        columns = []
         for hop in range(owners):
             target = lax.rem(row_at + owners - hop, owners)
             half = jnp.concatenate(
@@ -295,9 +295,8 @@
                     for at in range(half_cuts)
                 ]
             )
-            going.append(half)
             columns.append(half if hop == 0 else shift(half, "rows", owners, hop))
-        return columns, from_all(inverse, "rows", owners), going
+        return columns, inverse
 
     def from_members(columns, inverses):
         return from_all(jnp.stack(columns), "mp", members), from_all(inverses, "mp", members)
@@ -310,12 +309,16 @@
     chunks = len(sizes)
     head = sizes[0]
 
-    columns, inverses, going = from_owners(all_columns(own_tokens[:head]))
-    xs = [normed(*from_members(columns, inverses))]
-    rest = None
-    if chunks > 1:
-        rest, _ = lax.optimization_barrier((all_columns(own_tokens[head:]), going))
-        rest = from_owners(rest)
+    gathered = own_tokens[:head][None]
+    rest = own_tokens[head:][None] if chunks > 1 else None
+    for bit in bits:
+        gathered = doubled(gathered, bit)
+        if rest is not None:
+            rest = doubled(after(rest, gathered), bit)
+    first = from_owners(gathered)
+    if rest is not None:
+        rest = from_owners(after(rest, first))
+    xs = [normed(*from_members(first[0], from_all(first[1], "rows", owners)))]
 
     sums, hidden, layer, blocks, outs = ({} for _ in range(5))
     last = []
@@ -324,45 +327,56 @@
         pieces = 2 if t == 0 and gate_weight.shape[2] % 512 == 0 else 1
         sums[t] = []
         for piece in range(pieces):
-            own, *sends = gate_up(
-                xs[t], gate_weight, up_weight, piece, pieces, list(last)
-            )
+            own, *sends = gate_up(xs[t], gate_weight, up_weight, piece, pieces, list(last))
             last[:] = [own]
             if t == 0 and rest is not None:
-                last.extend(rest[2])
+                last.extend(rest[0])
             others = [send(sends[hop - 1], "rows", owners, hop) for hop in range(1, owners)]
             sums[t].append((own, others))
 
     def rest_of(_):
         if rest is None:
             return
-        (columns, inverses), _ = lax.optimization_barrier((rest[:2], sums[0][0][0]))
-        columns, inverses = from_members(columns, inverses)
+        inverses = from_all(after(rest[1], sums[0][-1][0]), "rows", owners)
+        columns, inverses = from_members(*after((rest[0], inverses), hidden[0][0]))
         for start, q in zip(starts[1:], sizes[1:]):
             rows = slice(start - head, start - head + q)
             xs.append(normed(columns[:, :, :, rows], inverses[:, :, rows]))
 
-    def ordered(values):
-        return lax.optimization_barrier((values, last[0]))[0]
-
     def hidden_of(t):
-        hidden[t] = [[] for _ in range(owners)]
+        units = []
         for own, others in sums[t]:
             acts = own
             for other in others:
                 acts = acts + other.astype(F32)
-            units = (jax.nn.silu(acts[0]) * acts[1]).astype(BF16)
-            hidden[t][0].append(units)
-            for hop in range(1, owners):
-                hidden[t][hop].append(shift(units, "rows", owners, hop))
-        last.append(hidden[t][0][-1])
+            units.append((jax.nn.silu(acts[0]) * acts[1]).astype(BF16))
+        units = jnp.concatenate(units, axis=1)
+        hidden[t] = [units] + [shift(units, "rows", owners, hop) for hop in range(1, owners)]
+        last.append(units)
+
+    def ordered(values):
+        return after(values, last[0])
+
+    def at_once(t):
+        return t == chunks - 1 and ranks == 4
 
     def down_of(t):
-        total, going = down(rank, hidden[t], down_weight, members, order, list(last))
+        total, going = down(rank, [[units] for units in hidden[t]], down_weight, members, order, list(last))
         last[:] = [total]
-        layer[t] = (total, swap(going, "hid", ranks, 1))
+        if at_once(t):
+            block = total.shape[0] // 2
+            far = total[block:].astype(BF16)
+            arrived = [
+                swap(part, "hid", ranks, offset)
+                for part, offset in ((going[block:], 3), (far, 2), (going[:block], 1))
+            ]
+            layer[t] = (total[:block], arrived)
+        else:
+            layer[t] = (total, swap(going, "hid", ranks, 1))
 
     def halve_of(t):
+        if at_once(t):
+            return
         total, arrived = ordered(layer[t])
         for bit in reversed(bits[:-1]):
             total = total + arrived.astype(F32)
@@ -374,11 +388,19 @@
 
     def settle_of(t):
         total, arrived = ordered(layer[t])
-        block = (total + arrived.astype(F32)).astype(BF16)
+        for part in arrived if at_once(t) else [arrived]:
+            total = total + part.astype(F32)
+        block = total.astype(BF16)
         last.append(block)
-        layer[t] = (block, swap(block, "hid", ranks, bits[0]))
+        if at_once(t):
+            third, second, first = (swap(block, "hid", ranks, offset) for offset in (3, 2, 1))
+            blocks[t] = (jnp.concatenate((block, second)), jnp.concatenate((first, third)))
+        else:
+            layer[t] = (block, swap(block, "hid", ranks, bits[0]))
 
     def double_of(t):
+        if at_once(t):
+            return
         near, far = ordered(layer[t])
         for bit in bits[1:]:
             near = jnp.concatenate((near, far))
@@ -413,11 +435,11 @@
         last.append(outs[t])
 
     stages = (
-        (gate_up_of, 0), (rest_of, 0), (gate_up_of, 1), (hidden_of, 0), (hidden_of, 1), (gate_up_of, 2),
-        (down_of, 0), (down_of, 1), (halve_of, 0), (halve_of, 1), (settle_of, 0), (hidden_of, 2),
-        (settle_of, 1), (double_of, 0), (double_of, 1), (down_of, 2), (features_of, 0),
-        (halve_of, 2), (share_of, 0), (features_of, 1), (settle_of, 2), (share_of, 1),
-        (double_of, 2), (finish_of, 0), (features_of, 2), (share_of, 2), (finish_of, 1),
+        (gate_up_of, 0), (hidden_of, 0), (rest_of, 0), (gate_up_of, 1), (down_of, 0),
+        (halve_of, 0), (hidden_of, 1), (gate_up_of, 2), (settle_of, 0), (down_of, 1),
+        (double_of, 0), (hidden_of, 2), (halve_of, 1), (features_of, 0), (down_of, 2),
+        (settle_of, 1), (share_of, 0), (settle_of, 2), (double_of, 1), (finish_of, 0),
+        (features_of, 1), (share_of, 1), (features_of, 2), (share_of, 2), (finish_of, 1),
         (finish_of, 2),
     )
     for stage, t in stages:

time: 280 us -> 276 us (0.986)
  waiting for transfers between devices: 149 us -> 136 us
  starting transfers between devices: 33 us -> 43.1 us
    ppermute x16 -> x18, waiting for transfers between devices: 81.2 us -> 54.2 us  [swap(): return lax.ppermute(value, axis, [(d, d ^ bit) for d in range(size)])]
    ppermute x12 -> x11, waiting for transfers between devices: 12.2 us -> 29.2 us  [shift(): lax.ppermute(value, axis, [((d + hop) % size, d) for d in range(size)])]
    ppermute x16 -> x18, starting transfers between devices: 17.1 us -> 29 us  [swap(): return lax.ppermute(value, axis, [(d, d ^ bit) for d in range(size)])]
    ppermute x10, waiting for transfers between devices: 56.1 us -> 52.2 us  [send(): lax.ppermute(value, axis, [(d, (d + hop) % size) for d in range(size)])]
    ppermute x12 -> x11, starting transfers between devices: 8.73 us -> 6.64 us  [shift(): lax.ppermute(value, axis, [((d + hop) % size, d) for d in range(size)])]
  transfers between devices with their start and end apart: 38 -> 39, of which waited for: 25 -> 25; matrix products, arithmetic and copies ran while one was open for 2% -> 2% of each run, Pallas kernels for 21% -> 21%
where the time goes in v5:
time: 276 us
  waiting for transfers between devices  136 us (49%)
  Pallas kernels  81.6 us (30%)
  starting transfers between devices  43.1 us (16%)
  other arithmetic  9.39 us (3%)
  local copies, waits for them, and re-layouts  5.28 us (2%)
    ppermute x18, waiting for transfers between devices, swap(): return lax.ppermute(value, axis, [(d, d ^ bit) for d in range(size)])  54.2 us
    ppermute x10, waiting for transfers between devices, send(): lax.ppermute(value, axis, [(d, (d + hop) % size) for d in range(size)])  52.2 us
    pallas_call x4, Pallas kernels, gate_up(): pl.pallas_call(functools.partial(gate_up_body, tiles, piece * tiles), gri...  37.5 us
    ppermute x11, waiting for transfers between devices, shift(): lax.ppermute(value, axis, [((d + hop) % size, d) for d in range(size)])  29.2 us
    ppermute x18, starting transfers between devices, swap(): return lax.ppermute(value, axis, [(d, d ^ bit) for d in range(size)])  29 us
    pallas_call x3, Pallas kernels, encode(): pl.pallas_call(functools.partial(encode_body, members, order, width // ti...  23.7 us
    pallas_call x3, Pallas kernels, down(): pl.pallas_call(functools.partial(down_body, owners, members, pieces, orde...  20.4 us
    ppermute x10, starting transfers between devices, send(): lax.ppermute(value, axis, [(d, (d + hop) % size) for d in range(size)])  7.46 us
  transfers between devices with their start and end apart: 39, of which 25 were waited for; matrix products, arithmetic and copies ran while one was open for 2% of the time, Pallas kernels for 21%

profile of v5, /device:TPU:0, one launch (start us, length us, event | category | flops | bytes accessed | tf_op | source)
XLA Modules:
  0.0 275.6 jit_solution(2097447772618429067)
XLA Ops:
  5.2 4.9 %collective-permute-done = bf16[1,48,1024]{2,1,0:T(8,128)(2,1)S(1)} collective-permute-done((bf16[1,48,1024]{2,1,0:T(8,128)(2,1)S(1)}, bf16[1,48,1024]{2,1,0:T(8,128)(2,1)S(1)}, u32[]{:S(2)}, u32[]{:S(2)}) %collective-permute-start) | collective-permute-done | bytes 98336 | tf_op jit(solution)/shard_map/ppermute | solution.py:26
  14.2 5.8 %collective-permute-done.7 = bf16[1,80,1024]{2,1,0:T(8,128)(2,1)S(1)} collective-permute-done((bf16[1,80,1024]{2,1,0:T(8,128)(2,1)S(1)}, bf16[1,80,1024]{2,1,0:T(8,128)(2,1)S(1)}, u32[]{:S(2)}, u32[]{:S(2)}) %collective-permute-start.7) | collective-permute-done | bytes 163872 | tf_op jit(solution)/shard_map/ppermute | solution.py:26
  31.7 7.2 %shard_map.82 = (f32[2,96,1792]{2,1,0:T(8,128)S(1)}, bf16[2,96,1792]{2,1,0:T(8,128)(2,1)S(1)}) custom-call(bf16[2,2,2,48,1024]{4,3,2,1,0:T(8,128)(2,1)S(1)} %multiply_convert_fusion.1.x_ref, bf16[1,2048,3584]{2,1,0:T(8,128)(2,1)} %gate_ref.7, bf16[1,2048,3584]{2,1,0:T(8,128)(2,1)} %up_ref.7), custom_call_target="tpu_custom_call" | custom-call | flops 1 | bytes 1 | tf_op jit(solution)/shard_map/pallas_call | solution.py:131
  41.4 19.7 %collective-permute-done.9.refs_2_ = bf16[2,80,1024]{2,1,0:T(8,128)(2,1)S(1)} collective-permute-done((bf16[2,80,1024]{2,1,0:T(8,128)(2,1)S(1)}, bf16[2,80,1024]{2,1,0:T(8,128)(2,1)S(1)}, u32[]{:S(2)}, u32[]{:S(2)}) %collective-permute-start.9) | collective-permute-done | bytes 327712 | tf_op jit(solution)/shard_map/ppermute | solution.py:18
  61.1 7.2 %shard_map.83 = (f32[2,96,1792]{2,1,0:T(8,128)S(1)}, bf16[2,96,1792]{2,1,0:T(8,128)(2,1)S(1)}) custom-call(bf16[2,2,2,48,1024]{4,3,2,1,0:T(8,128)(2,1)S(1)} %multiply_convert_fusion.1.x_ref, bf16[1,2048,3584]{2,1,0:T(8,128)(2,1)} %gate_ref.7, bf16[1,2048,3584]{2,1,0:T(8,128)(2,1)} %up_ref.7, f32[2,96,1792]{2,1,0:T(8,128)S(1)} %get-tuple-element.54.refs_0_, ...), custom_call_target="tpu_custom_call" | custom-call | flops 1 | bytes 1 | tf_op jit(solution)/shard_map/pallas_call | solution.py:131
  72.3 11.7 %collective-permute-done.10 = bf16[2,96,1792]{2,1,0:T(8,128)(2,1)S(1)} collective-permute-done((bf16[2,96,1792]{2,1,0:T(8,128)(2,1)S(1)}, bf16[2,96,1792]{2,1,0:T(8,128)(2,1)S(1)}, u32[]{:S(2)}, u32[]{:S(2)}) %collective-permute-start.10) | collective-permute-done | bytes 688160 | tf_op jit(solution)/shard_map/ppermute | solution.py:22
  86.9 11.7 %shard_map.84 = (f32[2,96,3584]{2,1,0:T(8,128)S(1)}, bf16[2,96,3584]{2,1,0:T(8,128)(2,1)S(1)}) custom-call(bf16[2,2,2,48,1024]{4,3,2,1,0:T(8,128)(2,1)S(1)} %multiply_convert_fusion.x_ref, bf16[1,2048,3584]{2,1,0:T(8,128)(2,1)} %gate_ref.7, bf16[1,2048,3584]{2,1,0:T(8,128)(2,1)} %up_ref.7, f32[2,96,1792]{2,1,0:T(8,128)S(1)} %get-tuple-element.59.refs_0_, ...), custom_call_target="tpu_custom_call" | custom-call | flops 1 | bytes 1 | tf_op jit(solution)/shard_map/pallas_call | solution.py:131
  102.5 7.2 %shard_map.85 = (f32[96,2048]{1,0:T(8,128)}, bf16[96,2048]{1,0:T(8,128)(2,1)S(1)}) custom-call(s32[1]{0:T(128)} %bitcast.rank_ref, bf16[96,3584]{1,0:T(8,128)(2,1)S(1)} %pad_maximum_fusion.1.refs_3_.refs_0_, bf16[96,3584]{1,0:T(8,128)(2,1)S(1)} %collective-permute-done.11.refs_1_, bf16[1,3584,2048]{2,1,0:T(8,128)(2,1)} %refs_2_.5, f32[2,96,3584]{2,1,0:T(8,128)} %copy-done.2), custom_call_target="tpu_custom_call" | custom-call | flops 1 | bytes 1 | tf_op jit(solution)/shard_map/pallas_call | solution.py:179
  110.6 9.3 %collective-permute-done.15 = bf16[96,2048]{1,0:T(8,128)(2,1)S(1)} collective-permute-done((bf16[96,2048]{1,0:T(8,128)(2,1)S(1)}, bf16[96,2048]{1,0:T(8,128)(2,1)S(1)}, u32[]{:S(2)}, u32[]{:S(2)}) %collective-permute-start.15) | collective-permute-done | bytes 393248 | tf_op jit(solution)/shard_map/ppermute | solution.py:26
  124.1 8.3 %collective-permute-done.17 = bf16[2,96,3584]{2,1,0:T(8,128)(2,1)S(1)} collective-permute-done((bf16[2,96,3584]{2,1,0:T(8,128)(2,1)S(1)}, bf16[2,96,3584]{2,1,0:T(8,128)(2,1)S(1)}, u32[]{:S(2)}, u32[]{:S(2)}) %collective-permute-start.17) | collective-permute-done | bytes 1376288 | tf_op jit(solution)/shard_map/ppermute | solution.py:22
  134.1 11.4 %shard_map.86 = (f32[2,64,3584]{2,1,0:T(8,128)S(1)}, bf16[2,64,3584]{2,1,0:T(8,128)(2,1)S(1)}) custom-call(bf16[2,2,2,32,1024]{4,3,2,1,0:T(8,128)(2,1)S(1)} %multiply_convert_fusion.2.x_ref, bf16[1,2048,3584]{2,1,0:T(8,128)(2,1)} %gate_ref.7, bf16[1,2048,3584]{2,1,0:T(8,128)(2,1)} %up_ref.7, f32[96,2048]{1,0:T(8,128)S(1)} %copy-done.6, ...), custom_call_target="tpu_custom_call" | custom-call | flops 1 | bytes 1 | tf_op jit(solution)/shard_map/pallas_call | solution.py:131
  150.9 7.1 %shard_map.87 = (f32[96,2048]{1,0:T(8,128)}, bf16[96,2048]{1,0:T(8,128)(2,1)S(1)}) custom-call(s32[1]{0:T(128)} %bitcast.rank_ref, bf16[96,3584]{1,0:T(8,128)(2,1)S(1)} %fusion.1.refs_2_.refs_0_, bf16[96,3584]{1,0:T(8,128)(2,1)S(1)} %collective-permute-done.19.refs_1_, bf16[1,3584,2048]{2,1,0:T(8,128)(2,1)} %refs_2_.5, f32[2,64,3584]{2,1,0:T(8,128)} %copy-done.4, ...), custom_call_target="tpu_custom_call" | custom-call | flops 1 | bytes 1 | tf_op jit(solution)/shard_map/pallas_call | solution.py:179
  160.3 9.1 %collective-permute-done.21 = bf16[2,64,3584]{2,1,0:T(8,128)(2,1)S(1)} collective-permute-done((bf16[2,64,3584]{2,1,0:T(8,128)(2,1)S(1)}, bf16[2,64,3584]{2,1,0:T(8,128)(2,1)S(1)}, u32[]{:S(2)}, u32[]{:S(2)}) %collective-permute-start.21) | collective-permute-done | bytes 917536 | tf_op jit(solution)/shard_map/ppermute | solution.py:22
  173.7 5.7 %collective-permute-done.20.far_ref = bf16[96,2048]{1,0:T(8,128)(2,1)S(1)} collective-permute-done((bf16[96,2048]{1,0:T(8,128)(2,1)S(1)}, bf16[96,2048]{1,0:T(8,128)(2,1)S(1)}, u32[]{:S(2)}, u32[]{:S(2)}) %collective-permute-start.20) | collective-permute-done | bytes 393248 | tf_op jit(solution)/shard_map/ppermute | solution.py:26
  179.4 8.1 %shard_map.88 = (f32[96,4096]{1,0:T(8,128)}, bf16[96,4096]{1,0:T(8,128)(2,1)}) custom-call(s32[1]{0:T(128)} %bitcast.rank_ref, bf16[96,2048]{1,0:T(8,128)(2,1)S(1)} %constant_dynamic-update-slice_fusion.near_ref.refs_1_, bf16[96,2048]{1,0:T(8,128)(2,1)S(1)} %collective-permute-done.20.far_ref, bf16[1,2048,4096]{2,1,0:T(8,128)(2,1)} %weight_ref.5, ...), custom_call_target="tpu_custom_call" | custom-call | flops 1 | bytes 1 | tf_op jit(solution)/shard_map/pallas_call | solution.py:224
  187.6 6.1 %shard_map.89 = (f32[64,2048]{1,0:T(8,128)S(1)}, bf16[64,2048]{1,0:T(8,128)(2,1)S(1)}) custom-call(s32[1]{0:T(128)} %bitcast.rank_ref, bf16[64,3584]{1,0:T(8,128)(2,1)S(1)} %fusion.3.refs_2_.refs_0_, bf16[64,3584]{1,0:T(8,128)(2,1)S(1)} %collective-permute-done.24.refs_1_, bf16[1,3584,2048]{2,1,0:T(8,128)(2,1)} %refs_2_.5, f32[96,4096]{1,0:T(8,128)} %get-tuple-element.84.refs_3_), custom_call_target="tpu_custom_call" | custom-call | flops 1 | bytes 1 | tf_op jit(solution)/shard_map/pallas_call | solution.py:179
  202.1 4.6 %collective-permute-done.31 = bf16[32,2048]{1,0:T(8,128)(2,1)S(1)} collective-permute-done((bf16[32,2048]{1,0:T(8,128)(2,1)S(1)}, bf16[32,2048]{1,0:T(8,128)(2,1)S(1)}, u32[]{:S(2)}, u32[]{:S(2)}) %collective-permute-start.31) | collective-permute-done | bytes 131104 | tf_op jit(solution)/shard_map/ppermute | solution.py:26
  206.8 8.8 %collective-permute-done.27 = bf16[48,2048]{1,0:T(8,128)(2,1)S(1)} collective-permute-done((bf16[48,2048]{1,0:T(8,128)(2,1)S(1)}, bf16[48,2048]{1,0:T(8,128)(2,1)S(1)}, u32[]{:S(2)}, u32[]{:S(2)}) %collective-permute-start.27) | collective-permute-done | bytes 196640 | tf_op jit(solution)/shard_map/ppermute | solution.py:26
  216.7 10.3 %collective-permute-done.25 = bf16[48,4096]{1,0:T(8,128)(2,1)S(1)} collective-permute-done((bf16[48,4096]{1,0:T(8,128)(2,1)S(1)}, bf16[48,4096]{1,0:T(8,128)(2,1)S(1)}, u32[]{:S(2)}, u32[]{:S(2)}) %collective-permute-start.25) | collective-permute-done | bytes 393248 | tf_op jit(solution)/shard_map/ppermute | solution.py:22
  227.5 8.0 %shard_map.90 = (f32[96,4096]{1,0:T(8,128)}, bf16[96,4096]{1,0:T(8,128)(2,1)}) custom-call(s32[1]{0:T(128)} %bitcast.rank_ref, bf16[96,2048]{1,0:T(8,128)(2,1)S(1)} %constant_dynamic-update-slice_fusion.2.near_ref.refs_4_, bf16[96,2048]{1,0:T(8,128)(2,1)S(1)} %collective-permute-done.28.far_ref, bf16[1,2048,4096]{2,1,0:T(8,128)(2,1)} %weight_ref.5, ...), custom_call_target="tpu_custom_call" | custom-call | flops 1 | bytes 1 | tf_op jit(solution)/shard_map/pallas_call | solution.py:224
  240.1 5.4 %collective-permute-done.34 = bf16[32,2048]{1,0:T(8,128)(2,1)S(1)} collective-permute-done((bf16[32,2048]{1,0:T(8,128)(2,1)S(1)}, bf16[32,2048]{1,0:T(8,128)(2,1)S(1)}, u32[]{:S(2)}, u32[]{:S(2)}) %collective-permute-start.34) | collective-permute-done | bytes 131104 | tf_op jit(solution)/shard_map/ppermute | solution.py:26
  249.6 7.6 %shard_map.91 = (f32[64,4096]{1,0:T(8,128)}, bf16[64,4096]{1,0:T(8,128)(2,1)S(1)}) custom-call(s32[1]{0:T(128)} %bitcast.rank_ref, bf16[64,2048]{1,0:T(8,128)(2,1)S(1)} %pad_maximum_fusion.10.near_ref, bf16[64,2048]{1,0:T(8,128)(2,1)S(1)} %pad_maximum_fusion.11.far_ref, bf16[1,2048,4096]{2,1,0:T(8,128)(2,1)} %weight_ref.5, ...), custom_call_target="tpu_custom_call" | custom-call | flops 1 | bytes 1 | tf_op jit(solution)/shard_map/pallas_call | solution.py:224
  262.0 7.3 %collective-permute-done.33 = bf16[48,4096]{1,0:T(8,128)(2,1)S(1)} collective-permute-done((bf16[48,4096]{1,0:T(8,128)(2,1)S(1)}, bf16[48,4096]{1,0:T(8,128)(2,1)S(1)}, u32[]{:S(2)}, u32[]{:S(2)}) %collective-permute-start.33) | collective-permute-done | bytes 393248 | tf_op jit(solution)/shard_map/ppermute | solution.py:22
  269.5 5.0 %collective-permute-done.38 = bf16[32,4096]{1,0:T(8,128)(2,1)S(1)} collective-permute-done((bf16[32,4096]{1,0:T(8,128)(2,1)S(1)}, bf16[32,4096]{1,0:T(8,128)(2,1)S(1)}, u32[]{:S(2)}, u32[]{:S(2)}) %collective-permute-start.38) | collective-permute-done | bytes 262176 | tf_op jit(solution)/shard_map/ppermute | solution.py:22
  (160 shorter events, 77.4 us)
Async XLA Ops:
  10.8 10.0 %collective-permute-start.1 = (bf16[2,48,1024]{2,1,0:T(8,128)(2,1)S(1)}, bf16[2,48,1024]{2,1,0:T(8,128)(2,1)S(1)}, u32[]{:S(2)}, u32[]{:S(2)}) collective-permute-start(bf16[2,48,1024]{2,1,0:T(8,128)(2,1)S(1)} %pad_maximum_fusion.12), channel_id=1, source_target_pairs={{0,4},{4,0},{8,12},{12,8},{1,5},{5,1},{9,13},{13,9},{2,6},{6,2},{1... | collective-permute-start | bytes 589832 | tf_op jit(solution)/shard_map/ppermute | solution.py:26
  38.9 33.0 %collective-permute-start.6 = (bf16[2,96,1792]{2,1,0:T(8,128)(2,1)S(1)}, bf16[2,96,1792]{2,1,0:T(8,128)(2,1)S(1)}, u32[]{:S(2)}, u32[]{:S(2)}) collective-permute-start(bf16[2,96,1792]{2,1,0:T(8,128)(2,1)S(1)} %get-tuple-element.55), channel_id=1, source_target_pairs={{0,2},{2,0},{1,3},{3,1},{4,6},{6,4},{5,7},{7,5},{8,10},{10,8},{9,1... | collective-permute-start | bytes 2064392 | tf_op jit(solution)/shard_map/ppermute | solution.py:22
  40.7 20.4 %collective-permute-start.9 = (bf16[2,80,1024]{2,1,0:T(8,128)(2,1)S(1)}, bf16[2,80,1024]{2,1,0:T(8,128)(2,1)S(1)}, u32[]{:S(2)}, u32[]{:S(2)}) collective-permute-start(bf16[2,80,1024]{2,1,0:T(8,128)(2,1)S(1)} %pad_maximum_fusion.9), channel_id=1, source_target_pairs={{2,0},{0,2},{3,1},{1,3},{6,4},{4,6},{7,5},{5,7},{10,8},{8,10},{11,... | collective-permute-start | bytes 983048 | tf_op jit(solution)/shard_map/ppermute | solution.py:18
  70.1 13.9 %collective-permute-start.10 = (bf16[2,96,1792]{2,1,0:T(8,128)(2,1)S(1)}, bf16[2,96,1792]{2,1,0:T(8,128)(2,1)S(1)}, u32[]{:S(2)}, u32[]{:S(2)}) collective-permute-start(bf16[2,96,1792]{2,1,0:T(8,128)(2,1)S(1)} %get-tuple-element.60), channel_id=1, source_target_pairs={{0,2},{2,0},{1,3},{3,1},{4,6},{6,4},{5,7},{7,5},{8,10},{10,8},{9,1... | collective-permute-start | bytes 2064392 | tf_op jit(solution)/shard_map/ppermute | solution.py:22
  85.0 17.4 %collective-permute-start.11 = (bf16[96,3584]{1,0:T(8,128)(2,1)S(1)}, bf16[96,3584]{1,0:T(8,128)(2,1)S(1)}, u32[]{:S(2)}, u32[]{:S(2)}) collective-permute-start(bf16[96,3584]{1,0:T(8,128)(2,1)S(1)} %pad_maximum_fusion.1.refs_3_.refs_0_), channel_id=1, source_target_pairs={{2,0},{0,2},{3,1},{1,3},{6,4},{4,6},{7,5},{5,7},{10,8},{8,10},{11,... | collective-permute-start | bytes 2064392 | tf_op jit(solution)/shard_map/ppermute | solution.py:18
  100.1 32.2 %collective-permute-start.17 = (bf16[2,96,3584]{2,1,0:T(8,128)(2,1)S(1)}, bf16[2,96,3584]{2,1,0:T(8,128)(2,1)S(1)}, u32[]{:S(2)}, u32[]{:S(2)}) collective-permute-start(bf16[2,96,3584]{2,1,0:T(8,128)(2,1)S(1)} %get-tuple-element.70), channel_id=1, source_target_pairs={{0,2},{2,0},{1,3},{3,1},{4,6},{6,4},{5,7},{7,5},{8,10},{10,8},{9,1... | collective-permute-start | bytes 4128776 | tf_op jit(solution)/shard_map/ppermute | solution.py:22
  109.6 10.3 %collective-permute-start.15 = (bf16[96,2048]{1,0:T(8,128)(2,1)S(1)}, bf16[96,2048]{1,0:T(8,128)(2,1)S(1)}, u32[]{:S(2)}, u32[]{:S(2)}) collective-permute-start(bf16[96,2048]{1,0:T(8,128)(2,1)S(1)} %get-tuple-element.67), channel_id=1, source_target_pairs={{0,4},{4,0},{8,12},{12,8},{1,5},{5,1},{9,13},{13,9},{2,6},{6,2},{1... | collective-permute-start | bytes 1179656 | tf_op jit(solution)/shard_map/ppermute | solution.py:26
  121.2 25.6 %collective-permute-start.16 = (bf16[48,2048]{1,0:T(8,128)(2,1)S(1)}, bf16[48,2048]{1,0:T(8,128)(2,1)S(1)}, u32[]{:S(2)}, u32[]{:S(2)}) collective-permute-start(bf16[48,2048]{1,0:T(8,128)(2,1)S(1)} %slice.235.refs_1_), channel_id=1, source_target_pairs={{0,8},{4,12},{8,0},{12,4},{1,9},{5,13},{9,1},{13,5},{2,10},{6,14},... | collective-permute-start | bytes 589832 | tf_op jit(solution)/shard_map/ppermute | solution.py:26
  133.0 17.9 %collective-permute-start.19 = (bf16[96,3584]{1,0:T(8,128)(2,1)S(1)}, bf16[96,3584]{1,0:T(8,128)(2,1)S(1)}, u32[]{:S(2)}, u32[]{:S(2)}) collective-permute-start(bf16[96,3584]{1,0:T(8,128)(2,1)S(1)} %fusion.1.refs_2_.refs_0_), channel_id=1, source_target_pairs={{2,0},{0,2},{3,1},{1,3},{6,4},{4,6},{7,5},{5,7},{10,8},{8,10},{11,... | collective-permute-start | bytes 2064392 | tf_op jit(solution)/shard_map/ppermute | solution.py:18
  146.8 22.6 %collective-permute-start.21 = (bf16[2,64,3584]{2,1,0:T(8,128)(2,1)S(1)}, bf16[2,64,3584]{2,1,0:T(8,128)(2,1)S(1)}, u32[]{:S(2)}, u32[]{:S(2)}) collective-permute-start(bf16[2,64,3584]{2,1,0:T(8,128)(2,1)S(1)} %get-tuple-element.77), channel_id=1, source_target_pairs={{0,2},{2,0},{1,3},{3,1},{4,6},{6,4},{5,7},{7,5},{8,10},{10,8},{9,1... | collective-permute-start | bytes 2752520 | tf_op jit(solution)/shard_map/ppermute | solution.py:22
  148.0 11.0 %collective-permute-start.18 = (bf16[48,2048]{1,0:T(8,128)(2,1)S(1)}, bf16[48,2048]{1,0:T(8,128)(2,1)S(1)}, u32[]{:S(2)}, u32[]{:S(2)}) collective-permute-start(bf16[48,2048]{1,0:T(8,128)(2,1)S(1)} %add_convert_fusion.1.refs_4_), channel_id=1, source_target_pairs={{0,8},{4,12},{8,0},{12,4},{1,9},{5,13},{9,1},{13,5},{2,10},{6,14},... | collective-permute-start | bytes 589832 | tf_op jit(solution)/shard_map/ppermute | solution.py:26
  158.1 12.1 %collective-permute-start.22 = (bf16[96,2048]{1,0:T(8,128)(2,1)S(1)}, bf16[96,2048]{1,0:T(8,128)(2,1)S(1)}, u32[]{:S(2)}, u32[]{:S(2)}) collective-permute-start(bf16[96,2048]{1,0:T(8,128)(2,1)S(1)} %get-tuple-element.78), channel_id=1, source_target_pairs={{0,4},{4,0},{8,12},{12,8},{1,5},{5,1},{9,13},{13,9},{2,6},{6,2},{1... | collective-permute-start | bytes 1179656 | tf_op jit(solution)/shard_map/ppermute | solution.py:26
  159.1 20.3 %collective-permute-start.20 = (bf16[96,2048]{1,0:T(8,128)(2,1)S(1)}, bf16[96,2048]{1,0:T(8,128)(2,1)S(1)}, u32[]{:S(2)}, u32[]{:S(2)}) collective-permute-start(bf16[96,2048]{1,0:T(8,128)(2,1)S(1)} %constant_dynamic-update-slice_fusion.near_ref.refs_1_), channel_id=1, source_target_pairs={{0,4},{4,0},{8,12},{12,8},{1,5},{5,1},{9,13},{13,9},{2,6},{6,2},{1... | collective-permute-start | bytes 1179656 | tf_op jit(solution)/shard_map/ppermute | solution.py:26
  169.8 17.7 %collective-permute-start.24 = (bf16[64,3584]{1,0:T(8,128)(2,1)S(1)}, bf16[64,3584]{1,0:T(8,128)(2,1)S(1)}, u32[]{:S(2)}, u32[]{:S(2)}) collective-permute-start(bf16[64,3584]{1,0:T(8,128)(2,1)S(1)} %fusion.3.refs_2_.refs_0_), channel_id=1, source_target_pairs={{2,0},{0,2},{3,1},{1,3},{6,4},{4,6},{7,5},{5,7},{10,8},{8,10},{11,... | collective-permute-start | bytes 1376264 | tf_op jit(solution)/shard_map/ppermute | solution.py:18
  170.8 22.9 %collective-permute-start.26 = (bf16[48,2048]{1,0:T(8,128)(2,1)S(1)}, bf16[48,2048]{1,0:T(8,128)(2,1)S(1)}, u32[]{:S(2)}, u32[]{:S(2)}) collective-permute-start(bf16[48,2048]{1,0:T(8,128)(2,1)S(1)} %slice.234.refs_3_), channel_id=1, source_target_pairs={{0,8},{4,12},{8,0},{12,4},{1,9},{5,13},{9,1},{13,5},{2,10},{6,14},... | collective-permute-start | bytes 589832 | tf_op jit(solution)/shard_map/ppermute | solution.py:26
  187.5 28.1 %collective-permute-start.23 = (bf16[96,4096]{1,0:T(8,128)(2,1)}, bf16[96,4096]{1,0:T(8,128)(2,1)S(1)}, u32[]{:S(2)}, u32[]{:S(2)}) collective-permute-start(bf16[96,4096]{1,0:T(8,128)(2,1)} %get-tuple-element.82), channel_id=1, source_target_pairs={{0,1},{1,0},{2,3},{3,2},{4,5},{5,4},{6,7},{7,6},{8,9},{9,8},{10,11... | collective-permute-start | bytes 2359304 | tf_op jit(solution)/shard_map/ppermute | solution.py:22
  195.4 11.3 %collective-permute-start.31 = (bf16[32,2048]{1,0:T(8,128)(2,1)S(1)}, bf16[32,2048]{1,0:T(8,128)(2,1)S(1)}, u32[]{:S(2)}, u32[]{:S(2)}) collective-permute-start(bf16[32,2048]{1,0:T(8,128)(2,1)S(1)} %get-tuple-element.117), channel_id=1, source_target_pairs={{0,4},{4,0},{8,12},{12,8},{1,5},{5,1},{9,13},{13,9},{2,6},{6,2},{1... | collective-permute-start | bytes 393224 | tf_op jit(solution)/shard_map/ppermute | solution.py:26
  195.4 11.3 %collective-permute-start.30 = (bf16[32,2048]{1,0:T(8,128)(2,1)S(1)}, bf16[32,2048]{1,0:T(8,128)(2,1)S(1)}, u32[]{:S(2)}, u32[]{:S(2)}) collective-permute-start(bf16[32,2048]{1,0:T(8,128)(2,1)S(1)} %slice.236), channel_id=1, source_target_pairs={{0,8},{4,12},{8,0},{12,4},{1,9},{5,13},{9,1},{13,5},{2,10},{6,14},... | collective-permute-start | bytes 393224 | tf_op jit(solution)/shard_map/ppermute | solution.py:26
  198.3 17.3 %collective-permute-start.27 = (bf16[48,2048]{1,0:T(8,128)(2,1)S(1)}, bf16[48,2048]{1,0:T(8,128)(2,1)S(1)}, u32[]{:S(2)}, u32[]{:S(2)}) collective-permute-start(bf16[48,2048]{1,0:T(8,128)(2,1)S(1)} %add_convert_fusion.refs_1_), channel_id=1, source_target_pairs={{0,8},{4,12},{8,0},{12,4},{1,9},{5,13},{9,1},{13,5},{2,10},{6,14},... | collective-permute-start | bytes 589832 | tf_op jit(solution)/shard_map/ppermute | solution.py:26
  215.9 11.1 %collective-permute-start.25 = (bf16[48,4096]{1,0:T(8,128)(2,1)S(1)}, bf16[48,4096]{1,0:T(8,128)(2,1)S(1)}, u32[]{:S(2)}, u32[]{:S(2)}) collective-permute-start(bf16[48,4096]{1,0:T(8,128)(2,1)S(1)} %slice.232.refs_2_), channel_id=1, source_target_pairs={{0,2},{2,0},{1,3},{3,1},{4,6},{6,4},{5,7},{7,5},{8,10},{10,8},{9,1... | collective-permute-start | bytes 1179656 | tf_op jit(solution)/shard_map/ppermute | solution.py:22
  216.7 10.8 %collective-permute-start.28 = (bf16[96,2048]{1,0:T(8,128)(2,1)S(1)}, bf16[96,2048]{1,0:T(8,128)(2,1)S(1)}, u32[]{:S(2)}, u32[]{:S(2)}) collective-permute-start(bf16[96,2048]{1,0:T(8,128)(2,1)S(1)} %constant_dynamic-update-slice_fusion.2.near_ref.refs_4_), channel_id=1, source_target_pairs={{0,4},{4,0},{8,12},{12,8},{1,5},{5,1},{9,13},{13,9},{2,6},{6,2},{1... | collective-permute-start | bytes 1179656 | tf_op jit(solution)/shard_map/ppermute | solution.py:26
  235.5 12.4 %collective-permute-start.32 = (bf16[96,4096]{1,0:T(8,128)(2,1)}, bf16[96,4096]{1,0:T(8,128)(2,1)S(1)}, u32[]{:S(2)}, u32[]{:S(2)}) collective-permute-start(bf16[96,4096]{1,0:T(8,128)(2,1)} %get-tuple-element.96), channel_id=1, source_target_pairs={{0,1},{1,0},{2,3},{3,2},{4,5},{5,4},{6,7},{7,6},{8,9},{9,8},{10,11... | collective-permute-start | bytes 2359304 | tf_op jit(solution)/shard_map/ppermute | solution.py:22
  257.3 12.0 %collective-permute-start.33 = (bf16[48,4096]{1,0:T(8,128)(2,1)S(1)}, bf16[48,4096]{1,0:T(8,128)(2,1)S(1)}, u32[]{:S(2)}, u32[]{:S(2)}) collective-permute-start(bf16[48,4096]{1,0:T(8,128)(2,1)S(1)} %slice.231.refs_1_), channel_id=1, source_target_pairs={{0,2},{2,0},{1,3},{3,1},{4,6},{6,4},{5,7},{7,5},{8,10},{10,8},{9,1... | collective-permute-start | bytes 1179656 | tf_op jit(solution)/shard_map/ppermute | solution.py:22
  260.5 13.9 %collective-permute-start.38 = (bf16[32,4096]{1,0:T(8,128)(2,1)S(1)}, bf16[32,4096]{1,0:T(8,128)(2,1)S(1)}, u32[]{:S(2)}, u32[]{:S(2)}) collective-permute-start(bf16[32,4096]{1,0:T(8,128)(2,1)S(1)} %slice.233), channel_id=1, source_target_pairs={{0,2},{2,0},{1,3},{3,1},{4,6},{6,4},{5,7},{7,5},{8,10},{10,8},{9,1... | collective-permute-start | bytes 786440 | tf_op jit(solution)/shard_map/ppermute | solution.py:22
  (32 other events, 277.5 us)

commit v6 on v5

--- a/solution.py
+++ b/solution.py
@@ -296,10 +296,13 @@
                 ]
             )
             columns.append(half if hop == 0 else shift(half, "rows", owners, hop))
-        return columns, inverse
-
-    def from_members(columns, inverses):
-        return from_all(jnp.stack(columns), "mp", members), from_all(inverses, "mp", members)
+        return columns, from_all(inverse, "mp", members)
+
+    def scales(inverse):
+        return from_all(inverse, "rows", owners).transpose(1, 0, 2)
+
+    def from_members(columns):
+        return from_all(jnp.stack(columns), "mp", members)
 
     def normed(columns, inverses):
         return (columns.astype(F32) * inverses[:, :, None, :, None] * gain).astype(BF16)
@@ -318,7 +321,7 @@
     first = from_owners(gathered)
     if rest is not None:
         rest = from_owners(after(rest, first))
-    xs = [normed(*from_members(first[0], from_all(first[1], "rows", owners)))]
+    xs = [normed(from_members(first[0]), scales(first[1]))]
 
     sums, hidden, layer, blocks, outs = ({} for _ in range(5))
     last = []
@@ -337,8 +340,8 @@
     def rest_of(_):
         if rest is None:
             return
-        inverses = from_all(after(rest[1], sums[0][-1][0]), "rows", owners)
-        columns, inverses = from_members(*after((rest[0], inverses), hidden[0][0]))
+        columns = from_members(rest[0])
+        inverses = scales(after(rest[1], sums[0][-1][0]))
         for start, q in zip(starts[1:], sizes[1:]):
             rows = slice(start - head, start - head + q)
             xs.append(normed(columns[:, :, :, rows], inverses[:, :, rows]))
@@ -395,6 +398,7 @@
         if at_once(t):
             third, second, first = (swap(block, "hid", ranks, offset) for offset in (3, 2, 1))
             blocks[t] = (jnp.concatenate((block, second)), jnp.concatenate((first, third)))
+            last.extend(blocks[t])
         else:
             layer[t] = (block, swap(block, "hid", ranks, bits[0]))
 
@@ -402,6 +406,8 @@
         if at_once(t):
             return
         near, far = ordered(layer[t])
+        if t > 0:
+            near, far = after((near, far), sums[t - 1][0])
         for bit in bits[1:]:
             near = jnp.concatenate((near, far))
             last.append(near)
@@ -425,6 +431,9 @@
             others.append(send(going, "rows", owners, hop))
         sums[t] = (total[:q], others)
 
+    def shared_of(t):
+        last.extend(sums[t][1])
+
     def finish_of(t):
         pre, others = sums[t]
         for other in others:
@@ -432,15 +441,14 @@
         pre = pre + enc_bias[None, :]
         factor = adjoint[starts[t] : starts[t] + sizes[t]].astype(F32)
         outs[t] = (jnp.maximum(pre, 0.0) * factor).astype(BF16)
-        last.append(outs[t])
 
     stages = (
-        (gate_up_of, 0), (hidden_of, 0), (rest_of, 0), (gate_up_of, 1), (down_of, 0),
+        (gate_up_of, 0), (rest_of, 0), (hidden_of, 0), (gate_up_of, 1), (down_of, 0),
         (halve_of, 0), (hidden_of, 1), (gate_up_of, 2), (settle_of, 0), (down_of, 1),
         (double_of, 0), (hidden_of, 2), (halve_of, 1), (features_of, 0), (down_of, 2),
-        (settle_of, 1), (share_of, 0), (settle_of, 2), (double_of, 1), (finish_of, 0),
-        (features_of, 1), (share_of, 1), (features_of, 2), (share_of, 2), (finish_of, 1),
-        (finish_of, 2),
+        (settle_of, 1), (share_of, 0), (settle_of, 2), (double_of, 1), (shared_of, 0),
+        (features_of, 1), (share_of, 1), (features_of, 2), (share_of, 2), (finish_of, 0),
+        (finish_of, 1), (finish_of, 2),
     )
     for stage, t in stages:
         if t < chunks:

time: 276 us -> 258 us (0.935)
  waiting for transfers between devices: 136 us -> 116 us
    ppermute x11, waiting for transfers between devices: 29.2 us -> 11.8 us  [shift(): lax.ppermute(value, axis, [((d + hop) % size, d) for d in range(size)])]
    ppermute x10, waiting for transfers between devices: 52.2 us -> 46.8 us  [send(): lax.ppermute(value, axis, [(d, (d + hop) % size) for d in range(size)])]
    ppermute x18, waiting for transfers between devices: 54.2 us -> 57.4 us  [swap(): return lax.ppermute(value, axis, [(d, d ^ bit) for d in range(size)])]
  transfers between devices with their start and end apart: 39 -> 39, of which waited for: 25 -> 26; matrix products, arithmetic and copies ran while one was open for 2% -> 3% of each run, Pallas kernels for 21% -> 26%
where the time goes in v6:
time: 258 us
  waiting for transfers between devices  116 us (45%)
  Pallas kernels  81.7 us (32%)
  starting transfers between devices  44.1 us (17%)
  other arithmetic  9.47 us (4%)
  local copies, waits for them, and re-layouts  5.86 us (2%)
    ppermute x18, waiting for transfers between devices, swap(): return lax.ppermute(value, axis, [(d, d ^ bit) for d in range(size)])  57.4 us
    ppermute x10, waiting for transfers between devices, send(): lax.ppermute(value, axis, [(d, (d + hop) % size) for d in range(size)])  46.8 us
    pallas_call x4, Pallas kernels, gate_up(): pl.pallas_call(functools.partial(gate_up_body, tiles, piece * tiles), gri...  37.6 us
    ppermute x18, starting transfers between devices, swap(): return lax.ppermute(value, axis, [(d, d ^ bit) for d in range(size)])  27.9 us
    pallas_call x3, Pallas kernels, encode(): pl.pallas_call(functools.partial(encode_body, members, order, width // ti...  23.7 us
    pallas_call x3, Pallas kernels, down(): pl.pallas_call(functools.partial(down_body, owners, members, pieces, orde...  20.4 us
    ppermute x11, waiting for transfers between devices, shift(): lax.ppermute(value, axis, [((d + hop) % size, d) for d in range(size)])  11.8 us
    ppermute x11, starting transfers between devices, shift(): lax.ppermute(value, axis, [((d + hop) % size, d) for d in range(size)])  8.42 us
  transfers between devices with their start and end apart: 39, of which 26 were waited for; matrix products, arithmetic and copies ran while one was open for 3% of the time, Pallas kernels for 26%

profile of v6, /device:TPU:0, one launch (start us, length us, event | category | flops | bytes accessed | tf_op | source)
XLA Modules:
  0.0 257.8 jit_solution(16242823102334107406)
XLA Ops:
  5.2 4.9 %collective-permute-done = bf16[1,48,1024]{2,1,0:T(8,128)(2,1)S(1)} collective-permute-done((bf16[1,48,1024]{2,1,0:T(8,128)(2,1)S(1)}, bf16[1,48,1024]{2,1,0:T(8,128)(2,1)S(1)}, u32[]{:S(2)}, u32[]{:S(2)}) %collective-permute-start) | collective-permute-done | bytes 98336 | tf_op jit(solution)/shard_map/ppermute | solution.py:26
  15.0 5.1 %collective-permute-done.7 = bf16[1,80,1024]{2,1,0:T(8,128)(2,1)S(1)} collective-permute-done((bf16[1,80,1024]{2,1,0:T(8,128)(2,1)S(1)}, bf16[1,80,1024]{2,1,0:T(8,128)(2,1)S(1)}, u32[]{:S(2)}, u32[]{:S(2)}) %collective-permute-start.7) | collective-permute-done | bytes 163872 | tf_op jit(solution)/shard_map/ppermute | solution.py:26
  27.5 5.2 %collective-permute-done.8 = bf16[2,80,1024]{2,1,0:T(8,128)(2,1)S(1)} collective-permute-done((bf16[2,80,1024]{2,1,0:T(8,128)(2,1)S(1)}, bf16[2,80,1024]{2,1,0:T(8,128)(2,1)S(1)}, u32[]{:S(2)}, u32[]{:S(2)}) %collective-permute-start.8) | collective-permute-done | bytes 327712 | tf_op jit(solution)/shard_map/ppermute | solution.py:26
  34.0 7.2 %shard_map.82 = (f32[2,96,1792]{2,1,0:T(8,128)S(1)}, bf16[2,96,1792]{2,1,0:T(8,128)(2,1)S(1)}) custom-call(bf16[2,2,2,48,1024]{4,3,2,1,0:T(8,128)(2,1)S(1)} %multiply_convert_fusion.1.x_ref, bf16[1,2048,3584]{2,1,0:T(8,128)(2,1)} %gate_ref.7, bf16[1,2048,3584]{2,1,0:T(8,128)(2,1)} %up_ref.7), custom_call_target="tpu_custom_call" | custom-call | flops 1 | bytes 1 | tf_op jit(solution)/shard_map/pallas_call | solution.py:131
  43.9 7.2 %shard_map.83 = (f32[2,96,1792]{2,1,0:T(8,128)S(1)}, bf16[2,96,1792]{2,1,0:T(8,128)(2,1)S(1)}) custom-call(bf16[2,2,2,48,1024]{4,3,2,1,0:T(8,128)(2,1)S(1)} %multiply_convert_fusion.1.x_ref, bf16[1,2048,3584]{2,1,0:T(8,128)(2,1)} %gate_ref.7, bf16[1,2048,3584]{2,1,0:T(8,128)(2,1)} %up_ref.7, f32[2,96,1792]{2,1,0:T(8,128)S(1)} %get-tuple-element.53.refs_0_, ...), custom_call_target="tpu_custom_call" | custom-call | flops 1 | bytes 1 | tf_op jit(solution)/shard_map/pallas_call | solution.py:131
  53.5 6.3 %collective-permute-done.14 = f32[2,80]{1,0:T(2,128)S(1)} collective-permute-done((f32[2,80]{1,0:T(2,128)S(1)}, f32[2,80]{1,0:T(2,128)S(1)}, u32[]{:S(2)}, u32[]{:S(2)}) %collective-permute-start.14) | collective-permute-done | bytes 672 | tf_op jit(solution)/shard_map/ppermute | solution.py:18
  60.1 12.8 %collective-permute-done.10 = bf16[2,96,1792]{2,1,0:T(8,128)(2,1)S(1)} collective-permute-done((bf16[2,96,1792]{2,1,0:T(8,128)(2,1)S(1)}, bf16[2,96,1792]{2,1,0:T(8,128)(2,1)S(1)}, u32[]{:S(2)}, u32[]{:S(2)}) %collective-permute-start.10) | collective-permute-done | bytes 688160 | tf_op jit(solution)/shard_map/ppermute | solution.py:22
  75.0 11.7 %shard_map.84 = (f32[2,96,3584]{2,1,0:T(8,128)S(1)}, bf16[2,96,3584]{2,1,0:T(8,128)(2,1)S(1)}) custom-call(bf16[2,2,2,48,1024]{4,3,2,1,0:T(8,128)(2,1)S(1)} %multiply_convert_fusion.x_ref, bf16[1,2048,3584]{2,1,0:T(8,128)(2,1)} %gate_ref.7, bf16[1,2048,3584]{2,1,0:T(8,128)(2,1)} %up_ref.7, f32[2,96,1792]{2,1,0:T(8,128)S(1)} %get-tuple-element.58.refs_0_, ...), custom_call_target="tpu_custom_call" | custom-call | flops 1 | bytes 1 | tf_op jit(solution)/shard_map/pallas_call | solution.py:131
  89.2 7.2 %shard_map.85 = (f32[96,2048]{1,0:T(8,128)}, bf16[96,2048]{1,0:T(8,128)(2,1)S(1)}) custom-call(s32[1]{0:T(128)} %bitcast.rank_ref, bf16[96,3584]{1,0:T(8,128)(2,1)S(1)} %pad_maximum_fusion.1.refs_3_.refs_0_, bf16[96,3584]{1,0:T(8,128)(2,1)S(1)} %collective-permute-done.11.refs_1_, bf16[1,3584,2048]{2,1,0:T(8,128)(2,1)} %refs_2_.5, f32[2,96,3584]{2,1,0:T(8,128)} %copy-done.2), custom_call_target="tpu_custom_call" | custom-call | flops 1 | bytes 1 | tf_op jit(solution)/shard_map/pallas_call | solution.py:179
  97.2 7.8 %collective-permute-done.15 = bf16[96,2048]{1,0:T(8,128)(2,1)S(1)} collective-permute-done((bf16[96,2048]{1,0:T(8,128)(2,1)S(1)}, bf16[96,2048]{1,0:T(8,128)(2,1)S(1)}, u32[]{:S(2)}, u32[]{:S(2)}) %collective-permute-start.15) | collective-permute-done | bytes 393248 | tf_op jit(solution)/shard_map/ppermute | solution.py:26
  108.6 10.1 %collective-permute-done.17 = bf16[2,96,3584]{2,1,0:T(8,128)(2,1)S(1)} collective-permute-done((bf16[2,96,3584]{2,1,0:T(8,128)(2,1)S(1)}, bf16[2,96,3584]{2,1,0:T(8,128)(2,1)S(1)}, u32[]{:S(2)}, u32[]{:S(2)}) %collective-permute-start.17) | collective-permute-done | bytes 1376288 | tf_op jit(solution)/shard_map/ppermute | solution.py:22
  121.1 11.4 %shard_map.86 = (f32[2,64,3584]{2,1,0:T(8,128)S(1)}, bf16[2,64,3584]{2,1,0:T(8,128)(2,1)S(1)}) custom-call(bf16[2,2,2,32,1024]{4,3,2,1,0:T(8,128)(2,1)S(1)} %multiply_convert_fusion.2.x_ref, bf16[1,2048,3584]{2,1,0:T(8,128)(2,1)} %gate_ref.7, bf16[1,2048,3584]{2,1,0:T(8,128)(2,1)} %up_ref.7, f32[96,2048]{1,0:T(8,128)S(1)} %copy-done.6, ...), custom_call_target="tpu_custom_call" | custom-call | flops 1 | bytes 1 | tf_op jit(solution)/shard_map/pallas_call | solution.py:131
  136.9 7.1 %shard_map.87 = (f32[96,2048]{1,0:T(8,128)}, bf16[96,2048]{1,0:T(8,128)(2,1)S(1)}) custom-call(s32[1]{0:T(128)} %bitcast.rank_ref, bf16[96,3584]{1,0:T(8,128)(2,1)S(1)} %fusion.1.refs_2_.refs_0_, bf16[96,3584]{1,0:T(8,128)(2,1)S(1)} %collective-permute-done.19.refs_1_, bf16[1,3584,2048]{2,1,0:T(8,128)(2,1)} %refs_2_.5, f32[2,64,3584]{2,1,0:T(8,128)} %copy-done.4, ...), custom_call_target="tpu_custom_call" | custom-call | flops 1 | bytes 1 | tf_op jit(solution)/shard_map/pallas_call | solution.py:179
  146.3 8.1 %collective-permute-done.21 = bf16[2,64,3584]{2,1,0:T(8,128)(2,1)S(1)} collective-permute-done((bf16[2,64,3584]{2,1,0:T(8,128)(2,1)S(1)}, bf16[2,64,3584]{2,1,0:T(8,128)(2,1)S(1)}, u32[]{:S(2)}, u32[]{:S(2)}) %collective-permute-start.21) | collective-permute-done | bytes 917536 | tf_op jit(solution)/shard_map/ppermute | solution.py:22
  159.2 5.4 %collective-permute-done.20.far_ref = bf16[96,2048]{1,0:T(8,128)(2,1)S(1)} collective-permute-done((bf16[96,2048]{1,0:T(8,128)(2,1)S(1)}, bf16[96,2048]{1,0:T(8,128)(2,1)S(1)}, u32[]{:S(2)}, u32[]{:S(2)}) %collective-permute-start.20) | collective-permute-done | bytes 393248 | tf_op jit(solution)/shard_map/ppermute | solution.py:26
  164.6 8.1 %shard_map.88 = (f32[96,4096]{1,0:T(8,128)}, bf16[96,4096]{1,0:T(8,128)(2,1)}) custom-call(s32[1]{0:T(128)} %bitcast.rank_ref, bf16[96,2048]{1,0:T(8,128)(2,1)S(1)} %constant_dynamic-update-slice_fusion.near_ref.refs_1_, bf16[96,2048]{1,0:T(8,128)(2,1)S(1)} %collective-permute-done.20.far_ref, bf16[1,2048,4096]{2,1,0:T(8,128)(2,1)} %weight_ref.5, ...), custom_call_target="tpu_custom_call" | custom-call | flops 1 | bytes 1 | tf_op jit(solution)/shard_map/pallas_call | solution.py:224
  172.8 6.1 %shard_map.89 = (f32[64,2048]{1,0:T(8,128)S(1)}, bf16[64,2048]{1,0:T(8,128)(2,1)S(1)}) custom-call(s32[1]{0:T(128)} %bitcast.rank_ref, bf16[64,3584]{1,0:T(8,128)(2,1)S(1)} %fusion.3.refs_2_.refs_0_, bf16[64,3584]{1,0:T(8,128)(2,1)S(1)} %collective-permute-done.24.refs_1_, bf16[1,3584,2048]{2,1,0:T(8,128)(2,1)} %refs_2_.5, f32[96,4096]{1,0:T(8,128)} %get-tuple-element.80.refs_3_), custom_call_target="tpu_custom_call" | custom-call | flops 1 | bytes 1 | tf_op jit(solution)/shard_map/pallas_call | solution.py:179
  191.7 6.3 %collective-permute-done.30 = bf16[32,2048]{1,0:T(8,128)(2,1)S(1)} collective-permute-done((bf16[32,2048]{1,0:T(8,128)(2,1)S(1)}, bf16[32,2048]{1,0:T(8,128)(2,1)S(1)}, u32[]{:S(2)}, u32[]{:S(2)}) %collective-permute-start.30) | collective-permute-done | bytes 131104 | tf_op jit(solution)/shard_map/ppermute | solution.py:26
  201.6 4.8 %collective-permute-done.27 = bf16[48,2048]{1,0:T(8,128)(2,1)S(1)} collective-permute-done((bf16[48,2048]{1,0:T(8,128)(2,1)S(1)}, bf16[48,2048]{1,0:T(8,128)(2,1)S(1)}, u32[]{:S(2)}, u32[]{:S(2)}) %collective-permute-start.27) | collective-permute-done | bytes 196640 | tf_op jit(solution)/shard_map/ppermute | solution.py:26
  213.2 5.5 %collective-permute-done.28.far_ref = bf16[96,2048]{1,0:T(8,128)(2,1)S(1)} collective-permute-done((bf16[96,2048]{1,0:T(8,128)(2,1)S(1)}, bf16[96,2048]{1,0:T(8,128)(2,1)S(1)}, u32[]{:S(2)}, u32[]{:S(2)}) %collective-permute-start.28) | collective-permute-done | bytes 393248 | tf_op jit(solution)/shard_map/ppermute | solution.py:26
  219.5 8.0 %shard_map.90 = (f32[96,4096]{1,0:T(8,128)}, bf16[96,4096]{1,0:T(8,128)(2,1)}) custom-call(s32[1]{0:T(128)} %bitcast.rank_ref, bf16[96,2048]{1,0:T(8,128)(2,1)S(1)} %constant_dynamic-update-slice_fusion.2.near_ref.refs_6_, bf16[96,2048]{1,0:T(8,128)(2,1)S(1)} %collective-permute-done.28.far_ref, bf16[1,2048,4096]{2,1,0:T(8,128)(2,1)} %weight_ref.5, ...), custom_call_target="tpu_custom_call" | custom-call | flops 1 | bytes 1 | tf_op jit(solution)/shard_map/pallas_call | solution.py:224
  231.8 7.6 %shard_map.91 = (f32[64,4096]{1,0:T(8,128)}, bf16[64,4096]{1,0:T(8,128)(2,1)S(1)}) custom-call(s32[1]{0:T(128)} %bitcast.rank_ref, bf16[64,2048]{1,0:T(8,128)(2,1)S(1)} %pad_maximum_fusion.10.refs_4_.near_ref, bf16[64,2048]{1,0:T(8,128)(2,1)S(1)} %constant_dynamic-update-slice_fusion.4.refs_5_.far_ref, bf16[1,2048,4096]{2,1,0:T(8,128)(2,1)} %weight_ref.5, ...), custom_call_target="tpu_custom_call" | custom-call | flops 1 | bytes 1 | tf_op jit(solution)/shard_map/pallas_call | solution.py:224
  243.8 7.7 %collective-permute-done.36 = bf16[48,4096]{1,0:T(8,128)(2,1)S(1)} collective-permute-done((bf16[48,4096]{1,0:T(8,128)(2,1)S(1)}, bf16[48,4096]{1,0:T(8,128)(2,1)S(1)}, u32[]{:S(2)}, u32[]{:S(2)}) %collective-permute-start.36) | collective-permute-done | bytes 393248 | tf_op jit(solution)/shard_map/ppermute | solution.py:22
  251.9 4.7 %collective-permute-done.38 = bf16[32,4096]{1,0:T(8,128)(2,1)S(1)} collective-permute-done((bf16[32,4096]{1,0:T(8,128)(2,1)S(1)}, bf16[32,4096]{1,0:T(8,128)(2,1)S(1)}, u32[]{:S(2)}, u32[]{:S(2)}) %collective-permute-start.38) | collective-permute-done | bytes 262176 | tf_op jit(solution)/shard_map/ppermute | solution.py:22
  (167 shorter events, 80.7 us)
Async XLA Ops:
  22.6 10.1 %collective-permute-start.8 = (bf16[2,80,1024]{2,1,0:T(8,128)(2,1)S(1)}, bf16[2,80,1024]{2,1,0:T(8,128)(2,1)S(1)}, u32[]{:S(2)}, u32[]{:S(2)}) collective-permute-start(bf16[2,80,1024]{2,1,0:T(8,128)(2,1)S(1)} %pad_maximum_fusion.7), channel_id=1, source_target_pairs={{0,4},{4,0},{8,12},{12,8},{1,5},{5,1},{9,13},{13,9},{2,6},{6,2},{1... | collective-permute-start | bytes 983048 | tf_op jit(solution)/shard_map/ppermute | solution.py:26
  32.9 11.0 %collective-permute-start.9 = (bf16[2,80,1024]{2,1,0:T(8,128)(2,1)S(1)}, bf16[2,80,1024]{2,1,0:T(8,128)(2,1)S(1)}, u32[]{:S(2)}, u32[]{:S(2)}) collective-permute-start(bf16[2,80,1024]{2,1,0:T(8,128)(2,1)S(1)} %pad_maximum_fusion.9), channel_id=1, source_target_pairs={{2,0},{0,2},{3,1},{1,3},{6,4},{4,6},{7,5},{5,7},{10,8},{8,10},{11,... | collective-permute-start | bytes 983048 | tf_op jit(solution)/shard_map/ppermute | solution.py:18
  41.3 18.5 %collective-permute-start.6 = (bf16[2,96,1792]{2,1,0:T(8,128)(2,1)S(1)}, bf16[2,96,1792]{2,1,0:T(8,128)(2,1)S(1)}, u32[]{:S(2)}, u32[]{:S(2)}) collective-permute-start(bf16[2,96,1792]{2,1,0:T(8,128)(2,1)S(1)} %get-tuple-element.54), channel_id=1, source_target_pairs={{0,2},{2,0},{1,3},{3,1},{4,6},{6,4},{5,7},{7,5},{8,10},{10,8},{9,1... | collective-permute-start | bytes 2064392 | tf_op jit(solution)/shard_map/ppermute | solution.py:22
  51.9 22.9 %collective-permute-start.12 = (bf16[2,2,80,1024]{3,2,1,0:T(8,128)(2,1)S(1)}, bf16[2,2,80,1024]{3,2,1,0:T(8,128)(2,1)S(1)}, u32[]{:S(2)}, u32[]{:S(2)}) collective-permute-start(bf16[2,2,80,1024]{3,2,1,0:T(8,128)(2,1)S(1)} %get-tuple-element.106), channel_id=1, source_target_pairs={{1,0},{0,1},{3,2},{2,3},{5,4},{4,5},{7,6},{6,7},{9,8},{8,9},{11,10... | collective-permute-start | bytes 1966088 | tf_op jit(solution)/shard_map/ppermute | solution.py:18
  52.0 20.9 %collective-permute-start.10 = (bf16[2,96,1792]{2,1,0:T(8,128)(2,1)S(1)}, bf16[2,96,1792]{2,1,0:T(8,128)(2,1)S(1)}, u32[]{:S(2)}, u32[]{:S(2)}) collective-permute-start(bf16[2,96,1792]{2,1,0:T(8,128)(2,1)S(1)} %get-tuple-element.59), channel_id=1, source_target_pairs={{0,2},{2,0},{1,3},{3,1},{4,6},{6,4},{5,7},{7,5},{8,10},{10,8},{9,1... | collective-permute-start | bytes 2064392 | tf_op jit(solution)/shard_map/ppermute | solution.py:22
  73.3 15.9 %collective-permute-start.11 = (bf16[96,3584]{1,0:T(8,128)(2,1)S(1)}, bf16[96,3584]{1,0:T(8,128)(2,1)S(1)}, u32[]{:S(2)}, u32[]{:S(2)}) collective-permute-start(bf16[96,3584]{1,0:T(8,128)(2,1)S(1)} %pad_maximum_fusion.1.refs_3_.refs_0_), channel_id=1, source_target_pairs={{2,0},{0,2},{3,1},{1,3},{6,4},{4,6},{7,5},{5,7},{10,8},{8,10},{11,... | collective-permute-start | bytes 2064392 | tf_op jit(solution)/shard_map/ppermute | solution.py:18
  88.3 30.4 %collective-permute-start.17 = (bf16[2,96,3584]{2,1,0:T(8,128)(2,1)S(1)}, bf16[2,96,3584]{2,1,0:T(8,128)(2,1)S(1)}, u32[]{:S(2)}, u32[]{:S(2)}) collective-permute-start(bf16[2,96,3584]{2,1,0:T(8,128)(2,1)S(1)} %get-tuple-element.66), channel_id=1, source_target_pairs={{0,2},{2,0},{1,3},{3,1},{4,6},{6,4},{5,7},{7,5},{8,10},{10,8},{9,1... | collective-permute-start | bytes 4128776 | tf_op jit(solution)/shard_map/ppermute | solution.py:22
  106.3 27.5 %collective-permute-start.16 = (bf16[48,2048]{1,0:T(8,128)(2,1)S(1)}, bf16[48,2048]{1,0:T(8,128)(2,1)S(1)}, u32[]{:S(2)}, u32[]{:S(2)}) collective-permute-start(bf16[48,2048]{1,0:T(8,128)(2,1)S(1)} %slice.225.refs_1_), channel_id=1, source_target_pairs={{0,8},{4,12},{8,0},{12,4},{1,9},{5,13},{9,1},{13,5},{2,10},{6,14},... | collective-permute-start | bytes 589832 | tf_op jit(solution)/shard_map/ppermute | solution.py:26
  119.4 17.6 %collective-permute-start.19 = (bf16[96,3584]{1,0:T(8,128)(2,1)S(1)}, bf16[96,3584]{1,0:T(8,128)(2,1)S(1)}, u32[]{:S(2)}, u32[]{:S(2)}) collective-permute-start(bf16[96,3584]{1,0:T(8,128)(2,1)S(1)} %fusion.1.refs_2_.refs_0_), channel_id=1, source_target_pairs={{2,0},{0,2},{3,1},{1,3},{6,4},{4,6},{7,5},{5,7},{10,8},{8,10},{11,... | collective-permute-start | bytes 2064392 | tf_op jit(solution)/shard_map/ppermute | solution.py:18
  133.8 20.6 %collective-permute-start.21 = (bf16[2,64,3584]{2,1,0:T(8,128)(2,1)S(1)}, bf16[2,64,3584]{2,1,0:T(8,128)(2,1)S(1)}, u32[]{:S(2)}, u32[]{:S(2)}) collective-permute-start(bf16[2,64,3584]{2,1,0:T(8,128)(2,1)S(1)} %get-tuple-element.73), channel_id=1, source_target_pairs={{0,2},{2,0},{1,3},{3,1},{4,6},{6,4},{5,7},{7,5},{8,10},{10,8},{9,1... | collective-permute-start | bytes 2752520 | tf_op jit(solution)/shard_map/ppermute | solution.py:22
  134.7 11.2 %collective-permute-start.18 = (bf16[48,2048]{1,0:T(8,128)(2,1)S(1)}, bf16[48,2048]{1,0:T(8,128)(2,1)S(1)}, u32[]{:S(2)}, u32[]{:S(2)}) collective-permute-start(bf16[48,2048]{1,0:T(8,128)(2,1)S(1)} %add_convert_fusion.1.refs_4_), channel_id=1, source_target_pairs={{0,8},{4,12},{8,0},{12,4},{1,9},{5,13},{9,1},{13,5},{2,10},{6,14},... | collective-permute-start | bytes 589832 | tf_op jit(solution)/shard_map/ppermute | solution.py:26
  144.1 12.6 %collective-permute-start.22 = (bf16[96,2048]{1,0:T(8,128)(2,1)S(1)}, bf16[96,2048]{1,0:T(8,128)(2,1)S(1)}, u32[]{:S(2)}, u32[]{:S(2)}) collective-permute-start(bf16[96,2048]{1,0:T(8,128)(2,1)S(1)} %get-tuple-element.74), channel_id=1, source_target_pairs={{0,4},{4,0},{8,12},{12,8},{1,5},{5,1},{9,13},{13,9},{2,6},{6,2},{1... | collective-permute-start | bytes 1179656 | tf_op jit(solution)/shard_map/ppermute | solution.py:26
  145.9 18.7 %collective-permute-start.20 = (bf16[96,2048]{1,0:T(8,128)(2,1)S(1)}, bf16[96,2048]{1,0:T(8,128)(2,1)S(1)}, u32[]{:S(2)}, u32[]{:S(2)}) collective-permute-start(bf16[96,2048]{1,0:T(8,128)(2,1)S(1)} %constant_dynamic-update-slice_fusion.near_ref.refs_1_), channel_id=1, source_target_pairs={{0,4},{4,0},{8,12},{12,8},{1,5},{5,1},{9,13},{13,9},{2,6},{6,2},{1... | collective-permute-start | bytes 1179656 | tf_op jit(solution)/shard_map/ppermute | solution.py:26
  154.9 17.9 %collective-permute-start.24 = (bf16[64,3584]{1,0:T(8,128)(2,1)S(1)}, bf16[64,3584]{1,0:T(8,128)(2,1)S(1)}, u32[]{:S(2)}, u32[]{:S(2)}) collective-permute-start(bf16[64,3584]{1,0:T(8,128)(2,1)S(1)} %fusion.3.refs_2_.refs_0_), channel_id=1, source_target_pairs={{2,0},{0,2},{3,1},{1,3},{6,4},{4,6},{7,5},{5,7},{10,8},{8,10},{11,... | collective-permute-start | bytes 1376264 | tf_op jit(solution)/shard_map/ppermute | solution.py:18
  156.8 22.2 %collective-permute-start.26 = (bf16[48,2048]{1,0:T(8,128)(2,1)S(1)}, bf16[48,2048]{1,0:T(8,128)(2,1)S(1)}, u32[]{:S(2)}, u32[]{:S(2)}) collective-permute-start(bf16[48,2048]{1,0:T(8,128)(2,1)S(1)} %slice.224.refs_3_), channel_id=1, source_target_pairs={{0,8},{4,12},{8,0},{12,4},{1,9},{5,13},{9,1},{13,5},{2,10},{6,14},... | collective-permute-start | bytes 589832 | tf_op jit(solution)/shard_map/ppermute | solution.py:26
  172.7 34.9 %collective-permute-start.23 = (bf16[96,4096]{1,0:T(8,128)(2,1)}, bf16[96,4096]{1,0:T(8,128)(2,1)S(1)}, u32[]{:S(2)}, u32[]{:S(2)}) collective-permute-start(bf16[96,4096]{1,0:T(8,128)(2,1)} %get-tuple-element.78), channel_id=1, source_target_pairs={{0,1},{1,0},{2,3},{3,2},{4,5},{5,4},{6,7},{7,6},{8,9},{9,8},{10,11... | collective-permute-start | bytes 2359304 | tf_op jit(solution)/shard_map/ppermute | solution.py:22
  182.3 15.7 %collective-permute-start.30 = (bf16[32,2048]{1,0:T(8,128)(2,1)S(1)}, bf16[32,2048]{1,0:T(8,128)(2,1)S(1)}, u32[]{:S(2)}, u32[]{:S(2)}) collective-permute-start(bf16[32,2048]{1,0:T(8,128)(2,1)S(1)} %slice.226), channel_id=1, source_target_pairs={{0,8},{4,12},{8,0},{12,4},{1,9},{5,13},{9,1},{13,5},{2,10},{6,14},... | collective-permute-start | bytes 393224 | tf_op jit(solution)/shard_map/ppermute | solution.py:26
  183.6 22.8 %collective-permute-start.27 = (bf16[48,2048]{1,0:T(8,128)(2,1)S(1)}, bf16[48,2048]{1,0:T(8,128)(2,1)S(1)}, u32[]{:S(2)}, u32[]{:S(2)}) collective-permute-start(bf16[48,2048]{1,0:T(8,128)(2,1)S(1)} %add_convert_fusion.refs_1_), channel_id=1, source_target_pairs={{0,8},{4,12},{8,0},{12,4},{1,9},{5,13},{9,1},{13,5},{2,10},{6,14},... | collective-permute-start | bytes 589832 | tf_op jit(solution)/shard_map/ppermute | solution.py:26
  198.2 10.7 %collective-permute-start.34 = (bf16[32,2048]{1,0:T(8,128)(2,1)S(1)}, bf16[32,2048]{1,0:T(8,128)(2,1)S(1)}, u32[]{:S(2)}, u32[]{:S(2)}) collective-permute-start(bf16[32,2048]{1,0:T(8,128)(2,1)S(1)} %add_convert_fusion.2.refs_3_), channel_id=1, source_target_pairs={{0,12},{4,8},{8,4},{12,0},{1,13},{5,9},{9,5},{13,1},{2,14},{6,10},... | collective-permute-start | bytes 393224 | tf_op jit(solution)/shard_map/ppermute | solution.py:26
  199.1 14.0 %collective-permute-start.32 = (bf16[32,2048]{1,0:T(8,128)(2,1)S(1)}, bf16[32,2048]{1,0:T(8,128)(2,1)S(1)}, u32[]{:S(2)}, u32[]{:S(2)}) collective-permute-start(bf16[32,2048]{1,0:T(8,128)(2,1)S(1)} %add_convert_fusion.2.refs_3_), channel_id=1, source_target_pairs={{0,8},{4,12},{8,0},{12,4},{1,9},{5,13},{9,1},{13,5},{2,10},{6,14},... | collective-permute-start | bytes 393224 | tf_op jit(solution)/shard_map/ppermute | solution.py:26
  206.5 12.2 %collective-permute-start.28 = (bf16[96,2048]{1,0:T(8,128)(2,1)S(1)}, bf16[96,2048]{1,0:T(8,128)(2,1)S(1)}, u32[]{:S(2)}, u32[]{:S(2)}) collective-permute-start(bf16[96,2048]{1,0:T(8,128)(2,1)S(1)} %constant_dynamic-update-slice_fusion.2.near_ref.refs_6_), channel_id=1, source_target_pairs={{0,4},{4,0},{8,12},{12,8},{1,5},{5,1},{9,13},{13,9},{2,6},{6,2},{1... | collective-permute-start | bytes 1179656 | tf_op jit(solution)/shard_map/ppermute | solution.py:26
  207.9 10.9 %collective-permute-start.25 = (bf16[48,4096]{1,0:T(8,128)(2,1)S(1)}, bf16[48,4096]{1,0:T(8,128)(2,1)S(1)}, u32[]{:S(2)}, u32[]{:S(2)}) collective-permute-start(bf16[48,4096]{1,0:T(8,128)(2,1)S(1)} %slice.222.refs_2_), channel_id=1, source_target_pairs={{0,2},{2,0},{1,3},{3,1},{4,6},{6,4},{5,7},{7,5},{8,10},{10,8},{9,1... | collective-permute-start | bytes 1179656 | tf_op jit(solution)/shard_map/ppermute | solution.py:22
  239.6 11.9 %collective-permute-start.36 = (bf16[48,4096]{1,0:T(8,128)(2,1)S(1)}, bf16[48,4096]{1,0:T(8,128)(2,1)S(1)}, u32[]{:S(2)}, u32[]{:S(2)}) collective-permute-start(bf16[48,4096]{1,0:T(8,128)(2,1)S(1)} %slice.221.refs_1_), channel_id=1, source_target_pairs={{0,2},{2,0},{1,3},{3,1},{4,6},{6,4},{5,7},{7,5},{8,10},{10,8},{9,1... | collective-permute-start | bytes 1179656 | tf_op jit(solution)/shard_map/ppermute | solution.py:22
  242.8 13.7 %collective-permute-start.38 = (bf16[32,4096]{1,0:T(8,128)(2,1)S(1)}, bf16[32,4096]{1,0:T(8,128)(2,1)S(1)}, u32[]{:S(2)}, u32[]{:S(2)}) collective-permute-start(bf16[32,4096]{1,0:T(8,128)(2,1)S(1)} %slice.223), channel_id=1, source_target_pairs={{0,2},{2,0},{1,3},{3,1},{4,6},{6,4},{5,7},{7,5},{8,10},{10,8},{9,1... | collective-permute-start | bytes 786440 | tf_op jit(solution)/shard_map/ppermute | solution.py:22
  (34 other events, 307.1 us)

commit v7 on v6

--- a/solution.py
+++ b/solution.py
@@ -9,7 +9,7 @@
 
 BF16 = jnp.bfloat16
 F32 = jnp.float32
-VMEM_BYTES = 52 * 1024 * 1024
+VMEM_BYTES = 51 * 1024 * 1024
 GATE_UP_VMEM_BYTES = 44 * 1024 * 1024
 BUFFERS = 4
 
@@ -296,10 +296,7 @@
                 ]
             )
             columns.append(half if hop == 0 else shift(half, "rows", owners, hop))
-        return columns, from_all(inverse, "mp", members)
-
-    def scales(inverse):
-        return from_all(inverse, "rows", owners).transpose(1, 0, 2)
+        return columns, inverse
 
     def from_members(columns):
         return from_all(jnp.stack(columns), "mp", members)
@@ -313,15 +310,16 @@
     head = sizes[0]
 
     gathered = own_tokens[:head][None]
-    rest = own_tokens[head:][None] if chunks > 1 else None
     for bit in bits:
         gathered = doubled(gathered, bit)
-        if rest is not None:
-            rest = doubled(after(rest, gathered), bit)
-    first = from_owners(gathered)
-    if rest is not None:
-        rest = from_owners(after(rest, first))
-    xs = [normed(from_members(first[0]), scales(first[1]))]
+    columns, inverse = from_owners(gathered)
+    inverses = from_all(inverse, "rows", owners)
+    columns, inverses = after((columns, inverses), (columns, inverses))
+    xs = [normed(from_members(columns), from_all(inverses, "mp", members))]
+    rest = None
+    if chunks > 1:
+        rest = after(own_tokens[head:][None], gathered)
+        rest = [rest, swap(rest, "hid", ranks, bits[0])]
 
     sums, hidden, layer, blocks, outs = ({} for _ in range(5))
     last = []
@@ -332,27 +330,31 @@
         for piece in range(pieces):
             own, *sends = gate_up(xs[t], gate_weight, up_weight, piece, pieces, list(last))
             last[:] = [own]
-            if t == 0 and rest is not None:
-                last.extend(rest[0])
             others = [send(sends[hop - 1], "rows", owners, hop) for hop in range(1, owners)]
             sums[t].append((own, others))
 
-    def rest_of(_):
-        if rest is None:
-            return
-        columns = from_members(rest[0])
-        inverses = scales(after(rest[1], sums[0][-1][0]))
+    def rest_of(units):
+        gathered = jnp.concatenate(after(rest, sums[0][-1][0]))
+        for bit in bits[1:]:
+            gathered = doubled(after(gathered, sums[0][-1][0]), bit)
+        columns, inverse = from_owners(after(gathered, units))
+        inverses = from_all(inverse, "rows", owners)
+        columns, inverses = after((columns, inverses), (columns, inverses))
+        columns, inverses = from_members(columns), from_all(inverses, "mp", members)
         for start, q in zip(starts[1:], sizes[1:]):
             rows = slice(start - head, start - head + q)
             xs.append(normed(columns[:, :, :, rows], inverses[:, :, rows]))
 
     def hidden_of(t):
         units = []
-        for own, others in sums[t]:
+        parts = ordered(sums[t]) if 0 < t == chunks - 1 else sums[t]
+        for own, others in parts:
             acts = own
             for other in others:
                 acts = acts + other.astype(F32)
             units.append((jax.nn.silu(acts[0]) * acts[1]).astype(BF16))
+            if t == 0 and rest is not None and len(units) == 1:
+                rest_of(units[0])
         units = jnp.concatenate(units, axis=1)
         hidden[t] = [units] + [shift(units, "rows", owners, hop) for hop in range(1, owners)]
         last.append(units)
@@ -396,9 +398,7 @@
         block = total.astype(BF16)
         last.append(block)
         if at_once(t):
-            third, second, first = (swap(block, "hid", ranks, offset) for offset in (3, 2, 1))
-            blocks[t] = (jnp.concatenate((block, second)), jnp.concatenate((first, third)))
-            last.extend(blocks[t])
+            blocks[t] = [block] + [swap(block, "hid", ranks, offset) for offset in (1, 2, 3)]
         else:
             layer[t] = (block, swap(block, "hid", ranks, bits[0]))
 
@@ -408,6 +408,8 @@
         near, far = ordered(layer[t])
         if t > 0:
             near, far = after((near, far), sums[t - 1][0])
+        elif chunks > 1:
+            near, far = after((near, far), hidden[1])
         for bit in bits[1:]:
             near = jnp.concatenate((near, far))
             last.append(near)
@@ -415,7 +417,11 @@
         blocks[t] = (near, far)
 
     def features_of(t):
-        own, *sends = encode(rank, *blocks[t], enc_weight, members, order, list(last))
+        near_far = blocks[t]
+        if at_once(t):
+            parts = ordered(near_far) if t else near_far
+            near_far = (jnp.concatenate(parts[0::2]), jnp.concatenate(parts[1::2]))
+        own, *sends = encode(rank, *near_far, enc_weight, members, order, list(last))
         last[:] = [own]
         sums[t] = (own, [send(sends[hop - 1], "mp", members, hop) for hop in range(1, members)])
 
@@ -443,12 +449,12 @@
         outs[t] = (jnp.maximum(pre, 0.0) * factor).astype(BF16)
 
     stages = (
-        (gate_up_of, 0), (rest_of, 0), (hidden_of, 0), (gate_up_of, 1), (down_of, 0),
-        (halve_of, 0), (hidden_of, 1), (gate_up_of, 2), (settle_of, 0), (down_of, 1),
-        (double_of, 0), (hidden_of, 2), (halve_of, 1), (features_of, 0), (down_of, 2),
-        (settle_of, 1), (share_of, 0), (settle_of, 2), (double_of, 1), (shared_of, 0),
-        (features_of, 1), (share_of, 1), (features_of, 2), (share_of, 2), (finish_of, 0),
-        (finish_of, 1), (finish_of, 2),
+        (gate_up_of, 0), (hidden_of, 0), (gate_up_of, 1), (down_of, 0), (halve_of, 0),
+        (hidden_of, 1), (settle_of, 0), (gate_up_of, 2), (double_of, 0), (down_of, 1),
+        (features_of, 0), (hidden_of, 2), (halve_of, 1), (settle_of, 1), (down_of, 2),
+        (share_of, 0), (settle_of, 2), (double_of, 1), (shared_of, 0), (features_of, 1),
+        (features_of, 2), (share_of, 1), (share_of, 2), (finish_of, 0), (finish_of, 1),
+        (finish_of, 2),
     )
     for stage, t in stages:
         if t < chunks:

time: 258 us -> 239 us (0.926)
  waiting for transfers between devices: 116 us -> 104 us
  other arithmetic: 9.47 us -> 5.66 us
  Pallas kernels: 81.7 us -> 78.5 us
    ppermute x10, waiting for transfers between devices: 46.8 us -> 31.8 us  [send(): lax.ppermute(value, axis, [(d, (d + hop) % size) for d in range(size)])]
    ppermute x11, waiting for transfers between devices: 11.8 us -> 15 us  [shift(): lax.ppermute(value, axis, [((d + hop) % size, d) for d in range(size)])]
    add x3, other arithmetic: 3.26 us -> 0.48 us  [share_of(): total = total + other.astype(F32)]
  transfers between devices with their start and end apart: 39 -> 39, of which waited for: 26 -> 26; matrix products, arithmetic and copies ran while one was open for 3% -> 1% of each run, Pallas kernels for 26% -> 30%
where the time goes in v7:
time: 239 us
  waiting for transfers between devices  104 us (44%)
  Pallas kernels  78.5 us (33%)
  starting transfers between devices  45.2 us (19%)
  other arithmetic  5.66 us (2%)
  local copies, waits for them, and re-layouts  4.31 us (2%)
    ppermute x18, waiting for transfers between devices, swap(): return lax.ppermute(value, axis, [(d, d ^ bit) for d in range(size)])  57.5 us
    pallas_call x4, Pallas kernels, gate_up(): pl.pallas_call(functools.partial(gate_up_body, tiles, piece * tiles), gri...  37.5 us
    ppermute x10, waiting for transfers between devices, send(): lax.ppermute(value, axis, [(d, (d + hop) % size) for d in range(size)])  31.8 us
    ppermute x18, starting transfers between devices, swap(): return lax.ppermute(value, axis, [(d, d ^ bit) for d in range(size)])  27.4 us
    pallas_call x3, Pallas kernels, encode(): pl.pallas_call(functools.partial(encode_body, members, order, width // ti...  22.4 us
    pallas_call x3, Pallas kernels, down(): pl.pallas_call(functools.partial(down_body, owners, members, pieces, orde...  18.6 us
    ppermute x11, waiting for transfers between devices, shift(): lax.ppermute(value, axis, [((d + hop) % size, d) for d in range(size)])  15 us
    ppermute x10, starting transfers between devices, send(): lax.ppermute(value, axis, [(d, (d + hop) % size) for d in range(size)])  9.56 us
  transfers between devices with their start and end apart: 39, of which 26 were waited for; matrix products, arithmetic and copies ran while one was open for 1% of the time, Pallas kernels for 30%

profile of v7, /device:TPU:0, one launch (start us, length us, event | category | flops | bytes accessed | tf_op | source)
XLA Modules:
  0.0 238.6 jit_solution(1761729938607200232)
XLA Ops:
  1.1 4.1 %collective-permute-start = (bf16[1,48,1024]{2,1,0:T(8,128)(2,1)S(1)}, bf16[1,48,1024]{2,1,0:T(8,128)(2,1)S(1)}, u32[]{:S(2)}, u32[]{:S(2)}) collective-permute-start(bf16[1,48,1024]{2,1,0:T(8,128)(2,1)S(1)} %dynamic-slice_bitcast_fusion.1), channel_id=1, source_target_pairs={{0,8},{4,12},{8,0},{12,4},{1,9},{5,13},{9,1},{13,5},{2,10},{6,14},... | collective-permute-start | bytes 294920 | tf_op jit(solution)/shard_map/ppermute | solution.py:26
  5.1 4.9 %collective-permute-done = bf16[1,48,1024]{2,1,0:T(8,128)(2,1)S(1)} collective-permute-done((bf16[1,48,1024]{2,1,0:T(8,128)(2,1)S(1)}, bf16[1,48,1024]{2,1,0:T(8,128)(2,1)S(1)}, u32[]{:S(2)}, u32[]{:S(2)}) %collective-permute-start) | collective-permute-done | bytes 98336 | tf_op jit(solution)/shard_map/ppermute | solution.py:26
  10.9 5.4 %collective-permute-done.1 = bf16[2,48,1024]{2,1,0:T(8,128)(2,1)S(1)} collective-permute-done((bf16[2,48,1024]{2,1,0:T(8,128)(2,1)S(1)}, bf16[2,48,1024]{2,1,0:T(8,128)(2,1)S(1)}, u32[]{:S(2)}, u32[]{:S(2)}) %collective-permute-start.1) | collective-permute-done | bytes 196640 | tf_op jit(solution)/shard_map/ppermute | solution.py:26
  24.3 3.8 %collective-permute-start.9 = (bf16[1,80,1024]{2,1,0:T(8,128)(2,1)S(1)}, bf16[1,80,1024]{2,1,0:T(8,128)(2,1)S(1)}, u32[]{:S(2)}, u32[]{:S(2)}) collective-permute-start(bf16[1,80,1024]{2,1,0:T(8,128)(2,1)S(1)} %dynamic-slice_bitcast_fusion), channel_id=1, source_target_pairs={{0,8},{4,12},{8,0},{12,4},{1,9},{5,13},{9,1},{13,5},{2,10},{6,14},... | collective-permute-start | bytes 491528 | tf_op jit(solution)/shard_map/ppermute | solution.py:26
  28.3 7.2 %shard_map.82 = (f32[2,96,1792]{2,1,0:T(8,128)S(1)}, bf16[2,96,1792]{2,1,0:T(8,128)(2,1)S(1)}) custom-call(bf16[2,2,2,48,1024]{4,3,2,1,0:T(8,128)(2,1)S(1)} %multiply_convert_fusion.1.x_ref, bf16[1,2048,3584]{2,1,0:T(8,128)(2,1)} %gate_ref.7, bf16[1,2048,3584]{2,1,0:T(8,128)(2,1)} %up_ref.7), custom_call_target="tpu_custom_call" | custom-call | flops 1 | bytes 1 | tf_op jit(solution)/shard_map/pallas_call | solution.py:131
  36.2 7.2 %shard_map.83 = (f32[2,96,1792]{2,1,0:T(8,128)S(1)}, bf16[2,96,1792]{2,1,0:T(8,128)(2,1)S(1)}) custom-call(bf16[2,2,2,48,1024]{4,3,2,1,0:T(8,128)(2,1)S(1)} %multiply_convert_fusion.1.x_ref, bf16[1,2048,3584]{2,1,0:T(8,128)(2,1)} %gate_ref.7, bf16[1,2048,3584]{2,1,0:T(8,128)(2,1)} %up_ref.7, f32[2,96,1792]{2,1,0:T(8,128)S(1)} %get-tuple-element.71.refs_0_), custom_call_target="tpu_custom_call" | custom-call | flops 1 | bytes 1 | tf_op jit(solution)/shard_map/pallas_call | solution.py:131
  46.4 6.2 %collective-permute-done.10 = bf16[2,80,1024]{2,1,0:T(8,128)(2,1)S(1)} collective-permute-done((bf16[2,80,1024]{2,1,0:T(8,128)(2,1)S(1)}, bf16[2,80,1024]{2,1,0:T(8,128)(2,1)S(1)}, u32[]{:S(2)}, u32[]{:S(2)}) %collective-permute-start.10) | collective-permute-done | bytes 327712 | tf_op jit(solution)/shard_map/ppermute | solution.py:26
  56.8 11.9 %collective-permute-done.7 = bf16[2,96,1792]{2,1,0:T(8,128)(2,1)S(1)} collective-permute-done((bf16[2,96,1792]{2,1,0:T(8,128)(2,1)S(1)}, bf16[2,96,1792]{2,1,0:T(8,128)(2,1)S(1)}, u32[]{:S(2)}, u32[]{:S(2)}) %collective-permute-start.7) | collective-permute-done | bytes 688160 | tf_op jit(solution)/shard_map/ppermute | solution.py:22
  68.9 5.6 %collective-permute-done.11 = bf16[2,80,1024]{2,1,0:T(8,128)(2,1)S(1)} collective-permute-done((bf16[2,80,1024]{2,1,0:T(8,128)(2,1)S(1)}, bf16[2,80,1024]{2,1,0:T(8,128)(2,1)S(1)}, u32[]{:S(2)}, u32[]{:S(2)}) %collective-permute-start.11) | collective-permute-done | bytes 327712 | tf_op jit(solution)/shard_map/ppermute | solution.py:18
  77.0 11.7 %shard_map.84 = (f32[2,96,3584]{2,1,0:T(8,128)S(1)}, bf16[2,96,3584]{2,1,0:T(8,128)(2,1)S(1)}) custom-call(bf16[2,2,2,48,1024]{4,3,2,1,0:T(8,128)(2,1)S(1)} %multiply_convert_fusion.x_ref, bf16[1,2048,3584]{2,1,0:T(8,128)(2,1)} %gate_ref.7, bf16[1,2048,3584]{2,1,0:T(8,128)(2,1)} %up_ref.7, f32[2,96,1792]{2,1,0:T(8,128)S(1)} %get-tuple-element.73.refs_0_, ...), custom_call_target="tpu_custom_call" | custom-call | flops 1 | bytes 1 | tf_op jit(solution)/shard_map/pallas_call | solution.py:131
  92.8 6.3 %shard_map.85 = (f32[96,2048]{1,0:T(8,128)S(1)}, bf16[96,2048]{1,0:T(8,128)(2,1)S(1)}) custom-call(s32[1]{0:T(128)} %bitcast.rank_ref, bf16[96,3584]{1,0:T(8,128)(2,1)S(1)} %pad_maximum_fusion.1.refs_1_.refs_0_, bf16[96,3584]{1,0:T(8,128)(2,1)S(1)} %collective-permute-done.8.refs_1_, bf16[1,3584,2048]{2,1,0:T(8,128)(2,1)} %refs_2_.5, f32[2,96,3584]{2,1,0:T(8,128)} %copy-done.2), custom_call_target="tpu_custom_call" | custom-call | flops 1 | bytes 1 | tf_op jit(solution)/shard_map/pallas_call | solution.py:179
  100.6 9.3 %collective-permute-done.15 = bf16[96,2048]{1,0:T(8,128)(2,1)S(1)} collective-permute-done((bf16[96,2048]{1,0:T(8,128)(2,1)S(1)}, bf16[96,2048]{1,0:T(8,128)(2,1)S(1)}, u32[]{:S(2)}, u32[]{:S(2)}) %collective-permute-start.15) | collective-permute-done | bytes 393248 | tf_op jit(solution)/shard_map/ppermute | solution.py:26
  111.6 9.2 %collective-permute-done.16 = bf16[48,2048]{1,0:T(8,128)(2,1)S(1)} collective-permute-done((bf16[48,2048]{1,0:T(8,128)(2,1)S(1)}, bf16[48,2048]{1,0:T(8,128)(2,1)S(1)}, u32[]{:S(2)}, u32[]{:S(2)}) %collective-permute-start.16) | collective-permute-done | bytes 196640 | tf_op jit(solution)/shard_map/ppermute | solution.py:26
  126.4 11.4 %shard_map.86 = (f32[2,64,3584]{2,1,0:T(8,128)S(1)}, bf16[2,64,3584]{2,1,0:T(8,128)(2,1)S(1)}) custom-call(bf16[2,2,2,32,1024]{4,3,2,1,0:T(8,128)(2,1)S(1)} %multiply_convert_fusion.2.x_ref, bf16[1,2048,3584]{2,1,0:T(8,128)(2,1)} %gate_ref.7, bf16[1,2048,3584]{2,1,0:T(8,128)(2,1)} %up_ref.7, f32[96,2048]{1,0:T(8,128)S(1)} %get-tuple-element.86.refs_0_, ...), custom_call_target="tpu_custom_call" | custom-call | flops 1 | bytes 1 | tf_op jit(solution)/shard_map/pallas_call | solution.py:131
  141.4 6.3 %shard_map.87 = (f32[96,2048]{1,0:T(8,128)S(1)}, bf16[96,2048]{1,0:T(8,128)(2,1)S(1)}) custom-call(s32[1]{0:T(128)} %bitcast.rank_ref, bf16[96,3584]{1,0:T(8,128)(2,1)S(1)} %fusion.1.refs_2_.refs_0_, bf16[96,3584]{1,0:T(8,128)(2,1)S(1)} %collective-permute-done.19.refs_1_, bf16[1,3584,2048]{2,1,0:T(8,128)(2,1)} %refs_2_.5, f32[2,64,3584]{2,1,0:T(8,128)} %copy-done.4, ...), custom_call_target="tpu_custom_call" | custom-call | flops 1 | bytes 1 | tf_op jit(solution)/shard_map/pallas_call | solution.py:179
  150.2 7.8 %shard_map.88 = (f32[96,4096]{1,0:T(8,128)}, bf16[96,4096]{1,0:T(8,128)(2,1)S(1)}) custom-call(s32[1]{0:T(128)} %bitcast.rank_ref, bf16[96,2048]{1,0:T(8,128)(2,1)S(1)} %constant_dynamic-update-slice_fusion.refs_4_.near_ref, bf16[96,2048]{1,0:T(8,128)(2,1)S(1)} %collective-permute-done.20.far_ref, bf16[1,2048,4096]{2,1,0:T(8,128)(2,1)} %weight_ref.5, ...), custom_call_target="tpu_custom_call" | custom-call | flops 1 | bytes 1 | tf_op jit(solution)/shard_map/pallas_call | solution.py:224
  163.2 6.9 %collective-permute-done.25 = bf16[48,2048]{1,0:T(8,128)(2,1)S(1)} collective-permute-done((bf16[48,2048]{1,0:T(8,128)(2,1)S(1)}, bf16[48,2048]{1,0:T(8,128)(2,1)S(1)}, u32[]{:S(2)}, u32[]{:S(2)}) %collective-permute-start.25) | collective-permute-done | bytes 196640 | tf_op jit(solution)/shard_map/ppermute | solution.py:26
  172.4 6.1 %shard_map.89 = (f32[64,2048]{1,0:T(8,128)S(1)}, bf16[64,2048]{1,0:T(8,128)(2,1)S(1)}) custom-call(s32[1]{0:T(128)} %bitcast.rank_ref, bf16[64,3584]{1,0:T(8,128)(2,1)S(1)} %fusion.3.refs_0_.refs_4_, bf16[64,3584]{1,0:T(8,128)(2,1)S(1)} %collective-permute-done.23.refs_1_, bf16[1,3584,2048]{2,1,0:T(8,128)(2,1)} %refs_2_.5, ...), custom_call_target="tpu_custom_call" | custom-call | flops 1 | bytes 1 | tf_op jit(solution)/shard_map/pallas_call | solution.py:179
  185.6 5.5 %collective-permute-done.30 = bf16[32,2048]{1,0:T(8,128)(2,1)S(1)} collective-permute-done((bf16[32,2048]{1,0:T(8,128)(2,1)S(1)}, bf16[32,2048]{1,0:T(8,128)(2,1)S(1)}, u32[]{:S(2)}, u32[]{:S(2)}) %collective-permute-start.30) | collective-permute-done | bytes 131104 | tf_op jit(solution)/shard_map/ppermute | solution.py:26
  198.9 4.2 %collective-permute-done.28.far_ref = bf16[96,2048]{1,0:T(8,128)(2,1)S(1)} collective-permute-done((bf16[96,2048]{1,0:T(8,128)(2,1)S(1)}, bf16[96,2048]{1,0:T(8,128)(2,1)S(1)}, u32[]{:S(2)}, u32[]{:S(2)}) %collective-permute-start.28) | collective-permute-done | bytes 393248 | tf_op jit(solution)/shard_map/ppermute | solution.py:26
  203.1 7.8 %shard_map.90 = (f32[96,4096]{1,0:T(8,128)}, bf16[96,4096]{1,0:T(8,128)(2,1)S(1)}) custom-call(s32[1]{0:T(128)} %bitcast.rank_ref, bf16[96,2048]{1,0:T(8,128)(2,1)S(1)} %constant_dynamic-update-slice_fusion.2.near_ref.refs_3_, bf16[96,2048]{1,0:T(8,128)(2,1)S(1)} %collective-permute-done.28.far_ref, bf16[1,2048,4096]{2,1,0:T(8,128)(2,1)} %weight_ref.5, ...), custom_call_target="tpu_custom_call" | custom-call | flops 1 | bytes 1 | tf_op jit(solution)/shard_map/pallas_call | solution.py:224
  211.1 6.7 %shard_map.91 = (f32[64,4096]{1,0:T(8,128)S(1)}, bf16[64,4096]{1,0:T(8,128)(2,1)S(1)}) custom-call(s32[1]{0:T(128)} %bitcast.rank_ref, bf16[64,2048]{1,0:T(8,128)(2,1)S(1)} %get-tuple-element.153.near_ref, bf16[64,2048]{1,0:T(8,128)(2,1)S(1)} %get-tuple-element.154.far_ref, bf16[1,2048,4096]{2,1,0:T(8,128)(2,1)} %weight_ref.5, ...), custom_call_target="tpu_custom_call" | custom-call | flops 1 | bytes 1 | tf_op jit(solution)/shard_map/pallas_call | solution.py:224
  223.6 5.6 %collective-permute-done.38 = bf16[32,4096]{1,0:T(8,128)(2,1)S(1)} collective-permute-done((bf16[32,4096]{1,0:T(8,128)(2,1)S(1)}, bf16[32,4096]{1,0:T(8,128)(2,1)S(1)}, u32[]{:S(2)}, u32[]{:S(2)}) %collective-permute-start.38) | collective-permute-done | bytes 262176 | tf_op jit(solution)/shard_map/ppermute | solution.py:22
  229.3 7.8 %collective-permute-done.36 = bf16[48,4096]{1,0:T(8,128)(2,1)S(1)} collective-permute-done((bf16[48,4096]{1,0:T(8,128)(2,1)S(1)}, bf16[48,4096]{1,0:T(8,128)(2,1)S(1)}, u32[]{:S(2)}, u32[]{:S(2)}) %collective-permute-start.36) | collective-permute-done | bytes 393248 | tf_op jit(solution)/shard_map/ppermute | solution.py:22
  (148 shorter events, 69.0 us)
Async XLA Ops:
  24.3 19.1 %collective-permute-start.9 = (bf16[1,80,1024]{2,1,0:T(8,128)(2,1)S(1)}, bf16[1,80,1024]{2,1,0:T(8,128)(2,1)S(1)}, u32[]{:S(2)}, u32[]{:S(2)}) collective-permute-start(bf16[1,80,1024]{2,1,0:T(8,128)(2,1)S(1)} %dynamic-slice_bitcast_fusion), channel_id=1, source_target_pairs={{0,8},{4,12},{8,0},{12,4},{1,9},{5,13},{9,1},{13,5},{2,10},{6,14},... | collective-permute-start | bytes 491528 | tf_op jit(solution)/shard_map/ppermute | solution.py:26
  35.6 18.4 %collective-permute-start.6 = (bf16[2,96,1792]{2,1,0:T(8,128)(2,1)S(1)}, bf16[2,96,1792]{2,1,0:T(8,128)(2,1)S(1)}, u32[]{:S(2)}, u32[]{:S(2)}) collective-permute-start(bf16[2,96,1792]{2,1,0:T(8,128)(2,1)S(1)} %get-tuple-element.72), channel_id=1, source_target_pairs={{0,2},{2,0},{1,3},{3,1},{4,6},{6,4},{5,7},{7,5},{8,10},{10,8},{9,1... | collective-permute-start | bytes 2064392 | tf_op jit(solution)/shard_map/ppermute | solution.py:22
  44.9 23.8 %collective-permute-start.7 = (bf16[2,96,1792]{2,1,0:T(8,128)(2,1)S(1)}, bf16[2,96,1792]{2,1,0:T(8,128)(2,1)S(1)}, u32[]{:S(2)}, u32[]{:S(2)}) collective-permute-start(bf16[2,96,1792]{2,1,0:T(8,128)(2,1)S(1)} %get-tuple-element.74), channel_id=1, source_target_pairs={{0,2},{2,0},{1,3},{3,1},{4,6},{6,4},{5,7},{7,5},{8,10},{10,8},{9,1... | collective-permute-start | bytes 2064392 | tf_op jit(solution)/shard_map/ppermute | solution.py:22
  54.5 14.4 %collective-permute-start.12 = (f32[80]{0:T(128)S(1)}, f32[80]{0:T(128)S(1)}, u32[]{:S(2)}, u32[]{:S(2)}) collective-permute-start(f32[80]{0:T(128)S(1)} %get-tuple-element.150), channel_id=1, source_target_pairs={{2,0},{0,2},{3,1},{1,3},{6,4},{4,6},{7,5},{5,7},{10,8},{8,10},{11,... | collective-permute-start | bytes 968 | tf_op jit(solution)/shard_map/ppermute | solution.py:18
  55.2 19.3 %collective-permute-start.11 = (bf16[2,80,1024]{2,1,0:T(8,128)(2,1)S(1)}, bf16[2,80,1024]{2,1,0:T(8,128)(2,1)S(1)}, u32[]{:S(2)}, u32[]{:S(2)}) collective-permute-start(bf16[2,80,1024]{2,1,0:T(8,128)(2,1)S(1)} %pad_maximum_fusion.9), channel_id=1, source_target_pairs={{2,0},{0,2},{3,1},{1,3},{6,4},{4,6},{7,5},{5,7},{10,8},{8,10},{11,... | collective-permute-start | bytes 983048 | tf_op jit(solution)/shard_map/ppermute | solution.py:18
  74.9 17.9 %collective-permute-start.8 = (bf16[96,3584]{1,0:T(8,128)(2,1)S(1)}, bf16[96,3584]{1,0:T(8,128)(2,1)S(1)}, u32[]{:S(2)}, u32[]{:S(2)}) collective-permute-start(bf16[96,3584]{1,0:T(8,128)(2,1)S(1)} %pad_maximum_fusion.1.refs_1_.refs_0_), channel_id=1, source_target_pairs={{2,0},{0,2},{3,1},{1,3},{6,4},{4,6},{7,5},{5,7},{10,8},{8,10},{11,... | collective-permute-start | bytes 2064392 | tf_op jit(solution)/shard_map/ppermute | solution.py:18
  90.3 32.2 %collective-permute-start.18 = (bf16[2,96,3584]{2,1,0:T(8,128)(2,1)S(1)}, bf16[2,96,3584]{2,1,0:T(8,128)(2,1)S(1)}, u32[]{:S(2)}, u32[]{:S(2)}) collective-permute-start(bf16[2,96,3584]{2,1,0:T(8,128)(2,1)S(1)} %get-tuple-element.90), channel_id=1, source_target_pairs={{0,2},{2,0},{1,3},{3,1},{4,6},{6,4},{5,7},{7,5},{8,10},{10,8},{9,1... | collective-permute-start | bytes 4128776 | tf_op jit(solution)/shard_map/ppermute | solution.py:22
  99.1 10.8 %collective-permute-start.15 = (bf16[96,2048]{1,0:T(8,128)(2,1)S(1)}, bf16[96,2048]{1,0:T(8,128)(2,1)S(1)}, u32[]{:S(2)}, u32[]{:S(2)}) collective-permute-start(bf16[96,2048]{1,0:T(8,128)(2,1)S(1)} %get-tuple-element.85), channel_id=1, source_target_pairs={{0,4},{4,0},{8,12},{12,8},{1,5},{5,1},{9,13},{13,9},{2,6},{6,2},{1... | collective-permute-start | bytes 1179656 | tf_op jit(solution)/shard_map/ppermute | solution.py:26
  110.0 10.8 %collective-permute-start.16 = (bf16[48,2048]{1,0:T(8,128)(2,1)S(1)}, bf16[48,2048]{1,0:T(8,128)(2,1)S(1)}, u32[]{:S(2)}, u32[]{:S(2)}) collective-permute-start(bf16[48,2048]{1,0:T(8,128)(2,1)S(1)} %slice.227.refs_1_), channel_id=1, source_target_pairs={{0,8},{4,12},{8,0},{12,4},{1,9},{5,13},{9,1},{13,5},{2,10},{6,14},... | collective-permute-start | bytes 589832 | tf_op jit(solution)/shard_map/ppermute | solution.py:26
  123.1 16.7 %collective-permute-start.19 = (bf16[96,3584]{1,0:T(8,128)(2,1)S(1)}, bf16[96,3584]{1,0:T(8,128)(2,1)S(1)}, u32[]{:S(2)}, u32[]{:S(2)}) collective-permute-start(bf16[96,3584]{1,0:T(8,128)(2,1)S(1)} %fusion.1.refs_2_.refs_0_), channel_id=1, source_target_pairs={{2,0},{0,2},{3,1},{1,3},{6,4},{4,6},{7,5},{5,7},{10,8},{8,10},{11,... | collective-permute-start | bytes 2064392 | tf_op jit(solution)/shard_map/ppermute | solution.py:18
  124.7 14.9 %collective-permute-start.17 = (bf16[48,2048]{1,0:T(8,128)(2,1)S(1)}, bf16[48,2048]{1,0:T(8,128)(2,1)S(1)}, u32[]{:S(2)}, u32[]{:S(2)}) collective-permute-start(bf16[48,2048]{1,0:T(8,128)(2,1)S(1)} %add_convert_fusion.1.refs_3_), channel_id=1, source_target_pairs={{0,8},{4,12},{8,0},{12,4},{1,9},{5,13},{9,1},{13,5},{2,10},{6,14},... | collective-permute-start | bytes 589832 | tf_op jit(solution)/shard_map/ppermute | solution.py:26
  139.0 21.1 %collective-permute-start.22 = (bf16[2,64,3584]{2,1,0:T(8,128)(2,1)S(1)}, bf16[2,64,3584]{2,1,0:T(8,128)(2,1)S(1)}, u32[]{:S(2)}, u32[]{:S(2)}) collective-permute-start(bf16[2,64,3584]{2,1,0:T(8,128)(2,1)S(1)} %get-tuple-element.99), channel_id=1, source_target_pairs={{0,2},{2,0},{1,3},{3,1},{4,6},{6,4},{5,7},{7,5},{8,10},{10,8},{9,1... | collective-permute-start | bytes 2752520 | tf_op jit(solution)/shard_map/ppermute | solution.py:22
  139.9 10.3 %collective-permute-start.20 = (bf16[96,2048]{1,0:T(8,128)(2,1)S(1)}, bf16[96,2048]{1,0:T(8,128)(2,1)S(1)}, u32[]{:S(2)}, u32[]{:S(2)}) collective-permute-start(bf16[96,2048]{1,0:T(8,128)(2,1)S(1)} %constant_dynamic-update-slice_fusion.refs_4_.near_ref), channel_id=1, source_target_pairs={{0,4},{4,0},{8,12},{12,8},{1,5},{5,1},{9,13},{13,9},{2,6},{6,2},{1... | collective-permute-start | bytes 1179656 | tf_op jit(solution)/shard_map/ppermute | solution.py:26
  147.7 10.4 %collective-permute-start.24 = (bf16[96,2048]{1,0:T(8,128)(2,1)S(1)}, bf16[96,2048]{1,0:T(8,128)(2,1)S(1)}, u32[]{:S(2)}, u32[]{:S(2)}) collective-permute-start(bf16[96,2048]{1,0:T(8,128)(2,1)S(1)} %get-tuple-element.102), channel_id=1, source_target_pairs={{0,4},{4,0},{8,12},{12,8},{1,5},{5,1},{9,13},{13,9},{2,6},{6,2},{1... | collective-permute-start | bytes 1179656 | tf_op jit(solution)/shard_map/ppermute | solution.py:26
  162.3 10.1 %collective-permute-start.23 = (bf16[64,3584]{1,0:T(8,128)(2,1)S(1)}, bf16[64,3584]{1,0:T(8,128)(2,1)S(1)}, u32[]{:S(2)}, u32[]{:S(2)}) collective-permute-start(bf16[64,3584]{1,0:T(8,128)(2,1)S(1)} %fusion.3.refs_0_.refs_4_), channel_id=1, source_target_pairs={{2,0},{0,2},{3,1},{1,3},{6,4},{4,6},{7,5},{5,7},{10,8},{8,10},{11,... | collective-permute-start | bytes 1376264 | tf_op jit(solution)/shard_map/ppermute | solution.py:18
  170.2 10.8 %collective-permute-start.27 = (bf16[48,2048]{1,0:T(8,128)(2,1)S(1)}, bf16[48,2048]{1,0:T(8,128)(2,1)S(1)}, u32[]{:S(2)}, u32[]{:S(2)}) collective-permute-start(bf16[48,2048]{1,0:T(8,128)(2,1)S(1)} %add_convert_fusion.refs_6_), channel_id=1, source_target_pairs={{0,8},{4,12},{8,0},{12,4},{1,9},{5,13},{9,1},{13,5},{2,10},{6,14},... | collective-permute-start | bytes 589832 | tf_op jit(solution)/shard_map/ppermute | solution.py:26
  170.2 22.4 %collective-permute-start.21 = (bf16[96,4096]{1,0:T(8,128)(2,1)S(1)}, bf16[96,4096]{1,0:T(8,128)(2,1)S(1)}, u32[]{:S(2)}, u32[]{:S(2)}) collective-permute-start(bf16[96,4096]{1,0:T(8,128)(2,1)S(1)} %get-tuple-element.98), channel_id=1, source_target_pairs={{0,1},{1,0},{2,3},{3,2},{4,5},{5,4},{6,7},{7,6},{8,9},{9,8},{10,11... | collective-permute-start | bytes 2359304 | tf_op jit(solution)/shard_map/ppermute | solution.py:22
  181.0 11.0 %collective-permute-start.31 = (bf16[32,2048]{1,0:T(8,128)(2,1)S(1)}, bf16[32,2048]{1,0:T(8,128)(2,1)S(1)}, u32[]{:S(2)}, u32[]{:S(2)}) collective-permute-start(bf16[32,2048]{1,0:T(8,128)(2,1)S(1)} %get-tuple-element.147), channel_id=1, source_target_pairs={{0,4},{4,0},{8,12},{12,8},{1,5},{5,1},{9,13},{13,9},{2,6},{6,2},{1... | collective-permute-start | bytes 393224 | tf_op jit(solution)/shard_map/ppermute | solution.py:26
  185.5 17.6 %collective-permute-start.28 = (bf16[96,2048]{1,0:T(8,128)(2,1)S(1)}, bf16[96,2048]{1,0:T(8,128)(2,1)S(1)}, u32[]{:S(2)}, u32[]{:S(2)}) collective-permute-start(bf16[96,2048]{1,0:T(8,128)(2,1)S(1)} %constant_dynamic-update-slice_fusion.2.near_ref.refs_3_), channel_id=1, source_target_pairs={{0,4},{4,0},{8,12},{12,8},{1,5},{5,1},{9,13},{13,9},{2,6},{6,2},{1... | collective-permute-start | bytes 1179656 | tf_op jit(solution)/shard_map/ppermute | solution.py:26
  192.9 10.2 %collective-permute-start.26 = (bf16[48,4096]{1,0:T(8,128)(2,1)S(1)}, bf16[48,4096]{1,0:T(8,128)(2,1)S(1)}, u32[]{:S(2)}, u32[]{:S(2)}) collective-permute-start(bf16[48,4096]{1,0:T(8,128)(2,1)S(1)} %slice.224.refs_1_), channel_id=1, source_target_pairs={{0,2},{2,0},{1,3},{3,1},{4,6},{6,4},{5,7},{7,5},{8,10},{10,8},{9,1... | collective-permute-start | bytes 1179656 | tf_op jit(solution)/shard_map/ppermute | solution.py:22
  194.4 16.5 %collective-permute-start.35 = (bf16[32,2048]{1,0:T(8,128)(2,1)S(1)}, bf16[32,2048]{1,0:T(8,128)(2,1)S(1)}, u32[]{:S(2)}, u32[]{:S(2)}) collective-permute-start(bf16[32,2048]{1,0:T(8,128)(2,1)S(1)} %add_convert_fusion.2.refs_2_), channel_id=1, source_target_pairs={{0,12},{4,8},{8,4},{12,0},{1,13},{5,9},{9,5},{13,1},{2,14},{6,10},... | collective-permute-start | bytes 393224 | tf_op jit(solution)/shard_map/ppermute | solution.py:26
  196.8 14.2 %collective-permute-start.34 = (bf16[32,2048]{1,0:T(8,128)(2,1)S(1)}, bf16[32,2048]{1,0:T(8,128)(2,1)S(1)}, u32[]{:S(2)}, u32[]{:S(2)}) collective-permute-start(bf16[32,2048]{1,0:T(8,128)(2,1)S(1)} %add_convert_fusion.2.refs_2_), channel_id=1, source_target_pairs={{0,8},{4,12},{8,0},{12,4},{1,9},{5,13},{9,1},{13,5},{2,10},{6,14},... | collective-permute-start | bytes 393224 | tf_op jit(solution)/shard_map/ppermute | solution.py:26
  198.4 12.6 %collective-permute-start.33 = (bf16[32,2048]{1,0:T(8,128)(2,1)S(1)}, bf16[32,2048]{1,0:T(8,128)(2,1)S(1)}, u32[]{:S(2)}, u32[]{:S(2)}) collective-permute-start(bf16[32,2048]{1,0:T(8,128)(2,1)S(1)} %add_convert_fusion.2.refs_2_), channel_id=1, source_target_pairs={{0,4},{4,0},{8,12},{12,8},{1,5},{5,1},{9,13},{13,9},{2,6},{6,2},{1... | collective-permute-start | bytes 393224 | tf_op jit(solution)/shard_map/ppermute | solution.py:26
  222.4 14.8 %collective-permute-start.36 = (bf16[48,4096]{1,0:T(8,128)(2,1)S(1)}, bf16[48,4096]{1,0:T(8,128)(2,1)S(1)}, u32[]{:S(2)}, u32[]{:S(2)}) collective-permute-start(bf16[48,4096]{1,0:T(8,128)(2,1)S(1)} %slice.223), channel_id=1, source_target_pairs={{0,2},{2,0},{1,3},{3,1},{4,6},{6,4},{5,7},{7,5},{8,10},{10,8},{9,1... | collective-permute-start | bytes 1179656 | tf_op jit(solution)/shard_map/ppermute | solution.py:22
  (26 other events, 155.6 us)

commit v8 on v7

--- a/solution.py
+++ b/solution.py
@@ -122,14 +122,13 @@
             out_refs[hop][at] = taken.astype(out_refs[hop].dtype)
 
 
-def gate_up(x, gate_weight, up_weight, piece, pieces, after):
+def gate_up(x, gate_weight, up_weight, first, tiles, after):
     members, owners, cuts, q, cut = x.shape
     rows, depth, own_rows = members * owners * q, cuts * cut, members * q
-    width = gate_weight.shape[2] // pieces
-    tile = tile_of(width, 256)
-    tiles = width // tile
+    tile = tile_of(gate_weight.shape[2], 256)
+    width = tiles * tile
     return pl.pallas_call(
-        functools.partial(gate_up_body, tiles, piece * tiles),
+        functools.partial(gate_up_body, tiles, first),
         grid=(tiles,),
         in_specs=[whole(x.shape)] + in_hbm(2) + unread(after),
         out_specs=[pl.BlockSpec((2, own_rows, tile), lambda j: (0, 0, j))] * owners,
@@ -325,10 +324,13 @@
     last = []
 
     def gate_up_of(t):
-        pieces = 2 if t == 0 and gate_weight.shape[2] % 512 == 0 else 1
+        tiles = gate_weight.shape[2] // tile_of(gate_weight.shape[2], 256)
+        early = tiles * 5 // 14 if t == 0 and chunks > 1 else 0
         sums[t] = []
-        for piece in range(pieces):
-            own, *sends = gate_up(xs[t], gate_weight, up_weight, piece, pieces, list(last))
+        for first, count in ((0, early), (early, tiles - early)):
+            if not count:
+                continue
+            own, *sends = gate_up(xs[t], gate_weight, up_weight, first, count, list(last))
             last[:] = [own]
             others = [send(sends[hop - 1], "rows", owners, hop) for hop in range(1, owners)]
             sums[t].append((own, others))
@@ -337,7 +339,8 @@
         gathered = jnp.concatenate(after(rest, sums[0][-1][0]))
         for bit in bits[1:]:
             gathered = doubled(after(gathered, sums[0][-1][0]), bit)
-        columns, inverse = from_owners(after(gathered, units))
+        gathered = after(gathered, units)
+        columns, inverse = from_owners(gathered)
         inverses = from_all(inverse, "rows", owners)
         columns, inverses = after((columns, inverses), (columns, inverses))
         columns, inverses = from_members(columns), from_all(inverses, "mp", members)
@@ -353,7 +356,7 @@
             for other in others:
                 acts = acts + other.astype(F32)
             units.append((jax.nn.silu(acts[0]) * acts[1]).astype(BF16))
-            if t == 0 and rest is not None and len(units) == 1:
+            if t == 0 and chunks > 1 and len(units) == 1:
                 rest_of(units[0])
         units = jnp.concatenate(units, axis=1)
         hidden[t] = [units] + [shift(units, "rows", owners, hop) for hop in range(1, owners)]
@@ -383,6 +386,8 @@
         if at_once(t):
             return
         total, arrived = ordered(layer[t])
+        if chunks > 1 and t == chunks - 2:
+            total, arrived = after((total, arrived), hidden[t + 1][0])
         for bit in reversed(bits[:-1]):
             total = total + arrived.astype(F32)
             kept = total.shape[0] // 2
@@ -419,7 +424,7 @@
     def features_of(t):
         near_far = blocks[t]
         if at_once(t):
-            parts = ordered(near_far) if t else near_far
+            parts = ordered(near_far)
             near_far = (jnp.concatenate(parts[0::2]), jnp.concatenate(parts[1::2]))
         own, *sends = encode(rank, *near_far, enc_weight, members, order, list(last))
         last[:] = [own]

time: 239 us -> 239 us (level)
  starting transfers between devices: 45.2 us -> 42.4 us
    ppermute x10, waiting for transfers between devices: 31.8 us -> 19.6 us  [send(): lax.ppermute(value, axis, [(d, (d + hop) % size) for d in range(size)])]
    ppermute x11, waiting for transfers between devices: 15 us -> 26.8 us  [shift(): lax.ppermute(value, axis, [((d + hop) % size, d) for d in range(size)])]
    ppermute x10, starting transfers between devices: 9.56 us -> 6.66 us  [send(): lax.ppermute(value, axis, [(d, (d + hop) % size) for d in range(size)])]
    ppermute x18, waiting for transfers between devices: 57.5 us -> 60.1 us  [swap(): return lax.ppermute(value, axis, [(d, d ^ bit) for d in range(size)])]
  transfers between devices with their start and end apart: 39 -> 39, of which waited for: 26 -> 25; matrix products, arithmetic and copies ran while one was open for 1% -> 1% of each run, Pallas kernels for 30% -> 30%
where the time goes in v8:
time: 239 us; the launch traced here: 238 us
  waiting for transfers between devices  106 us (44%)
  Pallas kernels  78.7 us (33%)
  starting transfers between devices  42.4 us (18%)
  other arithmetic  5.62 us (2%)
  local copies, waits for them, and re-layouts  4.59 us (2%)
    ppermute x18, waiting for transfers between devices, swap(): return lax.ppermute(value, axis, [(d, d ^ bit) for d in range(size)])  60.1 us
    pallas_call x4, Pallas kernels, gate_up(): pl.pallas_call(functools.partial(gate_up_body, tiles, first), grid=(tiles...  37.5 us
    ppermute x18, starting transfers between devices, swap(): return lax.ppermute(value, axis, [(d, d ^ bit) for d in range(size)])  27.4 us
    ppermute x11, waiting for transfers between devices, shift(): lax.ppermute(value, axis, [((d + hop) % size, d) for d in range(size)])  26.8 us
    pallas_call x3, Pallas kernels, encode(): pl.pallas_call(functools.partial(encode_body, members, order, width // ti...  22.6 us
    ppermute x10, waiting for transfers between devices, send(): lax.ppermute(value, axis, [(d, (d + hop) % size) for d in range(size)])  19.6 us
    pallas_call x3, Pallas kernels, down(): pl.pallas_call(functools.partial(down_body, owners, members, pieces, orde...  18.6 us
    ppermute x11, starting transfers between devices, shift(): lax.ppermute(value, axis, [((d + hop) % size, d) for d in range(size)])  8.34 us
  transfers between devices with their start and end apart: 39, of which 25 were waited for; matrix products, arithmetic and copies ran while one was open for 1% of the time, Pallas kernels for 30%

profile of v8, /device:TPU:0, one launch (start us, length us, event | category | flops | bytes accessed | tf_op | source)
XLA Modules:
  0.0 238.4 jit_solution(10955085987838465729)
XLA Ops:
  1.1 4.1 %collective-permute-start = (bf16[1,48,1024]{2,1,0:T(8,128)(2,1)S(1)}, bf16[1,48,1024]{2,1,0:T(8,128)(2,1)S(1)}, u32[]{:S(2)}, u32[]{:S(2)}) collective-permute-start(bf16[1,48,1024]{2,1,0:T(8,128)(2,1)S(1)} %dynamic-slice_bitcast_fusion.1), channel_id=1, source_target_pairs={{0,8},{4,12},{8,0},{12,4},{1,9},{5,13},{9,1},{13,5},{2,10},{6,14},... | collective-permute-start | bytes 294920 | tf_op jit(solution)/shard_map/ppermute | solution.py:26
  5.1 4.9 %collective-permute-done = bf16[1,48,1024]{2,1,0:T(8,128)(2,1)S(1)} collective-permute-done((bf16[1,48,1024]{2,1,0:T(8,128)(2,1)S(1)}, bf16[1,48,1024]{2,1,0:T(8,128)(2,1)S(1)}, u32[]{:S(2)}, u32[]{:S(2)}) %collective-permute-start) | collective-permute-done | bytes 98336 | tf_op jit(solution)/shard_map/ppermute | solution.py:26
  10.9 5.4 %collective-permute-done.1 = bf16[2,48,1024]{2,1,0:T(8,128)(2,1)S(1)} collective-permute-done((bf16[2,48,1024]{2,1,0:T(8,128)(2,1)S(1)}, bf16[2,48,1024]{2,1,0:T(8,128)(2,1)S(1)}, u32[]{:S(2)}, u32[]{:S(2)}) %collective-permute-start.1) | collective-permute-done | bytes 196640 | tf_op jit(solution)/shard_map/ppermute | solution.py:26
  20.1 3.4 %collective-permute-done.2 = bf16[2,48,1024]{2,1,0:T(8,128)(2,1)S(1)} collective-permute-done((bf16[2,48,1024]{2,1,0:T(8,128)(2,1)S(1)}, bf16[2,48,1024]{2,1,0:T(8,128)(2,1)S(1)}, u32[]{:S(2)}, u32[]{:S(2)}) %collective-permute-start.2) | collective-permute-done | bytes 196640 | tf_op jit(solution)/shard_map/ppermute | solution.py:18
  24.3 3.8 %collective-permute-start.9 = (bf16[1,80,1024]{2,1,0:T(8,128)(2,1)S(1)}, bf16[1,80,1024]{2,1,0:T(8,128)(2,1)S(1)}, u32[]{:S(2)}, u32[]{:S(2)}) collective-permute-start(bf16[1,80,1024]{2,1,0:T(8,128)(2,1)S(1)} %dynamic-slice_bitcast_fusion), channel_id=1, source_target_pairs={{0,8},{4,12},{8,0},{12,4},{1,9},{5,13},{9,1},{13,5},{2,10},{6,14},... | collective-permute-start | bytes 491528 | tf_op jit(solution)/shard_map/ppermute | solution.py:26
  28.3 6.0 %shard_map.82 = (f32[2,96,1280]{2,1,0:T(8,128)S(1)}, bf16[2,96,1280]{2,1,0:T(8,128)(2,1)S(1)}) custom-call(bf16[2,2,2,48,1024]{4,3,2,1,0:T(8,128)(2,1)S(1)} %multiply_convert_fusion.1.x_ref, bf16[1,2048,3584]{2,1,0:T(8,128)(2,1)} %gate_ref.7, bf16[1,2048,3584]{2,1,0:T(8,128)(2,1)} %up_ref.7), custom_call_target="tpu_custom_call" | custom-call | flops 1 | bytes 1 | tf_op jit(solution)/shard_map/pallas_call | solution.py:130
  34.9 8.4 %shard_map.83 = (f32[2,96,2304]{2,1,0:T(8,128)S(1)}, bf16[2,96,2304]{2,1,0:T(8,128)(2,1)S(1)}) custom-call(bf16[2,2,2,48,1024]{4,3,2,1,0:T(8,128)(2,1)S(1)} %multiply_convert_fusion.1.x_ref, bf16[1,2048,3584]{2,1,0:T(8,128)(2,1)} %gate_ref.7, bf16[1,2048,3584]{2,1,0:T(8,128)(2,1)} %up_ref.7, f32[2,96,1280]{2,1,0:T(8,128)S(1)} %get-tuple-element.73.refs_0_), custom_call_target="tpu_custom_call" | custom-call | flops 1 | bytes 1 | tf_op jit(solution)/shard_map/pallas_call | solution.py:130
  46.4 6.2 %collective-permute-done.10 = bf16[2,80,1024]{2,1,0:T(8,128)(2,1)S(1)} collective-permute-done((bf16[2,80,1024]{2,1,0:T(8,128)(2,1)S(1)}, bf16[2,80,1024]{2,1,0:T(8,128)(2,1)S(1)}, u32[]{:S(2)}, u32[]{:S(2)}) %collective-permute-start.10) | collective-permute-done | bytes 327712 | tf_op jit(solution)/shard_map/ppermute | solution.py:26
  55.4 17.9 %collective-permute-done.12 = f32[80]{0:T(128)S(1)} collective-permute-done((f32[80]{0:T(128)S(1)}, f32[80]{0:T(128)S(1)}, u32[]{:S(2)}, u32[]{:S(2)}) %collective-permute-start.12) | collective-permute-done | bytes 352 | tf_op jit(solution)/shard_map/ppermute | solution.py:18
  76.4 11.7 %shard_map.84 = (f32[2,96,3584]{2,1,0:T(8,128)S(1)}, bf16[2,96,3584]{2,1,0:T(8,128)(2,1)S(1)}) custom-call(bf16[2,2,2,48,1024]{4,3,2,1,0:T(8,128)(2,1)S(1)} %multiply_convert_fusion.x_ref, bf16[1,2048,3584]{2,1,0:T(8,128)(2,1)} %gate_ref.7, bf16[1,2048,3584]{2,1,0:T(8,128)(2,1)} %up_ref.7, f32[2,96,2304]{2,1,0:T(8,128)S(1)} %get-tuple-element.75.refs_0_, ...), custom_call_target="tpu_custom_call" | custom-call | flops 1 | bytes 1 | tf_op jit(solution)/shard_map/pallas_call | solution.py:130
  91.9 6.3 %shard_map.85 = (f32[96,2048]{1,0:T(8,128)S(1)}, bf16[96,2048]{1,0:T(8,128)(2,1)S(1)}) custom-call(s32[1]{0:T(128)} %bitcast.rank_ref, bf16[96,3584]{1,0:T(8,128)(2,1)S(1)} %pad_maximum_fusion.1.refs_1_.refs_0_, bf16[96,3584]{1,0:T(8,128)(2,1)S(1)} %collective-permute-done.8.refs_1_, bf16[1,3584,2048]{2,1,0:T(8,128)(2,1)} %refs_2_.5, f32[2,96,3584]{2,1,0:T(8,128)} %copy-done.2), custom_call_target="tpu_custom_call" | custom-call | flops 1 | bytes 1 | tf_op jit(solution)/shard_map/pallas_call | solution.py:178
  99.7 9.3 %collective-permute-done.15 = bf16[96,2048]{1,0:T(8,128)(2,1)S(1)} collective-permute-done((bf16[96,2048]{1,0:T(8,128)(2,1)S(1)}, bf16[96,2048]{1,0:T(8,128)(2,1)S(1)}, u32[]{:S(2)}, u32[]{:S(2)}) %collective-permute-start.15) | collective-permute-done | bytes 393248 | tf_op jit(solution)/shard_map/ppermute | solution.py:26
  110.6 9.2 %collective-permute-done.16 = bf16[48,2048]{1,0:T(8,128)(2,1)S(1)} collective-permute-done((bf16[48,2048]{1,0:T(8,128)(2,1)S(1)}, bf16[48,2048]{1,0:T(8,128)(2,1)S(1)}, u32[]{:S(2)}, u32[]{:S(2)}) %collective-permute-start.16) | collective-permute-done | bytes 196640 | tf_op jit(solution)/shard_map/ppermute | solution.py:26
  125.4 11.4 %shard_map.86 = (f32[2,64,3584]{2,1,0:T(8,128)S(1)}, bf16[2,64,3584]{2,1,0:T(8,128)(2,1)S(1)}) custom-call(bf16[2,2,2,32,1024]{4,3,2,1,0:T(8,128)(2,1)S(1)} %multiply_convert_fusion.2.x_ref, bf16[1,2048,3584]{2,1,0:T(8,128)(2,1)} %gate_ref.7, bf16[1,2048,3584]{2,1,0:T(8,128)(2,1)} %up_ref.7, f32[96,2048]{1,0:T(8,128)S(1)} %get-tuple-element.88.refs_0_, ...), custom_call_target="tpu_custom_call" | custom-call | flops 1 | bytes 1 | tf_op jit(solution)/shard_map/pallas_call | solution.py:130
  140.5 6.3 %shard_map.87 = (f32[96,2048]{1,0:T(8,128)S(1)}, bf16[96,2048]{1,0:T(8,128)(2,1)S(1)}) custom-call(s32[1]{0:T(128)} %bitcast.rank_ref, bf16[96,3584]{1,0:T(8,128)(2,1)S(1)} %fusion.1.refs_2_.refs_0_, bf16[96,3584]{1,0:T(8,128)(2,1)S(1)} %collective-permute-done.19.refs_1_, bf16[1,3584,2048]{2,1,0:T(8,128)(2,1)} %refs_2_.5, f32[2,64,3584]{2,1,0:T(8,128)} %copy-done.4, ...), custom_call_target="tpu_custom_call" | custom-call | flops 1 | bytes 1 | tf_op jit(solution)/shard_map/pallas_call | solution.py:178
  150.2 8.0 %shard_map.88 = (f32[96,4096]{1,0:T(8,128)}, bf16[96,4096]{1,0:T(8,128)(2,1)S(1)}) custom-call(s32[1]{0:T(128)} %bitcast.rank_ref, bf16[96,2048]{1,0:T(8,128)(2,1)S(1)} %constant_dynamic-update-slice_fusion.refs_4_.near_ref, bf16[96,2048]{1,0:T(8,128)(2,1)S(1)} %collective-permute-done.20.far_ref, bf16[1,2048,4096]{2,1,0:T(8,128)(2,1)} %weight_ref.5, ...), custom_call_target="tpu_custom_call" | custom-call | flops 1 | bytes 1 | tf_op jit(solution)/shard_map/pallas_call | solution.py:223
  162.3 7.3 %collective-permute-done.25 = bf16[48,2048]{1,0:T(8,128)(2,1)S(1)} collective-permute-done((bf16[48,2048]{1,0:T(8,128)(2,1)S(1)}, bf16[48,2048]{1,0:T(8,128)(2,1)S(1)}, u32[]{:S(2)}, u32[]{:S(2)}) %collective-permute-start.25) | collective-permute-done | bytes 196640 | tf_op jit(solution)/shard_map/ppermute | solution.py:26
  171.4 6.1 %shard_map.89 = (f32[64,2048]{1,0:T(8,128)S(1)}, bf16[64,2048]{1,0:T(8,128)(2,1)S(1)}) custom-call(s32[1]{0:T(128)} %bitcast.rank_ref, bf16[64,3584]{1,0:T(8,128)(2,1)S(1)} %fusion.3.refs_0_.refs_4_, bf16[64,3584]{1,0:T(8,128)(2,1)S(1)} %collective-permute-done.23.refs_1_, bf16[1,3584,2048]{2,1,0:T(8,128)(2,1)} %refs_2_.5, ...), custom_call_target="tpu_custom_call" | custom-call | flops 1 | bytes 1 | tf_op jit(solution)/shard_map/pallas_call | solution.py:178
  185.0 5.5 %collective-permute-done.30 = bf16[32,2048]{1,0:T(8,128)(2,1)S(1)} collective-permute-done((bf16[32,2048]{1,0:T(8,128)(2,1)S(1)}, bf16[32,2048]{1,0:T(8,128)(2,1)S(1)}, u32[]{:S(2)}, u32[]{:S(2)}) %collective-permute-start.30) | collective-permute-done | bytes 131104 | tf_op jit(solution)/shard_map/ppermute | solution.py:26
  197.8 5.5 %collective-permute-done.28.far_ref = bf16[96,2048]{1,0:T(8,128)(2,1)S(1)} collective-permute-done((bf16[96,2048]{1,0:T(8,128)(2,1)S(1)}, bf16[96,2048]{1,0:T(8,128)(2,1)S(1)}, u32[]{:S(2)}, u32[]{:S(2)}) %collective-permute-start.28) | collective-permute-done | bytes 393248 | tf_op jit(solution)/shard_map/ppermute | solution.py:26
  203.4 7.8 %shard_map.90 = (f32[96,4096]{1,0:T(8,128)}, bf16[96,4096]{1,0:T(8,128)(2,1)S(1)}) custom-call(s32[1]{0:T(128)} %bitcast.rank_ref, bf16[96,2048]{1,0:T(8,128)(2,1)S(1)} %constant_dynamic-update-slice_fusion.2.near_ref.refs_3_, bf16[96,2048]{1,0:T(8,128)(2,1)S(1)} %collective-permute-done.28.far_ref, bf16[1,2048,4096]{2,1,0:T(8,128)(2,1)} %weight_ref.5, ...), custom_call_target="tpu_custom_call" | custom-call | flops 1 | bytes 1 | tf_op jit(solution)/shard_map/pallas_call | solution.py:223
  211.3 6.7 %shard_map.91 = (f32[64,4096]{1,0:T(8,128)S(1)}, bf16[64,4096]{1,0:T(8,128)(2,1)S(1)}) custom-call(s32[1]{0:T(128)} %bitcast.rank_ref, bf16[64,2048]{1,0:T(8,128)(2,1)S(1)} %get-tuple-element.157.near_ref, bf16[64,2048]{1,0:T(8,128)(2,1)S(1)} %get-tuple-element.158.far_ref, bf16[1,2048,4096]{2,1,0:T(8,128)(2,1)} %weight_ref.5, ...), custom_call_target="tpu_custom_call" | custom-call | flops 1 | bytes 1 | tf_op jit(solution)/shard_map/pallas_call | solution.py:223
  222.6 6.8 %collective-permute-done.38 = bf16[32,4096]{1,0:T(8,128)(2,1)S(1)} collective-permute-done((bf16[32,4096]{1,0:T(8,128)(2,1)S(1)}, bf16[32,4096]{1,0:T(8,128)(2,1)S(1)}, u32[]{:S(2)}, u32[]{:S(2)}) %collective-permute-start.38) | collective-permute-done | bytes 262176 | tf_op jit(solution)/shard_map/ppermute | solution.py:22
  229.5 7.5 %collective-permute-done.36 = bf16[48,4096]{1,0:T(8,128)(2,1)S(1)} collective-permute-done((bf16[48,4096]{1,0:T(8,128)(2,1)S(1)}, bf16[48,4096]{1,0:T(8,128)(2,1)S(1)}, u32[]{:S(2)}, u32[]{:S(2)}) %collective-permute-start.36) | collective-permute-done | bytes 393248 | tf_op jit(solution)/shard_map/ppermute | solution.py:22
  (148 shorter events, 62.4 us)
Async XLA Ops:
  24.3 19.1 %collective-permute-start.9 = (bf16[1,80,1024]{2,1,0:T(8,128)(2,1)S(1)}, bf16[1,80,1024]{2,1,0:T(8,128)(2,1)S(1)}, u32[]{:S(2)}, u32[]{:S(2)}) collective-permute-start(bf16[1,80,1024]{2,1,0:T(8,128)(2,1)S(1)} %dynamic-slice_bitcast_fusion), channel_id=1, source_target_pairs={{0,8},{4,12},{8,0},{12,4},{1,9},{5,13},{9,1},{13,5},{2,10},{6,14},... | collective-permute-start | bytes 491528 | tf_op jit(solution)/shard_map/ppermute | solution.py:26
  34.3 18.3 %collective-permute-start.6 = (bf16[2,96,1280]{2,1,0:T(8,128)(2,1)S(1)}, bf16[2,96,1280]{2,1,0:T(8,128)(2,1)S(1)}, u32[]{:S(2)}, u32[]{:S(2)}) collective-permute-start(bf16[2,96,1280]{2,1,0:T(8,128)(2,1)S(1)} %get-tuple-element.74), channel_id=1, source_target_pairs={{0,2},{2,0},{1,3},{3,1},{4,6},{6,4},{5,7},{7,5},{8,10},{10,8},{9,1... | collective-permute-start | bytes 1474568 | tf_op jit(solution)/shard_map/ppermute | solution.py:22
  44.9 28.6 %collective-permute-start.7 = (bf16[2,96,2304]{2,1,0:T(8,128)(2,1)S(1)}, bf16[2,96,2304]{2,1,0:T(8,128)(2,1)S(1)}, u32[]{:S(2)}, u32[]{:S(2)}) collective-permute-start(bf16[2,96,2304]{2,1,0:T(8,128)(2,1)S(1)} %get-tuple-element.76), channel_id=1, source_target_pairs={{0,2},{2,0},{1,3},{3,1},{4,6},{6,4},{5,7},{7,5},{8,10},{10,8},{9,1... | collective-permute-start | bytes 2654216 | tf_op jit(solution)/shard_map/ppermute | solution.py:22
  53.0 20.3 %collective-permute-start.11 = (bf16[2,80,1024]{2,1,0:T(8,128)(2,1)S(1)}, bf16[2,80,1024]{2,1,0:T(8,128)(2,1)S(1)}, u32[]{:S(2)}, u32[]{:S(2)}) collective-permute-start(bf16[2,80,1024]{2,1,0:T(8,128)(2,1)S(1)} %pad_maximum_fusion.9), channel_id=1, source_target_pairs={{2,0},{0,2},{3,1},{1,3},{6,4},{4,6},{7,5},{5,7},{10,8},{8,10},{11,... | collective-permute-start | bytes 983048 | tf_op jit(solution)/shard_map/ppermute | solution.py:18
  54.8 18.5 %collective-permute-start.12 = (f32[80]{0:T(128)S(1)}, f32[80]{0:T(128)S(1)}, u32[]{:S(2)}, u32[]{:S(2)}) collective-permute-start(f32[80]{0:T(128)S(1)} %get-tuple-element.154), channel_id=1, source_target_pairs={{2,0},{0,2},{3,1},{1,3},{6,4},{4,6},{7,5},{5,7},{10,8},{8,10},{11,... | collective-permute-start | bytes 968 | tf_op jit(solution)/shard_map/ppermute | solution.py:18
  74.0 17.9 %collective-permute-start.8 = (bf16[96,3584]{1,0:T(8,128)(2,1)S(1)}, bf16[96,3584]{1,0:T(8,128)(2,1)S(1)}, u32[]{:S(2)}, u32[]{:S(2)}) collective-permute-start(bf16[96,3584]{1,0:T(8,128)(2,1)S(1)} %pad_maximum_fusion.1.refs_1_.refs_0_), channel_id=1, source_target_pairs={{2,0},{0,2},{3,1},{1,3},{6,4},{4,6},{7,5},{5,7},{10,8},{8,10},{11,... | collective-permute-start | bytes 2064392 | tf_op jit(solution)/shard_map/ppermute | solution.py:18
  89.6 32.3 %collective-permute-start.18 = (bf16[2,96,3584]{2,1,0:T(8,128)(2,1)S(1)}, bf16[2,96,3584]{2,1,0:T(8,128)(2,1)S(1)}, u32[]{:S(2)}, u32[]{:S(2)}) collective-permute-start(bf16[2,96,3584]{2,1,0:T(8,128)(2,1)S(1)} %get-tuple-element.92), channel_id=1, source_target_pairs={{0,2},{2,0},{1,3},{3,1},{4,6},{6,4},{5,7},{7,5},{8,10},{10,8},{9,1... | collective-permute-start | bytes 4128776 | tf_op jit(solution)/shard_map/ppermute | solution.py:22
  98.2 10.8 %collective-permute-start.15 = (bf16[96,2048]{1,0:T(8,128)(2,1)S(1)}, bf16[96,2048]{1,0:T(8,128)(2,1)S(1)}, u32[]{:S(2)}, u32[]{:S(2)}) collective-permute-start(bf16[96,2048]{1,0:T(8,128)(2,1)S(1)} %get-tuple-element.87), channel_id=1, source_target_pairs={{0,4},{4,0},{8,12},{12,8},{1,5},{5,1},{9,13},{13,9},{2,6},{6,2},{1... | collective-permute-start | bytes 1179656 | tf_op jit(solution)/shard_map/ppermute | solution.py:26
  109.1 10.8 %collective-permute-start.16 = (bf16[48,2048]{1,0:T(8,128)(2,1)S(1)}, bf16[48,2048]{1,0:T(8,128)(2,1)S(1)}, u32[]{:S(2)}, u32[]{:S(2)}) collective-permute-start(bf16[48,2048]{1,0:T(8,128)(2,1)S(1)} %slice.227.refs_1_), channel_id=1, source_target_pairs={{0,8},{4,12},{8,0},{12,4},{1,9},{5,13},{9,1},{13,5},{2,10},{6,14},... | collective-permute-start | bytes 589832 | tf_op jit(solution)/shard_map/ppermute | solution.py:26
  122.6 16.8 %collective-permute-start.19 = (bf16[96,3584]{1,0:T(8,128)(2,1)S(1)}, bf16[96,3584]{1,0:T(8,128)(2,1)S(1)}, u32[]{:S(2)}, u32[]{:S(2)}) collective-permute-start(bf16[96,3584]{1,0:T(8,128)(2,1)S(1)} %fusion.1.refs_2_.refs_0_), channel_id=1, source_target_pairs={{2,0},{0,2},{3,1},{1,3},{6,4},{4,6},{7,5},{5,7},{10,8},{8,10},{11,... | collective-permute-start | bytes 2064392 | tf_op jit(solution)/shard_map/ppermute | solution.py:18
  123.8 15.2 %collective-permute-start.17 = (bf16[48,2048]{1,0:T(8,128)(2,1)S(1)}, bf16[48,2048]{1,0:T(8,128)(2,1)S(1)}, u32[]{:S(2)}, u32[]{:S(2)}) collective-permute-start(bf16[48,2048]{1,0:T(8,128)(2,1)S(1)} %add_convert_fusion.1.refs_3_), channel_id=1, source_target_pairs={{0,8},{4,12},{8,0},{12,4},{1,9},{5,13},{9,1},{13,5},{2,10},{6,14},... | collective-permute-start | bytes 589832 | tf_op jit(solution)/shard_map/ppermute | solution.py:26
  138.1 21.1 %collective-permute-start.22 = (bf16[2,64,3584]{2,1,0:T(8,128)(2,1)S(1)}, bf16[2,64,3584]{2,1,0:T(8,128)(2,1)S(1)}, u32[]{:S(2)}, u32[]{:S(2)}) collective-permute-start(bf16[2,64,3584]{2,1,0:T(8,128)(2,1)S(1)} %get-tuple-element.101), channel_id=1, source_target_pairs={{0,2},{2,0},{1,3},{3,1},{4,6},{6,4},{5,7},{7,5},{8,10},{10,8},{9,1... | collective-permute-start | bytes 2752520 | tf_op jit(solution)/shard_map/ppermute | solution.py:22
  139.4 10.8 %collective-permute-start.20 = (bf16[96,2048]{1,0:T(8,128)(2,1)S(1)}, bf16[96,2048]{1,0:T(8,128)(2,1)S(1)}, u32[]{:S(2)}, u32[]{:S(2)}) collective-permute-start(bf16[96,2048]{1,0:T(8,128)(2,1)S(1)} %constant_dynamic-update-slice_fusion.refs_4_.near_ref), channel_id=1, source_target_pairs={{0,4},{4,0},{8,12},{12,8},{1,5},{5,1},{9,13},{13,9},{2,6},{6,2},{1... | collective-permute-start | bytes 1179656 | tf_op jit(solution)/shard_map/ppermute | solution.py:26
  146.8 11.4 %collective-permute-start.24 = (bf16[96,2048]{1,0:T(8,128)(2,1)S(1)}, bf16[96,2048]{1,0:T(8,128)(2,1)S(1)}, u32[]{:S(2)}, u32[]{:S(2)}) collective-permute-start(bf16[96,2048]{1,0:T(8,128)(2,1)S(1)} %get-tuple-element.104), channel_id=1, source_target_pairs={{0,4},{4,0},{8,12},{12,8},{1,5},{5,1},{9,13},{13,9},{2,6},{6,2},{1... | collective-permute-start | bytes 1179656 | tf_op jit(solution)/shard_map/ppermute | solution.py:26
  161.3 10.1 %collective-permute-start.23 = (bf16[64,3584]{1,0:T(8,128)(2,1)S(1)}, bf16[64,3584]{1,0:T(8,128)(2,1)S(1)}, u32[]{:S(2)}, u32[]{:S(2)}) collective-permute-start(bf16[64,3584]{1,0:T(8,128)(2,1)S(1)} %fusion.3.refs_0_.refs_4_), channel_id=1, source_target_pairs={{2,0},{0,2},{3,1},{1,3},{6,4},{4,6},{7,5},{5,7},{10,8},{8,10},{11,... | collective-permute-start | bytes 1376264 | tf_op jit(solution)/shard_map/ppermute | solution.py:18
  169.6 10.8 %collective-permute-start.27 = (bf16[48,2048]{1,0:T(8,128)(2,1)S(1)}, bf16[48,2048]{1,0:T(8,128)(2,1)S(1)}, u32[]{:S(2)}, u32[]{:S(2)}) collective-permute-start(bf16[48,2048]{1,0:T(8,128)(2,1)S(1)} %add_convert_fusion.refs_6_), channel_id=1, source_target_pairs={{0,8},{4,12},{8,0},{12,4},{1,9},{5,13},{9,1},{13,5},{2,10},{6,14},... | collective-permute-start | bytes 589832 | tf_op jit(solution)/shard_map/ppermute | solution.py:26
  169.7 22.4 %collective-permute-start.21 = (bf16[96,4096]{1,0:T(8,128)(2,1)S(1)}, bf16[96,4096]{1,0:T(8,128)(2,1)S(1)}, u32[]{:S(2)}, u32[]{:S(2)}) collective-permute-start(bf16[96,4096]{1,0:T(8,128)(2,1)S(1)} %get-tuple-element.100), channel_id=1, source_target_pairs={{0,1},{1,0},{2,3},{3,2},{4,5},{5,4},{6,7},{7,6},{8,9},{9,8},{10,11... | collective-permute-start | bytes 2359304 | tf_op jit(solution)/shard_map/ppermute | solution.py:22
  180.5 11.0 %collective-permute-start.31 = (bf16[32,2048]{1,0:T(8,128)(2,1)S(1)}, bf16[32,2048]{1,0:T(8,128)(2,1)S(1)}, u32[]{:S(2)}, u32[]{:S(2)}) collective-permute-start(bf16[32,2048]{1,0:T(8,128)(2,1)S(1)} %get-tuple-element.151), channel_id=1, source_target_pairs={{0,4},{4,0},{8,12},{12,8},{1,5},{5,1},{9,13},{13,9},{2,6},{6,2},{1... | collective-permute-start | bytes 393224 | tf_op jit(solution)/shard_map/ppermute | solution.py:26
  185.0 18.4 %collective-permute-start.28 = (bf16[96,2048]{1,0:T(8,128)(2,1)S(1)}, bf16[96,2048]{1,0:T(8,128)(2,1)S(1)}, u32[]{:S(2)}, u32[]{:S(2)}) collective-permute-start(bf16[96,2048]{1,0:T(8,128)(2,1)S(1)} %constant_dynamic-update-slice_fusion.2.near_ref.refs_3_), channel_id=1, source_target_pairs={{0,4},{4,0},{8,12},{12,8},{1,5},{5,1},{9,13},{13,9},{2,6},{6,2},{1... | collective-permute-start | bytes 1179656 | tf_op jit(solution)/shard_map/ppermute | solution.py:26
  192.4 11.0 %collective-permute-start.26 = (bf16[48,4096]{1,0:T(8,128)(2,1)S(1)}, bf16[48,4096]{1,0:T(8,128)(2,1)S(1)}, u32[]{:S(2)}, u32[]{:S(2)}) collective-permute-start(bf16[48,4096]{1,0:T(8,128)(2,1)S(1)} %slice.224.refs_1_), channel_id=1, source_target_pairs={{0,2},{2,0},{1,3},{3,1},{4,6},{6,4},{5,7},{7,5},{8,10},{10,8},{9,1... | collective-permute-start | bytes 1179656 | tf_op jit(solution)/shard_map/ppermute | solution.py:22
  193.4 17.8 %collective-permute-start.35 = (bf16[32,2048]{1,0:T(8,128)(2,1)S(1)}, bf16[32,2048]{1,0:T(8,128)(2,1)S(1)}, u32[]{:S(2)}, u32[]{:S(2)}) collective-permute-start(bf16[32,2048]{1,0:T(8,128)(2,1)S(1)} %add_convert_fusion.2.refs_2_), channel_id=1, source_target_pairs={{0,12},{4,8},{8,4},{12,0},{1,13},{5,9},{9,5},{13,1},{2,14},{6,10},... | collective-permute-start | bytes 393224 | tf_op jit(solution)/shard_map/ppermute | solution.py:26
  195.6 15.6 %collective-permute-start.34 = (bf16[32,2048]{1,0:T(8,128)(2,1)S(1)}, bf16[32,2048]{1,0:T(8,128)(2,1)S(1)}, u32[]{:S(2)}, u32[]{:S(2)}) collective-permute-start(bf16[32,2048]{1,0:T(8,128)(2,1)S(1)} %add_convert_fusion.2.refs_2_), channel_id=1, source_target_pairs={{0,8},{4,12},{8,0},{12,4},{1,9},{5,13},{9,1},{13,5},{2,10},{6,14},... | collective-permute-start | bytes 393224 | tf_op jit(solution)/shard_map/ppermute | solution.py:26
  197.1 14.1 %collective-permute-start.33 = (bf16[32,2048]{1,0:T(8,128)(2,1)S(1)}, bf16[32,2048]{1,0:T(8,128)(2,1)S(1)}, u32[]{:S(2)}, u32[]{:S(2)}) collective-permute-start(bf16[32,2048]{1,0:T(8,128)(2,1)S(1)} %add_convert_fusion.2.refs_2_), channel_id=1, source_target_pairs={{0,4},{4,0},{8,12},{12,8},{1,5},{5,1},{9,13},{13,9},{2,6},{6,2},{1... | collective-permute-start | bytes 393224 | tf_op jit(solution)/shard_map/ppermute | solution.py:26
  221.7 15.3 %collective-permute-start.36 = (bf16[48,4096]{1,0:T(8,128)(2,1)S(1)}, bf16[48,4096]{1,0:T(8,128)(2,1)S(1)}, u32[]{:S(2)}, u32[]{:S(2)}) collective-permute-start(bf16[48,4096]{1,0:T(8,128)(2,1)S(1)} %slice.223), channel_id=1, source_target_pairs={{0,2},{2,0},{1,3},{3,1},{4,6},{6,4},{5,7},{7,5},{8,10},{10,8},{9,1... | collective-permute-start | bytes 1179656 | tf_op jit(solution)/shard_map/ppermute | solution.py:22
  (26 other events, 159.7 us)

commit v9 on v8

--- a/solution.py
+++ b/solution.py
@@ -11,7 +11,7 @@
 F32 = jnp.float32
 VMEM_BYTES = 51 * 1024 * 1024
 GATE_UP_VMEM_BYTES = 44 * 1024 * 1024
-BUFFERS = 4
+BUFFERS = 3
 
 
 def shift(value, axis, size, hop):
@@ -132,7 +132,7 @@
         grid=(tiles,),
         in_specs=[whole(x.shape)] + in_hbm(2) + unread(after),
         out_specs=[pl.BlockSpec((2, own_rows, tile), lambda j: (0, 0, j))] * owners,
-        out_shape=[jax.ShapeDtypeStruct((2, own_rows, width), F32)]
+        out_shape=[pltpu.HBM((2, own_rows, width), F32)]
         + [jax.ShapeDtypeStruct((2, own_rows, width), BF16)] * (owners - 1),
         scratch_shapes=[pltpu.VMEM((rows, depth), BF16)] + slots(depth, tile, tiles) * 2,
         compiler_params=params(GATE_UP_VMEM_BYTES),
@@ -464,7 +464,10 @@
     for stage, t in stages:
         if t < chunks:
             stage(t)
-    return jnp.concatenate([outs[t] for t in range(chunks)], axis=0)
+    gated = jnp.zeros(adjoint.shape, BF16)
+    for t in range(chunks):
+        gated = lax.dynamic_update_slice(gated, outs[t], (starts[t], 0))
+    return gated
 
 
 def solution(mesh):

time: 239 us -> 246 us (1.029)
  Pallas kernels: 78.7 us -> 90.8 us
  waiting for transfers between devices: 106 us -> 102 us
    pallas_call x4, Pallas kernels: 37.5 us -> 45.3 us  [gate_up(): pl.pallas_call(functools.partial(gate_up_body, tiles, first), grid=(tiles...]
  transfers between devices with their start and end apart: 39 -> 39, of which waited for: 25 -> 21; matrix products, arithmetic and copies ran while one was open for 1% -> 1% of each run, Pallas kernels for 30% -> 37%
where the time goes in v9:
time: 246 us; the launch traced here: 245 us
  waiting for transfers between devices  102 us (41%)
  Pallas kernels  90.8 us (37%)
  starting transfers between devices  44.1 us (18%)
  other arithmetic  5.38 us (2%)
  local copies, waits for them, and re-layouts  2.83 us (1%)
    ppermute x18, waiting for transfers between devices, swap(): return lax.ppermute(value, axis, [(d, d ^ bit) for d in range(size)])  58.3 us
    pallas_call x4, Pallas kernels, gate_up(): pl.pallas_call(functools.partial(gate_up_body, tiles, first), grid=(tiles...  45.3 us
    ppermute x18, starting transfers between devices, swap(): return lax.ppermute(value, axis, [(d, d ^ bit) for d in range(size)])  26.6 us
    ppermute x11, waiting for transfers between devices, shift(): lax.ppermute(value, axis, [((d + hop) % size, d) for d in range(size)])  24.7 us
    pallas_call x3, Pallas kernels, encode(): pl.pallas_call(functools.partial(encode_body, members, order, width // ti...  24.5 us
    pallas_call x3, Pallas kernels, down(): pl.pallas_call(functools.partial(down_body, owners, members, pieces, orde...  21.1 us
    ppermute x10, waiting for transfers between devices, send(): lax.ppermute(value, axis, [(d, (d + hop) % size) for d in range(size)])  18.8 us
    ppermute x11, starting transfers between devices, shift(): lax.ppermute(value, axis, [((d + hop) % size, d) for d in range(size)])  8.9 us
  transfers between devices with their start and end apart: 39, of which 21 were waited for; matrix products, arithmetic and copies ran while one was open for 1% of the time, Pallas kernels for 37%

profile of v9, /device:TPU:0, one launch (start us, length us, event | category | flops | bytes accessed | tf_op | source)
XLA Modules:
  0.0 245.4 jit_solution(1520546339061633542)
XLA Ops:
  1.1 4.1 %collective-permute-start = (bf16[1,48,1024]{2,1,0:T(8,128)(2,1)S(1)}, bf16[1,48,1024]{2,1,0:T(8,128)(2,1)S(1)}, u32[]{:S(2)}, u32[]{:S(2)}) collective-permute-start(bf16[1,48,1024]{2,1,0:T(8,128)(2,1)S(1)} %dynamic-slice_bitcast_fusion.1), channel_id=1, source_target_pairs={{0,8},{4,12},{8,0},{12,4},{1,9},{5,13},{9,1},{13,5},{2,10},{6,14},... | collective-permute-start | bytes 294920 | tf_op jit(solution)/shard_map/ppermute | solution.py:26
  5.1 4.9 %collective-permute-done = bf16[1,48,1024]{2,1,0:T(8,128)(2,1)S(1)} collective-permute-done((bf16[1,48,1024]{2,1,0:T(8,128)(2,1)S(1)}, bf16[1,48,1024]{2,1,0:T(8,128)(2,1)S(1)}, u32[]{:S(2)}, u32[]{:S(2)}) %collective-permute-start) | collective-permute-done | bytes 98336 | tf_op jit(solution)/shard_map/ppermute | solution.py:26
  10.9 5.4 %collective-permute-done.1 = bf16[2,48,1024]{2,1,0:T(8,128)(2,1)S(1)} collective-permute-done((bf16[2,48,1024]{2,1,0:T(8,128)(2,1)S(1)}, bf16[2,48,1024]{2,1,0:T(8,128)(2,1)S(1)}, u32[]{:S(2)}, u32[]{:S(2)}) %collective-permute-start.1) | collective-permute-done | bytes 196640 | tf_op jit(solution)/shard_map/ppermute | solution.py:26
  20.1 3.4 %collective-permute-done.2 = bf16[2,48,1024]{2,1,0:T(8,128)(2,1)S(1)} collective-permute-done((bf16[2,48,1024]{2,1,0:T(8,128)(2,1)S(1)}, bf16[2,48,1024]{2,1,0:T(8,128)(2,1)S(1)}, u32[]{:S(2)}, u32[]{:S(2)}) %collective-permute-start.2) | collective-permute-done | bytes 196640 | tf_op jit(solution)/shard_map/ppermute | solution.py:18
  24.3 3.8 %collective-permute-start.9 = (bf16[1,80,1024]{2,1,0:T(8,128)(2,1)S(1)}, bf16[1,80,1024]{2,1,0:T(8,128)(2,1)S(1)}, u32[]{:S(2)}, u32[]{:S(2)}) collective-permute-start(bf16[1,80,1024]{2,1,0:T(8,128)(2,1)S(1)} %dynamic-slice_bitcast_fusion), channel_id=1, source_target_pairs={{0,8},{4,12},{8,0},{12,4},{1,9},{5,13},{9,1},{13,5},{2,10},{6,14},... | collective-permute-start | bytes 491528 | tf_op jit(solution)/shard_map/ppermute | solution.py:26
  28.3 7.1 %shard_map.82 = (f32[2,96,1280]{2,1,0:T(8,128)}, bf16[2,96,1280]{2,1,0:T(8,128)(2,1)S(1)}) custom-call(bf16[2,2,2,48,1024]{4,3,2,1,0:T(8,128)(2,1)S(1)} %multiply_convert_fusion.1.x_ref, bf16[1,2048,3584]{2,1,0:T(8,128)(2,1)} %gate_ref.7, bf16[1,2048,3584]{2,1,0:T(8,128)(2,1)} %up_ref.7), custom_call_target="tpu_custom_call" | custom-call | flops 1 | bytes 1 | tf_op jit(solution)/shard_map/pallas_call | solution.py:130
  37.3 10.2 %shard_map.83 = (f32[2,96,2304]{2,1,0:T(8,128)}, bf16[2,96,2304]{2,1,0:T(8,128)(2,1)S(1)}) custom-call(bf16[2,2,2,48,1024]{4,3,2,1,0:T(8,128)(2,1)S(1)} %multiply_convert_fusion.1.x_ref, bf16[1,2048,3584]{2,1,0:T(8,128)(2,1)} %gate_ref.7, bf16[1,2048,3584]{2,1,0:T(8,128)(2,1)} %up_ref.7, f32[2,96,1280]{2,1,0:T(8,128)S(1)} %copy-done.3), custom_call_target="tpu_custom_call" | custom-call | flops 1 | bytes 1 | tf_op jit(solution)/shard_map/pallas_call | solution.py:130
  50.5 6.2 %collective-permute-done.10 = bf16[2,80,1024]{2,1,0:T(8,128)(2,1)S(1)} collective-permute-done((bf16[2,80,1024]{2,1,0:T(8,128)(2,1)S(1)}, bf16[2,80,1024]{2,1,0:T(8,128)(2,1)S(1)}, u32[]{:S(2)}, u32[]{:S(2)}) %collective-permute-start.10) | collective-permute-done | bytes 327712 | tf_op jit(solution)/shard_map/ppermute | solution.py:26
  59.5 17.3 %collective-permute-done.12 = f32[80]{0:T(128)S(1)} collective-permute-done((f32[80]{0:T(128)S(1)}, f32[80]{0:T(128)S(1)}, u32[]{:S(2)}, u32[]{:S(2)}) %collective-permute-start.12) | collective-permute-done | bytes 352 | tf_op jit(solution)/shard_map/ppermute | solution.py:18
  80.4 14.4 %shard_map.84 = (f32[2,96,3584]{2,1,0:T(8,128)}, bf16[2,96,3584]{2,1,0:T(8,128)(2,1)S(1)}) custom-call(bf16[2,2,2,48,1024]{4,3,2,1,0:T(8,128)(2,1)S(1)} %multiply_convert_fusion.x_ref, bf16[1,2048,3584]{2,1,0:T(8,128)(2,1)} %gate_ref.7, bf16[1,2048,3584]{2,1,0:T(8,128)(2,1)} %up_ref.7, f32[2,96,2304]{2,1,0:T(8,128)S(1)} %copy-done.2, ...), custom_call_target="tpu_custom_call" | custom-call | flops 1 | bytes 1 | tf_op jit(solution)/shard_map/pallas_call | solution.py:130
  95.5 7.1 %shard_map.85 = (f32[96,2048]{1,0:T(8,128)S(1)}, bf16[96,2048]{1,0:T(8,128)(2,1)S(1)}) custom-call(s32[1]{0:T(128)} %bitcast.rank_ref, bf16[96,3584]{1,0:T(8,128)(2,1)S(1)} %pad_maximum_fusion.refs_1_.refs_0_, bf16[96,3584]{1,0:T(8,128)(2,1)S(1)} %collective-permute-done.8.refs_1_, bf16[1,3584,2048]{2,1,0:T(8,128)(2,1)} %refs_2_.5, ...), custom_call_target="tpu_custom_call" | custom-call | flops 1 | bytes 1 | tf_op jit(solution)/shard_map/pallas_call | solution.py:178
  103.3 10.3 %collective-permute-done.15 = bf16[96,2048]{1,0:T(8,128)(2,1)S(1)} collective-permute-done((bf16[96,2048]{1,0:T(8,128)(2,1)S(1)}, bf16[96,2048]{1,0:T(8,128)(2,1)S(1)}, u32[]{:S(2)}, u32[]{:S(2)}) %collective-permute-start.15) | collective-permute-done | bytes 393248 | tf_op jit(solution)/shard_map/ppermute | solution.py:26
  115.3 9.5 %collective-permute-done.16 = bf16[48,2048]{1,0:T(8,128)(2,1)S(1)} collective-permute-done((bf16[48,2048]{1,0:T(8,128)(2,1)S(1)}, bf16[48,2048]{1,0:T(8,128)(2,1)S(1)}, u32[]{:S(2)}, u32[]{:S(2)}) %collective-permute-start.16) | collective-permute-done | bytes 196640 | tf_op jit(solution)/shard_map/ppermute | solution.py:26
  130.3 13.6 %shard_map.86 = (f32[2,64,3584]{2,1,0:T(8,128)}, bf16[2,64,3584]{2,1,0:T(8,128)(2,1)S(1)}) custom-call(bf16[2,2,2,32,1024]{4,3,2,1,0:T(8,128)(2,1)S(1)} %multiply_convert_fusion.2.x_ref, bf16[1,2048,3584]{2,1,0:T(8,128)(2,1)} %gate_ref.7, bf16[1,2048,3584]{2,1,0:T(8,128)(2,1)} %up_ref.7, f32[96,2048]{1,0:T(8,128)S(1)} %get-tuple-element.88.refs_0_, ...), custom_call_target="tpu_custom_call" | custom-call | flops 1 | bytes 1 | tf_op jit(solution)/shard_map/pallas_call | solution.py:130
  146.1 7.1 %shard_map.87 = (f32[96,2048]{1,0:T(8,128)S(1)}, bf16[96,2048]{1,0:T(8,128)(2,1)S(1)}) custom-call(s32[1]{0:T(128)} %bitcast.rank_ref, bf16[96,3584]{1,0:T(8,128)(2,1)S(1)} %fusion.1.refs_2_.refs_0_, bf16[96,3584]{1,0:T(8,128)(2,1)S(1)} %collective-permute-done.19.refs_1_, bf16[1,3584,2048]{2,1,0:T(8,128)(2,1)} %refs_2_.5, ...), custom_call_target="tpu_custom_call" | custom-call | flops 1 | bytes 1 | tf_op jit(solution)/shard_map/pallas_call | solution.py:178
  155.9 8.7 %shard_map.88 = (f32[96,4096]{1,0:T(8,128)}, bf16[96,4096]{1,0:T(8,128)(2,1)S(1)}) custom-call(s32[1]{0:T(128)} %bitcast.rank_ref, bf16[96,2048]{1,0:T(8,128)(2,1)S(1)} %constant_dynamic-update-slice_fusion.refs_4_.near_ref, bf16[96,2048]{1,0:T(8,128)(2,1)S(1)} %collective-permute-done.20.far_ref, bf16[1,2048,4096]{2,1,0:T(8,128)(2,1)} %weight_ref.5, ...), custom_call_target="tpu_custom_call" | custom-call | flops 1 | bytes 1 | tf_op jit(solution)/shard_map/pallas_call | solution.py:223
  168.7 6.7 %collective-permute-done.25 = bf16[48,2048]{1,0:T(8,128)(2,1)S(1)} collective-permute-done((bf16[48,2048]{1,0:T(8,128)(2,1)S(1)}, bf16[48,2048]{1,0:T(8,128)(2,1)S(1)}, u32[]{:S(2)}, u32[]{:S(2)}) %collective-permute-start.25) | collective-permute-done | bytes 196640 | tf_op jit(solution)/shard_map/ppermute | solution.py:26
  177.2 6.8 %shard_map.89 = (f32[64,2048]{1,0:T(8,128)S(1)}, bf16[64,2048]{1,0:T(8,128)(2,1)S(1)}) custom-call(s32[1]{0:T(128)} %bitcast.rank_ref, bf16[64,3584]{1,0:T(8,128)(2,1)S(1)} %fusion.3.refs_0_.refs_4_, bf16[64,3584]{1,0:T(8,128)(2,1)S(1)} %collective-permute-done.23.refs_1_, bf16[1,3584,2048]{2,1,0:T(8,128)(2,1)} %refs_2_.5, ...), custom_call_target="tpu_custom_call" | custom-call | flops 1 | bytes 1 | tf_op jit(solution)/shard_map/pallas_call | solution.py:178
  190.0 5.0 %collective-permute-done.30 = bf16[32,2048]{1,0:T(8,128)(2,1)S(1)} collective-permute-done((bf16[32,2048]{1,0:T(8,128)(2,1)S(1)}, bf16[32,2048]{1,0:T(8,128)(2,1)S(1)}, u32[]{:S(2)}, u32[]{:S(2)}) %collective-permute-start.30) | collective-permute-done | bytes 131104 | tf_op jit(solution)/shard_map/ppermute | solution.py:26
  204.1 5.0 %collective-permute-done.28.far_ref = bf16[96,2048]{1,0:T(8,128)(2,1)S(1)} collective-permute-done((bf16[96,2048]{1,0:T(8,128)(2,1)S(1)}, bf16[96,2048]{1,0:T(8,128)(2,1)S(1)}, u32[]{:S(2)}, u32[]{:S(2)}) %collective-permute-start.28) | collective-permute-done | bytes 393248 | tf_op jit(solution)/shard_map/ppermute | solution.py:26
  209.1 8.5 %shard_map.90 = (f32[96,4096]{1,0:T(8,128)}, bf16[96,4096]{1,0:T(8,128)(2,1)S(1)}) custom-call(s32[1]{0:T(128)} %bitcast.rank_ref, bf16[96,2048]{1,0:T(8,128)(2,1)S(1)} %constant_dynamic-update-slice_fusion.2.near_ref.refs_3_, bf16[96,2048]{1,0:T(8,128)(2,1)S(1)} %collective-permute-done.28.far_ref, bf16[1,2048,4096]{2,1,0:T(8,128)(2,1)} %weight_ref.5, ...), custom_call_target="tpu_custom_call" | custom-call | flops 1 | bytes 1 | tf_op jit(solution)/shard_map/pallas_call | solution.py:223
  217.7 7.3 %shard_map.91 = (f32[64,4096]{1,0:T(8,128)S(1)}, bf16[64,4096]{1,0:T(8,128)(2,1)S(1)}) custom-call(s32[1]{0:T(128)} %bitcast.rank_ref, bf16[64,2048]{1,0:T(8,128)(2,1)S(1)} %get-tuple-element.155.near_ref, bf16[64,2048]{1,0:T(8,128)(2,1)S(1)} %get-tuple-element.156.far_ref, bf16[1,2048,4096]{2,1,0:T(8,128)(2,1)} %weight_ref.5, ...), custom_call_target="tpu_custom_call" | custom-call | flops 1 | bytes 1 | tf_op jit(solution)/shard_map/pallas_call | solution.py:223
  229.8 9.7 %collective-permute-done.36 = bf16[48,4096]{1,0:T(8,128)(2,1)S(1)} collective-permute-done((bf16[48,4096]{1,0:T(8,128)(2,1)S(1)}, bf16[48,4096]{1,0:T(8,128)(2,1)S(1)}, u32[]{:S(2)}, u32[]{:S(2)}) %collective-permute-start.36) | collective-permute-done | bytes 393248 | tf_op jit(solution)/shard_map/ppermute | solution.py:22
  239.6 5.0 %collective-permute-done.38 = bf16[32,4096]{1,0:T(8,128)(2,1)S(1)} collective-permute-done((bf16[32,4096]{1,0:T(8,128)(2,1)S(1)}, bf16[32,4096]{1,0:T(8,128)(2,1)S(1)}, u32[]{:S(2)}, u32[]{:S(2)}) %collective-permute-start.38) | collective-permute-done | bytes 262176 | tf_op jit(solution)/shard_map/ppermute | solution.py:22
  (151 shorter events, 57.9 us)
Async XLA Ops:
  24.3 23.2 %collective-permute-start.9 = (bf16[1,80,1024]{2,1,0:T(8,128)(2,1)S(1)}, bf16[1,80,1024]{2,1,0:T(8,128)(2,1)S(1)}, u32[]{:S(2)}, u32[]{:S(2)}) collective-permute-start(bf16[1,80,1024]{2,1,0:T(8,128)(2,1)S(1)} %dynamic-slice_bitcast_fusion), channel_id=1, source_target_pairs={{0,8},{4,12},{8,0},{12,4},{1,9},{5,13},{9,1},{13,5},{2,10},{6,14},... | collective-permute-start | bytes 491528 | tf_op jit(solution)/shard_map/ppermute | solution.py:26
  35.5 21.3 %collective-permute-start.6 = (bf16[2,96,1280]{2,1,0:T(8,128)(2,1)S(1)}, bf16[2,96,1280]{2,1,0:T(8,128)(2,1)S(1)}, u32[]{:S(2)}, u32[]{:S(2)}) collective-permute-start(bf16[2,96,1280]{2,1,0:T(8,128)(2,1)S(1)} %get-tuple-element.74), channel_id=1, source_target_pairs={{0,2},{2,0},{1,3},{3,1},{4,6},{6,4},{5,7},{7,5},{8,10},{10,8},{9,1... | collective-permute-start | bytes 1474568 | tf_op jit(solution)/shard_map/ppermute | solution.py:22
  49.0 28.0 %collective-permute-start.7 = (bf16[2,96,2304]{2,1,0:T(8,128)(2,1)S(1)}, bf16[2,96,2304]{2,1,0:T(8,128)(2,1)S(1)}, u32[]{:S(2)}, u32[]{:S(2)}) collective-permute-start(bf16[2,96,2304]{2,1,0:T(8,128)(2,1)S(1)} %get-tuple-element.76), channel_id=1, source_target_pairs={{0,2},{2,0},{1,3},{3,1},{4,6},{6,4},{5,7},{7,5},{8,10},{10,8},{9,1... | collective-permute-start | bytes 2654216 | tf_op jit(solution)/shard_map/ppermute | solution.py:22
  57.1 19.7 %collective-permute-start.11 = (bf16[2,80,1024]{2,1,0:T(8,128)(2,1)S(1)}, bf16[2,80,1024]{2,1,0:T(8,128)(2,1)S(1)}, u32[]{:S(2)}, u32[]{:S(2)}) collective-permute-start(bf16[2,80,1024]{2,1,0:T(8,128)(2,1)S(1)} %pad_maximum_fusion.8), channel_id=1, source_target_pairs={{2,0},{0,2},{3,1},{1,3},{6,4},{4,6},{7,5},{5,7},{10,8},{8,10},{11,... | collective-permute-start | bytes 983048 | tf_op jit(solution)/shard_map/ppermute | solution.py:18
  58.9 17.9 %collective-permute-start.12 = (f32[80]{0:T(128)S(1)}, f32[80]{0:T(128)S(1)}, u32[]{:S(2)}, u32[]{:S(2)}) collective-permute-start(f32[80]{0:T(128)S(1)} %get-tuple-element.152), channel_id=1, source_target_pairs={{2,0},{0,2},{3,1},{1,3},{6,4},{4,6},{7,5},{5,7},{10,8},{8,10},{11,... | collective-permute-start | bytes 968 | tf_op jit(solution)/shard_map/ppermute | solution.py:18
  77.5 18.0 %collective-permute-start.8 = (bf16[96,3584]{1,0:T(8,128)(2,1)S(1)}, bf16[96,3584]{1,0:T(8,128)(2,1)S(1)}, u32[]{:S(2)}, u32[]{:S(2)}) collective-permute-start(bf16[96,3584]{1,0:T(8,128)(2,1)S(1)} %pad_maximum_fusion.refs_1_.refs_0_), channel_id=1, source_target_pairs={{2,0},{0,2},{3,1},{1,3},{6,4},{4,6},{7,5},{5,7},{10,8},{8,10},{11,... | collective-permute-start | bytes 2064392 | tf_op jit(solution)/shard_map/ppermute | solution.py:18
  94.9 32.3 %collective-permute-start.18 = (bf16[2,96,3584]{2,1,0:T(8,128)(2,1)S(1)}, bf16[2,96,3584]{2,1,0:T(8,128)(2,1)S(1)}, u32[]{:S(2)}, u32[]{:S(2)}) collective-permute-start(bf16[2,96,3584]{2,1,0:T(8,128)(2,1)S(1)} %get-tuple-element.92), channel_id=1, source_target_pairs={{0,2},{2,0},{1,3},{3,1},{4,6},{6,4},{5,7},{7,5},{8,10},{10,8},{9,1... | collective-permute-start | bytes 4128776 | tf_op jit(solution)/shard_map/ppermute | solution.py:22
  102.6 11.0 %collective-permute-start.15 = (bf16[96,2048]{1,0:T(8,128)(2,1)S(1)}, bf16[96,2048]{1,0:T(8,128)(2,1)S(1)}, u32[]{:S(2)}, u32[]{:S(2)}) collective-permute-start(bf16[96,2048]{1,0:T(8,128)(2,1)S(1)} %get-tuple-element.87), channel_id=1, source_target_pairs={{0,4},{4,0},{8,12},{12,8},{1,5},{5,1},{9,13},{13,9},{2,6},{6,2},{1... | collective-permute-start | bytes 1179656 | tf_op jit(solution)/shard_map/ppermute | solution.py:26
  113.8 11.0 %collective-permute-start.16 = (bf16[48,2048]{1,0:T(8,128)(2,1)S(1)}, bf16[48,2048]{1,0:T(8,128)(2,1)S(1)}, u32[]{:S(2)}, u32[]{:S(2)}) collective-permute-start(bf16[48,2048]{1,0:T(8,128)(2,1)S(1)} %slice.231.refs_1_), channel_id=1, source_target_pairs={{0,8},{4,12},{8,0},{12,4},{1,9},{5,13},{9,1},{13,5},{2,10},{6,14},... | collective-permute-start | bytes 589832 | tf_op jit(solution)/shard_map/ppermute | solution.py:26
  128.0 17.5 %collective-permute-start.19 = (bf16[96,3584]{1,0:T(8,128)(2,1)S(1)}, bf16[96,3584]{1,0:T(8,128)(2,1)S(1)}, u32[]{:S(2)}, u32[]{:S(2)}) collective-permute-start(bf16[96,3584]{1,0:T(8,128)(2,1)S(1)} %fusion.1.refs_2_.refs_0_), channel_id=1, source_target_pairs={{2,0},{0,2},{3,1},{1,3},{6,4},{4,6},{7,5},{5,7},{10,8},{8,10},{11,... | collective-permute-start | bytes 2064392 | tf_op jit(solution)/shard_map/ppermute | solution.py:18
  128.6 16.8 %collective-permute-start.17 = (bf16[48,2048]{1,0:T(8,128)(2,1)S(1)}, bf16[48,2048]{1,0:T(8,128)(2,1)S(1)}, u32[]{:S(2)}, u32[]{:S(2)}) collective-permute-start(bf16[48,2048]{1,0:T(8,128)(2,1)S(1)} %add_convert_fusion.1.refs_3_), channel_id=1, source_target_pairs={{0,8},{4,12},{8,0},{12,4},{1,9},{5,13},{9,1},{13,5},{2,10},{6,14},... | collective-permute-start | bytes 589832 | tf_op jit(solution)/shard_map/ppermute | solution.py:26
  143.9 21.1 %collective-permute-start.22 = (bf16[2,64,3584]{2,1,0:T(8,128)(2,1)S(1)}, bf16[2,64,3584]{2,1,0:T(8,128)(2,1)S(1)}, u32[]{:S(2)}, u32[]{:S(2)}) collective-permute-start(bf16[2,64,3584]{2,1,0:T(8,128)(2,1)S(1)} %get-tuple-element.101), channel_id=1, source_target_pairs={{0,2},{2,0},{1,3},{3,1},{4,6},{6,4},{5,7},{7,5},{8,10},{10,8},{9,1... | collective-permute-start | bytes 2752520 | tf_op jit(solution)/shard_map/ppermute | solution.py:22
  145.5 10.4 %collective-permute-start.20 = (bf16[96,2048]{1,0:T(8,128)(2,1)S(1)}, bf16[96,2048]{1,0:T(8,128)(2,1)S(1)}, u32[]{:S(2)}, u32[]{:S(2)}) collective-permute-start(bf16[96,2048]{1,0:T(8,128)(2,1)S(1)} %constant_dynamic-update-slice_fusion.refs_4_.near_ref), channel_id=1, source_target_pairs={{0,4},{4,0},{8,12},{12,8},{1,5},{5,1},{9,13},{13,9},{2,6},{6,2},{1... | collective-permute-start | bytes 1179656 | tf_op jit(solution)/shard_map/ppermute | solution.py:26
  153.3 11.3 %collective-permute-start.24 = (bf16[96,2048]{1,0:T(8,128)(2,1)S(1)}, bf16[96,2048]{1,0:T(8,128)(2,1)S(1)}, u32[]{:S(2)}, u32[]{:S(2)}) collective-permute-start(bf16[96,2048]{1,0:T(8,128)(2,1)S(1)} %get-tuple-element.104), channel_id=1, source_target_pairs={{0,4},{4,0},{8,12},{12,8},{1,5},{5,1},{9,13},{13,9},{2,6},{6,2},{1... | collective-permute-start | bytes 1179656 | tf_op jit(solution)/shard_map/ppermute | solution.py:26
  167.2 10.1 %collective-permute-start.23 = (bf16[64,3584]{1,0:T(8,128)(2,1)S(1)}, bf16[64,3584]{1,0:T(8,128)(2,1)S(1)}, u32[]{:S(2)}, u32[]{:S(2)}) collective-permute-start(bf16[64,3584]{1,0:T(8,128)(2,1)S(1)} %fusion.3.refs_0_.refs_4_), channel_id=1, source_target_pairs={{2,0},{0,2},{3,1},{1,3},{6,4},{4,6},{7,5},{5,7},{10,8},{8,10},{11,... | collective-permute-start | bytes 1376264 | tf_op jit(solution)/shard_map/ppermute | solution.py:18
  175.6 22.3 %collective-permute-start.21 = (bf16[96,4096]{1,0:T(8,128)(2,1)S(1)}, bf16[96,4096]{1,0:T(8,128)(2,1)S(1)}, u32[]{:S(2)}, u32[]{:S(2)}) collective-permute-start(bf16[96,4096]{1,0:T(8,128)(2,1)S(1)} %get-tuple-element.100), channel_id=1, source_target_pairs={{0,1},{1,0},{2,3},{3,2},{4,5},{5,4},{6,7},{7,6},{8,9},{9,8},{10,11... | collective-permute-start | bytes 2359304 | tf_op jit(solution)/shard_map/ppermute | solution.py:22
  185.6 12.2 %collective-permute-start.31 = (bf16[32,2048]{1,0:T(8,128)(2,1)S(1)}, bf16[32,2048]{1,0:T(8,128)(2,1)S(1)}, u32[]{:S(2)}, u32[]{:S(2)}) collective-permute-start(bf16[32,2048]{1,0:T(8,128)(2,1)S(1)} %get-tuple-element.149), channel_id=1, source_target_pairs={{0,4},{4,0},{8,12},{12,8},{1,5},{5,1},{9,13},{13,9},{2,6},{6,2},{1... | collective-permute-start | bytes 393224 | tf_op jit(solution)/shard_map/ppermute | solution.py:26
  189.9 19.2 %collective-permute-start.28 = (bf16[96,2048]{1,0:T(8,128)(2,1)S(1)}, bf16[96,2048]{1,0:T(8,128)(2,1)S(1)}, u32[]{:S(2)}, u32[]{:S(2)}) collective-permute-start(bf16[96,2048]{1,0:T(8,128)(2,1)S(1)} %constant_dynamic-update-slice_fusion.2.near_ref.refs_3_), channel_id=1, source_target_pairs={{0,4},{4,0},{8,12},{12,8},{1,5},{5,1},{9,13},{13,9},{2,6},{6,2},{1... | collective-permute-start | bytes 1179656 | tf_op jit(solution)/shard_map/ppermute | solution.py:26
  198.1 11.0 %collective-permute-start.26 = (bf16[48,4096]{1,0:T(8,128)(2,1)S(1)}, bf16[48,4096]{1,0:T(8,128)(2,1)S(1)}, u32[]{:S(2)}, u32[]{:S(2)}) collective-permute-start(bf16[48,4096]{1,0:T(8,128)(2,1)S(1)} %slice.228.refs_1_), channel_id=1, source_target_pairs={{0,2},{2,0},{1,3},{3,1},{4,6},{6,4},{5,7},{7,5},{8,10},{10,8},{9,1... | collective-permute-start | bytes 1179656 | tf_op jit(solution)/shard_map/ppermute | solution.py:22
  199.7 17.9 %collective-permute-start.35 = (bf16[32,2048]{1,0:T(8,128)(2,1)S(1)}, bf16[32,2048]{1,0:T(8,128)(2,1)S(1)}, u32[]{:S(2)}, u32[]{:S(2)}) collective-permute-start(bf16[32,2048]{1,0:T(8,128)(2,1)S(1)} %add_convert_fusion.2.refs_2_), channel_id=1, source_target_pairs={{0,12},{4,8},{8,4},{12,0},{1,13},{5,9},{9,5},{13,1},{2,14},{6,10},... | collective-permute-start | bytes 393224 | tf_op jit(solution)/shard_map/ppermute | solution.py:26
  201.3 16.2 %collective-permute-start.34 = (bf16[32,2048]{1,0:T(8,128)(2,1)S(1)}, bf16[32,2048]{1,0:T(8,128)(2,1)S(1)}, u32[]{:S(2)}, u32[]{:S(2)}) collective-permute-start(bf16[32,2048]{1,0:T(8,128)(2,1)S(1)} %add_convert_fusion.2.refs_2_), channel_id=1, source_target_pairs={{0,8},{4,12},{8,0},{12,4},{1,9},{5,13},{9,1},{13,5},{2,10},{6,14},... | collective-permute-start | bytes 393224 | tf_op jit(solution)/shard_map/ppermute | solution.py:26
  203.8 13.8 %collective-permute-start.33 = (bf16[32,2048]{1,0:T(8,128)(2,1)S(1)}, bf16[32,2048]{1,0:T(8,128)(2,1)S(1)}, u32[]{:S(2)}, u32[]{:S(2)}) collective-permute-start(bf16[32,2048]{1,0:T(8,128)(2,1)S(1)} %add_convert_fusion.2.refs_2_), channel_id=1, source_target_pairs={{0,4},{4,0},{8,12},{12,8},{1,5},{5,1},{9,13},{13,9},{2,6},{6,2},{1... | collective-permute-start | bytes 393224 | tf_op jit(solution)/shard_map/ppermute | solution.py:26
  227.5 12.0 %collective-permute-start.36 = (bf16[48,4096]{1,0:T(8,128)(2,1)S(1)}, bf16[48,4096]{1,0:T(8,128)(2,1)S(1)}, u32[]{:S(2)}, u32[]{:S(2)}) collective-permute-start(bf16[48,4096]{1,0:T(8,128)(2,1)S(1)} %slice.227), channel_id=1, source_target_pairs={{0,2},{2,0},{1,3},{3,1},{4,6},{6,4},{5,7},{7,5},{8,10},{10,8},{9,1... | collective-permute-start | bytes 1179656 | tf_op jit(solution)/shard_map/ppermute | solution.py:22
  229.5 15.1 %collective-permute-start.38 = (bf16[32,4096]{1,0:T(8,128)(2,1)S(1)}, bf16[32,4096]{1,0:T(8,128)(2,1)S(1)}, u32[]{:S(2)}, u32[]{:S(2)}) collective-permute-start(bf16[32,4096]{1,0:T(8,128)(2,1)S(1)} %slice.229), channel_id=1, source_target_pairs={{0,2},{2,0},{1,3},{3,1},{4,6},{6,4},{5,7},{7,5},{8,10},{10,8},{9,1... | collective-permute-start | bytes 786440 | tf_op jit(solution)/shard_map/ppermute | solution.py:22
  (27 other events, 203.1 us)

commit v10 on v9

--- a/solution.py
+++ b/solution.py
@@ -11,7 +11,7 @@
 F32 = jnp.float32
 VMEM_BYTES = 51 * 1024 * 1024
 GATE_UP_VMEM_BYTES = 44 * 1024 * 1024
-BUFFERS = 3
+BUFFERS = 8
 
 
 def shift(value, axis, size, hop):
@@ -132,7 +132,7 @@
         grid=(tiles,),
         in_specs=[whole(x.shape)] + in_hbm(2) + unread(after),
         out_specs=[pl.BlockSpec((2, own_rows, tile), lambda j: (0, 0, j))] * owners,
-        out_shape=[pltpu.HBM((2, own_rows, width), F32)]
+        out_shape=[jax.ShapeDtypeStruct((2, own_rows, width), F32)]
         + [jax.ShapeDtypeStruct((2, own_rows, width), BF16)] * (owners - 1),
         scratch_shapes=[pltpu.VMEM((rows, depth), BF16)] + slots(depth, tile, tiles) * 2,
         compiler_params=params(GATE_UP_VMEM_BYTES),

time: 246 us -> 242 us (0.984)
  Pallas kernels: 90.8 us -> 80.9 us
  waiting for transfers between devices: 102 us -> 108 us
    pallas_call x4, Pallas kernels: 45.3 us -> 40.5 us  [gate_up(): pl.pallas_call(functools.partial(gate_up_body, tiles, first), grid=(tiles...]
    ppermute x18, waiting for transfers between devices: 58.3 us -> 62.7 us  [swap(): return lax.ppermute(value, axis, [(d, d ^ bit) for d in range(size)])]
    pallas_call x3, Pallas kernels: 21.1 us -> 18.4 us  [down(): pl.pallas_call(functools.partial(down_body, owners, members, pieces, orde...]
  transfers between devices with their start and end apart: 39 -> 39, of which waited for: 21 -> 23; matrix products, arithmetic and copies ran while one was open for 1% -> 1% of each run, Pallas kernels for 37% -> 33%
where the time goes in v10:
time: 242 us
  waiting for transfers between devices  108 us (45%)
  Pallas kernels  80.9 us (33%)
  starting transfers between devices  42.3 us (17%)
  other arithmetic  5.3 us (2%)
  local copies, waits for them, and re-layouts  4.4 us (2%)
    ppermute x18, waiting for transfers between devices, swap(): return lax.ppermute(value, axis, [(d, d ^ bit) for d in range(size)])  62.7 us
    pallas_call x4, Pallas kernels, gate_up(): pl.pallas_call(functools.partial(gate_up_body, tiles, first), grid=(tiles...  40.5 us
    ppermute x18, starting transfers between devices, swap(): return lax.ppermute(value, axis, [(d, d ^ bit) for d in range(size)])  26.4 us
    ppermute x11, waiting for transfers between devices, shift(): lax.ppermute(value, axis, [((d + hop) % size, d) for d in range(size)])  25.6 us
    pallas_call x3, Pallas kernels, encode(): pl.pallas_call(functools.partial(encode_body, members, order, width // ti...  22 us
    ppermute x10, waiting for transfers between devices, send(): lax.ppermute(value, axis, [(d, (d + hop) % size) for d in range(size)])  19.7 us
    pallas_call x3, Pallas kernels, down(): pl.pallas_call(functools.partial(down_body, owners, members, pieces, orde...  18.4 us
    ppermute x11, starting transfers between devices, shift(): lax.ppermute(value, axis, [((d + hop) % size, d) for d in range(size)])  8.42 us
  transfers between devices with their start and end apart: 39, of which 23 were waited for; matrix products, arithmetic and copies ran while one was open for 1% of the time, Pallas kernels for 33%

profile of v10, /device:TPU:0, one launch (start us, length us, event | category | flops | bytes accessed | tf_op | source)
XLA Modules:
  0.0 241.6 jit_solution(4601734425118953461)
XLA Ops:
  1.1 4.1 %collective-permute-start = (bf16[1,48,1024]{2,1,0:T(8,128)(2,1)S(1)}, bf16[1,48,1024]{2,1,0:T(8,128)(2,1)S(1)}, u32[]{:S(2)}, u32[]{:S(2)}) collective-permute-start(bf16[1,48,1024]{2,1,0:T(8,128)(2,1)S(1)} %dynamic-slice_bitcast_fusion.1), channel_id=1, source_target_pairs={{0,8},{4,12},{8,0},{12,4},{1,9},{5,13},{9,1},{13,5},{2,10},{6,14},... | collective-permute-start | bytes 294920 | tf_op jit(solution)/shard_map/ppermute | solution.py:26
  5.1 4.9 %collective-permute-done = bf16[1,48,1024]{2,1,0:T(8,128)(2,1)S(1)} collective-permute-done((bf16[1,48,1024]{2,1,0:T(8,128)(2,1)S(1)}, bf16[1,48,1024]{2,1,0:T(8,128)(2,1)S(1)}, u32[]{:S(2)}, u32[]{:S(2)}) %collective-permute-start) | collective-permute-done | bytes 98336 | tf_op jit(solution)/shard_map/ppermute | solution.py:26
  10.9 5.4 %collective-permute-done.1 = bf16[2,48,1024]{2,1,0:T(8,128)(2,1)S(1)} collective-permute-done((bf16[2,48,1024]{2,1,0:T(8,128)(2,1)S(1)}, bf16[2,48,1024]{2,1,0:T(8,128)(2,1)S(1)}, u32[]{:S(2)}, u32[]{:S(2)}) %collective-permute-start.1) | collective-permute-done | bytes 196640 | tf_op jit(solution)/shard_map/ppermute | solution.py:26
  20.1 3.4 %collective-permute-done.2 = bf16[2,48,1024]{2,1,0:T(8,128)(2,1)S(1)} collective-permute-done((bf16[2,48,1024]{2,1,0:T(8,128)(2,1)S(1)}, bf16[2,48,1024]{2,1,0:T(8,128)(2,1)S(1)}, u32[]{:S(2)}, u32[]{:S(2)}) %collective-permute-start.2) | collective-permute-done | bytes 196640 | tf_op jit(solution)/shard_map/ppermute | solution.py:18
  24.3 3.8 %collective-permute-start.9 = (bf16[1,80,1024]{2,1,0:T(8,128)(2,1)S(1)}, bf16[1,80,1024]{2,1,0:T(8,128)(2,1)S(1)}, u32[]{:S(2)}, u32[]{:S(2)}) collective-permute-start(bf16[1,80,1024]{2,1,0:T(8,128)(2,1)S(1)} %dynamic-slice_bitcast_fusion), channel_id=1, source_target_pairs={{0,8},{4,12},{8,0},{12,4},{1,9},{5,13},{9,1},{13,5},{2,10},{6,14},... | collective-permute-start | bytes 491528 | tf_op jit(solution)/shard_map/ppermute | solution.py:26
  28.3 6.3 %shard_map.82 = (f32[2,96,1280]{2,1,0:T(8,128)S(1)}, bf16[2,96,1280]{2,1,0:T(8,128)(2,1)S(1)}) custom-call(bf16[2,2,2,48,1024]{4,3,2,1,0:T(8,128)(2,1)S(1)} %multiply_convert_fusion.1.x_ref, bf16[1,2048,3584]{2,1,0:T(8,128)(2,1)} %gate_ref.7, bf16[1,2048,3584]{2,1,0:T(8,128)(2,1)} %up_ref.7), custom_call_target="tpu_custom_call" | custom-call | flops 1 | bytes 1 | tf_op jit(solution)/shard_map/pallas_call | solution.py:130
  35.3 9.9 %shard_map.83 = (f32[2,96,2304]{2,1,0:T(8,128)S(1)}, bf16[2,96,2304]{2,1,0:T(8,128)(2,1)S(1)}) custom-call(bf16[2,2,2,48,1024]{4,3,2,1,0:T(8,128)(2,1)S(1)} %multiply_convert_fusion.1.x_ref, bf16[1,2048,3584]{2,1,0:T(8,128)(2,1)} %gate_ref.7, bf16[1,2048,3584]{2,1,0:T(8,128)(2,1)} %up_ref.7, f32[2,96,1280]{2,1,0:T(8,128)S(1)} %get-tuple-element.73.refs_0_), custom_call_target="tpu_custom_call" | custom-call | flops 1 | bytes 1 | tf_op jit(solution)/shard_map/pallas_call | solution.py:130
  48.2 6.2 %collective-permute-done.10 = bf16[2,80,1024]{2,1,0:T(8,128)(2,1)S(1)} collective-permute-done((bf16[2,80,1024]{2,1,0:T(8,128)(2,1)S(1)}, bf16[2,80,1024]{2,1,0:T(8,128)(2,1)S(1)}, u32[]{:S(2)}, u32[]{:S(2)}) %collective-permute-start.10) | collective-permute-done | bytes 327712 | tf_op jit(solution)/shard_map/ppermute | solution.py:26
  57.2 17.3 %collective-permute-done.12 = f32[80]{0:T(128)S(1)} collective-permute-done((f32[80]{0:T(128)S(1)}, f32[80]{0:T(128)S(1)}, u32[]{:S(2)}, u32[]{:S(2)}) %collective-permute-start.12) | collective-permute-done | bytes 352 | tf_op jit(solution)/shard_map/ppermute | solution.py:18
  78.2 13.1 %shard_map.84 = (f32[2,96,3584]{2,1,0:T(8,128)S(1)}, bf16[2,96,3584]{2,1,0:T(8,128)(2,1)S(1)}) custom-call(bf16[2,2,2,48,1024]{4,3,2,1,0:T(8,128)(2,1)S(1)} %multiply_convert_fusion.x_ref, bf16[1,2048,3584]{2,1,0:T(8,128)(2,1)} %gate_ref.7, bf16[1,2048,3584]{2,1,0:T(8,128)(2,1)} %up_ref.7, f32[2,96,2304]{2,1,0:T(8,128)S(1)} %get-tuple-element.75.refs_0_, ...), custom_call_target="tpu_custom_call" | custom-call | flops 1 | bytes 1 | tf_op jit(solution)/shard_map/pallas_call | solution.py:130
  93.3 6.3 %shard_map.85 = (f32[96,2048]{1,0:T(8,128)S(1)}, bf16[96,2048]{1,0:T(8,128)(2,1)S(1)}) custom-call(s32[1]{0:T(128)} %bitcast.rank_ref, bf16[96,3584]{1,0:T(8,128)(2,1)S(1)} %pad_maximum_fusion.refs_1_.refs_0_, bf16[96,3584]{1,0:T(8,128)(2,1)S(1)} %collective-permute-done.8.refs_1_, bf16[1,3584,2048]{2,1,0:T(8,128)(2,1)} %refs_2_.5, f32[2,96,3584]{2,1,0:T(8,128)} %copy-done.2), custom_call_target="tpu_custom_call" | custom-call | flops 1 | bytes 1 | tf_op jit(solution)/shard_map/pallas_call | solution.py:178
  100.3 10.3 %collective-permute-done.15 = bf16[96,2048]{1,0:T(8,128)(2,1)S(1)} collective-permute-done((bf16[96,2048]{1,0:T(8,128)(2,1)S(1)}, bf16[96,2048]{1,0:T(8,128)(2,1)S(1)}, u32[]{:S(2)}, u32[]{:S(2)}) %collective-permute-start.15) | collective-permute-done | bytes 393248 | tf_op jit(solution)/shard_map/ppermute | solution.py:26
  112.3 9.5 %collective-permute-done.16 = bf16[48,2048]{1,0:T(8,128)(2,1)S(1)} collective-permute-done((bf16[48,2048]{1,0:T(8,128)(2,1)S(1)}, bf16[48,2048]{1,0:T(8,128)(2,1)S(1)}, u32[]{:S(2)}, u32[]{:S(2)}) %collective-permute-start.16) | collective-permute-done | bytes 196640 | tf_op jit(solution)/shard_map/ppermute | solution.py:26
  128.0 11.2 %shard_map.86 = (f32[2,64,3584]{2,1,0:T(8,128)S(1)}, bf16[2,64,3584]{2,1,0:T(8,128)(2,1)S(1)}) custom-call(bf16[2,2,2,32,1024]{4,3,2,1,0:T(8,128)(2,1)S(1)} %multiply_convert_fusion.2.x_ref, bf16[1,2048,3584]{2,1,0:T(8,128)(2,1)} %gate_ref.7, bf16[1,2048,3584]{2,1,0:T(8,128)(2,1)} %up_ref.7, f32[96,2048]{1,0:T(8,128)S(1)} %get-tuple-element.88.refs_0_, ...), custom_call_target="tpu_custom_call" | custom-call | flops 1 | bytes 1 | tf_op jit(solution)/shard_map/pallas_call | solution.py:130
  143.8 6.3 %shard_map.87 = (f32[96,2048]{1,0:T(8,128)S(1)}, bf16[96,2048]{1,0:T(8,128)(2,1)S(1)}) custom-call(s32[1]{0:T(128)} %bitcast.rank_ref, bf16[96,3584]{1,0:T(8,128)(2,1)S(1)} %fusion.1.refs_2_.refs_0_, bf16[96,3584]{1,0:T(8,128)(2,1)S(1)} %collective-permute-done.19.refs_1_, bf16[1,3584,2048]{2,1,0:T(8,128)(2,1)} %refs_2_.5, f32[2,64,3584]{2,1,0:T(8,128)} %copy-done.4, ...), custom_call_target="tpu_custom_call" | custom-call | flops 1 | bytes 1 | tf_op jit(solution)/shard_map/pallas_call | solution.py:178
  153.7 7.8 %shard_map.88 = (f32[96,4096]{1,0:T(8,128)}, bf16[96,4096]{1,0:T(8,128)(2,1)S(1)}) custom-call(s32[1]{0:T(128)} %bitcast.rank_ref, bf16[96,2048]{1,0:T(8,128)(2,1)S(1)} %constant_dynamic-update-slice_fusion.refs_4_.near_ref, bf16[96,2048]{1,0:T(8,128)(2,1)S(1)} %collective-permute-done.20.far_ref, bf16[1,2048,4096]{2,1,0:T(8,128)(2,1)} %weight_ref.5, ...), custom_call_target="tpu_custom_call" | custom-call | flops 1 | bytes 1 | tf_op jit(solution)/shard_map/pallas_call | solution.py:223
  165.3 7.9 %collective-permute-done.25 = bf16[48,2048]{1,0:T(8,128)(2,1)S(1)} collective-permute-done((bf16[48,2048]{1,0:T(8,128)(2,1)S(1)}, bf16[48,2048]{1,0:T(8,128)(2,1)S(1)}, u32[]{:S(2)}, u32[]{:S(2)}) %collective-permute-start.25) | collective-permute-done | bytes 196640 | tf_op jit(solution)/shard_map/ppermute | solution.py:26
  174.8 5.9 %shard_map.89 = (f32[64,2048]{1,0:T(8,128)S(1)}, bf16[64,2048]{1,0:T(8,128)(2,1)S(1)}) custom-call(s32[1]{0:T(128)} %bitcast.rank_ref, bf16[64,3584]{1,0:T(8,128)(2,1)S(1)} %fusion.3.refs_0_.refs_4_, bf16[64,3584]{1,0:T(8,128)(2,1)S(1)} %collective-permute-done.23.refs_1_, bf16[1,3584,2048]{2,1,0:T(8,128)(2,1)} %refs_2_.5, ...), custom_call_target="tpu_custom_call" | custom-call | flops 1 | bytes 1 | tf_op jit(solution)/shard_map/pallas_call | solution.py:178
  187.6 6.0 %collective-permute-done.30 = bf16[32,2048]{1,0:T(8,128)(2,1)S(1)} collective-permute-done((bf16[32,2048]{1,0:T(8,128)(2,1)S(1)}, bf16[32,2048]{1,0:T(8,128)(2,1)S(1)}, u32[]{:S(2)}, u32[]{:S(2)}) %collective-permute-start.30) | collective-permute-done | bytes 131104 | tf_op jit(solution)/shard_map/ppermute | solution.py:26
  200.7 6.1 %collective-permute-done.28.far_ref = bf16[96,2048]{1,0:T(8,128)(2,1)S(1)} collective-permute-done((bf16[96,2048]{1,0:T(8,128)(2,1)S(1)}, bf16[96,2048]{1,0:T(8,128)(2,1)S(1)}, u32[]{:S(2)}, u32[]{:S(2)}) %collective-permute-start.28) | collective-permute-done | bytes 393248 | tf_op jit(solution)/shard_map/ppermute | solution.py:26
  206.9 7.6 %shard_map.90 = (f32[96,4096]{1,0:T(8,128)}, bf16[96,4096]{1,0:T(8,128)(2,1)S(1)}) custom-call(s32[1]{0:T(128)} %bitcast.rank_ref, bf16[96,2048]{1,0:T(8,128)(2,1)S(1)} %constant_dynamic-update-slice_fusion.2.near_ref.refs_3_, bf16[96,2048]{1,0:T(8,128)(2,1)S(1)} %collective-permute-done.28.far_ref, bf16[1,2048,4096]{2,1,0:T(8,128)(2,1)} %weight_ref.5, ...), custom_call_target="tpu_custom_call" | custom-call | flops 1 | bytes 1 | tf_op jit(solution)/shard_map/pallas_call | solution.py:223
  214.7 6.6 %shard_map.91 = (f32[64,4096]{1,0:T(8,128)S(1)}, bf16[64,4096]{1,0:T(8,128)(2,1)S(1)}) custom-call(s32[1]{0:T(128)} %bitcast.rank_ref, bf16[64,2048]{1,0:T(8,128)(2,1)S(1)} %get-tuple-element.155.near_ref, bf16[64,2048]{1,0:T(8,128)(2,1)S(1)} %get-tuple-element.156.far_ref, bf16[1,2048,4096]{2,1,0:T(8,128)(2,1)} %weight_ref.5, ...), custom_call_target="tpu_custom_call" | custom-call | flops 1 | bytes 1 | tf_op jit(solution)/shard_map/pallas_call | solution.py:223
  226.0 9.7 %collective-permute-done.36 = bf16[48,4096]{1,0:T(8,128)(2,1)S(1)} collective-permute-done((bf16[48,4096]{1,0:T(8,128)(2,1)S(1)}, bf16[48,4096]{1,0:T(8,128)(2,1)S(1)}, u32[]{:S(2)}, u32[]{:S(2)}) %collective-permute-start.36) | collective-permute-done | bytes 393248 | tf_op jit(solution)/shard_map/ppermute | solution.py:22
  235.9 4.9 %collective-permute-done.38 = bf16[32,4096]{1,0:T(8,128)(2,1)S(1)} collective-permute-done((bf16[32,4096]{1,0:T(8,128)(2,1)S(1)}, bf16[32,4096]{1,0:T(8,128)(2,1)S(1)}, u32[]{:S(2)}, u32[]{:S(2)}) %collective-permute-start.38) | collective-permute-done | bytes 262176 | tf_op jit(solution)/shard_map/ppermute | solution.py:22
  (151 shorter events, 60.5 us)
Async XLA Ops:
  24.3 20.9 %collective-permute-start.9 = (bf16[1,80,1024]{2,1,0:T(8,128)(2,1)S(1)}, bf16[1,80,1024]{2,1,0:T(8,128)(2,1)S(1)}, u32[]{:S(2)}, u32[]{:S(2)}) collective-permute-start(bf16[1,80,1024]{2,1,0:T(8,128)(2,1)S(1)} %dynamic-slice_bitcast_fusion), channel_id=1, source_target_pairs={{0,8},{4,12},{8,0},{12,4},{1,9},{5,13},{9,1},{13,5},{2,10},{6,14},... | collective-permute-start | bytes 491528 | tf_op jit(solution)/shard_map/ppermute | solution.py:26
  34.7 19.7 %collective-permute-start.6 = (bf16[2,96,1280]{2,1,0:T(8,128)(2,1)S(1)}, bf16[2,96,1280]{2,1,0:T(8,128)(2,1)S(1)}, u32[]{:S(2)}, u32[]{:S(2)}) collective-permute-start(bf16[2,96,1280]{2,1,0:T(8,128)(2,1)S(1)} %get-tuple-element.74), channel_id=1, source_target_pairs={{0,2},{2,0},{1,3},{3,1},{4,6},{6,4},{5,7},{7,5},{8,10},{10,8},{9,1... | collective-permute-start | bytes 1474568 | tf_op jit(solution)/shard_map/ppermute | solution.py:22
  46.7 28.0 %collective-permute-start.7 = (bf16[2,96,2304]{2,1,0:T(8,128)(2,1)S(1)}, bf16[2,96,2304]{2,1,0:T(8,128)(2,1)S(1)}, u32[]{:S(2)}, u32[]{:S(2)}) collective-permute-start(bf16[2,96,2304]{2,1,0:T(8,128)(2,1)S(1)} %get-tuple-element.76), channel_id=1, source_target_pairs={{0,2},{2,0},{1,3},{3,1},{4,6},{6,4},{5,7},{7,5},{8,10},{10,8},{9,1... | collective-permute-start | bytes 2654216 | tf_op jit(solution)/shard_map/ppermute | solution.py:22
  54.8 19.8 %collective-permute-start.11 = (bf16[2,80,1024]{2,1,0:T(8,128)(2,1)S(1)}, bf16[2,80,1024]{2,1,0:T(8,128)(2,1)S(1)}, u32[]{:S(2)}, u32[]{:S(2)}) collective-permute-start(bf16[2,80,1024]{2,1,0:T(8,128)(2,1)S(1)} %pad_maximum_fusion.8), channel_id=1, source_target_pairs={{2,0},{0,2},{3,1},{1,3},{6,4},{4,6},{7,5},{5,7},{10,8},{8,10},{11,... | collective-permute-start | bytes 983048 | tf_op jit(solution)/shard_map/ppermute | solution.py:18
  56.6 17.9 %collective-permute-start.12 = (f32[80]{0:T(128)S(1)}, f32[80]{0:T(128)S(1)}, u32[]{:S(2)}, u32[]{:S(2)}) collective-permute-start(f32[80]{0:T(128)S(1)} %get-tuple-element.152), channel_id=1, source_target_pairs={{2,0},{0,2},{3,1},{1,3},{6,4},{4,6},{7,5},{5,7},{10,8},{8,10},{11,... | collective-permute-start | bytes 968 | tf_op jit(solution)/shard_map/ppermute | solution.py:18
  75.2 18.1 %collective-permute-start.8 = (bf16[96,3584]{1,0:T(8,128)(2,1)S(1)}, bf16[96,3584]{1,0:T(8,128)(2,1)S(1)}, u32[]{:S(2)}, u32[]{:S(2)}) collective-permute-start(bf16[96,3584]{1,0:T(8,128)(2,1)S(1)} %pad_maximum_fusion.refs_1_.refs_0_), channel_id=1, source_target_pairs={{2,0},{0,2},{3,1},{1,3},{6,4},{4,6},{7,5},{5,7},{10,8},{8,10},{11,... | collective-permute-start | bytes 2064392 | tf_op jit(solution)/shard_map/ppermute | solution.py:18
  92.7 32.3 %collective-permute-start.18 = (bf16[2,96,3584]{2,1,0:T(8,128)(2,1)S(1)}, bf16[2,96,3584]{2,1,0:T(8,128)(2,1)S(1)}, u32[]{:S(2)}, u32[]{:S(2)}) collective-permute-start(bf16[2,96,3584]{2,1,0:T(8,128)(2,1)S(1)} %get-tuple-element.92), channel_id=1, source_target_pairs={{0,2},{2,0},{1,3},{3,1},{4,6},{6,4},{5,7},{7,5},{8,10},{10,8},{9,1... | collective-permute-start | bytes 4128776 | tf_op jit(solution)/shard_map/ppermute | solution.py:22
  99.6 11.0 %collective-permute-start.15 = (bf16[96,2048]{1,0:T(8,128)(2,1)S(1)}, bf16[96,2048]{1,0:T(8,128)(2,1)S(1)}, u32[]{:S(2)}, u32[]{:S(2)}) collective-permute-start(bf16[96,2048]{1,0:T(8,128)(2,1)S(1)} %get-tuple-element.87), channel_id=1, source_target_pairs={{0,4},{4,0},{8,12},{12,8},{1,5},{5,1},{9,13},{13,9},{2,6},{6,2},{1... | collective-permute-start | bytes 1179656 | tf_op jit(solution)/shard_map/ppermute | solution.py:26
  110.7 11.1 %collective-permute-start.16 = (bf16[48,2048]{1,0:T(8,128)(2,1)S(1)}, bf16[48,2048]{1,0:T(8,128)(2,1)S(1)}, u32[]{:S(2)}, u32[]{:S(2)}) collective-permute-start(bf16[48,2048]{1,0:T(8,128)(2,1)S(1)} %slice.231.refs_1_), channel_id=1, source_target_pairs={{0,8},{4,12},{8,0},{12,4},{1,9},{5,13},{9,1},{13,5},{2,10},{6,14},... | collective-permute-start | bytes 589832 | tf_op jit(solution)/shard_map/ppermute | solution.py:26
  125.7 17.3 %collective-permute-start.19 = (bf16[96,3584]{1,0:T(8,128)(2,1)S(1)}, bf16[96,3584]{1,0:T(8,128)(2,1)S(1)}, u32[]{:S(2)}, u32[]{:S(2)}) collective-permute-start(bf16[96,3584]{1,0:T(8,128)(2,1)S(1)} %fusion.1.refs_2_.refs_0_), channel_id=1, source_target_pairs={{2,0},{0,2},{3,1},{1,3},{6,4},{4,6},{7,5},{5,7},{10,8},{8,10},{11,... | collective-permute-start | bytes 2064392 | tf_op jit(solution)/shard_map/ppermute | solution.py:18
  126.4 15.6 %collective-permute-start.17 = (bf16[48,2048]{1,0:T(8,128)(2,1)S(1)}, bf16[48,2048]{1,0:T(8,128)(2,1)S(1)}, u32[]{:S(2)}, u32[]{:S(2)}) collective-permute-start(bf16[48,2048]{1,0:T(8,128)(2,1)S(1)} %add_convert_fusion.1.refs_3_), channel_id=1, source_target_pairs={{0,8},{4,12},{8,0},{12,4},{1,9},{5,13},{9,1},{13,5},{2,10},{6,14},... | collective-permute-start | bytes 589832 | tf_op jit(solution)/shard_map/ppermute | solution.py:26
  140.5 21.7 %collective-permute-start.22 = (bf16[2,64,3584]{2,1,0:T(8,128)(2,1)S(1)}, bf16[2,64,3584]{2,1,0:T(8,128)(2,1)S(1)}, u32[]{:S(2)}, u32[]{:S(2)}) collective-permute-start(bf16[2,64,3584]{2,1,0:T(8,128)(2,1)S(1)} %get-tuple-element.101), channel_id=1, source_target_pairs={{0,2},{2,0},{1,3},{3,1},{4,6},{6,4},{5,7},{7,5},{8,10},{10,8},{9,1... | collective-permute-start | bytes 2752520 | tf_op jit(solution)/shard_map/ppermute | solution.py:22
  143.1 10.7 %collective-permute-start.20 = (bf16[96,2048]{1,0:T(8,128)(2,1)S(1)}, bf16[96,2048]{1,0:T(8,128)(2,1)S(1)}, u32[]{:S(2)}, u32[]{:S(2)}) collective-permute-start(bf16[96,2048]{1,0:T(8,128)(2,1)S(1)} %constant_dynamic-update-slice_fusion.refs_4_.near_ref), channel_id=1, source_target_pairs={{0,4},{4,0},{8,12},{12,8},{1,5},{5,1},{9,13},{13,9},{2,6},{6,2},{1... | collective-permute-start | bytes 1179656 | tf_op jit(solution)/shard_map/ppermute | solution.py:26
  150.1 11.5 %collective-permute-start.24 = (bf16[96,2048]{1,0:T(8,128)(2,1)S(1)}, bf16[96,2048]{1,0:T(8,128)(2,1)S(1)}, u32[]{:S(2)}, u32[]{:S(2)}) collective-permute-start(bf16[96,2048]{1,0:T(8,128)(2,1)S(1)} %get-tuple-element.104), channel_id=1, source_target_pairs={{0,4},{4,0},{8,12},{12,8},{1,5},{5,1},{9,13},{13,9},{2,6},{6,2},{1... | collective-permute-start | bytes 1179656 | tf_op jit(solution)/shard_map/ppermute | solution.py:26
  164.2 10.6 %collective-permute-start.23 = (bf16[64,3584]{1,0:T(8,128)(2,1)S(1)}, bf16[64,3584]{1,0:T(8,128)(2,1)S(1)}, u32[]{:S(2)}, u32[]{:S(2)}) collective-permute-start(bf16[64,3584]{1,0:T(8,128)(2,1)S(1)} %fusion.3.refs_0_.refs_4_), channel_id=1, source_target_pairs={{2,0},{0,2},{3,1},{1,3},{6,4},{4,6},{7,5},{5,7},{10,8},{8,10},{11,... | collective-permute-start | bytes 1376264 | tf_op jit(solution)/shard_map/ppermute | solution.py:18
  173.3 22.2 %collective-permute-start.21 = (bf16[96,4096]{1,0:T(8,128)(2,1)S(1)}, bf16[96,4096]{1,0:T(8,128)(2,1)S(1)}, u32[]{:S(2)}, u32[]{:S(2)}) collective-permute-start(bf16[96,4096]{1,0:T(8,128)(2,1)S(1)} %get-tuple-element.100), channel_id=1, source_target_pairs={{0,1},{1,0},{2,3},{3,2},{4,5},{5,4},{6,7},{7,6},{8,9},{9,8},{10,11... | collective-permute-start | bytes 2359304 | tf_op jit(solution)/shard_map/ppermute | solution.py:22
  183.0 12.2 %collective-permute-start.31 = (bf16[32,2048]{1,0:T(8,128)(2,1)S(1)}, bf16[32,2048]{1,0:T(8,128)(2,1)S(1)}, u32[]{:S(2)}, u32[]{:S(2)}) collective-permute-start(bf16[32,2048]{1,0:T(8,128)(2,1)S(1)} %get-tuple-element.149), channel_id=1, source_target_pairs={{0,4},{4,0},{8,12},{12,8},{1,5},{5,1},{9,13},{13,9},{2,6},{6,2},{1... | collective-permute-start | bytes 393224 | tf_op jit(solution)/shard_map/ppermute | solution.py:26
  187.5 19.3 %collective-permute-start.28 = (bf16[96,2048]{1,0:T(8,128)(2,1)S(1)}, bf16[96,2048]{1,0:T(8,128)(2,1)S(1)}, u32[]{:S(2)}, u32[]{:S(2)}) collective-permute-start(bf16[96,2048]{1,0:T(8,128)(2,1)S(1)} %constant_dynamic-update-slice_fusion.2.near_ref.refs_3_), channel_id=1, source_target_pairs={{0,4},{4,0},{8,12},{12,8},{1,5},{5,1},{9,13},{13,9},{2,6},{6,2},{1... | collective-permute-start | bytes 1179656 | tf_op jit(solution)/shard_map/ppermute | solution.py:26
  195.7 11.1 %collective-permute-start.26 = (bf16[48,4096]{1,0:T(8,128)(2,1)S(1)}, bf16[48,4096]{1,0:T(8,128)(2,1)S(1)}, u32[]{:S(2)}, u32[]{:S(2)}) collective-permute-start(bf16[48,4096]{1,0:T(8,128)(2,1)S(1)} %slice.228.refs_1_), channel_id=1, source_target_pairs={{0,2},{2,0},{1,3},{3,1},{4,6},{6,4},{5,7},{7,5},{8,10},{10,8},{9,1... | collective-permute-start | bytes 1179656 | tf_op jit(solution)/shard_map/ppermute | solution.py:22
  196.3 18.2 %collective-permute-start.35 = (bf16[32,2048]{1,0:T(8,128)(2,1)S(1)}, bf16[32,2048]{1,0:T(8,128)(2,1)S(1)}, u32[]{:S(2)}, u32[]{:S(2)}) collective-permute-start(bf16[32,2048]{1,0:T(8,128)(2,1)S(1)} %add_convert_fusion.2.refs_2_), channel_id=1, source_target_pairs={{0,12},{4,8},{8,4},{12,0},{1,13},{5,9},{9,5},{13,1},{2,14},{6,10},... | collective-permute-start | bytes 393224 | tf_op jit(solution)/shard_map/ppermute | solution.py:26
  197.9 16.6 %collective-permute-start.34 = (bf16[32,2048]{1,0:T(8,128)(2,1)S(1)}, bf16[32,2048]{1,0:T(8,128)(2,1)S(1)}, u32[]{:S(2)}, u32[]{:S(2)}) collective-permute-start(bf16[32,2048]{1,0:T(8,128)(2,1)S(1)} %add_convert_fusion.2.refs_2_), channel_id=1, source_target_pairs={{0,8},{4,12},{8,0},{12,4},{1,9},{5,13},{9,1},{13,5},{2,10},{6,14},... | collective-permute-start | bytes 393224 | tf_op jit(solution)/shard_map/ppermute | solution.py:26
  200.4 14.1 %collective-permute-start.33 = (bf16[32,2048]{1,0:T(8,128)(2,1)S(1)}, bf16[32,2048]{1,0:T(8,128)(2,1)S(1)}, u32[]{:S(2)}, u32[]{:S(2)}) collective-permute-start(bf16[32,2048]{1,0:T(8,128)(2,1)S(1)} %add_convert_fusion.2.refs_2_), channel_id=1, source_target_pairs={{0,4},{4,0},{8,12},{12,8},{1,5},{5,1},{9,13},{13,9},{2,6},{6,2},{1... | collective-permute-start | bytes 393224 | tf_op jit(solution)/shard_map/ppermute | solution.py:26
  223.7 12.0 %collective-permute-start.36 = (bf16[48,4096]{1,0:T(8,128)(2,1)S(1)}, bf16[48,4096]{1,0:T(8,128)(2,1)S(1)}, u32[]{:S(2)}, u32[]{:S(2)}) collective-permute-start(bf16[48,4096]{1,0:T(8,128)(2,1)S(1)} %slice.227), channel_id=1, source_target_pairs={{0,2},{2,0},{1,3},{3,1},{4,6},{6,4},{5,7},{7,5},{8,10},{10,8},{9,1... | collective-permute-start | bytes 1179656 | tf_op jit(solution)/shard_map/ppermute | solution.py:22
  224.2 16.6 %collective-permute-start.38 = (bf16[32,4096]{1,0:T(8,128)(2,1)S(1)}, bf16[32,4096]{1,0:T(8,128)(2,1)S(1)}, u32[]{:S(2)}, u32[]{:S(2)}) collective-permute-start(bf16[32,4096]{1,0:T(8,128)(2,1)S(1)} %slice.229), channel_id=1, source_target_pairs={{0,2},{2,0},{1,3},{3,1},{4,6},{6,4},{5,7},{7,5},{8,10},{10,8},{9,1... | collective-permute-start | bytes 786440 | tf_op jit(solution)/shard_map/ppermute | solution.py:22
  (27 other events, 186.2 us)

commit v11 on v10

--- a/solution.py
+++ b/solution.py
@@ -12,6 +12,7 @@
 VMEM_BYTES = 51 * 1024 * 1024
 GATE_UP_VMEM_BYTES = 44 * 1024 * 1024
 BUFFERS = 8
+GATE_UP_BUFFERS = 4
 
 
 def shift(value, axis, size, hop):
@@ -45,12 +46,8 @@
     return pl.BlockSpec(shape, lambda j, *_: (0,) * len(shape))
 
 
-def slots_of(tiles):
-    return min(BUFFERS, tiles)
-
-
-def slots(depth, tile, tiles):
-    count = slots_of(tiles)
+def slots(depth, tile, tiles, most=BUFFERS):
+    count = min(most, tiles)
     return [pltpu.VMEM((count, depth, tile), BF16), pltpu.SemaphoreType.DMA((count,))]
 
 
@@ -134,7 +131,7 @@
         out_specs=[pl.BlockSpec((2, own_rows, tile), lambda j: (0, 0, j))] * owners,
         out_shape=[jax.ShapeDtypeStruct((2, own_rows, width), F32)]
         + [jax.ShapeDtypeStruct((2, own_rows, width), BF16)] * (owners - 1),
-        scratch_shapes=[pltpu.VMEM((rows, depth), BF16)] + slots(depth, tile, tiles) * 2,
+        scratch_shapes=[pltpu.VMEM((rows, depth), BF16)] + slots(depth, tile, tiles, GATE_UP_BUFFERS) * 2,
         compiler_params=params(GATE_UP_VMEM_BYTES),
         cost_estimate=NO_COST,
     )(x, gate_weight, up_weight, *after)
@@ -220,8 +217,9 @@
     width = enc_weight.shape[2]
     rows_each = rows // members
     tile = tile_of(width, 512)
+    tiles = width // tile
     return pl.pallas_call(
-        functools.partial(encode_body, members, order, width // tile),
+        functools.partial(encode_body, members, order, tiles),
         grid_spec=pltpu.PrefetchScalarGridSpec(
             num_scalar_prefetch=1,
             grid=(width // tile,),
@@ -309,39 +307,38 @@
     head = sizes[0]
 
     gathered = own_tokens[:head][None]
+    rest = own_tokens[head:][None] if chunks > 1 else None
     for bit in bits:
         gathered = doubled(gathered, bit)
+        if rest is not None:
+            rest = doubled(after(rest, gathered), bit)
     columns, inverse = from_owners(gathered)
+    if rest is not None:
+        rest = from_owners(after(rest, (columns, inverse)))
     inverses = from_all(inverse, "rows", owners)
     columns, inverses = after((columns, inverses), (columns, inverses))
     xs = [normed(from_members(columns), from_all(inverses, "mp", members))]
-    rest = None
-    if chunks > 1:
-        rest = after(own_tokens[head:][None], gathered)
-        rest = [rest, swap(rest, "hid", ranks, bits[0])]
 
     sums, hidden, layer, blocks, outs = ({} for _ in range(5))
     last = []
 
     def gate_up_of(t):
         tiles = gate_weight.shape[2] // tile_of(gate_weight.shape[2], 256)
-        early = tiles * 5 // 14 if t == 0 and chunks > 1 else 0
+        early = tiles * 3 // 7 if t == 0 and chunks > 1 else 0
         sums[t] = []
         for first, count in ((0, early), (early, tiles - early)):
             if not count:
                 continue
             own, *sends = gate_up(xs[t], gate_weight, up_weight, first, count, list(last))
             last[:] = [own]
+            if t == 0 and rest is not None:
+                last.extend(rest[0])
             others = [send(sends[hop - 1], "rows", owners, hop) for hop in range(1, owners)]
             sums[t].append((own, others))
 
-    def rest_of(units):
-        gathered = jnp.concatenate(after(rest, sums[0][-1][0]))
-        for bit in bits[1:]:
-            gathered = doubled(after(gathered, sums[0][-1][0]), bit)
-        gathered = after(gathered, units)
-        columns, inverse = from_owners(gathered)
-        inverses = from_all(inverse, "rows", owners)
+    def rest_of():
+        columns, inverse = rest
+        inverses = from_all(after(inverse, sums[0][-1][0]), "rows", owners)
         columns, inverses = after((columns, inverses), (columns, inverses))
         columns, inverses = from_members(columns), from_all(inverses, "mp", members)
         for start, q in zip(starts[1:], sizes[1:]):
@@ -356,8 +353,8 @@
             for other in others:
                 acts = acts + other.astype(F32)
             units.append((jax.nn.silu(acts[0]) * acts[1]).astype(BF16))
-            if t == 0 and chunks > 1 and len(units) == 1:
-                rest_of(units[0])
+        if t == 0 and rest is not None:
+            rest_of()
         units = jnp.concatenate(units, axis=1)
         hidden[t] = [units] + [shift(units, "rows", owners, hop) for hop in range(1, owners)]
         last.append(units)

time: 242 us -> 255 us (1.054)
  waiting for transfers between devices: 108 us -> 117 us
  starting transfers between devices: 42.3 us -> 48.1 us
  Pallas kernels: 80.9 us -> 78 us
    ppermute x10, waiting for transfers between devices: 19.7 us -> 31.1 us  [send(): lax.ppermute(value, axis, [(d, (d + hop) % size) for d in range(size)])]
    ppermute x18, starting transfers between devices: 26.4 us -> 33.1 us  [swap(): return lax.ppermute(value, axis, [(d, d ^ bit) for d in range(size)])]
    ppermute x18, waiting for transfers between devices: 62.7 us -> 57.9 us  [swap(): return lax.ppermute(value, axis, [(d, d ^ bit) for d in range(size)])]
    pallas_call x4, Pallas kernels: 40.5 us -> 37.5 us  [gate_up(): pl.pallas_call(functools.partial(gate_up_body, tiles, first), grid=(tiles...]
    ppermute x11, waiting for transfers between devices: 25.6 us -> 28.5 us  [shift(): lax.ppermute(value, axis, [((d + hop) % size, d) for d in range(size)])]
  transfers between devices with their start and end apart: 39 -> 39, of which waited for: 23 -> 26; matrix products, arithmetic and copies ran while one was open for 1% -> 2% of each run, Pallas kernels for 33% -> 28%
where the time goes in v11:
time: 255 us
  waiting for transfers between devices  117 us (46%)
  Pallas kernels  78 us (31%)
  starting transfers between devices  48.1 us (19%)
  other arithmetic  5.41 us (2%)
  local copies, waits for them, and re-layouts  5.08 us (2%)
    ppermute x18, waiting for transfers between devices, swap(): return lax.ppermute(value, axis, [(d, d ^ bit) for d in range(size)])  57.9 us
    pallas_call x4, Pallas kernels, gate_up(): pl.pallas_call(functools.partial(gate_up_body, tiles, first), grid=(tiles...  37.5 us
    ppermute x18, starting transfers between devices, swap(): return lax.ppermute(value, axis, [(d, d ^ bit) for d in range(size)])  33.1 us
    ppermute x10, waiting for transfers between devices, send(): lax.ppermute(value, axis, [(d, (d + hop) % size) for d in range(size)])  31.1 us
    ppermute x11, waiting for transfers between devices, shift(): lax.ppermute(value, axis, [((d + hop) % size, d) for d in range(size)])  28.5 us
    pallas_call x3, Pallas kernels, encode(): pl.pallas_call(functools.partial(encode_body, members, order, tiles), gri...  22 us
    pallas_call x3, Pallas kernels, down(): pl.pallas_call(functools.partial(down_body, owners, members, pieces, orde...  18.4 us
    ppermute x11, starting transfers between devices, shift(): lax.ppermute(value, axis, [((d + hop) % size, d) for d in range(size)])  7.82 us
  transfers between devices with their start and end apart: 39, of which 26 were waited for; matrix products, arithmetic and copies ran while one was open for 2% of the time, Pallas kernels for 28%

profile of v11, /device:TPU:0, one launch (start us, length us, event | category | flops | bytes accessed | tf_op | source)
XLA Modules:
  0.0 254.6 jit_solution(10703587953462614212)
XLA Ops:
  1.1 4.1 %collective-permute-start = (bf16[1,48,1024]{2,1,0:T(8,128)(2,1)S(1)}, bf16[1,48,1024]{2,1,0:T(8,128)(2,1)S(1)}, u32[]{:S(2)}, u32[]{:S(2)}) collective-permute-start(bf16[1,48,1024]{2,1,0:T(8,128)(2,1)S(1)} %dynamic-slice_bitcast_fusion.1), channel_id=1, source_target_pairs={{0,8},{4,12},{8,0},{12,4},{1,9},{5,13},{9,1},{13,5},{2,10},{6,14},... | collective-permute-start | bytes 294920 | tf_op jit(solution)/shard_map/ppermute | solution.py:27
  5.2 4.9 %collective-permute-done = bf16[1,48,1024]{2,1,0:T(8,128)(2,1)S(1)} collective-permute-done((bf16[1,48,1024]{2,1,0:T(8,128)(2,1)S(1)}, bf16[1,48,1024]{2,1,0:T(8,128)(2,1)S(1)}, u32[]{:S(2)}, u32[]{:S(2)}) %collective-permute-start) | collective-permute-done | bytes 98336 | tf_op jit(solution)/shard_map/ppermute | solution.py:27
  15.0 5.1 %collective-permute-done.7 = bf16[1,80,1024]{2,1,0:T(8,128)(2,1)S(1)} collective-permute-done((bf16[1,80,1024]{2,1,0:T(8,128)(2,1)S(1)}, bf16[1,80,1024]{2,1,0:T(8,128)(2,1)S(1)}, u32[]{:S(2)}, u32[]{:S(2)}) %collective-permute-start.7) | collective-permute-done | bytes 163872 | tf_op jit(solution)/shard_map/ppermute | solution.py:27
  24.6 3.8 %collective-permute-done.2 = bf16[2,48,1024]{2,1,0:T(8,128)(2,1)S(1)} collective-permute-done((bf16[2,48,1024]{2,1,0:T(8,128)(2,1)S(1)}, bf16[2,48,1024]{2,1,0:T(8,128)(2,1)S(1)}, u32[]{:S(2)}, u32[]{:S(2)}) %collective-permute-start.2) | collective-permute-done | bytes 196640 | tf_op jit(solution)/shard_map/ppermute | solution.py:19
  31.7 6.6 %shard_map.82 = (f32[2,96,1536]{2,1,0:T(8,128)S(1)}, bf16[2,96,1536]{2,1,0:T(8,128)(2,1)S(1)}) custom-call(bf16[2,2,2,48,1024]{4,3,2,1,0:T(8,128)(2,1)S(1)} %multiply_convert_fusion.1.x_ref, bf16[1,2048,3584]{2,1,0:T(8,128)(2,1)} %gate_ref.7, bf16[1,2048,3584]{2,1,0:T(8,128)(2,1)} %up_ref.7), custom_call_target="tpu_custom_call" | custom-call | flops 1 | bytes 1 | tf_op jit(solution)/shard_map/pallas_call | solution.py:127
  40.6 19.4 %collective-permute-done.9.refs_2_ = bf16[2,80,1024]{2,1,0:T(8,128)(2,1)S(1)} collective-permute-done((bf16[2,80,1024]{2,1,0:T(8,128)(2,1)S(1)}, bf16[2,80,1024]{2,1,0:T(8,128)(2,1)S(1)}, u32[]{:S(2)}, u32[]{:S(2)}) %collective-permute-start.9) | collective-permute-done | bytes 327712 | tf_op jit(solution)/shard_map/ppermute | solution.py:19
  60.0 7.8 %shard_map.83 = (f32[2,96,2048]{2,1,0:T(8,128)S(1)}, bf16[2,96,2048]{2,1,0:T(8,128)(2,1)S(1)}) custom-call(bf16[2,2,2,48,1024]{4,3,2,1,0:T(8,128)(2,1)S(1)} %multiply_convert_fusion.1.x_ref, bf16[1,2048,3584]{2,1,0:T(8,128)(2,1)} %gate_ref.7, bf16[1,2048,3584]{2,1,0:T(8,128)(2,1)} %up_ref.7, f32[2,96,1536]{2,1,0:T(8,128)S(1)} %get-tuple-element.72.refs_0_, ...), custom_call_target="tpu_custom_call" | custom-call | flops 1 | bytes 1 | tf_op jit(solution)/shard_map/pallas_call | solution.py:127
  72.0 14.0 %collective-permute-done.10 = bf16[2,96,2048]{2,1,0:T(8,128)(2,1)S(1)} collective-permute-done((bf16[2,96,2048]{2,1,0:T(8,128)(2,1)S(1)}, bf16[2,96,2048]{2,1,0:T(8,128)(2,1)S(1)}, u32[]{:S(2)}, u32[]{:S(2)}) %collective-permute-start.10) | collective-permute-done | bytes 786464 | tf_op jit(solution)/shard_map/ppermute | solution.py:23
  89.5 11.7 %shard_map.84 = (f32[2,96,3584]{2,1,0:T(8,128)S(1)}, bf16[2,96,3584]{2,1,0:T(8,128)(2,1)S(1)}) custom-call(bf16[2,2,2,48,1024]{4,3,2,1,0:T(8,128)(2,1)S(1)} %multiply_convert_fusion.x_ref, bf16[1,2048,3584]{2,1,0:T(8,128)(2,1)} %gate_ref.7, bf16[1,2048,3584]{2,1,0:T(8,128)(2,1)} %up_ref.7, f32[2,96,2048]{2,1,0:T(8,128)S(1)} %get-tuple-element.77.refs_0_, ...), custom_call_target="tpu_custom_call" | custom-call | flops 1 | bytes 1 | tf_op jit(solution)/shard_map/pallas_call | solution.py:127
  103.3 6.3 %shard_map.85 = (f32[96,2048]{1,0:T(8,128)S(1)}, bf16[96,2048]{1,0:T(8,128)(2,1)S(1)}) custom-call(s32[1]{0:T(128)} %bitcast.rank_ref, bf16[96,3584]{1,0:T(8,128)(2,1)S(1)} %pad_maximum_fusion.refs_3_.refs_0_, bf16[96,3584]{1,0:T(8,128)(2,1)S(1)} %collective-permute-done.11.refs_1_, bf16[1,3584,2048]{2,1,0:T(8,128)(2,1)} %refs_2_.5, f32[2,96,3584]{2,1,0:T(8,128)} %copy-done.2), custom_call_target="tpu_custom_call" | custom-call | flops 1 | bytes 1 | tf_op jit(solution)/shard_map/pallas_call | solution.py:175
  112.7 9.2 %collective-permute-done.15 = bf16[96,2048]{1,0:T(8,128)(2,1)S(1)} collective-permute-done((bf16[96,2048]{1,0:T(8,128)(2,1)S(1)}, bf16[96,2048]{1,0:T(8,128)(2,1)S(1)}, u32[]{:S(2)}, u32[]{:S(2)}) %collective-permute-start.15) | collective-permute-done | bytes 393248 | tf_op jit(solution)/shard_map/ppermute | solution.py:27
  125.7 8.2 %collective-permute-done.16 = bf16[48,2048]{1,0:T(8,128)(2,1)S(1)} collective-permute-done((bf16[48,2048]{1,0:T(8,128)(2,1)S(1)}, bf16[48,2048]{1,0:T(8,128)(2,1)S(1)}, u32[]{:S(2)}, u32[]{:S(2)}) %collective-permute-start.16) | collective-permute-done | bytes 196640 | tf_op jit(solution)/shard_map/ppermute | solution.py:27
  136.3 5.0 %collective-permute-start.17 = (bf16[48,2048]{1,0:T(8,128)(2,1)S(1)}, bf16[48,2048]{1,0:T(8,128)(2,1)S(1)}, u32[]{:S(2)}, u32[]{:S(2)}) collective-permute-start(bf16[48,2048]{1,0:T(8,128)(2,1)S(1)} %add_convert_fusion.1.refs_3_), channel_id=1, source_target_pairs={{0,8},{4,12},{8,0},{12,4},{1,9},{5,13},{9,1},{13,5},{2,10},{6,14},... | collective-permute-start | bytes 589832 | tf_op jit(solution)/shard_map/ppermute | solution.py:27
  141.5 11.4 %shard_map.86 = (f32[2,64,3584]{2,1,0:T(8,128)S(1)}, bf16[2,64,3584]{2,1,0:T(8,128)(2,1)S(1)}) custom-call(bf16[2,2,2,32,1024]{4,3,2,1,0:T(8,128)(2,1)S(1)} %multiply_convert_fusion.2.x_ref, bf16[1,2048,3584]{2,1,0:T(8,128)(2,1)} %gate_ref.7, bf16[1,2048,3584]{2,1,0:T(8,128)(2,1)} %up_ref.7, f32[96,2048]{1,0:T(8,128)S(1)} %get-tuple-element.86.refs_0_, ...), custom_call_target="tpu_custom_call" | custom-call | flops 1 | bytes 1 | tf_op jit(solution)/shard_map/pallas_call | solution.py:127
  156.1 6.3 %shard_map.87 = (f32[96,2048]{1,0:T(8,128)S(1)}, bf16[96,2048]{1,0:T(8,128)(2,1)S(1)}) custom-call(s32[1]{0:T(128)} %bitcast.rank_ref, bf16[96,3584]{1,0:T(8,128)(2,1)S(1)} %fusion.1.refs_2_.refs_0_, bf16[96,3584]{1,0:T(8,128)(2,1)S(1)} %collective-permute-done.19.refs_1_, bf16[1,3584,2048]{2,1,0:T(8,128)(2,1)} %refs_2_.5, f32[2,64,3584]{2,1,0:T(8,128)} %copy-done.4, ...), custom_call_target="tpu_custom_call" | custom-call | flops 1 | bytes 1 | tf_op jit(solution)/shard_map/pallas_call | solution.py:175
  167.2 7.8 %shard_map.88 = (f32[96,4096]{1,0:T(8,128)}, bf16[96,4096]{1,0:T(8,128)(2,1)S(1)}) custom-call(s32[1]{0:T(128)} %bitcast.rank_ref, bf16[96,2048]{1,0:T(8,128)(2,1)S(1)} %constant_dynamic-update-slice_fusion.refs_4_.near_ref, bf16[96,2048]{1,0:T(8,128)(2,1)S(1)} %collective-permute-done.20.far_ref, bf16[1,2048,4096]{2,1,0:T(8,128)(2,1)} %weight_ref.5, ...), custom_call_target="tpu_custom_call" | custom-call | flops 1 | bytes 1 | tf_op jit(solution)/shard_map/pallas_call | solution.py:221
  178.2 9.4 %collective-permute-done.25 = bf16[48,2048]{1,0:T(8,128)(2,1)S(1)} collective-permute-done((bf16[48,2048]{1,0:T(8,128)(2,1)S(1)}, bf16[48,2048]{1,0:T(8,128)(2,1)S(1)}, u32[]{:S(2)}, u32[]{:S(2)}) %collective-permute-start.25) | collective-permute-done | bytes 196640 | tf_op jit(solution)/shard_map/ppermute | solution.py:27
  188.5 5.9 %shard_map.89 = (f32[64,2048]{1,0:T(8,128)S(1)}, bf16[64,2048]{1,0:T(8,128)(2,1)S(1)}) custom-call(s32[1]{0:T(128)} %bitcast.rank_ref, bf16[64,3584]{1,0:T(8,128)(2,1)S(1)} %fusion.3.refs_0_.refs_4_, bf16[64,3584]{1,0:T(8,128)(2,1)S(1)} %collective-permute-done.23.refs_1_, bf16[1,3584,2048]{2,1,0:T(8,128)(2,1)} %refs_2_.5, ...), custom_call_target="tpu_custom_call" | custom-call | flops 1 | bytes 1 | tf_op jit(solution)/shard_map/pallas_call | solution.py:175
  201.4 5.2 %collective-permute-done.30 = bf16[32,2048]{1,0:T(8,128)(2,1)S(1)} collective-permute-done((bf16[32,2048]{1,0:T(8,128)(2,1)S(1)}, bf16[32,2048]{1,0:T(8,128)(2,1)S(1)}, u32[]{:S(2)}, u32[]{:S(2)}) %collective-permute-start.30) | collective-permute-done | bytes 131104 | tf_op jit(solution)/shard_map/ppermute | solution.py:27
  213.6 6.3 %collective-permute-done.28.far_ref = bf16[96,2048]{1,0:T(8,128)(2,1)S(1)} collective-permute-done((bf16[96,2048]{1,0:T(8,128)(2,1)S(1)}, bf16[96,2048]{1,0:T(8,128)(2,1)S(1)}, u32[]{:S(2)}, u32[]{:S(2)}) %collective-permute-start.28) | collective-permute-done | bytes 393248 | tf_op jit(solution)/shard_map/ppermute | solution.py:27
  219.9 7.6 %shard_map.90 = (f32[96,4096]{1,0:T(8,128)}, bf16[96,4096]{1,0:T(8,128)(2,1)S(1)}) custom-call(s32[1]{0:T(128)} %bitcast.rank_ref, bf16[96,2048]{1,0:T(8,128)(2,1)S(1)} %constant_dynamic-update-slice_fusion.2.near_ref.refs_3_, bf16[96,2048]{1,0:T(8,128)(2,1)S(1)} %collective-permute-done.28.far_ref, bf16[1,2048,4096]{2,1,0:T(8,128)(2,1)} %weight_ref.5, ...), custom_call_target="tpu_custom_call" | custom-call | flops 1 | bytes 1 | tf_op jit(solution)/shard_map/pallas_call | solution.py:221
  227.7 6.6 %shard_map.91 = (f32[64,4096]{1,0:T(8,128)S(1)}, bf16[64,4096]{1,0:T(8,128)(2,1)S(1)}) custom-call(s32[1]{0:T(128)} %bitcast.rank_ref, bf16[64,2048]{1,0:T(8,128)(2,1)S(1)} %get-tuple-element.151.near_ref, bf16[64,2048]{1,0:T(8,128)(2,1)S(1)} %get-tuple-element.152.far_ref, bf16[1,2048,4096]{2,1,0:T(8,128)(2,1)} %weight_ref.5, ...), custom_call_target="tpu_custom_call" | custom-call | flops 1 | bytes 1 | tf_op jit(solution)/shard_map/pallas_call | solution.py:221
  239.0 9.7 %collective-permute-done.36 = bf16[48,4096]{1,0:T(8,128)(2,1)S(1)} collective-permute-done((bf16[48,4096]{1,0:T(8,128)(2,1)S(1)}, bf16[48,4096]{1,0:T(8,128)(2,1)S(1)}, u32[]{:S(2)}, u32[]{:S(2)}) %collective-permute-start.36) | collective-permute-done | bytes 393248 | tf_op jit(solution)/shard_map/ppermute | solution.py:23
  248.9 4.9 %collective-permute-done.38 = bf16[32,4096]{1,0:T(8,128)(2,1)S(1)} collective-permute-done((bf16[32,4096]{1,0:T(8,128)(2,1)S(1)}, bf16[32,4096]{1,0:T(8,128)(2,1)S(1)}, u32[]{:S(2)}, u32[]{:S(2)}) %collective-permute-start.38) | collective-permute-done | bytes 262176 | tf_op jit(solution)/shard_map/ppermute | solution.py:23
  (149 shorter events, 67.0 us)
Async XLA Ops:
  38.4 33.3 %collective-permute-start.6 = (bf16[2,96,1536]{2,1,0:T(8,128)(2,1)S(1)}, bf16[2,96,1536]{2,1,0:T(8,128)(2,1)S(1)}, u32[]{:S(2)}, u32[]{:S(2)}) collective-permute-start(bf16[2,96,1536]{2,1,0:T(8,128)(2,1)S(1)} %get-tuple-element.73), channel_id=1, source_target_pairs={{0,2},{2,0},{1,3},{3,1},{4,6},{6,4},{5,7},{7,5},{8,10},{10,8},{9,1... | collective-permute-start | bytes 1769480 | tf_op jit(solution)/shard_map/ppermute | solution.py:23
  38.8 21.2 %collective-permute-start.9 = (bf16[2,80,1024]{2,1,0:T(8,128)(2,1)S(1)}, bf16[2,80,1024]{2,1,0:T(8,128)(2,1)S(1)}, u32[]{:S(2)}, u32[]{:S(2)}) collective-permute-start(bf16[2,80,1024]{2,1,0:T(8,128)(2,1)S(1)} %pad_maximum_fusion.8), channel_id=1, source_target_pairs={{2,0},{0,2},{3,1},{1,3},{6,4},{4,6},{7,5},{5,7},{10,8},{8,10},{11,... | collective-permute-start | bytes 983048 | tf_op jit(solution)/shard_map/ppermute | solution.py:19
  68.4 17.7 %collective-permute-start.10 = (bf16[2,96,2048]{2,1,0:T(8,128)(2,1)S(1)}, bf16[2,96,2048]{2,1,0:T(8,128)(2,1)S(1)}, u32[]{:S(2)}, u32[]{:S(2)}) collective-permute-start(bf16[2,96,2048]{2,1,0:T(8,128)(2,1)S(1)} %get-tuple-element.78), channel_id=1, source_target_pairs={{0,2},{2,0},{1,3},{3,1},{4,6},{6,4},{5,7},{7,5},{8,10},{10,8},{9,1... | collective-permute-start | bytes 2359304 | tf_op jit(solution)/shard_map/ppermute | solution.py:23
  71.6 17.6 %collective-permute-start.13 = (bf16[2,2,80,1024]{3,2,1,0:T(8,128)(2,1)S(1)}, bf16[2,2,80,1024]{3,2,1,0:T(8,128)(2,1)S(1)}, u32[]{:S(2)}, u32[]{:S(2)}) collective-permute-start(bf16[2,2,80,1024]{3,2,1,0:T(8,128)(2,1)S(1)} %get-tuple-element.135), channel_id=1, source_target_pairs={{1,0},{0,1},{3,2},{2,3},{5,4},{4,5},{7,6},{6,7},{9,8},{8,9},{11,10... | collective-permute-start | bytes 1966088 | tf_op jit(solution)/shard_map/ppermute | solution.py:19
  86.5 16.7 %collective-permute-start.11 = (bf16[96,3584]{1,0:T(8,128)(2,1)S(1)}, bf16[96,3584]{1,0:T(8,128)(2,1)S(1)}, u32[]{:S(2)}, u32[]{:S(2)}) collective-permute-start(bf16[96,3584]{1,0:T(8,128)(2,1)S(1)} %pad_maximum_fusion.refs_3_.refs_0_), channel_id=1, source_target_pairs={{2,0},{0,2},{3,1},{1,3},{6,4},{4,6},{7,5},{5,7},{10,8},{8,10},{11,... | collective-permute-start | bytes 2064392 | tf_op jit(solution)/shard_map/ppermute | solution.py:19
  102.7 32.3 %collective-permute-start.18 = (bf16[2,96,3584]{2,1,0:T(8,128)(2,1)S(1)}, bf16[2,96,3584]{2,1,0:T(8,128)(2,1)S(1)}, u32[]{:S(2)}, u32[]{:S(2)}) collective-permute-start(bf16[2,96,3584]{2,1,0:T(8,128)(2,1)S(1)} %get-tuple-element.90), channel_id=1, source_target_pairs={{0,2},{2,0},{1,3},{3,1},{4,6},{6,4},{5,7},{7,5},{8,10},{10,8},{9,1... | collective-permute-start | bytes 4128776 | tf_op jit(solution)/shard_map/ppermute | solution.py:23
  109.6 12.3 %collective-permute-start.15 = (bf16[96,2048]{1,0:T(8,128)(2,1)S(1)}, bf16[96,2048]{1,0:T(8,128)(2,1)S(1)}, u32[]{:S(2)}, u32[]{:S(2)}) collective-permute-start(bf16[96,2048]{1,0:T(8,128)(2,1)S(1)} %get-tuple-element.85), channel_id=1, source_target_pairs={{0,4},{4,0},{8,12},{12,8},{1,5},{5,1},{9,13},{13,9},{2,6},{6,2},{1... | collective-permute-start | bytes 1179656 | tf_op jit(solution)/shard_map/ppermute | solution.py:27
  122.0 11.9 %collective-permute-start.16 = (bf16[48,2048]{1,0:T(8,128)(2,1)S(1)}, bf16[48,2048]{1,0:T(8,128)(2,1)S(1)}, u32[]{:S(2)}, u32[]{:S(2)}) collective-permute-start(bf16[48,2048]{1,0:T(8,128)(2,1)S(1)} %slice.231.refs_1_), channel_id=1, source_target_pairs={{0,8},{4,12},{8,0},{12,4},{1,9},{5,13},{9,1},{13,5},{2,10},{6,14},... | collective-permute-start | bytes 589832 | tf_op jit(solution)/shard_map/ppermute | solution.py:27
  135.6 20.0 %collective-permute-start.19 = (bf16[96,3584]{1,0:T(8,128)(2,1)S(1)}, bf16[96,3584]{1,0:T(8,128)(2,1)S(1)}, u32[]{:S(2)}, u32[]{:S(2)}) collective-permute-start(bf16[96,3584]{1,0:T(8,128)(2,1)S(1)} %fusion.1.refs_2_.refs_0_), channel_id=1, source_target_pairs={{2,0},{0,2},{3,1},{1,3},{6,4},{4,6},{7,5},{5,7},{10,8},{8,10},{11,... | collective-permute-start | bytes 2064392 | tf_op jit(solution)/shard_map/ppermute | solution.py:19
  136.3 19.3 %collective-permute-start.17 = (bf16[48,2048]{1,0:T(8,128)(2,1)S(1)}, bf16[48,2048]{1,0:T(8,128)(2,1)S(1)}, u32[]{:S(2)}, u32[]{:S(2)}) collective-permute-start(bf16[48,2048]{1,0:T(8,128)(2,1)S(1)} %add_convert_fusion.1.refs_3_), channel_id=1, source_target_pairs={{0,8},{4,12},{8,0},{12,4},{1,9},{5,13},{9,1},{13,5},{2,10},{6,14},... | collective-permute-start | bytes 589832 | tf_op jit(solution)/shard_map/ppermute | solution.py:27
  154.1 21.1 %collective-permute-start.22 = (bf16[2,64,3584]{2,1,0:T(8,128)(2,1)S(1)}, bf16[2,64,3584]{2,1,0:T(8,128)(2,1)S(1)}, u32[]{:S(2)}, u32[]{:S(2)}) collective-permute-start(bf16[2,64,3584]{2,1,0:T(8,128)(2,1)S(1)} %get-tuple-element.99), channel_id=1, source_target_pairs={{0,2},{2,0},{1,3},{3,1},{4,6},{6,4},{5,7},{7,5},{8,10},{10,8},{9,1... | collective-permute-start | bytes 2752520 | tf_op jit(solution)/shard_map/ppermute | solution.py:23
  155.7 11.6 %collective-permute-start.20 = (bf16[96,2048]{1,0:T(8,128)(2,1)S(1)}, bf16[96,2048]{1,0:T(8,128)(2,1)S(1)}, u32[]{:S(2)}, u32[]{:S(2)}) collective-permute-start(bf16[96,2048]{1,0:T(8,128)(2,1)S(1)} %constant_dynamic-update-slice_fusion.refs_4_.near_ref), channel_id=1, source_target_pairs={{0,4},{4,0},{8,12},{12,8},{1,5},{5,1},{9,13},{13,9},{2,6},{6,2},{1... | collective-permute-start | bytes 1179656 | tf_op jit(solution)/shard_map/ppermute | solution.py:27
  162.3 12.6 %collective-permute-start.24 = (bf16[96,2048]{1,0:T(8,128)(2,1)S(1)}, bf16[96,2048]{1,0:T(8,128)(2,1)S(1)}, u32[]{:S(2)}, u32[]{:S(2)}) collective-permute-start(bf16[96,2048]{1,0:T(8,128)(2,1)S(1)} %get-tuple-element.102), channel_id=1, source_target_pairs={{0,4},{4,0},{8,12},{12,8},{1,5},{5,1},{9,13},{13,9},{2,6},{6,2},{1... | collective-permute-start | bytes 1179656 | tf_op jit(solution)/shard_map/ppermute | solution.py:27
  175.7 11.9 %collective-permute-start.25 = (bf16[48,2048]{1,0:T(8,128)(2,1)S(1)}, bf16[48,2048]{1,0:T(8,128)(2,1)S(1)}, u32[]{:S(2)}, u32[]{:S(2)}) collective-permute-start(bf16[48,2048]{1,0:T(8,128)(2,1)S(1)} %slice.230.refs_5_), channel_id=1, source_target_pairs={{0,8},{4,12},{8,0},{12,4},{1,9},{5,13},{9,1},{13,5},{2,10},{6,14},... | collective-permute-start | bytes 589832 | tf_op jit(solution)/shard_map/ppermute | solution.py:27
  177.6 10.9 %collective-permute-start.23 = (bf16[64,3584]{1,0:T(8,128)(2,1)S(1)}, bf16[64,3584]{1,0:T(8,128)(2,1)S(1)}, u32[]{:S(2)}, u32[]{:S(2)}) collective-permute-start(bf16[64,3584]{1,0:T(8,128)(2,1)S(1)} %fusion.3.refs_0_.refs_4_), channel_id=1, source_target_pairs={{2,0},{0,2},{3,1},{1,3},{6,4},{4,6},{7,5},{5,7},{10,8},{8,10},{11,... | collective-permute-start | bytes 1376264 | tf_op jit(solution)/shard_map/ppermute | solution.py:19
  187.7 20.8 %collective-permute-start.21 = (bf16[96,4096]{1,0:T(8,128)(2,1)S(1)}, bf16[96,4096]{1,0:T(8,128)(2,1)S(1)}, u32[]{:S(2)}, u32[]{:S(2)}) collective-permute-start(bf16[96,4096]{1,0:T(8,128)(2,1)S(1)} %get-tuple-element.98), channel_id=1, source_target_pairs={{0,1},{1,0},{2,3},{3,2},{4,5},{5,4},{6,7},{7,6},{8,9},{9,8},{10,11... | collective-permute-start | bytes 2359304 | tf_op jit(solution)/shard_map/ppermute | solution.py:23
  196.9 11.4 %collective-permute-start.31 = (bf16[32,2048]{1,0:T(8,128)(2,1)S(1)}, bf16[32,2048]{1,0:T(8,128)(2,1)S(1)}, u32[]{:S(2)}, u32[]{:S(2)}) collective-permute-start(bf16[32,2048]{1,0:T(8,128)(2,1)S(1)} %get-tuple-element.147), channel_id=1, source_target_pairs={{0,4},{4,0},{8,12},{12,8},{1,5},{5,1},{9,13},{13,9},{2,6},{6,2},{1... | collective-permute-start | bytes 393224 | tf_op jit(solution)/shard_map/ppermute | solution.py:27
  201.4 18.5 %collective-permute-start.28 = (bf16[96,2048]{1,0:T(8,128)(2,1)S(1)}, bf16[96,2048]{1,0:T(8,128)(2,1)S(1)}, u32[]{:S(2)}, u32[]{:S(2)}) collective-permute-start(bf16[96,2048]{1,0:T(8,128)(2,1)S(1)} %constant_dynamic-update-slice_fusion.2.near_ref.refs_3_), channel_id=1, source_target_pairs={{0,4},{4,0},{8,12},{12,8},{1,5},{5,1},{9,13},{13,9},{2,6},{6,2},{1... | collective-permute-start | bytes 1179656 | tf_op jit(solution)/shard_map/ppermute | solution.py:27
  208.8 11.1 %collective-permute-start.26 = (bf16[48,4096]{1,0:T(8,128)(2,1)S(1)}, bf16[48,4096]{1,0:T(8,128)(2,1)S(1)}, u32[]{:S(2)}, u32[]{:S(2)}) collective-permute-start(bf16[48,4096]{1,0:T(8,128)(2,1)S(1)} %slice.228.refs_1_), channel_id=1, source_target_pairs={{0,2},{2,0},{1,3},{3,1},{4,6},{6,4},{5,7},{7,5},{8,10},{10,8},{9,1... | collective-permute-start | bytes 1179656 | tf_op jit(solution)/shard_map/ppermute | solution.py:23
  209.2 18.4 %collective-permute-start.35 = (bf16[32,2048]{1,0:T(8,128)(2,1)S(1)}, bf16[32,2048]{1,0:T(8,128)(2,1)S(1)}, u32[]{:S(2)}, u32[]{:S(2)}) collective-permute-start(bf16[32,2048]{1,0:T(8,128)(2,1)S(1)} %add_convert_fusion.2.refs_2_), channel_id=1, source_target_pairs={{0,12},{4,8},{8,4},{12,0},{1,13},{5,9},{9,5},{13,1},{2,14},{6,10},... | collective-permute-start | bytes 393224 | tf_op jit(solution)/shard_map/ppermute | solution.py:27
  211.3 16.2 %collective-permute-start.34 = (bf16[32,2048]{1,0:T(8,128)(2,1)S(1)}, bf16[32,2048]{1,0:T(8,128)(2,1)S(1)}, u32[]{:S(2)}, u32[]{:S(2)}) collective-permute-start(bf16[32,2048]{1,0:T(8,128)(2,1)S(1)} %add_convert_fusion.2.refs_2_), channel_id=1, source_target_pairs={{0,8},{4,12},{8,0},{12,4},{1,9},{5,13},{9,1},{13,5},{2,10},{6,14},... | collective-permute-start | bytes 393224 | tf_op jit(solution)/shard_map/ppermute | solution.py:27
  213.5 14.1 %collective-permute-start.33 = (bf16[32,2048]{1,0:T(8,128)(2,1)S(1)}, bf16[32,2048]{1,0:T(8,128)(2,1)S(1)}, u32[]{:S(2)}, u32[]{:S(2)}) collective-permute-start(bf16[32,2048]{1,0:T(8,128)(2,1)S(1)} %add_convert_fusion.2.refs_2_), channel_id=1, source_target_pairs={{0,4},{4,0},{8,12},{12,8},{1,5},{5,1},{9,13},{13,9},{2,6},{6,2},{1... | collective-permute-start | bytes 393224 | tf_op jit(solution)/shard_map/ppermute | solution.py:27
  236.7 12.0 %collective-permute-start.36 = (bf16[48,4096]{1,0:T(8,128)(2,1)S(1)}, bf16[48,4096]{1,0:T(8,128)(2,1)S(1)}, u32[]{:S(2)}, u32[]{:S(2)}) collective-permute-start(bf16[48,4096]{1,0:T(8,128)(2,1)S(1)} %slice.227), channel_id=1, source_target_pairs={{0,2},{2,0},{1,3},{3,1},{4,6},{6,4},{5,7},{7,5},{8,10},{10,8},{9,1... | collective-permute-start | bytes 1179656 | tf_op jit(solution)/shard_map/ppermute | solution.py:23
  237.1 16.7 %collective-permute-start.38 = (bf16[32,4096]{1,0:T(8,128)(2,1)S(1)}, bf16[32,4096]{1,0:T(8,128)(2,1)S(1)}, u32[]{:S(2)}, u32[]{:S(2)}) collective-permute-start(bf16[32,4096]{1,0:T(8,128)(2,1)S(1)} %slice.229), channel_id=1, source_target_pairs={{0,2},{2,0},{1,3},{3,1},{4,6},{6,4},{5,7},{7,5},{8,10},{10,8},{9,1... | collective-permute-start | bytes 786440 | tf_op jit(solution)/shard_map/ppermute | solution.py:23
  (26 other events, 173.5 us)

commit v12 on v11

--- a/solution.py
+++ b/solution.py
@@ -314,7 +314,8 @@
             rest = doubled(after(rest, gathered), bit)
     columns, inverse = from_owners(gathered)
     if rest is not None:
-        rest = from_owners(after(rest, (columns, inverse)))
+        rest_columns, rest_inverse = from_owners(after(rest, (columns, inverse)))
+        rest = [rest_columns, rest_inverse]
     inverses = from_all(inverse, "rows", owners)
     columns, inverses = after((columns, inverses), (columns, inverses))
     xs = [normed(from_members(columns), from_all(inverses, "mp", members))]
@@ -324,7 +325,7 @@
 
     def gate_up_of(t):
         tiles = gate_weight.shape[2] // tile_of(gate_weight.shape[2], 256)
-        early = tiles * 3 // 7 if t == 0 and chunks > 1 else 0
+        early = tiles // 2 if t == 0 and chunks > 1 else 0
         sums[t] = []
         for first, count in ((0, early), (early, tiles - early)):
             if not count:
@@ -332,20 +333,24 @@
             own, *sends = gate_up(xs[t], gate_weight, up_weight, first, count, list(last))
             last[:] = [own]
             if t == 0 and rest is not None:
+                if not first:
+                    rest[1] = from_all(after(rest[1], own), "mp", members)
                 last.extend(rest[0])
+                last.append(rest[1])
             others = [send(sends[hop - 1], "rows", owners, hop) for hop in range(1, owners)]
             sums[t].append((own, others))
 
     def rest_of():
-        columns, inverse = rest
-        inverses = from_all(after(inverse, sums[0][-1][0]), "rows", owners)
-        columns, inverses = after((columns, inverses), (columns, inverses))
-        columns, inverses = from_members(columns), from_all(inverses, "mp", members)
+        inverses = from_all(after(rest[1], sums[0][-1][0]), "rows", owners).transpose(1, 0, 2)
+        sums[0][-1] = after(sums[0][-1], inverses)
+        columns = from_members(rest[0])
         for start, q in zip(starts[1:], sizes[1:]):
             rows = slice(start - head, start - head + q)
             xs.append(normed(columns[:, :, :, rows], inverses[:, :, rows]))
 
     def hidden_of(t):
+        if t == 0 and rest is not None:
+            rest_of()
         units = []
         parts = ordered(sums[t]) if 0 < t == chunks - 1 else sums[t]
         for own, others in parts:
@@ -353,8 +358,6 @@
             for other in others:
                 acts = acts + other.astype(F32)
             units.append((jax.nn.silu(acts[0]) * acts[1]).astype(BF16))
-        if t == 0 and rest is not None:
-            rest_of()
         units = jnp.concatenate(units, axis=1)
         hidden[t] = [units] + [shift(units, "rows", owners, hop) for hop in range(1, owners)]
         last.append(units)

time: 255 us -> 234 us (0.918)
  waiting for transfers between devices: 117 us -> 92.7 us
  starting transfers between devices: 48.1 us -> 52 us
    ppermute x11, waiting for transfers between devices: 28.5 us -> 14.1 us  [shift(): lax.ppermute(value, axis, [((d + hop) % size, d) for d in range(size)])]
    ppermute x18, waiting for transfers between devices: 57.9 us -> 44.5 us  [swap(): return lax.ppermute(value, axis, [(d, d ^ bit) for d in range(size)])]
    ppermute x10, starting transfers between devices: 7.25 us -> 10.7 us  [send(): lax.ppermute(value, axis, [(d, (d + hop) % size) for d in range(size)])]
    ppermute x10, waiting for transfers between devices: 31.1 us -> 34.1 us  [send(): lax.ppermute(value, axis, [(d, (d + hop) % size) for d in range(size)])]
  transfers between devices with their start and end apart: 39 -> 39, of which waited for: 26 -> 25; matrix products, arithmetic and copies ran while one was open for 2% -> 2% of each run, Pallas kernels for 28% -> 33%
where the time goes in v12:
time: 234 us
  waiting for transfers between devices  92.7 us (40%)
  Pallas kernels  78 us (33%)
  starting transfers between devices  52 us (22%)
  other arithmetic  5.3 us (2%)
  local copies, waits for them, and re-layouts  5.15 us (2%)
    ppermute x18, waiting for transfers between devices, swap(): return lax.ppermute(value, axis, [(d, d ^ bit) for d in range(size)])  44.5 us
    pallas_call x4, Pallas kernels, gate_up(): pl.pallas_call(functools.partial(gate_up_body, tiles, first), grid=(tiles...  37.5 us
    ppermute x10, waiting for transfers between devices, send(): lax.ppermute(value, axis, [(d, (d + hop) % size) for d in range(size)])  34.1 us
    ppermute x18, starting transfers between devices, swap(): return lax.ppermute(value, axis, [(d, d ^ bit) for d in range(size)])  33.8 us
    pallas_call x3, Pallas kernels, encode(): pl.pallas_call(functools.partial(encode_body, members, order, tiles), gri...  22 us
    pallas_call x3, Pallas kernels, down(): pl.pallas_call(functools.partial(down_body, owners, members, pieces, orde...  18.5 us
    ppermute x11, waiting for transfers between devices, shift(): lax.ppermute(value, axis, [((d + hop) % size, d) for d in range(size)])  14.1 us
    ppermute x10, starting transfers between devices, send(): lax.ppermute(value, axis, [(d, (d + hop) % size) for d in range(size)])  10.7 us
  transfers between devices with their start and end apart: 39, of which 25 were waited for; matrix products, arithmetic and copies ran while one was open for 2% of the time, Pallas kernels for 33%

profile of v12, /device:TPU:0, one launch (start us, length us, event | category | flops | bytes accessed | tf_op | source)
XLA Modules:
  0.0 233.7 jit_solution(18221749882571773392)
XLA Ops:
  1.1 4.1 %collective-permute-start = (bf16[1,48,1024]{2,1,0:T(8,128)(2,1)S(1)}, bf16[1,48,1024]{2,1,0:T(8,128)(2,1)S(1)}, u32[]{:S(2)}, u32[]{:S(2)}) collective-permute-start(bf16[1,48,1024]{2,1,0:T(8,128)(2,1)S(1)} %dynamic-slice_bitcast_fusion.1), channel_id=1, source_target_pairs={{0,8},{4,12},{8,0},{12,4},{1,9},{5,13},{9,1},{13,5},{2,10},{6,14},... | collective-permute-start | bytes 294920 | tf_op jit(solution)/shard_map/ppermute | solution.py:27
  5.2 4.9 %collective-permute-done = bf16[1,48,1024]{2,1,0:T(8,128)(2,1)S(1)} collective-permute-done((bf16[1,48,1024]{2,1,0:T(8,128)(2,1)S(1)}, bf16[1,48,1024]{2,1,0:T(8,128)(2,1)S(1)}, u32[]{:S(2)}, u32[]{:S(2)}) %collective-permute-start) | collective-permute-done | bytes 98336 | tf_op jit(solution)/shard_map/ppermute | solution.py:27
  15.0 5.1 %collective-permute-done.7 = bf16[1,80,1024]{2,1,0:T(8,128)(2,1)S(1)} collective-permute-done((bf16[1,80,1024]{2,1,0:T(8,128)(2,1)S(1)}, bf16[1,80,1024]{2,1,0:T(8,128)(2,1)S(1)}, u32[]{:S(2)}, u32[]{:S(2)}) %collective-permute-start.7) | collective-permute-done | bytes 163872 | tf_op jit(solution)/shard_map/ppermute | solution.py:27
  24.6 3.8 %collective-permute-done.2 = bf16[2,48,1024]{2,1,0:T(8,128)(2,1)S(1)} collective-permute-done((bf16[2,48,1024]{2,1,0:T(8,128)(2,1)S(1)}, bf16[2,48,1024]{2,1,0:T(8,128)(2,1)S(1)}, u32[]{:S(2)}, u32[]{:S(2)}) %collective-permute-start.2) | collective-permute-done | bytes 196640 | tf_op jit(solution)/shard_map/ppermute | solution.py:19
  32.2 7.2 %shard_map.82 = (f32[2,96,1792]{2,1,0:T(8,128)S(1)}, bf16[2,96,1792]{2,1,0:T(8,128)(2,1)S(1)}) custom-call(bf16[2,2,2,48,1024]{4,3,2,1,0:T(8,128)(2,1)S(1)} %multiply_convert_fusion.1.x_ref, bf16[1,2048,3584]{2,1,0:T(8,128)(2,1)} %gate_ref.7, bf16[1,2048,3584]{2,1,0:T(8,128)(2,1)} %up_ref.7), custom_call_target="tpu_custom_call" | custom-call | flops 1 | bytes 1 | tf_op jit(solution)/shard_map/pallas_call | solution.py:127
  42.3 7.2 %shard_map.83 = (f32[2,96,1792]{2,1,0:T(8,128)S(1)}, bf16[2,96,1792]{2,1,0:T(8,128)(2,1)S(1)}) custom-call(bf16[2,2,2,48,1024]{4,3,2,1,0:T(8,128)(2,1)S(1)} %multiply_convert_fusion.1.x_ref, bf16[1,2048,3584]{2,1,0:T(8,128)(2,1)} %gate_ref.7, bf16[1,2048,3584]{2,1,0:T(8,128)(2,1)} %up_ref.7, f32[2,96,1792]{2,1,0:T(8,128)S(1)} %get-tuple-element.72.refs_0_, ...), custom_call_target="tpu_custom_call" | custom-call | flops 1 | bytes 1 | tf_op jit(solution)/shard_map/pallas_call | solution.py:127
  51.9 6.1 %collective-permute-done.12 = f32[2,80]{1,0:T(2,128)S(1)} collective-permute-done((f32[2,80]{1,0:T(2,128)S(1)}, f32[2,80]{1,0:T(2,128)S(1)}, u32[]{:S(2)}, u32[]{:S(2)}) %collective-permute-start.12) | collective-permute-done | bytes 672 | tf_op jit(solution)/shard_map/ppermute | solution.py:19
  58.3 12.2 %collective-permute-done.11 = bf16[2,96,1792]{2,1,0:T(8,128)(2,1)S(1)} collective-permute-done((bf16[2,96,1792]{2,1,0:T(8,128)(2,1)S(1)}, bf16[2,96,1792]{2,1,0:T(8,128)(2,1)S(1)}, u32[]{:S(2)}, u32[]{:S(2)}) %collective-permute-start.11) | collective-permute-done | bytes 688160 | tf_op jit(solution)/shard_map/ppermute | solution.py:23
  72.4 11.7 %shard_map.84 = (f32[2,96,3584]{2,1,0:T(8,128)S(1)}, bf16[2,96,3584]{2,1,0:T(8,128)(2,1)S(1)}) custom-call(bf16[2,2,2,48,1024]{4,3,2,1,0:T(8,128)(2,1)S(1)} %multiply_convert_fusion.x_ref, bf16[1,2048,3584]{2,1,0:T(8,128)(2,1)} %gate_ref.7, bf16[1,2048,3584]{2,1,0:T(8,128)(2,1)} %up_ref.7, f32[2,96,1792]{2,1,0:T(8,128)S(1)} %get-tuple-element.81.refs_0_, ...), custom_call_target="tpu_custom_call" | custom-call | flops 1 | bytes 1 | tf_op jit(solution)/shard_map/pallas_call | solution.py:127
  86.4 6.3 %shard_map.85 = (f32[96,2048]{1,0:T(8,128)S(1)}, bf16[96,2048]{1,0:T(8,128)(2,1)S(1)}) custom-call(s32[1]{0:T(128)} %bitcast.rank_ref, bf16[96,3584]{1,0:T(8,128)(2,1)S(1)} %pad_maximum_fusion.refs_4_.refs_0_, bf16[96,3584]{1,0:T(8,128)(2,1)S(1)} %collective-permute-done.13.refs_1_, bf16[1,3584,2048]{2,1,0:T(8,128)(2,1)} %refs_2_.5, f32[2,96,3584]{2,1,0:T(8,128)} %copy-done.2), custom_call_target="tpu_custom_call" | custom-call | flops 1 | bytes 1 | tf_op jit(solution)/shard_map/pallas_call | solution.py:175
  96.4 7.1 %collective-permute-done.15 = bf16[96,2048]{1,0:T(8,128)(2,1)S(1)} collective-permute-done((bf16[96,2048]{1,0:T(8,128)(2,1)S(1)}, bf16[96,2048]{1,0:T(8,128)(2,1)S(1)}, u32[]{:S(2)}, u32[]{:S(2)}) %collective-permute-start.15) | collective-permute-done | bytes 393248 | tf_op jit(solution)/shard_map/ppermute | solution.py:27
  103.7 4.6 %collective-permute-start.16 = (bf16[48,2048]{1,0:T(8,128)(2,1)S(1)}, bf16[48,2048]{1,0:T(8,128)(2,1)S(1)}, u32[]{:S(2)}, u32[]{:S(2)}) collective-permute-start(bf16[48,2048]{1,0:T(8,128)(2,1)S(1)} %slice.229.refs_1_), channel_id=1, source_target_pairs={{0,8},{4,12},{8,0},{12,4},{1,9},{5,13},{9,1},{13,5},{2,10},{6,14},... | collective-permute-start | bytes 589832 | tf_op jit(solution)/shard_map/ppermute | solution.py:27
  108.4 5.2 %collective-permute-done.16 = bf16[48,2048]{1,0:T(8,128)(2,1)S(1)} collective-permute-done((bf16[48,2048]{1,0:T(8,128)(2,1)S(1)}, bf16[48,2048]{1,0:T(8,128)(2,1)S(1)}, u32[]{:S(2)}, u32[]{:S(2)}) %collective-permute-start.16) | collective-permute-done | bytes 196640 | tf_op jit(solution)/shard_map/ppermute | solution.py:27
  117.9 4.6 %collective-permute-start.17 = (bf16[48,2048]{1,0:T(8,128)(2,1)S(1)}, bf16[48,2048]{1,0:T(8,128)(2,1)S(1)}, u32[]{:S(2)}, u32[]{:S(2)}) collective-permute-start(bf16[48,2048]{1,0:T(8,128)(2,1)S(1)} %add_convert_fusion.1.refs_3_), channel_id=1, source_target_pairs={{0,8},{4,12},{8,0},{12,4},{1,9},{5,13},{9,1},{13,5},{2,10},{6,14},... | collective-permute-start | bytes 589832 | tf_op jit(solution)/shard_map/ppermute | solution.py:27
  122.7 11.4 %shard_map.86 = (f32[2,64,3584]{2,1,0:T(8,128)S(1)}, bf16[2,64,3584]{2,1,0:T(8,128)(2,1)S(1)}) custom-call(bf16[2,2,2,32,1024]{4,3,2,1,0:T(8,128)(2,1)S(1)} %multiply_convert_fusion.2.x_ref, bf16[1,2048,3584]{2,1,0:T(8,128)(2,1)} %gate_ref.7, bf16[1,2048,3584]{2,1,0:T(8,128)(2,1)} %up_ref.7, f32[96,2048]{1,0:T(8,128)S(1)} %get-tuple-element.86.refs_0_, ...), custom_call_target="tpu_custom_call" | custom-call | flops 1 | bytes 1 | tf_op jit(solution)/shard_map/pallas_call | solution.py:127
  136.6 6.3 %shard_map.87 = (f32[96,2048]{1,0:T(8,128)S(1)}, bf16[96,2048]{1,0:T(8,128)(2,1)S(1)}) custom-call(s32[1]{0:T(128)} %bitcast.rank_ref, bf16[96,3584]{1,0:T(8,128)(2,1)S(1)} %fusion.1.refs_2_.refs_0_, bf16[96,3584]{1,0:T(8,128)(2,1)S(1)} %collective-permute-done.19.refs_1_, bf16[1,3584,2048]{2,1,0:T(8,128)(2,1)} %refs_2_.5, f32[2,64,3584]{2,1,0:T(8,128)} %copy-done.4, ...), custom_call_target="tpu_custom_call" | custom-call | flops 1 | bytes 1 | tf_op jit(solution)/shard_map/pallas_call | solution.py:175
  147.2 7.8 %shard_map.88 = (f32[96,4096]{1,0:T(8,128)}, bf16[96,4096]{1,0:T(8,128)(2,1)S(1)}) custom-call(s32[1]{0:T(128)} %bitcast.rank_ref, bf16[96,2048]{1,0:T(8,128)(2,1)S(1)} %constant_dynamic-update-slice_fusion.refs_4_.near_ref, bf16[96,2048]{1,0:T(8,128)(2,1)S(1)} %collective-permute-done.20.far_ref, bf16[1,2048,4096]{2,1,0:T(8,128)(2,1)} %weight_ref.5, ...), custom_call_target="tpu_custom_call" | custom-call | flops 1 | bytes 1 | tf_op jit(solution)/shard_map/pallas_call | solution.py:221
  158.6 8.1 %collective-permute-done.25 = bf16[48,2048]{1,0:T(8,128)(2,1)S(1)} collective-permute-done((bf16[48,2048]{1,0:T(8,128)(2,1)S(1)}, bf16[48,2048]{1,0:T(8,128)(2,1)S(1)}, u32[]{:S(2)}, u32[]{:S(2)}) %collective-permute-start.25) | collective-permute-done | bytes 196640 | tf_op jit(solution)/shard_map/ppermute | solution.py:27
  168.2 5.9 %shard_map.89 = (f32[64,2048]{1,0:T(8,128)S(1)}, bf16[64,2048]{1,0:T(8,128)(2,1)S(1)}) custom-call(s32[1]{0:T(128)} %bitcast.rank_ref, bf16[64,3584]{1,0:T(8,128)(2,1)S(1)} %fusion.3.refs_0_.refs_4_, bf16[64,3584]{1,0:T(8,128)(2,1)S(1)} %collective-permute-done.23.refs_1_, bf16[1,3584,2048]{2,1,0:T(8,128)(2,1)} %refs_2_.5, ...), custom_call_target="tpu_custom_call" | custom-call | flops 1 | bytes 1 | tf_op jit(solution)/shard_map/pallas_call | solution.py:175
  179.7 7.0 %collective-permute-done.30 = bf16[32,2048]{1,0:T(8,128)(2,1)S(1)} collective-permute-done((bf16[32,2048]{1,0:T(8,128)(2,1)S(1)}, bf16[32,2048]{1,0:T(8,128)(2,1)S(1)}, u32[]{:S(2)}, u32[]{:S(2)}) %collective-permute-start.30) | collective-permute-done | bytes 131104 | tf_op jit(solution)/shard_map/ppermute | solution.py:27
  197.9 7.6 %shard_map.90 = (f32[96,4096]{1,0:T(8,128)}, bf16[96,4096]{1,0:T(8,128)(2,1)S(1)}) custom-call(s32[1]{0:T(128)} %bitcast.rank_ref, bf16[96,2048]{1,0:T(8,128)(2,1)S(1)} %constant_dynamic-update-slice_fusion.2.near_ref.refs_3_, bf16[96,2048]{1,0:T(8,128)(2,1)S(1)} %collective-permute-done.28.far_ref, bf16[1,2048,4096]{2,1,0:T(8,128)(2,1)} %weight_ref.5, ...), custom_call_target="tpu_custom_call" | custom-call | flops 1 | bytes 1 | tf_op jit(solution)/shard_map/pallas_call | solution.py:221
  205.7 6.6 %shard_map.91 = (f32[64,4096]{1,0:T(8,128)S(1)}, bf16[64,4096]{1,0:T(8,128)(2,1)S(1)}) custom-call(s32[1]{0:T(128)} %bitcast.rank_ref, bf16[64,2048]{1,0:T(8,128)(2,1)S(1)} %get-tuple-element.153.near_ref, bf16[64,2048]{1,0:T(8,128)(2,1)S(1)} %get-tuple-element.154.far_ref, bf16[1,2048,4096]{2,1,0:T(8,128)(2,1)} %weight_ref.5, ...), custom_call_target="tpu_custom_call" | custom-call | flops 1 | bytes 1 | tf_op jit(solution)/shard_map/pallas_call | solution.py:221
  217.9 9.7 %collective-permute-done.36 = bf16[48,4096]{1,0:T(8,128)(2,1)S(1)} collective-permute-done((bf16[48,4096]{1,0:T(8,128)(2,1)S(1)}, bf16[48,4096]{1,0:T(8,128)(2,1)S(1)}, u32[]{:S(2)}, u32[]{:S(2)}) %collective-permute-start.36) | collective-permute-done | bytes 393248 | tf_op jit(solution)/shard_map/ppermute | solution.py:23
  227.8 5.1 %collective-permute-done.38 = bf16[32,4096]{1,0:T(8,128)(2,1)S(1)} collective-permute-done((bf16[32,4096]{1,0:T(8,128)(2,1)S(1)}, bf16[32,4096]{1,0:T(8,128)(2,1)S(1)}, u32[]{:S(2)}, u32[]{:S(2)}) %collective-permute-start.38) | collective-permute-done | bytes 262176 | tf_op jit(solution)/shard_map/ppermute | solution.py:23
  (151 shorter events, 67.6 us)
Async XLA Ops:
  31.3 11.0 %collective-permute-start.9 = (bf16[2,80,1024]{2,1,0:T(8,128)(2,1)S(1)}, bf16[2,80,1024]{2,1,0:T(8,128)(2,1)S(1)}, u32[]{:S(2)}, u32[]{:S(2)}) collective-permute-start(bf16[2,80,1024]{2,1,0:T(8,128)(2,1)S(1)} %pad_maximum_fusion.8), channel_id=1, source_target_pairs={{2,0},{0,2},{3,1},{1,3},{6,4},{4,6},{7,5},{5,7},{10,8},{8,10},{11,... | collective-permute-start | bytes 983048 | tf_op jit(solution)/shard_map/ppermute | solution.py:19
  39.4 18.5 %collective-permute-start.6 = (bf16[2,96,1792]{2,1,0:T(8,128)(2,1)S(1)}, bf16[2,96,1792]{2,1,0:T(8,128)(2,1)S(1)}, u32[]{:S(2)}, u32[]{:S(2)}) collective-permute-start(bf16[2,96,1792]{2,1,0:T(8,128)(2,1)S(1)} %get-tuple-element.73), channel_id=1, source_target_pairs={{0,2},{2,0},{1,3},{3,1},{4,6},{6,4},{5,7},{7,5},{8,10},{10,8},{9,1... | collective-permute-start | bytes 2064392 | tf_op jit(solution)/shard_map/ppermute | solution.py:23
  50.1 22.1 %collective-permute-start.14 = (bf16[2,2,80,1024]{3,2,1,0:T(8,128)(2,1)S(1)}, bf16[2,2,80,1024]{3,2,1,0:T(8,128)(2,1)S(1)}, u32[]{:S(2)}, u32[]{:S(2)}) collective-permute-start(bf16[2,2,80,1024]{3,2,1,0:T(8,128)(2,1)S(1)} %get-tuple-element.135), channel_id=1, source_target_pairs={{1,0},{0,1},{3,2},{2,3},{5,4},{4,5},{7,6},{6,7},{9,8},{8,9},{11,10... | collective-permute-start | bytes 1966088 | tf_op jit(solution)/shard_map/ppermute | solution.py:19
  50.1 20.3 %collective-permute-start.11 = (bf16[2,96,1792]{2,1,0:T(8,128)(2,1)S(1)}, bf16[2,96,1792]{2,1,0:T(8,128)(2,1)S(1)}, u32[]{:S(2)}, u32[]{:S(2)}) collective-permute-start(bf16[2,96,1792]{2,1,0:T(8,128)(2,1)S(1)} %get-tuple-element.79), channel_id=1, source_target_pairs={{0,2},{2,0},{1,3},{3,1},{4,6},{6,4},{5,7},{7,5},{8,10},{10,8},{9,1... | collective-permute-start | bytes 2064392 | tf_op jit(solution)/shard_map/ppermute | solution.py:23
  70.9 15.6 %collective-permute-start.13 = (bf16[96,3584]{1,0:T(8,128)(2,1)S(1)}, bf16[96,3584]{1,0:T(8,128)(2,1)S(1)}, u32[]{:S(2)}, u32[]{:S(2)}) collective-permute-start(bf16[96,3584]{1,0:T(8,128)(2,1)S(1)} %pad_maximum_fusion.refs_4_.refs_0_), channel_id=1, source_target_pairs={{2,0},{0,2},{3,1},{1,3},{6,4},{4,6},{7,5},{5,7},{10,8},{8,10},{11,... | collective-permute-start | bytes 2064392 | tf_op jit(solution)/shard_map/ppermute | solution.py:19
  85.6 30.1 %collective-permute-start.18 = (bf16[2,96,3584]{2,1,0:T(8,128)(2,1)S(1)}, bf16[2,96,3584]{2,1,0:T(8,128)(2,1)S(1)}, u32[]{:S(2)}, u32[]{:S(2)}) collective-permute-start(bf16[2,96,3584]{2,1,0:T(8,128)(2,1)S(1)} %get-tuple-element.90), channel_id=1, source_target_pairs={{0,2},{2,0},{1,3},{3,1},{4,6},{6,4},{5,7},{7,5},{8,10},{10,8},{9,1... | collective-permute-start | bytes 4128776 | tf_op jit(solution)/shard_map/ppermute | solution.py:23
  92.7 10.8 %collective-permute-start.15 = (bf16[96,2048]{1,0:T(8,128)(2,1)S(1)}, bf16[96,2048]{1,0:T(8,128)(2,1)S(1)}, u32[]{:S(2)}, u32[]{:S(2)}) collective-permute-start(bf16[96,2048]{1,0:T(8,128)(2,1)S(1)} %get-tuple-element.85), channel_id=1, source_target_pairs={{0,4},{4,0},{8,12},{12,8},{1,5},{5,1},{9,13},{13,9},{2,6},{6,2},{1... | collective-permute-start | bytes 1179656 | tf_op jit(solution)/shard_map/ppermute | solution.py:27
  116.4 20.1 %collective-permute-start.19 = (bf16[96,3584]{1,0:T(8,128)(2,1)S(1)}, bf16[96,3584]{1,0:T(8,128)(2,1)S(1)}, u32[]{:S(2)}, u32[]{:S(2)}) collective-permute-start(bf16[96,3584]{1,0:T(8,128)(2,1)S(1)} %fusion.1.refs_2_.refs_0_), channel_id=1, source_target_pairs={{2,0},{0,2},{3,1},{1,3},{6,4},{4,6},{7,5},{5,7},{10,8},{8,10},{11,... | collective-permute-start | bytes 2064392 | tf_op jit(solution)/shard_map/ppermute | solution.py:19
  117.9 18.6 %collective-permute-start.17 = (bf16[48,2048]{1,0:T(8,128)(2,1)S(1)}, bf16[48,2048]{1,0:T(8,128)(2,1)S(1)}, u32[]{:S(2)}, u32[]{:S(2)}) collective-permute-start(bf16[48,2048]{1,0:T(8,128)(2,1)S(1)} %add_convert_fusion.1.refs_3_), channel_id=1, source_target_pairs={{0,8},{4,12},{8,0},{12,4},{1,9},{5,13},{9,1},{13,5},{2,10},{6,14},... | collective-permute-start | bytes 589832 | tf_op jit(solution)/shard_map/ppermute | solution.py:27
  135.3 20.2 %collective-permute-start.22 = (bf16[2,64,3584]{2,1,0:T(8,128)(2,1)S(1)}, bf16[2,64,3584]{2,1,0:T(8,128)(2,1)S(1)}, u32[]{:S(2)}, u32[]{:S(2)}) collective-permute-start(bf16[2,64,3584]{2,1,0:T(8,128)(2,1)S(1)} %get-tuple-element.99), channel_id=1, source_target_pairs={{0,2},{2,0},{1,3},{3,1},{4,6},{6,4},{5,7},{7,5},{8,10},{10,8},{9,1... | collective-permute-start | bytes 2752520 | tf_op jit(solution)/shard_map/ppermute | solution.py:23
  136.5 10.6 %collective-permute-start.20 = (bf16[96,2048]{1,0:T(8,128)(2,1)S(1)}, bf16[96,2048]{1,0:T(8,128)(2,1)S(1)}, u32[]{:S(2)}, u32[]{:S(2)}) collective-permute-start(bf16[96,2048]{1,0:T(8,128)(2,1)S(1)} %constant_dynamic-update-slice_fusion.refs_4_.near_ref), channel_id=1, source_target_pairs={{0,4},{4,0},{8,12},{12,8},{1,5},{5,1},{9,13},{13,9},{2,6},{6,2},{1... | collective-permute-start | bytes 1179656 | tf_op jit(solution)/shard_map/ppermute | solution.py:27
  142.9 12.0 %collective-permute-start.24 = (bf16[96,2048]{1,0:T(8,128)(2,1)S(1)}, bf16[96,2048]{1,0:T(8,128)(2,1)S(1)}, u32[]{:S(2)}, u32[]{:S(2)}) collective-permute-start(bf16[96,2048]{1,0:T(8,128)(2,1)S(1)} %get-tuple-element.102), channel_id=1, source_target_pairs={{0,4},{4,0},{8,12},{12,8},{1,5},{5,1},{9,13},{13,9},{2,6},{6,2},{1... | collective-permute-start | bytes 1179656 | tf_op jit(solution)/shard_map/ppermute | solution.py:27
  156.0 10.6 %collective-permute-start.25 = (bf16[48,2048]{1,0:T(8,128)(2,1)S(1)}, bf16[48,2048]{1,0:T(8,128)(2,1)S(1)}, u32[]{:S(2)}, u32[]{:S(2)}) collective-permute-start(bf16[48,2048]{1,0:T(8,128)(2,1)S(1)} %slice.228.refs_5_), channel_id=1, source_target_pairs={{0,8},{4,12},{8,0},{12,4},{1,9},{5,13},{9,1},{13,5},{2,10},{6,14},... | collective-permute-start | bytes 589832 | tf_op jit(solution)/shard_map/ppermute | solution.py:27
  157.6 10.6 %collective-permute-start.23 = (bf16[64,3584]{1,0:T(8,128)(2,1)S(1)}, bf16[64,3584]{1,0:T(8,128)(2,1)S(1)}, u32[]{:S(2)}, u32[]{:S(2)}) collective-permute-start(bf16[64,3584]{1,0:T(8,128)(2,1)S(1)} %fusion.3.refs_0_.refs_4_), channel_id=1, source_target_pairs={{2,0},{0,2},{3,1},{1,3},{6,4},{4,6},{7,5},{5,7},{10,8},{8,10},{11,... | collective-permute-start | bytes 1376264 | tf_op jit(solution)/shard_map/ppermute | solution.py:19
  166.8 20.4 %collective-permute-start.21 = (bf16[96,4096]{1,0:T(8,128)(2,1)S(1)}, bf16[96,4096]{1,0:T(8,128)(2,1)S(1)}, u32[]{:S(2)}, u32[]{:S(2)}) collective-permute-start(bf16[96,4096]{1,0:T(8,128)(2,1)S(1)} %get-tuple-element.98), channel_id=1, source_target_pairs={{0,1},{1,0},{2,3},{3,2},{4,5},{5,4},{6,7},{7,6},{8,9},{9,8},{10,11... | collective-permute-start | bytes 2359304 | tf_op jit(solution)/shard_map/ppermute | solution.py:23
  175.1 11.6 %collective-permute-start.30 = (bf16[32,2048]{1,0:T(8,128)(2,1)S(1)}, bf16[32,2048]{1,0:T(8,128)(2,1)S(1)}, u32[]{:S(2)}, u32[]{:S(2)}) collective-permute-start(bf16[32,2048]{1,0:T(8,128)(2,1)S(1)} %slice.230), channel_id=1, source_target_pairs={{0,8},{4,12},{8,0},{12,4},{1,9},{5,13},{9,1},{13,5},{2,10},{6,14},... | collective-permute-start | bytes 393224 | tf_op jit(solution)/shard_map/ppermute | solution.py:27
  175.7 10.9 %collective-permute-start.31 = (bf16[32,2048]{1,0:T(8,128)(2,1)S(1)}, bf16[32,2048]{1,0:T(8,128)(2,1)S(1)}, u32[]{:S(2)}, u32[]{:S(2)}) collective-permute-start(bf16[32,2048]{1,0:T(8,128)(2,1)S(1)} %get-tuple-element.149), channel_id=1, source_target_pairs={{0,4},{4,0},{8,12},{12,8},{1,5},{5,1},{9,13},{13,9},{2,6},{6,2},{1... | collective-permute-start | bytes 393224 | tf_op jit(solution)/shard_map/ppermute | solution.py:27
  179.6 15.1 %collective-permute-start.28 = (bf16[96,2048]{1,0:T(8,128)(2,1)S(1)}, bf16[96,2048]{1,0:T(8,128)(2,1)S(1)}, u32[]{:S(2)}, u32[]{:S(2)}) collective-permute-start(bf16[96,2048]{1,0:T(8,128)(2,1)S(1)} %constant_dynamic-update-slice_fusion.2.near_ref.refs_3_), channel_id=1, source_target_pairs={{0,4},{4,0},{8,12},{12,8},{1,5},{5,1},{9,13},{13,9},{2,6},{6,2},{1... | collective-permute-start | bytes 1179656 | tf_op jit(solution)/shard_map/ppermute | solution.py:27
  187.5 10.4 %collective-permute-start.26 = (bf16[48,4096]{1,0:T(8,128)(2,1)S(1)}, bf16[48,4096]{1,0:T(8,128)(2,1)S(1)}, u32[]{:S(2)}, u32[]{:S(2)}) collective-permute-start(bf16[48,4096]{1,0:T(8,128)(2,1)S(1)} %slice.226.refs_1_), channel_id=1, source_target_pairs={{0,2},{2,0},{1,3},{3,1},{4,6},{6,4},{5,7},{7,5},{8,10},{10,8},{9,1... | collective-permute-start | bytes 1179656 | tf_op jit(solution)/shard_map/ppermute | solution.py:23
  189.1 16.4 %collective-permute-start.35 = (bf16[32,2048]{1,0:T(8,128)(2,1)S(1)}, bf16[32,2048]{1,0:T(8,128)(2,1)S(1)}, u32[]{:S(2)}, u32[]{:S(2)}) collective-permute-start(bf16[32,2048]{1,0:T(8,128)(2,1)S(1)} %add_convert_fusion.2.refs_2_), channel_id=1, source_target_pairs={{0,12},{4,8},{8,4},{12,0},{1,13},{5,9},{9,5},{13,1},{2,14},{6,10},... | collective-permute-start | bytes 393224 | tf_op jit(solution)/shard_map/ppermute | solution.py:27
  191.1 14.5 %collective-permute-start.34 = (bf16[32,2048]{1,0:T(8,128)(2,1)S(1)}, bf16[32,2048]{1,0:T(8,128)(2,1)S(1)}, u32[]{:S(2)}, u32[]{:S(2)}) collective-permute-start(bf16[32,2048]{1,0:T(8,128)(2,1)S(1)} %add_convert_fusion.2.refs_2_), channel_id=1, source_target_pairs={{0,8},{4,12},{8,0},{12,4},{1,9},{5,13},{9,1},{13,5},{2,10},{6,14},... | collective-permute-start | bytes 393224 | tf_op jit(solution)/shard_map/ppermute | solution.py:27
  192.5 13.0 %collective-permute-start.33 = (bf16[32,2048]{1,0:T(8,128)(2,1)S(1)}, bf16[32,2048]{1,0:T(8,128)(2,1)S(1)}, u32[]{:S(2)}, u32[]{:S(2)}) collective-permute-start(bf16[32,2048]{1,0:T(8,128)(2,1)S(1)} %add_convert_fusion.2.refs_2_), channel_id=1, source_target_pairs={{0,4},{4,0},{8,12},{12,8},{1,5},{5,1},{9,13},{13,9},{2,6},{6,2},{1... | collective-permute-start | bytes 393224 | tf_op jit(solution)/shard_map/ppermute | solution.py:27
  214.7 12.9 %collective-permute-start.36 = (bf16[48,4096]{1,0:T(8,128)(2,1)S(1)}, bf16[48,4096]{1,0:T(8,128)(2,1)S(1)}, u32[]{:S(2)}, u32[]{:S(2)}) collective-permute-start(bf16[48,4096]{1,0:T(8,128)(2,1)S(1)} %slice.225), channel_id=1, source_target_pairs={{0,2},{2,0},{1,3},{3,1},{4,6},{6,4},{5,7},{7,5},{8,10},{10,8},{9,1... | collective-permute-start | bytes 1179656 | tf_op jit(solution)/shard_map/ppermute | solution.py:23
  217.8 15.1 %collective-permute-start.38 = (bf16[32,4096]{1,0:T(8,128)(2,1)S(1)}, bf16[32,4096]{1,0:T(8,128)(2,1)S(1)}, u32[]{:S(2)}, u32[]{:S(2)}) collective-permute-start(bf16[32,4096]{1,0:T(8,128)(2,1)S(1)} %slice.227), channel_id=1, source_target_pairs={{0,2},{2,0},{1,3},{3,1},{4,6},{6,4},{5,7},{7,5},{8,10},{10,8},{9,1... | collective-permute-start | bytes 786440 | tf_op jit(solution)/shard_map/ppermute | solution.py:23
  (26 other events, 175.7 us)

commit v13 on v12

--- a/solution.py
+++ b/solution.py
@@ -455,9 +455,9 @@
 
     stages = (
         (gate_up_of, 0), (hidden_of, 0), (gate_up_of, 1), (down_of, 0), (halve_of, 0),
-        (hidden_of, 1), (settle_of, 0), (gate_up_of, 2), (double_of, 0), (down_of, 1),
-        (features_of, 0), (hidden_of, 2), (halve_of, 1), (settle_of, 1), (down_of, 2),
-        (share_of, 0), (settle_of, 2), (double_of, 1), (shared_of, 0), (features_of, 1),
+        (hidden_of, 1), (gate_up_of, 2), (settle_of, 0), (down_of, 1), (double_of, 0),
+        (hidden_of, 2), (halve_of, 1), (features_of, 0), (settle_of, 1), (down_of, 2),
+        (share_of, 0), (settle_of, 2), (double_of, 1), (features_of, 1), (shared_of, 0),
         (features_of, 2), (share_of, 1), (share_of, 2), (finish_of, 0), (finish_of, 1),
         (finish_of, 2),
     )

time: 234 us -> 237 us (1.013)
  waiting for transfers between devices: 92.7 us -> 102 us
  starting transfers between devices: 52 us -> 45 us
    ppermute x10, waiting for transfers between devices: 34.1 us -> 47.3 us  [send(): lax.ppermute(value, axis, [(d, (d + hop) % size) for d in range(size)])]
    ppermute x18, starting transfers between devices: 33.8 us -> 28.5 us  [swap(): return lax.ppermute(value, axis, [(d, d ^ bit) for d in range(size)])]
    ppermute x11, waiting for transfers between devices: 14.1 us -> 11 us  [shift(): lax.ppermute(value, axis, [((d + hop) % size, d) for d in range(size)])]
  transfers between devices with their start and end apart: 39 -> 39, of which waited for: 25 -> 22; matrix products, arithmetic and copies ran while one was open for 2% -> 2% of each run, Pallas kernels for 33% -> 33%
where the time goes in v13:
time: 237 us
  waiting for transfers between devices  102 us (43%)
  Pallas kernels  78.2 us (33%)
  starting transfers between devices  45 us (19%)
  local copies, waits for them, and re-layouts  5.69 us (2%)
  other arithmetic  5.24 us (2%)
    ppermute x10, waiting for transfers between devices, send(): lax.ppermute(value, axis, [(d, (d + hop) % size) for d in range(size)])  47.3 us
    ppermute x18, waiting for transfers between devices, swap(): return lax.ppermute(value, axis, [(d, d ^ bit) for d in range(size)])  43.9 us
    pallas_call x4, Pallas kernels, gate_up(): pl.pallas_call(functools.partial(gate_up_body, tiles, first), grid=(tiles...  37.6 us
    ppermute x18, starting transfers between devices, swap(): return lax.ppermute(value, axis, [(d, d ^ bit) for d in range(size)])  28.5 us
    pallas_call x3, Pallas kernels, encode(): pl.pallas_call(functools.partial(encode_body, members, order, tiles), gri...  21.9 us
    pallas_call x3, Pallas kernels, down(): pl.pallas_call(functools.partial(down_body, owners, members, pieces, orde...  18.7 us
    ppermute x11, waiting for transfers between devices, shift(): lax.ppermute(value, axis, [((d + hop) % size, d) for d in range(size)])  11 us
    ppermute x10, starting transfers between devices, send(): lax.ppermute(value, axis, [(d, (d + hop) % size) for d in range(size)])  8.37 us
  transfers between devices with their start and end apart: 39, of which 22 were waited for; matrix products, arithmetic and copies ran while one was open for 2% of the time, Pallas kernels for 33%

profile of v13, /device:TPU:0, one launch (start us, length us, event | category | flops | bytes accessed | tf_op | source)
XLA Modules:
  0.0 236.9 jit_solution(15092094509962283806)
XLA Ops:
  1.1 4.1 %collective-permute-start = (bf16[1,48,1024]{2,1,0:T(8,128)(2,1)S(1)}, bf16[1,48,1024]{2,1,0:T(8,128)(2,1)S(1)}, u32[]{:S(2)}, u32[]{:S(2)}) collective-permute-start(bf16[1,48,1024]{2,1,0:T(8,128)(2,1)S(1)} %dynamic-slice_bitcast_fusion.1), channel_id=1, source_target_pairs={{0,8},{4,12},{8,0},{12,4},{1,9},{5,13},{9,1},{13,5},{2,10},{6,14},... | collective-permute-start | bytes 294920 | tf_op jit(solution)/shard_map/ppermute | solution.py:27
  5.2 4.9 %collective-permute-done = bf16[1,48,1024]{2,1,0:T(8,128)(2,1)S(1)} collective-permute-done((bf16[1,48,1024]{2,1,0:T(8,128)(2,1)S(1)}, bf16[1,48,1024]{2,1,0:T(8,128)(2,1)S(1)}, u32[]{:S(2)}, u32[]{:S(2)}) %collective-permute-start) | collective-permute-done | bytes 98336 | tf_op jit(solution)/shard_map/ppermute | solution.py:27
  15.0 5.1 %collective-permute-done.7 = bf16[1,80,1024]{2,1,0:T(8,128)(2,1)S(1)} collective-permute-done((bf16[1,80,1024]{2,1,0:T(8,128)(2,1)S(1)}, bf16[1,80,1024]{2,1,0:T(8,128)(2,1)S(1)}, u32[]{:S(2)}, u32[]{:S(2)}) %collective-permute-start.7) | collective-permute-done | bytes 163872 | tf_op jit(solution)/shard_map/ppermute | solution.py:27
  23.2 3.8 %collective-permute-done.3 = f32[48]{0:T(128)S(1)} collective-permute-done((f32[48]{0:T(128)S(1)}, f32[48]{0:T(128)S(1)}, u32[]{:S(2)}, u32[]{:S(2)}) %collective-permute-start.3) | collective-permute-done | bytes 224 | tf_op jit(solution)/shard_map/ppermute | solution.py:19
  32.3 7.2 %shard_map.82 = (f32[2,96,1792]{2,1,0:T(8,128)S(1)}, bf16[2,96,1792]{2,1,0:T(8,128)(2,1)S(1)}) custom-call(bf16[2,2,2,48,1024]{4,3,2,1,0:T(8,128)(2,1)S(1)} %multiply_convert_fusion.1.x_ref, bf16[1,2048,3584]{2,1,0:T(8,128)(2,1)} %gate_ref.7, bf16[1,2048,3584]{2,1,0:T(8,128)(2,1)} %up_ref.7), custom_call_target="tpu_custom_call" | custom-call | flops 1 | bytes 1 | tf_op jit(solution)/shard_map/pallas_call | solution.py:127
  42.4 7.2 %shard_map.83 = (f32[2,96,1792]{2,1,0:T(8,128)S(1)}, bf16[2,96,1792]{2,1,0:T(8,128)(2,1)S(1)}) custom-call(bf16[2,2,2,48,1024]{4,3,2,1,0:T(8,128)(2,1)S(1)} %multiply_convert_fusion.1.x_ref, bf16[1,2048,3584]{2,1,0:T(8,128)(2,1)} %gate_ref.7, bf16[1,2048,3584]{2,1,0:T(8,128)(2,1)} %up_ref.7, f32[2,96,1792]{2,1,0:T(8,128)S(1)} %get-tuple-element.72.refs_0_, ...), custom_call_target="tpu_custom_call" | custom-call | flops 1 | bytes 1 | tf_op jit(solution)/shard_map/pallas_call | solution.py:127
  51.9 5.2 %collective-permute-done.12 = f32[2,80]{1,0:T(2,128)S(1)} collective-permute-done((f32[2,80]{1,0:T(2,128)S(1)}, f32[2,80]{1,0:T(2,128)S(1)}, u32[]{:S(2)}, u32[]{:S(2)}) %collective-permute-start.12) | collective-permute-done | bytes 672 | tf_op jit(solution)/shard_map/ppermute | solution.py:19
  57.5 12.5 %collective-permute-done.11 = bf16[2,96,1792]{2,1,0:T(8,128)(2,1)S(1)} collective-permute-done((bf16[2,96,1792]{2,1,0:T(8,128)(2,1)S(1)}, bf16[2,96,1792]{2,1,0:T(8,128)(2,1)S(1)}, u32[]{:S(2)}, u32[]{:S(2)}) %collective-permute-start.11) | collective-permute-done | bytes 688160 | tf_op jit(solution)/shard_map/ppermute | solution.py:23
  71.8 11.7 %shard_map.84 = (f32[2,96,3584]{2,1,0:T(8,128)S(1)}, bf16[2,96,3584]{2,1,0:T(8,128)(2,1)S(1)}) custom-call(bf16[2,2,2,48,1024]{4,3,2,1,0:T(8,128)(2,1)S(1)} %multiply_convert_fusion.x_ref, bf16[1,2048,3584]{2,1,0:T(8,128)(2,1)} %gate_ref.7, bf16[1,2048,3584]{2,1,0:T(8,128)(2,1)} %up_ref.7, f32[2,96,1792]{2,1,0:T(8,128)S(1)} %get-tuple-element.81.refs_0_, ...), custom_call_target="tpu_custom_call" | custom-call | flops 1 | bytes 1 | tf_op jit(solution)/shard_map/pallas_call | solution.py:127
  86.4 6.4 %shard_map.85 = (f32[96,2048]{1,0:T(8,128)S(1)}, bf16[96,2048]{1,0:T(8,128)(2,1)S(1)}) custom-call(s32[1]{0:T(128)} %bitcast.rank_ref, bf16[96,3584]{1,0:T(8,128)(2,1)S(1)} %pad_maximum_fusion.refs_4_.refs_0_, bf16[96,3584]{1,0:T(8,128)(2,1)S(1)} %collective-permute-done.13.refs_1_, bf16[1,3584,2048]{2,1,0:T(8,128)(2,1)} %refs_2_.5, f32[2,96,3584]{2,1,0:T(8,128)} %copy-done.2), custom_call_target="tpu_custom_call" | custom-call | flops 1 | bytes 1 | tf_op jit(solution)/shard_map/pallas_call | solution.py:175
  93.2 7.9 %collective-permute-done.15 = bf16[96,2048]{1,0:T(8,128)(2,1)S(1)} collective-permute-done((bf16[96,2048]{1,0:T(8,128)(2,1)S(1)}, bf16[96,2048]{1,0:T(8,128)(2,1)S(1)}, u32[]{:S(2)}, u32[]{:S(2)}) %collective-permute-start.15) | collective-permute-done | bytes 393248 | tf_op jit(solution)/shard_map/ppermute | solution.py:27
  104.6 11.0 %collective-permute-done.17 = bf16[2,96,3584]{2,1,0:T(8,128)(2,1)S(1)} collective-permute-done((bf16[2,96,3584]{2,1,0:T(8,128)(2,1)S(1)}, bf16[2,96,3584]{2,1,0:T(8,128)(2,1)S(1)}, u32[]{:S(2)}, u32[]{:S(2)}) %collective-permute-start.17) | collective-permute-done | bytes 1376288 | tf_op jit(solution)/shard_map/ppermute | solution.py:23
  118.1 11.4 %shard_map.86 = (f32[2,64,3584]{2,1,0:T(8,128)S(1)}, bf16[2,64,3584]{2,1,0:T(8,128)(2,1)S(1)}) custom-call(bf16[2,2,2,32,1024]{4,3,2,1,0:T(8,128)(2,1)S(1)} %multiply_convert_fusion.2.x_ref, bf16[1,2048,3584]{2,1,0:T(8,128)(2,1)} %gate_ref.7, bf16[1,2048,3584]{2,1,0:T(8,128)(2,1)} %up_ref.7, f32[96,2048]{1,0:T(8,128)S(1)} %get-tuple-element.86.refs_0_, ...), custom_call_target="tpu_custom_call" | custom-call | flops 1 | bytes 1 | tf_op jit(solution)/shard_map/pallas_call | solution.py:127
  133.8 6.4 %shard_map.87 = (f32[96,2048]{1,0:T(8,128)S(1)}, bf16[96,2048]{1,0:T(8,128)(2,1)S(1)}) custom-call(s32[1]{0:T(128)} %bitcast.rank_ref, bf16[96,3584]{1,0:T(8,128)(2,1)S(1)} %fusion.1.refs_2_.refs_0_, bf16[96,3584]{1,0:T(8,128)(2,1)S(1)} %collective-permute-done.19.refs_1_, bf16[1,3584,2048]{2,1,0:T(8,128)(2,1)} %refs_2_.5, f32[2,64,3584]{2,1,0:T(8,128)} %copy-done.4, ...), custom_call_target="tpu_custom_call" | custom-call | flops 1 | bytes 1 | tf_op jit(solution)/shard_map/pallas_call | solution.py:175
  142.4 9.0 %collective-permute-done.21 = bf16[2,64,3584]{2,1,0:T(8,128)(2,1)S(1)} collective-permute-done((bf16[2,64,3584]{2,1,0:T(8,128)(2,1)S(1)}, bf16[2,64,3584]{2,1,0:T(8,128)(2,1)S(1)}, u32[]{:S(2)}, u32[]{:S(2)}) %collective-permute-start.21) | collective-permute-done | bytes 917536 | tf_op jit(solution)/shard_map/ppermute | solution.py:23
  156.1 5.7 %collective-permute-done.20.far_ref = bf16[96,2048]{1,0:T(8,128)(2,1)S(1)} collective-permute-done((bf16[96,2048]{1,0:T(8,128)(2,1)S(1)}, bf16[96,2048]{1,0:T(8,128)(2,1)S(1)}, u32[]{:S(2)}, u32[]{:S(2)}) %collective-permute-start.20) | collective-permute-done | bytes 393248 | tf_op jit(solution)/shard_map/ppermute | solution.py:27
  161.9 7.6 %shard_map.88 = (f32[96,4096]{1,0:T(8,128)}, bf16[96,4096]{1,0:T(8,128)(2,1)S(1)}) custom-call(s32[1]{0:T(128)} %bitcast.rank_ref, bf16[96,2048]{1,0:T(8,128)(2,1)S(1)} %constant_dynamic-update-slice_fusion.near_ref.refs_1_, bf16[96,2048]{1,0:T(8,128)(2,1)S(1)} %collective-permute-done.20.far_ref, bf16[1,2048,4096]{2,1,0:T(8,128)(2,1)} %weight_ref.5, ...), custom_call_target="tpu_custom_call" | custom-call | flops 1 | bytes 1 | tf_op jit(solution)/shard_map/pallas_call | solution.py:221
  170.7 5.9 %shard_map.89 = (f32[64,2048]{1,0:T(8,128)S(1)}, bf16[64,2048]{1,0:T(8,128)(2,1)S(1)}) custom-call(s32[1]{0:T(128)} %bitcast.rank_ref, bf16[64,3584]{1,0:T(8,128)(2,1)S(1)} %fusion.3.refs_2_.refs_0_, bf16[64,3584]{1,0:T(8,128)(2,1)S(1)} %collective-permute-done.24.refs_1_, bf16[1,3584,2048]{2,1,0:T(8,128)(2,1)} %refs_2_.5, ...), custom_call_target="tpu_custom_call" | custom-call | flops 1 | bytes 1 | tf_op jit(solution)/shard_map/pallas_call | solution.py:175
  181.1 4.3 %collective-permute-done.27 = bf16[48,2048]{1,0:T(8,128)(2,1)S(1)} collective-permute-done((bf16[48,2048]{1,0:T(8,128)(2,1)S(1)}, bf16[48,2048]{1,0:T(8,128)(2,1)S(1)}, u32[]{:S(2)}, u32[]{:S(2)}) %collective-permute-start.27) | collective-permute-done | bytes 196640 | tf_op jit(solution)/shard_map/ppermute | solution.py:27
  187.9 5.7 %collective-permute-done.30 = bf16[32,2048]{1,0:T(8,128)(2,1)S(1)} collective-permute-done((bf16[32,2048]{1,0:T(8,128)(2,1)S(1)}, bf16[32,2048]{1,0:T(8,128)(2,1)S(1)}, u32[]{:S(2)}, u32[]{:S(2)}) %collective-permute-start.30) | collective-permute-done | bytes 131104 | tf_op jit(solution)/shard_map/ppermute | solution.py:27
  202.8 7.6 %shard_map.90 = (f32[96,4096]{1,0:T(8,128)}, bf16[96,4096]{1,0:T(8,128)(2,1)S(1)}) custom-call(s32[1]{0:T(128)} %bitcast.rank_ref, bf16[96,2048]{1,0:T(8,128)(2,1)S(1)} %constant_dynamic-update-slice_fusion.2.near_ref.refs_3_, bf16[96,2048]{1,0:T(8,128)(2,1)S(1)} %collective-permute-done.28.far_ref, bf16[1,2048,4096]{2,1,0:T(8,128)(2,1)} %weight_ref.5, ...), custom_call_target="tpu_custom_call" | custom-call | flops 1 | bytes 1 | tf_op jit(solution)/shard_map/pallas_call | solution.py:221
  210.6 6.6 %shard_map.91 = (f32[64,4096]{1,0:T(8,128)S(1)}, bf16[64,4096]{1,0:T(8,128)(2,1)S(1)}) custom-call(s32[1]{0:T(128)} %bitcast.rank_ref, bf16[64,2048]{1,0:T(8,128)(2,1)S(1)} %get-tuple-element.153.near_ref, bf16[64,2048]{1,0:T(8,128)(2,1)S(1)} %get-tuple-element.154.far_ref, bf16[1,2048,4096]{2,1,0:T(8,128)(2,1)} %weight_ref.5, ...), custom_call_target="tpu_custom_call" | custom-call | flops 1 | bytes 1 | tf_op jit(solution)/shard_map/pallas_call | solution.py:221
  221.2 9.7 %collective-permute-done.36 = bf16[48,4096]{1,0:T(8,128)(2,1)S(1)} collective-permute-done((bf16[48,4096]{1,0:T(8,128)(2,1)S(1)}, bf16[48,4096]{1,0:T(8,128)(2,1)S(1)}, u32[]{:S(2)}, u32[]{:S(2)}) %collective-permute-start.36) | collective-permute-done | bytes 393248 | tf_op jit(solution)/shard_map/ppermute | solution.py:23
  231.0 5.0 %collective-permute-done.38 = bf16[32,4096]{1,0:T(8,128)(2,1)S(1)} collective-permute-done((bf16[32,4096]{1,0:T(8,128)(2,1)S(1)}, bf16[32,4096]{1,0:T(8,128)(2,1)S(1)}, u32[]{:S(2)}, u32[]{:S(2)}) %collective-permute-start.38) | collective-permute-done | bytes 262176 | tf_op jit(solution)/shard_map/ppermute | solution.py:23
  (154 shorter events, 64.2 us)
Async XLA Ops:
  31.4 11.0 %collective-permute-start.9 = (bf16[2,80,1024]{2,1,0:T(8,128)(2,1)S(1)}, bf16[2,80,1024]{2,1,0:T(8,128)(2,1)S(1)}, u32[]{:S(2)}, u32[]{:S(2)}) collective-permute-start(bf16[2,80,1024]{2,1,0:T(8,128)(2,1)S(1)} %pad_maximum_fusion.8), channel_id=1, source_target_pairs={{2,0},{0,2},{3,1},{1,3},{6,4},{4,6},{7,5},{5,7},{10,8},{8,10},{11,... | collective-permute-start | bytes 983048 | tf_op jit(solution)/shard_map/ppermute | solution.py:19
  39.5 17.7 %collective-permute-start.6 = (bf16[2,96,1792]{2,1,0:T(8,128)(2,1)S(1)}, bf16[2,96,1792]{2,1,0:T(8,128)(2,1)S(1)}, u32[]{:S(2)}, u32[]{:S(2)}) collective-permute-start(bf16[2,96,1792]{2,1,0:T(8,128)(2,1)S(1)} %get-tuple-element.73), channel_id=1, source_target_pairs={{0,2},{2,0},{1,3},{3,1},{4,6},{6,4},{5,7},{7,5},{8,10},{10,8},{9,1... | collective-permute-start | bytes 2064392 | tf_op jit(solution)/shard_map/ppermute | solution.py:23
  50.1 21.4 %collective-permute-start.14 = (bf16[2,2,80,1024]{3,2,1,0:T(8,128)(2,1)S(1)}, bf16[2,2,80,1024]{3,2,1,0:T(8,128)(2,1)S(1)}, u32[]{:S(2)}, u32[]{:S(2)}) collective-permute-start(bf16[2,2,80,1024]{3,2,1,0:T(8,128)(2,1)S(1)} %get-tuple-element.135), channel_id=1, source_target_pairs={{1,0},{0,1},{3,2},{2,3},{5,4},{4,5},{7,6},{6,7},{9,8},{8,9},{11,10... | collective-permute-start | bytes 1966088 | tf_op jit(solution)/shard_map/ppermute | solution.py:19
  50.2 19.8 %collective-permute-start.11 = (bf16[2,96,1792]{2,1,0:T(8,128)(2,1)S(1)}, bf16[2,96,1792]{2,1,0:T(8,128)(2,1)S(1)}, u32[]{:S(2)}, u32[]{:S(2)}) collective-permute-start(bf16[2,96,1792]{2,1,0:T(8,128)(2,1)S(1)} %get-tuple-element.79), channel_id=1, source_target_pairs={{0,2},{2,0},{1,3},{3,1},{4,6},{6,4},{5,7},{7,5},{8,10},{10,8},{9,1... | collective-permute-start | bytes 2064392 | tf_op jit(solution)/shard_map/ppermute | solution.py:23
  70.4 16.0 %collective-permute-start.13 = (bf16[96,3584]{1,0:T(8,128)(2,1)S(1)}, bf16[96,3584]{1,0:T(8,128)(2,1)S(1)}, u32[]{:S(2)}, u32[]{:S(2)}) collective-permute-start(bf16[96,3584]{1,0:T(8,128)(2,1)S(1)} %pad_maximum_fusion.refs_4_.refs_0_), channel_id=1, source_target_pairs={{2,0},{0,2},{3,1},{1,3},{6,4},{4,6},{7,5},{5,7},{10,8},{8,10},{11,... | collective-permute-start | bytes 2064392 | tf_op jit(solution)/shard_map/ppermute | solution.py:19
  85.0 30.6 %collective-permute-start.17 = (bf16[2,96,3584]{2,1,0:T(8,128)(2,1)S(1)}, bf16[2,96,3584]{2,1,0:T(8,128)(2,1)S(1)}, u32[]{:S(2)}, u32[]{:S(2)}) collective-permute-start(bf16[2,96,3584]{2,1,0:T(8,128)(2,1)S(1)} %get-tuple-element.88), channel_id=1, source_target_pairs={{0,2},{2,0},{1,3},{3,1},{4,6},{6,4},{5,7},{7,5},{8,10},{10,8},{9,1... | collective-permute-start | bytes 4128776 | tf_op jit(solution)/shard_map/ppermute | solution.py:23
  101.3 29.6 %collective-permute-start.16 = (bf16[48,2048]{1,0:T(8,128)(2,1)S(1)}, bf16[48,2048]{1,0:T(8,128)(2,1)S(1)}, u32[]{:S(2)}, u32[]{:S(2)}) collective-permute-start(bf16[48,2048]{1,0:T(8,128)(2,1)S(1)} %slice.229.refs_1_), channel_id=1, source_target_pairs={{0,8},{4,12},{8,0},{12,4},{1,9},{5,13},{9,1},{13,5},{2,10},{6,14},... | collective-permute-start | bytes 589832 | tf_op jit(solution)/shard_map/ppermute | solution.py:27
  116.3 17.5 %collective-permute-start.19 = (bf16[96,3584]{1,0:T(8,128)(2,1)S(1)}, bf16[96,3584]{1,0:T(8,128)(2,1)S(1)}, u32[]{:S(2)}, u32[]{:S(2)}) collective-permute-start(bf16[96,3584]{1,0:T(8,128)(2,1)S(1)} %fusion.1.refs_2_.refs_0_), channel_id=1, source_target_pairs={{2,0},{0,2},{3,1},{1,3},{6,4},{4,6},{7,5},{5,7},{10,8},{8,10},{11,... | collective-permute-start | bytes 2064392 | tf_op jit(solution)/shard_map/ppermute | solution.py:19
  130.8 20.6 %collective-permute-start.21 = (bf16[2,64,3584]{2,1,0:T(8,128)(2,1)S(1)}, bf16[2,64,3584]{2,1,0:T(8,128)(2,1)S(1)}, u32[]{:S(2)}, u32[]{:S(2)}) collective-permute-start(bf16[2,64,3584]{2,1,0:T(8,128)(2,1)S(1)} %get-tuple-element.97), channel_id=1, source_target_pairs={{0,2},{2,0},{1,3},{3,1},{4,6},{6,4},{5,7},{7,5},{8,10},{10,8},{9,1... | collective-permute-start | bytes 2752520 | tf_op jit(solution)/shard_map/ppermute | solution.py:23
  131.3 10.4 %collective-permute-start.18 = (bf16[48,2048]{1,0:T(8,128)(2,1)S(1)}, bf16[48,2048]{1,0:T(8,128)(2,1)S(1)}, u32[]{:S(2)}, u32[]{:S(2)}) collective-permute-start(bf16[48,2048]{1,0:T(8,128)(2,1)S(1)} %add_convert_fusion.1.refs_4_), channel_id=1, source_target_pairs={{0,8},{4,12},{8,0},{12,4},{1,9},{5,13},{9,1},{13,5},{2,10},{6,14},... | collective-permute-start | bytes 589832 | tf_op jit(solution)/shard_map/ppermute | solution.py:27
  140.2 12.1 %collective-permute-start.22 = (bf16[96,2048]{1,0:T(8,128)(2,1)S(1)}, bf16[96,2048]{1,0:T(8,128)(2,1)S(1)}, u32[]{:S(2)}, u32[]{:S(2)}) collective-permute-start(bf16[96,2048]{1,0:T(8,128)(2,1)S(1)} %get-tuple-element.100), channel_id=1, source_target_pairs={{0,4},{4,0},{8,12},{12,8},{1,5},{5,1},{9,13},{13,9},{2,6},{6,2},{1... | collective-permute-start | bytes 1179656 | tf_op jit(solution)/shard_map/ppermute | solution.py:27
  141.8 20.1 %collective-permute-start.20 = (bf16[96,2048]{1,0:T(8,128)(2,1)S(1)}, bf16[96,2048]{1,0:T(8,128)(2,1)S(1)}, u32[]{:S(2)}, u32[]{:S(2)}) collective-permute-start(bf16[96,2048]{1,0:T(8,128)(2,1)S(1)} %constant_dynamic-update-slice_fusion.near_ref.refs_1_), channel_id=1, source_target_pairs={{0,4},{4,0},{8,12},{12,8},{1,5},{5,1},{9,13},{13,9},{2,6},{6,2},{1... | collective-permute-start | bytes 1179656 | tf_op jit(solution)/shard_map/ppermute | solution.py:27
  152.5 17.2 %collective-permute-start.25 = (bf16[48,2048]{1,0:T(8,128)(2,1)S(1)}, bf16[48,2048]{1,0:T(8,128)(2,1)S(1)}, u32[]{:S(2)}, u32[]{:S(2)}) collective-permute-start(bf16[48,2048]{1,0:T(8,128)(2,1)S(1)} %slice.228.refs_3_), channel_id=1, source_target_pairs={{0,8},{4,12},{8,0},{12,4},{1,9},{5,13},{9,1},{13,5},{2,10},{6,14},... | collective-permute-start | bytes 589832 | tf_op jit(solution)/shard_map/ppermute | solution.py:27
  154.4 16.3 %collective-permute-start.24 = (bf16[64,3584]{1,0:T(8,128)(2,1)S(1)}, bf16[64,3584]{1,0:T(8,128)(2,1)S(1)}, u32[]{:S(2)}, u32[]{:S(2)}) collective-permute-start(bf16[64,3584]{1,0:T(8,128)(2,1)S(1)} %fusion.3.refs_2_.refs_0_), channel_id=1, source_target_pairs={{2,0},{0,2},{3,1},{1,3},{6,4},{4,6},{7,5},{5,7},{10,8},{8,10},{11,... | collective-permute-start | bytes 1376264 | tf_op jit(solution)/shard_map/ppermute | solution.py:19
  169.6 24.0 %collective-permute-start.23 = (bf16[96,4096]{1,0:T(8,128)(2,1)S(1)}, bf16[96,4096]{1,0:T(8,128)(2,1)S(1)}, u32[]{:S(2)}, u32[]{:S(2)}) collective-permute-start(bf16[96,4096]{1,0:T(8,128)(2,1)S(1)} %get-tuple-element.106), channel_id=1, source_target_pairs={{0,1},{1,0},{2,3},{3,2},{4,5},{5,4},{6,7},{7,6},{8,9},{9,8},{10,11... | collective-permute-start | bytes 2359304 | tf_op jit(solution)/shard_map/ppermute | solution.py:23
  169.7 15.7 %collective-permute-start.27 = (bf16[48,2048]{1,0:T(8,128)(2,1)S(1)}, bf16[48,2048]{1,0:T(8,128)(2,1)S(1)}, u32[]{:S(2)}, u32[]{:S(2)}) collective-permute-start(bf16[48,2048]{1,0:T(8,128)(2,1)S(1)} %add_convert_fusion.refs_4_), channel_id=1, source_target_pairs={{0,8},{4,12},{8,0},{12,4},{1,9},{5,13},{9,1},{13,5},{2,10},{6,14},... | collective-permute-start | bytes 589832 | tf_op jit(solution)/shard_map/ppermute | solution.py:27
  179.6 13.9 %collective-permute-start.30 = (bf16[32,2048]{1,0:T(8,128)(2,1)S(1)}, bf16[32,2048]{1,0:T(8,128)(2,1)S(1)}, u32[]{:S(2)}, u32[]{:S(2)}) collective-permute-start(bf16[32,2048]{1,0:T(8,128)(2,1)S(1)} %slice.230), channel_id=1, source_target_pairs={{0,8},{4,12},{8,0},{12,4},{1,9},{5,13},{9,1},{13,5},{2,10},{6,14},... | collective-permute-start | bytes 393224 | tf_op jit(solution)/shard_map/ppermute | solution.py:27
  185.5 17.3 %collective-permute-start.28 = (bf16[96,2048]{1,0:T(8,128)(2,1)S(1)}, bf16[96,2048]{1,0:T(8,128)(2,1)S(1)}, u32[]{:S(2)}, u32[]{:S(2)}) collective-permute-start(bf16[96,2048]{1,0:T(8,128)(2,1)S(1)} %constant_dynamic-update-slice_fusion.2.near_ref.refs_3_), channel_id=1, source_target_pairs={{0,4},{4,0},{8,12},{12,8},{1,5},{5,1},{9,13},{13,9},{2,6},{6,2},{1... | collective-permute-start | bytes 1179656 | tf_op jit(solution)/shard_map/ppermute | solution.py:27
  193.8 16.8 %collective-permute-start.26 = (bf16[48,4096]{1,0:T(8,128)(2,1)S(1)}, bf16[48,4096]{1,0:T(8,128)(2,1)S(1)}, u32[]{:S(2)}, u32[]{:S(2)}) collective-permute-start(bf16[48,4096]{1,0:T(8,128)(2,1)S(1)} %slice.226.refs_1_), channel_id=1, source_target_pairs={{0,2},{2,0},{1,3},{3,1},{4,6},{6,4},{5,7},{7,5},{8,10},{10,8},{9,1... | collective-permute-start | bytes 1179656 | tf_op jit(solution)/shard_map/ppermute | solution.py:23
  194.6 15.8 %collective-permute-start.33 = (bf16[32,2048]{1,0:T(8,128)(2,1)S(1)}, bf16[32,2048]{1,0:T(8,128)(2,1)S(1)}, u32[]{:S(2)}, u32[]{:S(2)}) collective-permute-start(bf16[32,2048]{1,0:T(8,128)(2,1)S(1)} %add_convert_fusion.2.refs_2_), channel_id=1, source_target_pairs={{0,4},{4,0},{8,12},{12,8},{1,5},{5,1},{9,13},{13,9},{2,6},{6,2},{1... | collective-permute-start | bytes 393224 | tf_op jit(solution)/shard_map/ppermute | solution.py:27
  194.7 15.8 %collective-permute-start.34 = (bf16[32,2048]{1,0:T(8,128)(2,1)S(1)}, bf16[32,2048]{1,0:T(8,128)(2,1)S(1)}, u32[]{:S(2)}, u32[]{:S(2)}) collective-permute-start(bf16[32,2048]{1,0:T(8,128)(2,1)S(1)} %add_convert_fusion.2.refs_2_), channel_id=1, source_target_pairs={{0,8},{4,12},{8,0},{12,4},{1,9},{5,13},{9,1},{13,5},{2,10},{6,14},... | collective-permute-start | bytes 393224 | tf_op jit(solution)/shard_map/ppermute | solution.py:27
  197.4 13.0 %collective-permute-start.35 = (bf16[32,2048]{1,0:T(8,128)(2,1)S(1)}, bf16[32,2048]{1,0:T(8,128)(2,1)S(1)}, u32[]{:S(2)}, u32[]{:S(2)}) collective-permute-start(bf16[32,2048]{1,0:T(8,128)(2,1)S(1)} %add_convert_fusion.2.refs_2_), channel_id=1, source_target_pairs={{0,12},{4,8},{8,4},{12,0},{1,13},{5,9},{9,5},{13,1},{2,14},{6,10},... | collective-permute-start | bytes 393224 | tf_op jit(solution)/shard_map/ppermute | solution.py:27
  218.9 12.0 %collective-permute-start.36 = (bf16[48,4096]{1,0:T(8,128)(2,1)S(1)}, bf16[48,4096]{1,0:T(8,128)(2,1)S(1)}, u32[]{:S(2)}, u32[]{:S(2)}) collective-permute-start(bf16[48,4096]{1,0:T(8,128)(2,1)S(1)} %slice.225), channel_id=1, source_target_pairs={{0,2},{2,0},{1,3},{3,1},{4,6},{6,4},{5,7},{7,5},{8,10},{10,8},{9,1... | collective-permute-start | bytes 1179656 | tf_op jit(solution)/shard_map/ppermute | solution.py:23
  219.5 16.6 %collective-permute-start.38 = (bf16[32,4096]{1,0:T(8,128)(2,1)S(1)}, bf16[32,4096]{1,0:T(8,128)(2,1)S(1)}, u32[]{:S(2)}, u32[]{:S(2)}) collective-permute-start(bf16[32,4096]{1,0:T(8,128)(2,1)S(1)} %slice.227), channel_id=1, source_target_pairs={{0,2},{2,0},{1,3},{3,1},{4,6},{6,4},{5,7},{7,5},{8,10},{10,8},{9,1... | collective-permute-start | bytes 786440 | tf_op jit(solution)/shard_map/ppermute | solution.py:23
  (28 other events, 234.4 us)

commit v14 on v12

--- a/solution.py
+++ b/solution.py
@@ -457,7 +457,7 @@
         (gate_up_of, 0), (hidden_of, 0), (gate_up_of, 1), (down_of, 0), (halve_of, 0),
         (hidden_of, 1), (settle_of, 0), (gate_up_of, 2), (double_of, 0), (down_of, 1),
         (features_of, 0), (hidden_of, 2), (halve_of, 1), (settle_of, 1), (down_of, 2),
-        (share_of, 0), (settle_of, 2), (double_of, 1), (shared_of, 0), (features_of, 1),
+        (share_of, 0), (settle_of, 2), (double_of, 1), (features_of, 1), (shared_of, 0),
         (features_of, 2), (share_of, 1), (share_of, 2), (finish_of, 0), (finish_of, 1),
         (finish_of, 2),
     )

time: 234 us -> 233 us (level)
  waiting for transfers between devices: 92.7 us -> 89.7 us
    ppermute x10, waiting for transfers between devices: 34.1 us -> 29.4 us  [send(): lax.ppermute(value, axis, [(d, (d + hop) % size) for d in range(size)])]
  transfers between devices with their start and end apart: 39 -> 39, of which waited for: 25 -> 24; matrix products, arithmetic and copies ran while one was open for 2% -> 2% of each run, Pallas kernels for 33% -> 33%
where the time goes in v14:
time: 233 us
  waiting for transfers between devices  89.7 us (38%)
  Pallas kernels  78 us (33%)
  starting transfers between devices  54 us (23%)
  local copies, waits for them, and re-layouts  5.69 us (2%)
  other arithmetic  5.19 us (2%)
    ppermute x18, waiting for transfers between devices, swap(): return lax.ppermute(value, axis, [(d, d ^ bit) for d in range(size)])  46.2 us
    pallas_call x4, Pallas kernels, gate_up(): pl.pallas_call(functools.partial(gate_up_body, tiles, first), grid=(tiles...  37.5 us
    ppermute x18, starting transfers between devices, swap(): return lax.ppermute(value, axis, [(d, d ^ bit) for d in range(size)])  33.8 us
    ppermute x10, waiting for transfers between devices, send(): lax.ppermute(value, axis, [(d, (d + hop) % size) for d in range(size)])  29.4 us
    pallas_call x3, Pallas kernels, encode(): pl.pallas_call(functools.partial(encode_body, members, order, tiles), gri...  22 us
    pallas_call x3, Pallas kernels, down(): pl.pallas_call(functools.partial(down_body, owners, members, pieces, orde...  18.5 us
    ppermute x11, waiting for transfers between devices, shift(): lax.ppermute(value, axis, [((d + hop) % size, d) for d in range(size)])  14.1 us
    ppermute x10, starting transfers between devices, send(): lax.ppermute(value, axis, [(d, (d + hop) % size) for d in range(size)])  12.7 us
  transfers between devices with their start and end apart: 39, of which 24 were waited for; matrix products, arithmetic and copies ran while one was open for 2% of the time, Pallas kernels for 33%

profile of v14, /device:TPU:0, one launch (start us, length us, event | category | flops | bytes accessed | tf_op | source)
XLA Modules:
  0.0 233.1 jit_solution(17319754996211385204)
XLA Ops:
  1.1 4.1 %collective-permute-start = (bf16[1,48,1024]{2,1,0:T(8,128)(2,1)S(1)}, bf16[1,48,1024]{2,1,0:T(8,128)(2,1)S(1)}, u32[]{:S(2)}, u32[]{:S(2)}) collective-permute-start(bf16[1,48,1024]{2,1,0:T(8,128)(2,1)S(1)} %dynamic-slice_bitcast_fusion.1), channel_id=1, source_target_pairs={{0,8},{4,12},{8,0},{12,4},{1,9},{5,13},{9,1},{13,5},{2,10},{6,14},... | collective-permute-start | bytes 294920 | tf_op jit(solution)/shard_map/ppermute | solution.py:27
  5.2 4.9 %collective-permute-done = bf16[1,48,1024]{2,1,0:T(8,128)(2,1)S(1)} collective-permute-done((bf16[1,48,1024]{2,1,0:T(8,128)(2,1)S(1)}, bf16[1,48,1024]{2,1,0:T(8,128)(2,1)S(1)}, u32[]{:S(2)}, u32[]{:S(2)}) %collective-permute-start) | collective-permute-done | bytes 98336 | tf_op jit(solution)/shard_map/ppermute | solution.py:27
  15.0 5.1 %collective-permute-done.7 = bf16[1,80,1024]{2,1,0:T(8,128)(2,1)S(1)} collective-permute-done((bf16[1,80,1024]{2,1,0:T(8,128)(2,1)S(1)}, bf16[1,80,1024]{2,1,0:T(8,128)(2,1)S(1)}, u32[]{:S(2)}, u32[]{:S(2)}) %collective-permute-start.7) | collective-permute-done | bytes 163872 | tf_op jit(solution)/shard_map/ppermute | solution.py:27
  32.2 7.2 %shard_map.82 = (f32[2,96,1792]{2,1,0:T(8,128)S(1)}, bf16[2,96,1792]{2,1,0:T(8,128)(2,1)S(1)}) custom-call(bf16[2,2,2,48,1024]{4,3,2,1,0:T(8,128)(2,1)S(1)} %multiply_convert_fusion.1.x_ref, bf16[1,2048,3584]{2,1,0:T(8,128)(2,1)} %gate_ref.7, bf16[1,2048,3584]{2,1,0:T(8,128)(2,1)} %up_ref.7), custom_call_target="tpu_custom_call" | custom-call | flops 1 | bytes 1 | tf_op jit(solution)/shard_map/pallas_call | solution.py:127
  42.3 7.2 %shard_map.83 = (f32[2,96,1792]{2,1,0:T(8,128)S(1)}, bf16[2,96,1792]{2,1,0:T(8,128)(2,1)S(1)}) custom-call(bf16[2,2,2,48,1024]{4,3,2,1,0:T(8,128)(2,1)S(1)} %multiply_convert_fusion.1.x_ref, bf16[1,2048,3584]{2,1,0:T(8,128)(2,1)} %gate_ref.7, bf16[1,2048,3584]{2,1,0:T(8,128)(2,1)} %up_ref.7, f32[2,96,1792]{2,1,0:T(8,128)S(1)} %get-tuple-element.72.refs_0_, ...), custom_call_target="tpu_custom_call" | custom-call | flops 1 | bytes 1 | tf_op jit(solution)/shard_map/pallas_call | solution.py:127
  51.9 6.1 %collective-permute-done.12 = f32[2,80]{1,0:T(2,128)S(1)} collective-permute-done((f32[2,80]{1,0:T(2,128)S(1)}, f32[2,80]{1,0:T(2,128)S(1)}, u32[]{:S(2)}, u32[]{:S(2)}) %collective-permute-start.12) | collective-permute-done | bytes 672 | tf_op jit(solution)/shard_map/ppermute | solution.py:19
  58.3 12.2 %collective-permute-done.11 = bf16[2,96,1792]{2,1,0:T(8,128)(2,1)S(1)} collective-permute-done((bf16[2,96,1792]{2,1,0:T(8,128)(2,1)S(1)}, bf16[2,96,1792]{2,1,0:T(8,128)(2,1)S(1)}, u32[]{:S(2)}, u32[]{:S(2)}) %collective-permute-start.11) | collective-permute-done | bytes 688160 | tf_op jit(solution)/shard_map/ppermute | solution.py:23
  72.4 11.7 %shard_map.84 = (f32[2,96,3584]{2,1,0:T(8,128)S(1)}, bf16[2,96,3584]{2,1,0:T(8,128)(2,1)S(1)}) custom-call(bf16[2,2,2,48,1024]{4,3,2,1,0:T(8,128)(2,1)S(1)} %multiply_convert_fusion.x_ref, bf16[1,2048,3584]{2,1,0:T(8,128)(2,1)} %gate_ref.7, bf16[1,2048,3584]{2,1,0:T(8,128)(2,1)} %up_ref.7, f32[2,96,1792]{2,1,0:T(8,128)S(1)} %get-tuple-element.81.refs_0_, ...), custom_call_target="tpu_custom_call" | custom-call | flops 1 | bytes 1 | tf_op jit(solution)/shard_map/pallas_call | solution.py:127
  86.4 6.3 %shard_map.85 = (f32[96,2048]{1,0:T(8,128)S(1)}, bf16[96,2048]{1,0:T(8,128)(2,1)S(1)}) custom-call(s32[1]{0:T(128)} %bitcast.rank_ref, bf16[96,3584]{1,0:T(8,128)(2,1)S(1)} %pad_maximum_fusion.refs_4_.refs_0_, bf16[96,3584]{1,0:T(8,128)(2,1)S(1)} %collective-permute-done.13.refs_1_, bf16[1,3584,2048]{2,1,0:T(8,128)(2,1)} %refs_2_.5, f32[2,96,3584]{2,1,0:T(8,128)} %copy-done.2), custom_call_target="tpu_custom_call" | custom-call | flops 1 | bytes 1 | tf_op jit(solution)/shard_map/pallas_call | solution.py:175
  96.4 7.1 %collective-permute-done.15 = bf16[96,2048]{1,0:T(8,128)(2,1)S(1)} collective-permute-done((bf16[96,2048]{1,0:T(8,128)(2,1)S(1)}, bf16[96,2048]{1,0:T(8,128)(2,1)S(1)}, u32[]{:S(2)}, u32[]{:S(2)}) %collective-permute-start.15) | collective-permute-done | bytes 393248 | tf_op jit(solution)/shard_map/ppermute | solution.py:27
  103.7 4.6 %collective-permute-start.16 = (bf16[48,2048]{1,0:T(8,128)(2,1)S(1)}, bf16[48,2048]{1,0:T(8,128)(2,1)S(1)}, u32[]{:S(2)}, u32[]{:S(2)}) collective-permute-start(bf16[48,2048]{1,0:T(8,128)(2,1)S(1)} %slice.229.refs_1_), channel_id=1, source_target_pairs={{0,8},{4,12},{8,0},{12,4},{1,9},{5,13},{9,1},{13,5},{2,10},{6,14},... | collective-permute-start | bytes 589832 | tf_op jit(solution)/shard_map/ppermute | solution.py:27
  108.4 5.2 %collective-permute-done.16 = bf16[48,2048]{1,0:T(8,128)(2,1)S(1)} collective-permute-done((bf16[48,2048]{1,0:T(8,128)(2,1)S(1)}, bf16[48,2048]{1,0:T(8,128)(2,1)S(1)}, u32[]{:S(2)}, u32[]{:S(2)}) %collective-permute-start.16) | collective-permute-done | bytes 196640 | tf_op jit(solution)/shard_map/ppermute | solution.py:27
  117.9 4.6 %collective-permute-start.17 = (bf16[48,2048]{1,0:T(8,128)(2,1)S(1)}, bf16[48,2048]{1,0:T(8,128)(2,1)S(1)}, u32[]{:S(2)}, u32[]{:S(2)}) collective-permute-start(bf16[48,2048]{1,0:T(8,128)(2,1)S(1)} %add_convert_fusion.1.refs_3_), channel_id=1, source_target_pairs={{0,8},{4,12},{8,0},{12,4},{1,9},{5,13},{9,1},{13,5},{2,10},{6,14},... | collective-permute-start | bytes 589832 | tf_op jit(solution)/shard_map/ppermute | solution.py:27
  122.7 11.4 %shard_map.86 = (f32[2,64,3584]{2,1,0:T(8,128)S(1)}, bf16[2,64,3584]{2,1,0:T(8,128)(2,1)S(1)}) custom-call(bf16[2,2,2,32,1024]{4,3,2,1,0:T(8,128)(2,1)S(1)} %multiply_convert_fusion.2.x_ref, bf16[1,2048,3584]{2,1,0:T(8,128)(2,1)} %gate_ref.7, bf16[1,2048,3584]{2,1,0:T(8,128)(2,1)} %up_ref.7, f32[96,2048]{1,0:T(8,128)S(1)} %get-tuple-element.86.refs_0_, ...), custom_call_target="tpu_custom_call" | custom-call | flops 1 | bytes 1 | tf_op jit(solution)/shard_map/pallas_call | solution.py:127
  136.6 6.3 %shard_map.87 = (f32[96,2048]{1,0:T(8,128)S(1)}, bf16[96,2048]{1,0:T(8,128)(2,1)S(1)}) custom-call(s32[1]{0:T(128)} %bitcast.rank_ref, bf16[96,3584]{1,0:T(8,128)(2,1)S(1)} %fusion.1.refs_2_.refs_0_, bf16[96,3584]{1,0:T(8,128)(2,1)S(1)} %collective-permute-done.19.refs_1_, bf16[1,3584,2048]{2,1,0:T(8,128)(2,1)} %refs_2_.5, f32[2,64,3584]{2,1,0:T(8,128)} %copy-done.4, ...), custom_call_target="tpu_custom_call" | custom-call | flops 1 | bytes 1 | tf_op jit(solution)/shard_map/pallas_call | solution.py:175
  147.2 7.8 %shard_map.88 = (f32[96,4096]{1,0:T(8,128)}, bf16[96,4096]{1,0:T(8,128)(2,1)S(1)}) custom-call(s32[1]{0:T(128)} %bitcast.rank_ref, bf16[96,2048]{1,0:T(8,128)(2,1)S(1)} %constant_dynamic-update-slice_fusion.refs_4_.near_ref, bf16[96,2048]{1,0:T(8,128)(2,1)S(1)} %collective-permute-done.20.far_ref, bf16[1,2048,4096]{2,1,0:T(8,128)(2,1)} %weight_ref.5, ...), custom_call_target="tpu_custom_call" | custom-call | flops 1 | bytes 1 | tf_op jit(solution)/shard_map/pallas_call | solution.py:221
  158.6 8.1 %collective-permute-done.25 = bf16[48,2048]{1,0:T(8,128)(2,1)S(1)} collective-permute-done((bf16[48,2048]{1,0:T(8,128)(2,1)S(1)}, bf16[48,2048]{1,0:T(8,128)(2,1)S(1)}, u32[]{:S(2)}, u32[]{:S(2)}) %collective-permute-start.25) | collective-permute-done | bytes 196640 | tf_op jit(solution)/shard_map/ppermute | solution.py:27
  168.2 5.9 %shard_map.89 = (f32[64,2048]{1,0:T(8,128)S(1)}, bf16[64,2048]{1,0:T(8,128)(2,1)S(1)}) custom-call(s32[1]{0:T(128)} %bitcast.rank_ref, bf16[64,3584]{1,0:T(8,128)(2,1)S(1)} %fusion.3.refs_0_.refs_4_, bf16[64,3584]{1,0:T(8,128)(2,1)S(1)} %collective-permute-done.23.refs_1_, bf16[1,3584,2048]{2,1,0:T(8,128)(2,1)} %refs_2_.5, ...), custom_call_target="tpu_custom_call" | custom-call | flops 1 | bytes 1 | tf_op jit(solution)/shard_map/pallas_call | solution.py:175
  179.7 7.0 %collective-permute-done.30 = bf16[32,2048]{1,0:T(8,128)(2,1)S(1)} collective-permute-done((bf16[32,2048]{1,0:T(8,128)(2,1)S(1)}, bf16[32,2048]{1,0:T(8,128)(2,1)S(1)}, u32[]{:S(2)}, u32[]{:S(2)}) %collective-permute-start.30) | collective-permute-done | bytes 131104 | tf_op jit(solution)/shard_map/ppermute | solution.py:27
  194.9 7.6 %shard_map.90 = (f32[96,4096]{1,0:T(8,128)}, bf16[96,4096]{1,0:T(8,128)(2,1)S(1)}) custom-call(s32[1]{0:T(128)} %bitcast.rank_ref, bf16[96,2048]{1,0:T(8,128)(2,1)S(1)} %constant_dynamic-update-slice_fusion.2.near_ref.refs_3_, bf16[96,2048]{1,0:T(8,128)(2,1)S(1)} %collective-permute-done.28.far_ref, bf16[1,2048,4096]{2,1,0:T(8,128)(2,1)} %weight_ref.5, ...), custom_call_target="tpu_custom_call" | custom-call | flops 1 | bytes 1 | tf_op jit(solution)/shard_map/pallas_call | solution.py:221
  204.1 6.6 %shard_map.91 = (f32[64,4096]{1,0:T(8,128)S(1)}, bf16[64,4096]{1,0:T(8,128)(2,1)S(1)}) custom-call(s32[1]{0:T(128)} %bitcast.rank_ref, bf16[64,2048]{1,0:T(8,128)(2,1)S(1)} %get-tuple-element.153.near_ref, bf16[64,2048]{1,0:T(8,128)(2,1)S(1)} %get-tuple-element.154.far_ref, bf16[1,2048,4096]{2,1,0:T(8,128)(2,1)} %weight_ref.5, ...), custom_call_target="tpu_custom_call" | custom-call | flops 1 | bytes 1 | tf_op jit(solution)/shard_map/pallas_call | solution.py:221
  212.3 4.6 %collective-permute-start.36 = (bf16[48,4096]{1,0:T(8,128)(2,1)S(1)}, bf16[48,4096]{1,0:T(8,128)(2,1)S(1)}, u32[]{:S(2)}, u32[]{:S(2)}) collective-permute-start(bf16[48,4096]{1,0:T(8,128)(2,1)S(1)} %slice.225), channel_id=1, source_target_pairs={{0,2},{2,0},{1,3},{3,1},{4,6},{6,4},{5,7},{7,5},{8,10},{10,8},{9,1... | collective-permute-start | bytes 1179656 | tf_op jit(solution)/shard_map/ppermute | solution.py:23
  217.6 9.3 %collective-permute-done.36 = bf16[48,4096]{1,0:T(8,128)(2,1)S(1)} collective-permute-done((bf16[48,4096]{1,0:T(8,128)(2,1)S(1)}, bf16[48,4096]{1,0:T(8,128)(2,1)S(1)}, u32[]{:S(2)}, u32[]{:S(2)}) %collective-permute-start.36) | collective-permute-done | bytes 393248 | tf_op jit(solution)/shard_map/ppermute | solution.py:23
  227.0 5.2 %collective-permute-done.38 = bf16[32,4096]{1,0:T(8,128)(2,1)S(1)} collective-permute-done((bf16[32,4096]{1,0:T(8,128)(2,1)S(1)}, bf16[32,4096]{1,0:T(8,128)(2,1)S(1)}, u32[]{:S(2)}, u32[]{:S(2)}) %collective-permute-start.38) | collective-permute-done | bytes 262176 | tf_op jit(solution)/shard_map/ppermute | solution.py:23
  (151 shorter events, 66.6 us)
Async XLA Ops:
  31.3 11.0 %collective-permute-start.9 = (bf16[2,80,1024]{2,1,0:T(8,128)(2,1)S(1)}, bf16[2,80,1024]{2,1,0:T(8,128)(2,1)S(1)}, u32[]{:S(2)}, u32[]{:S(2)}) collective-permute-start(bf16[2,80,1024]{2,1,0:T(8,128)(2,1)S(1)} %pad_maximum_fusion.8), channel_id=1, source_target_pairs={{2,0},{0,2},{3,1},{1,3},{6,4},{4,6},{7,5},{5,7},{10,8},{8,10},{11,... | collective-permute-start | bytes 983048 | tf_op jit(solution)/shard_map/ppermute | solution.py:19
  39.4 18.5 %collective-permute-start.6 = (bf16[2,96,1792]{2,1,0:T(8,128)(2,1)S(1)}, bf16[2,96,1792]{2,1,0:T(8,128)(2,1)S(1)}, u32[]{:S(2)}, u32[]{:S(2)}) collective-permute-start(bf16[2,96,1792]{2,1,0:T(8,128)(2,1)S(1)} %get-tuple-element.73), channel_id=1, source_target_pairs={{0,2},{2,0},{1,3},{3,1},{4,6},{6,4},{5,7},{7,5},{8,10},{10,8},{9,1... | collective-permute-start | bytes 2064392 | tf_op jit(solution)/shard_map/ppermute | solution.py:23
  50.1 22.1 %collective-permute-start.14 = (bf16[2,2,80,1024]{3,2,1,0:T(8,128)(2,1)S(1)}, bf16[2,2,80,1024]{3,2,1,0:T(8,128)(2,1)S(1)}, u32[]{:S(2)}, u32[]{:S(2)}) collective-permute-start(bf16[2,2,80,1024]{3,2,1,0:T(8,128)(2,1)S(1)} %get-tuple-element.135), channel_id=1, source_target_pairs={{1,0},{0,1},{3,2},{2,3},{5,4},{4,5},{7,6},{6,7},{9,8},{8,9},{11,10... | collective-permute-start | bytes 1966088 | tf_op jit(solution)/shard_map/ppermute | solution.py:19
  50.1 20.3 %collective-permute-start.11 = (bf16[2,96,1792]{2,1,0:T(8,128)(2,1)S(1)}, bf16[2,96,1792]{2,1,0:T(8,128)(2,1)S(1)}, u32[]{:S(2)}, u32[]{:S(2)}) collective-permute-start(bf16[2,96,1792]{2,1,0:T(8,128)(2,1)S(1)} %get-tuple-element.79), channel_id=1, source_target_pairs={{0,2},{2,0},{1,3},{3,1},{4,6},{6,4},{5,7},{7,5},{8,10},{10,8},{9,1... | collective-permute-start | bytes 2064392 | tf_op jit(solution)/shard_map/ppermute | solution.py:23
  70.9 15.6 %collective-permute-start.13 = (bf16[96,3584]{1,0:T(8,128)(2,1)S(1)}, bf16[96,3584]{1,0:T(8,128)(2,1)S(1)}, u32[]{:S(2)}, u32[]{:S(2)}) collective-permute-start(bf16[96,3584]{1,0:T(8,128)(2,1)S(1)} %pad_maximum_fusion.refs_4_.refs_0_), channel_id=1, source_target_pairs={{2,0},{0,2},{3,1},{1,3},{6,4},{4,6},{7,5},{5,7},{10,8},{8,10},{11,... | collective-permute-start | bytes 2064392 | tf_op jit(solution)/shard_map/ppermute | solution.py:19
  85.6 30.1 %collective-permute-start.18 = (bf16[2,96,3584]{2,1,0:T(8,128)(2,1)S(1)}, bf16[2,96,3584]{2,1,0:T(8,128)(2,1)S(1)}, u32[]{:S(2)}, u32[]{:S(2)}) collective-permute-start(bf16[2,96,3584]{2,1,0:T(8,128)(2,1)S(1)} %get-tuple-element.90), channel_id=1, source_target_pairs={{0,2},{2,0},{1,3},{3,1},{4,6},{6,4},{5,7},{7,5},{8,10},{10,8},{9,1... | collective-permute-start | bytes 4128776 | tf_op jit(solution)/shard_map/ppermute | solution.py:23
  92.7 10.8 %collective-permute-start.15 = (bf16[96,2048]{1,0:T(8,128)(2,1)S(1)}, bf16[96,2048]{1,0:T(8,128)(2,1)S(1)}, u32[]{:S(2)}, u32[]{:S(2)}) collective-permute-start(bf16[96,2048]{1,0:T(8,128)(2,1)S(1)} %get-tuple-element.85), channel_id=1, source_target_pairs={{0,4},{4,0},{8,12},{12,8},{1,5},{5,1},{9,13},{13,9},{2,6},{6,2},{1... | collective-permute-start | bytes 1179656 | tf_op jit(solution)/shard_map/ppermute | solution.py:27
  116.4 20.1 %collective-permute-start.19 = (bf16[96,3584]{1,0:T(8,128)(2,1)S(1)}, bf16[96,3584]{1,0:T(8,128)(2,1)S(1)}, u32[]{:S(2)}, u32[]{:S(2)}) collective-permute-start(bf16[96,3584]{1,0:T(8,128)(2,1)S(1)} %fusion.1.refs_2_.refs_0_), channel_id=1, source_target_pairs={{2,0},{0,2},{3,1},{1,3},{6,4},{4,6},{7,5},{5,7},{10,8},{8,10},{11,... | collective-permute-start | bytes 2064392 | tf_op jit(solution)/shard_map/ppermute | solution.py:19
  117.9 18.6 %collective-permute-start.17 = (bf16[48,2048]{1,0:T(8,128)(2,1)S(1)}, bf16[48,2048]{1,0:T(8,128)(2,1)S(1)}, u32[]{:S(2)}, u32[]{:S(2)}) collective-permute-start(bf16[48,2048]{1,0:T(8,128)(2,1)S(1)} %add_convert_fusion.1.refs_3_), channel_id=1, source_target_pairs={{0,8},{4,12},{8,0},{12,4},{1,9},{5,13},{9,1},{13,5},{2,10},{6,14},... | collective-permute-start | bytes 589832 | tf_op jit(solution)/shard_map/ppermute | solution.py:27
  135.3 20.2 %collective-permute-start.22 = (bf16[2,64,3584]{2,1,0:T(8,128)(2,1)S(1)}, bf16[2,64,3584]{2,1,0:T(8,128)(2,1)S(1)}, u32[]{:S(2)}, u32[]{:S(2)}) collective-permute-start(bf16[2,64,3584]{2,1,0:T(8,128)(2,1)S(1)} %get-tuple-element.99), channel_id=1, source_target_pairs={{0,2},{2,0},{1,3},{3,1},{4,6},{6,4},{5,7},{7,5},{8,10},{10,8},{9,1... | collective-permute-start | bytes 2752520 | tf_op jit(solution)/shard_map/ppermute | solution.py:23
  136.5 10.6 %collective-permute-start.20 = (bf16[96,2048]{1,0:T(8,128)(2,1)S(1)}, bf16[96,2048]{1,0:T(8,128)(2,1)S(1)}, u32[]{:S(2)}, u32[]{:S(2)}) collective-permute-start(bf16[96,2048]{1,0:T(8,128)(2,1)S(1)} %constant_dynamic-update-slice_fusion.refs_4_.near_ref), channel_id=1, source_target_pairs={{0,4},{4,0},{8,12},{12,8},{1,5},{5,1},{9,13},{13,9},{2,6},{6,2},{1... | collective-permute-start | bytes 1179656 | tf_op jit(solution)/shard_map/ppermute | solution.py:27
  142.9 12.0 %collective-permute-start.24 = (bf16[96,2048]{1,0:T(8,128)(2,1)S(1)}, bf16[96,2048]{1,0:T(8,128)(2,1)S(1)}, u32[]{:S(2)}, u32[]{:S(2)}) collective-permute-start(bf16[96,2048]{1,0:T(8,128)(2,1)S(1)} %get-tuple-element.102), channel_id=1, source_target_pairs={{0,4},{4,0},{8,12},{12,8},{1,5},{5,1},{9,13},{13,9},{2,6},{6,2},{1... | collective-permute-start | bytes 1179656 | tf_op jit(solution)/shard_map/ppermute | solution.py:27
  156.0 10.6 %collective-permute-start.25 = (bf16[48,2048]{1,0:T(8,128)(2,1)S(1)}, bf16[48,2048]{1,0:T(8,128)(2,1)S(1)}, u32[]{:S(2)}, u32[]{:S(2)}) collective-permute-start(bf16[48,2048]{1,0:T(8,128)(2,1)S(1)} %slice.228.refs_5_), channel_id=1, source_target_pairs={{0,8},{4,12},{8,0},{12,4},{1,9},{5,13},{9,1},{13,5},{2,10},{6,14},... | collective-permute-start | bytes 589832 | tf_op jit(solution)/shard_map/ppermute | solution.py:27
  157.6 10.6 %collective-permute-start.23 = (bf16[64,3584]{1,0:T(8,128)(2,1)S(1)}, bf16[64,3584]{1,0:T(8,128)(2,1)S(1)}, u32[]{:S(2)}, u32[]{:S(2)}) collective-permute-start(bf16[64,3584]{1,0:T(8,128)(2,1)S(1)} %fusion.3.refs_0_.refs_4_), channel_id=1, source_target_pairs={{2,0},{0,2},{3,1},{1,3},{6,4},{4,6},{7,5},{5,7},{10,8},{8,10},{11,... | collective-permute-start | bytes 1376264 | tf_op jit(solution)/shard_map/ppermute | solution.py:19
  166.8 20.4 %collective-permute-start.21 = (bf16[96,4096]{1,0:T(8,128)(2,1)S(1)}, bf16[96,4096]{1,0:T(8,128)(2,1)S(1)}, u32[]{:S(2)}, u32[]{:S(2)}) collective-permute-start(bf16[96,4096]{1,0:T(8,128)(2,1)S(1)} %get-tuple-element.98), channel_id=1, source_target_pairs={{0,1},{1,0},{2,3},{3,2},{4,5},{5,4},{6,7},{7,6},{8,9},{9,8},{10,11... | collective-permute-start | bytes 2359304 | tf_op jit(solution)/shard_map/ppermute | solution.py:23
  175.1 11.6 %collective-permute-start.30 = (bf16[32,2048]{1,0:T(8,128)(2,1)S(1)}, bf16[32,2048]{1,0:T(8,128)(2,1)S(1)}, u32[]{:S(2)}, u32[]{:S(2)}) collective-permute-start(bf16[32,2048]{1,0:T(8,128)(2,1)S(1)} %slice.230), channel_id=1, source_target_pairs={{0,8},{4,12},{8,0},{12,4},{1,9},{5,13},{9,1},{13,5},{2,10},{6,14},... | collective-permute-start | bytes 393224 | tf_op jit(solution)/shard_map/ppermute | solution.py:27
  175.7 10.9 %collective-permute-start.31 = (bf16[32,2048]{1,0:T(8,128)(2,1)S(1)}, bf16[32,2048]{1,0:T(8,128)(2,1)S(1)}, u32[]{:S(2)}, u32[]{:S(2)}) collective-permute-start(bf16[32,2048]{1,0:T(8,128)(2,1)S(1)} %get-tuple-element.149), channel_id=1, source_target_pairs={{0,4},{4,0},{8,12},{12,8},{1,5},{5,1},{9,13},{13,9},{2,6},{6,2},{1... | collective-permute-start | bytes 393224 | tf_op jit(solution)/shard_map/ppermute | solution.py:27
  179.6 15.3 %collective-permute-start.28 = (bf16[96,2048]{1,0:T(8,128)(2,1)S(1)}, bf16[96,2048]{1,0:T(8,128)(2,1)S(1)}, u32[]{:S(2)}, u32[]{:S(2)}) collective-permute-start(bf16[96,2048]{1,0:T(8,128)(2,1)S(1)} %constant_dynamic-update-slice_fusion.2.near_ref.refs_3_), channel_id=1, source_target_pairs={{0,4},{4,0},{8,12},{12,8},{1,5},{5,1},{9,13},{13,9},{2,6},{6,2},{1... | collective-permute-start | bytes 1179656 | tf_op jit(solution)/shard_map/ppermute | solution.py:27
  187.4 16.6 %collective-permute-start.26 = (bf16[48,4096]{1,0:T(8,128)(2,1)S(1)}, bf16[48,4096]{1,0:T(8,128)(2,1)S(1)}, u32[]{:S(2)}, u32[]{:S(2)}) collective-permute-start(bf16[48,4096]{1,0:T(8,128)(2,1)S(1)} %slice.226.refs_1_), channel_id=1, source_target_pairs={{0,2},{2,0},{1,3},{3,1},{4,6},{6,4},{5,7},{7,5},{8,10},{10,8},{9,1... | collective-permute-start | bytes 1179656 | tf_op jit(solution)/shard_map/ppermute | solution.py:23
  189.1 13.4 %collective-permute-start.35 = (bf16[32,2048]{1,0:T(8,128)(2,1)S(1)}, bf16[32,2048]{1,0:T(8,128)(2,1)S(1)}, u32[]{:S(2)}, u32[]{:S(2)}) collective-permute-start(bf16[32,2048]{1,0:T(8,128)(2,1)S(1)} %add_convert_fusion.2.refs_2_), channel_id=1, source_target_pairs={{0,12},{4,8},{8,4},{12,0},{1,13},{5,9},{9,5},{13,1},{2,14},{6,10},... | collective-permute-start | bytes 393224 | tf_op jit(solution)/shard_map/ppermute | solution.py:27
  191.0 13.0 %collective-permute-start.34 = (bf16[32,2048]{1,0:T(8,128)(2,1)S(1)}, bf16[32,2048]{1,0:T(8,128)(2,1)S(1)}, u32[]{:S(2)}, u32[]{:S(2)}) collective-permute-start(bf16[32,2048]{1,0:T(8,128)(2,1)S(1)} %add_convert_fusion.2.refs_2_), channel_id=1, source_target_pairs={{0,8},{4,12},{8,0},{12,4},{1,9},{5,13},{9,1},{13,5},{2,10},{6,14},... | collective-permute-start | bytes 393224 | tf_op jit(solution)/shard_map/ppermute | solution.py:27
  192.5 11.5 %collective-permute-start.33 = (bf16[32,2048]{1,0:T(8,128)(2,1)S(1)}, bf16[32,2048]{1,0:T(8,128)(2,1)S(1)}, u32[]{:S(2)}, u32[]{:S(2)}) collective-permute-start(bf16[32,2048]{1,0:T(8,128)(2,1)S(1)} %add_convert_fusion.2.refs_2_), channel_id=1, source_target_pairs={{0,4},{4,0},{8,12},{12,8},{1,5},{5,1},{9,13},{13,9},{2,6},{6,2},{1... | collective-permute-start | bytes 393224 | tf_op jit(solution)/shard_map/ppermute | solution.py:27
  212.3 14.5 %collective-permute-start.36 = (bf16[48,4096]{1,0:T(8,128)(2,1)S(1)}, bf16[48,4096]{1,0:T(8,128)(2,1)S(1)}, u32[]{:S(2)}, u32[]{:S(2)}) collective-permute-start(bf16[48,4096]{1,0:T(8,128)(2,1)S(1)} %slice.225), channel_id=1, source_target_pairs={{0,2},{2,0},{1,3},{3,1},{4,6},{6,4},{5,7},{7,5},{8,10},{10,8},{9,1... | collective-permute-start | bytes 1179656 | tf_op jit(solution)/shard_map/ppermute | solution.py:23
  217.1 15.2 %collective-permute-start.38 = (bf16[32,4096]{1,0:T(8,128)(2,1)S(1)}, bf16[32,4096]{1,0:T(8,128)(2,1)S(1)}, u32[]{:S(2)}, u32[]{:S(2)}) collective-permute-start(bf16[32,4096]{1,0:T(8,128)(2,1)S(1)} %slice.227), channel_id=1, source_target_pairs={{0,2},{2,0},{1,3},{3,1},{4,6},{6,4},{5,7},{7,5},{8,10},{10,8},{9,1... | collective-permute-start | bytes 786440 | tf_op jit(solution)/shard_map/ppermute | solution.py:23
  (26 other events, 178.0 us)

commit v15 on v14

--- a/solution.py
+++ b/solution.py
@@ -216,7 +216,7 @@
     rows, depth = 2 * near.shape[0], near.shape[1]
     width = enc_weight.shape[2]
     rows_each = rows // members
-    tile = tile_of(width, 512)
+    tile = tile_of(width, 256)
     tiles = width // tile
     return pl.pallas_call(
         functools.partial(encode_body, members, order, tiles),

time: 233 us -> 239 us (1.026)
  Pallas kernels: 78 us -> 82.9 us
  waiting for transfers between devices: 89.7 us -> 93.9 us
  starting transfers between devices: 54 us -> 50.3 us
    ppermute x18, waiting for transfers between devices: 46.2 us -> 52.1 us  [swap(): return lax.ppermute(value, axis, [(d, d ^ bit) for d in range(size)])]
    pallas_call x3, Pallas kernels: 22 us -> 26.9 us  [encode(): pl.pallas_call(functools.partial(encode_body, members, order, tiles), gri...]
    ppermute x10, starting transfers between devices: 12.7 us -> 9.77 us  [send(): lax.ppermute(value, axis, [(d, (d + hop) % size) for d in range(size)])]
  transfers between devices with their start and end apart: 39 -> 39, of which waited for: 24 -> 21; matrix products, arithmetic and copies ran while one was open for 2% -> 2% of each run, Pallas kernels for 33% -> 35%
where the time goes in v15:
time: 239 us
  waiting for transfers between devices  93.9 us (39%)
  Pallas kernels  82.9 us (35%)
  starting transfers between devices  50.3 us (21%)
  local copies, waits for them, and re-layouts  5.71 us (2%)
  other arithmetic  5.19 us (2%)
    ppermute x18, waiting for transfers between devices, swap(): return lax.ppermute(value, axis, [(d, d ^ bit) for d in range(size)])  52.1 us
    pallas_call x4, Pallas kernels, gate_up(): pl.pallas_call(functools.partial(gate_up_body, tiles, first), grid=(tiles...  37.5 us
    ppermute x18, starting transfers between devices, swap(): return lax.ppermute(value, axis, [(d, d ^ bit) for d in range(size)])  33.6 us
    ppermute x10, waiting for transfers between devices, send(): lax.ppermute(value, axis, [(d, (d + hop) % size) for d in range(size)])  29 us
    pallas_call x3, Pallas kernels, encode(): pl.pallas_call(functools.partial(encode_body, members, order, tiles), gri...  26.9 us
    pallas_call x3, Pallas kernels, down(): pl.pallas_call(functools.partial(down_body, owners, members, pieces, orde...  18.5 us
    ppermute x11, waiting for transfers between devices, shift(): lax.ppermute(value, axis, [((d + hop) % size, d) for d in range(size)])  12.8 us
    ppermute x10, starting transfers between devices, send(): lax.ppermute(value, axis, [(d, (d + hop) % size) for d in range(size)])  9.77 us
  transfers between devices with their start and end apart: 39, of which 21 were waited for; matrix products, arithmetic and copies ran while one was open for 2% of the time, Pallas kernels for 35%

profile of v15, /device:TPU:0, one launch (start us, length us, event | category | flops | bytes accessed | tf_op | source)
XLA Modules:
  0.0 238.6 jit_solution(14154725971409453769)
XLA Ops:
  1.1 4.1 %collective-permute-start = (bf16[1,48,1024]{2,1,0:T(8,128)(2,1)S(1)}, bf16[1,48,1024]{2,1,0:T(8,128)(2,1)S(1)}, u32[]{:S(2)}, u32[]{:S(2)}) collective-permute-start(bf16[1,48,1024]{2,1,0:T(8,128)(2,1)S(1)} %dynamic-slice_bitcast_fusion.1), channel_id=1, source_target_pairs={{0,8},{4,12},{8,0},{12,4},{1,9},{5,13},{9,1},{13,5},{2,10},{6,14},... | collective-permute-start | bytes 294920 | tf_op jit(solution)/shard_map/ppermute | solution.py:27
  5.2 4.9 %collective-permute-done = bf16[1,48,1024]{2,1,0:T(8,128)(2,1)S(1)} collective-permute-done((bf16[1,48,1024]{2,1,0:T(8,128)(2,1)S(1)}, bf16[1,48,1024]{2,1,0:T(8,128)(2,1)S(1)}, u32[]{:S(2)}, u32[]{:S(2)}) %collective-permute-start) | collective-permute-done | bytes 98336 | tf_op jit(solution)/shard_map/ppermute | solution.py:27
  15.0 5.1 %collective-permute-done.7 = bf16[1,80,1024]{2,1,0:T(8,128)(2,1)S(1)} collective-permute-done((bf16[1,80,1024]{2,1,0:T(8,128)(2,1)S(1)}, bf16[1,80,1024]{2,1,0:T(8,128)(2,1)S(1)}, u32[]{:S(2)}, u32[]{:S(2)}) %collective-permute-start.7) | collective-permute-done | bytes 163872 | tf_op jit(solution)/shard_map/ppermute | solution.py:27
  32.2 7.2 %shard_map.82 = (f32[2,96,1792]{2,1,0:T(8,128)S(1)}, bf16[2,96,1792]{2,1,0:T(8,128)(2,1)S(1)}) custom-call(bf16[2,2,2,48,1024]{4,3,2,1,0:T(8,128)(2,1)S(1)} %multiply_convert_fusion.1.x_ref, bf16[1,2048,3584]{2,1,0:T(8,128)(2,1)} %gate_ref.7, bf16[1,2048,3584]{2,1,0:T(8,128)(2,1)} %up_ref.7), custom_call_target="tpu_custom_call" | custom-call | flops 1 | bytes 1 | tf_op jit(solution)/shard_map/pallas_call | solution.py:127
  42.3 7.2 %shard_map.83 = (f32[2,96,1792]{2,1,0:T(8,128)S(1)}, bf16[2,96,1792]{2,1,0:T(8,128)(2,1)S(1)}) custom-call(bf16[2,2,2,48,1024]{4,3,2,1,0:T(8,128)(2,1)S(1)} %multiply_convert_fusion.1.x_ref, bf16[1,2048,3584]{2,1,0:T(8,128)(2,1)} %gate_ref.7, bf16[1,2048,3584]{2,1,0:T(8,128)(2,1)} %up_ref.7, f32[2,96,1792]{2,1,0:T(8,128)S(1)} %get-tuple-element.72.refs_0_, ...), custom_call_target="tpu_custom_call" | custom-call | flops 1 | bytes 1 | tf_op jit(solution)/shard_map/pallas_call | solution.py:127
  51.9 6.1 %collective-permute-done.12 = f32[2,80]{1,0:T(2,128)S(1)} collective-permute-done((f32[2,80]{1,0:T(2,128)S(1)}, f32[2,80]{1,0:T(2,128)S(1)}, u32[]{:S(2)}, u32[]{:S(2)}) %collective-permute-start.12) | collective-permute-done | bytes 672 | tf_op jit(solution)/shard_map/ppermute | solution.py:19
  58.3 12.2 %collective-permute-done.11 = bf16[2,96,1792]{2,1,0:T(8,128)(2,1)S(1)} collective-permute-done((bf16[2,96,1792]{2,1,0:T(8,128)(2,1)S(1)}, bf16[2,96,1792]{2,1,0:T(8,128)(2,1)S(1)}, u32[]{:S(2)}, u32[]{:S(2)}) %collective-permute-start.11) | collective-permute-done | bytes 688160 | tf_op jit(solution)/shard_map/ppermute | solution.py:23
  72.4 11.7 %shard_map.84 = (f32[2,96,3584]{2,1,0:T(8,128)S(1)}, bf16[2,96,3584]{2,1,0:T(8,128)(2,1)S(1)}) custom-call(bf16[2,2,2,48,1024]{4,3,2,1,0:T(8,128)(2,1)S(1)} %multiply_convert_fusion.x_ref, bf16[1,2048,3584]{2,1,0:T(8,128)(2,1)} %gate_ref.7, bf16[1,2048,3584]{2,1,0:T(8,128)(2,1)} %up_ref.7, f32[2,96,1792]{2,1,0:T(8,128)S(1)} %get-tuple-element.81.refs_0_, ...), custom_call_target="tpu_custom_call" | custom-call | flops 1 | bytes 1 | tf_op jit(solution)/shard_map/pallas_call | solution.py:127
  86.4 6.3 %shard_map.85 = (f32[96,2048]{1,0:T(8,128)S(1)}, bf16[96,2048]{1,0:T(8,128)(2,1)S(1)}) custom-call(s32[1]{0:T(128)} %bitcast.rank_ref, bf16[96,3584]{1,0:T(8,128)(2,1)S(1)} %pad_maximum_fusion.refs_4_.refs_0_, bf16[96,3584]{1,0:T(8,128)(2,1)S(1)} %collective-permute-done.13.refs_1_, bf16[1,3584,2048]{2,1,0:T(8,128)(2,1)} %refs_2_.5, f32[2,96,3584]{2,1,0:T(8,128)} %copy-done.2), custom_call_target="tpu_custom_call" | custom-call | flops 1 | bytes 1 | tf_op jit(solution)/shard_map/pallas_call | solution.py:175
  96.4 7.1 %collective-permute-done.15 = bf16[96,2048]{1,0:T(8,128)(2,1)S(1)} collective-permute-done((bf16[96,2048]{1,0:T(8,128)(2,1)S(1)}, bf16[96,2048]{1,0:T(8,128)(2,1)S(1)}, u32[]{:S(2)}, u32[]{:S(2)}) %collective-permute-start.15) | collective-permute-done | bytes 393248 | tf_op jit(solution)/shard_map/ppermute | solution.py:27
  103.7 4.6 %collective-permute-start.16 = (bf16[48,2048]{1,0:T(8,128)(2,1)S(1)}, bf16[48,2048]{1,0:T(8,128)(2,1)S(1)}, u32[]{:S(2)}, u32[]{:S(2)}) collective-permute-start(bf16[48,2048]{1,0:T(8,128)(2,1)S(1)} %slice.229.refs_1_), channel_id=1, source_target_pairs={{0,8},{4,12},{8,0},{12,4},{1,9},{5,13},{9,1},{13,5},{2,10},{6,14},... | collective-permute-start | bytes 589832 | tf_op jit(solution)/shard_map/ppermute | solution.py:27
  108.4 5.2 %collective-permute-done.16 = bf16[48,2048]{1,0:T(8,128)(2,1)S(1)} collective-permute-done((bf16[48,2048]{1,0:T(8,128)(2,1)S(1)}, bf16[48,2048]{1,0:T(8,128)(2,1)S(1)}, u32[]{:S(2)}, u32[]{:S(2)}) %collective-permute-start.16) | collective-permute-done | bytes 196640 | tf_op jit(solution)/shard_map/ppermute | solution.py:27
  117.9 4.6 %collective-permute-start.17 = (bf16[48,2048]{1,0:T(8,128)(2,1)S(1)}, bf16[48,2048]{1,0:T(8,128)(2,1)S(1)}, u32[]{:S(2)}, u32[]{:S(2)}) collective-permute-start(bf16[48,2048]{1,0:T(8,128)(2,1)S(1)} %add_convert_fusion.1.refs_3_), channel_id=1, source_target_pairs={{0,8},{4,12},{8,0},{12,4},{1,9},{5,13},{9,1},{13,5},{2,10},{6,14},... | collective-permute-start | bytes 589832 | tf_op jit(solution)/shard_map/ppermute | solution.py:27
  122.7 11.4 %shard_map.86 = (f32[2,64,3584]{2,1,0:T(8,128)S(1)}, bf16[2,64,3584]{2,1,0:T(8,128)(2,1)S(1)}) custom-call(bf16[2,2,2,32,1024]{4,3,2,1,0:T(8,128)(2,1)S(1)} %multiply_convert_fusion.2.x_ref, bf16[1,2048,3584]{2,1,0:T(8,128)(2,1)} %gate_ref.7, bf16[1,2048,3584]{2,1,0:T(8,128)(2,1)} %up_ref.7, f32[96,2048]{1,0:T(8,128)S(1)} %get-tuple-element.86.refs_0_, ...), custom_call_target="tpu_custom_call" | custom-call | flops 1 | bytes 1 | tf_op jit(solution)/shard_map/pallas_call | solution.py:127
  136.6 6.3 %shard_map.87 = (f32[96,2048]{1,0:T(8,128)S(1)}, bf16[96,2048]{1,0:T(8,128)(2,1)S(1)}) custom-call(s32[1]{0:T(128)} %bitcast.rank_ref, bf16[96,3584]{1,0:T(8,128)(2,1)S(1)} %fusion.1.refs_2_.refs_0_, bf16[96,3584]{1,0:T(8,128)(2,1)S(1)} %collective-permute-done.19.refs_1_, bf16[1,3584,2048]{2,1,0:T(8,128)(2,1)} %refs_2_.5, f32[2,64,3584]{2,1,0:T(8,128)} %copy-done.4, ...), custom_call_target="tpu_custom_call" | custom-call | flops 1 | bytes 1 | tf_op jit(solution)/shard_map/pallas_call | solution.py:175
  147.2 10.0 %shard_map.88 = (f32[96,4096]{1,0:T(8,128)}, bf16[96,4096]{1,0:T(8,128)(2,1)S(1)}) custom-call(s32[1]{0:T(128)} %bitcast.rank_ref, bf16[96,2048]{1,0:T(8,128)(2,1)S(1)} %constant_dynamic-update-slice_fusion.refs_4_.near_ref, bf16[96,2048]{1,0:T(8,128)(2,1)S(1)} %collective-permute-done.20.far_ref, bf16[1,2048,4096]{2,1,0:T(8,128)(2,1)} %weight_ref.5, ...), custom_call_target="tpu_custom_call" | custom-call | flops 1 | bytes 1 | tf_op jit(solution)/shard_map/pallas_call | solution.py:221
  159.5 10.0 %collective-permute-done.25 = bf16[48,2048]{1,0:T(8,128)(2,1)S(1)} collective-permute-done((bf16[48,2048]{1,0:T(8,128)(2,1)S(1)}, bf16[48,2048]{1,0:T(8,128)(2,1)S(1)}, u32[]{:S(2)}, u32[]{:S(2)}) %collective-permute-start.25) | collective-permute-done | bytes 196640 | tf_op jit(solution)/shard_map/ppermute | solution.py:27
  169.8 5.9 %shard_map.89 = (f32[64,2048]{1,0:T(8,128)S(1)}, bf16[64,2048]{1,0:T(8,128)(2,1)S(1)}) custom-call(s32[1]{0:T(128)} %bitcast.rank_ref, bf16[64,3584]{1,0:T(8,128)(2,1)S(1)} %fusion.3.refs_0_.refs_4_, bf16[64,3584]{1,0:T(8,128)(2,1)S(1)} %collective-permute-done.23.refs_1_, bf16[1,3584,2048]{2,1,0:T(8,128)(2,1)} %refs_2_.5, ...), custom_call_target="tpu_custom_call" | custom-call | flops 1 | bytes 1 | tf_op jit(solution)/shard_map/pallas_call | solution.py:175
  180.8 5.8 %collective-permute-done.30 = bf16[32,2048]{1,0:T(8,128)(2,1)S(1)} collective-permute-done((bf16[32,2048]{1,0:T(8,128)(2,1)S(1)}, bf16[32,2048]{1,0:T(8,128)(2,1)S(1)}, u32[]{:S(2)}, u32[]{:S(2)}) %collective-permute-start.30) | collective-permute-done | bytes 131104 | tf_op jit(solution)/shard_map/ppermute | solution.py:27
  196.2 5.7 %collective-permute-done.28.far_ref = bf16[96,2048]{1,0:T(8,128)(2,1)S(1)} collective-permute-done((bf16[96,2048]{1,0:T(8,128)(2,1)S(1)}, bf16[96,2048]{1,0:T(8,128)(2,1)S(1)}, u32[]{:S(2)}, u32[]{:S(2)}) %collective-permute-start.28) | collective-permute-done | bytes 393248 | tf_op jit(solution)/shard_map/ppermute | solution.py:27
  201.9 9.9 %shard_map.90 = (f32[96,4096]{1,0:T(8,128)}, bf16[96,4096]{1,0:T(8,128)(2,1)S(1)}) custom-call(s32[1]{0:T(128)} %bitcast.rank_ref, bf16[96,2048]{1,0:T(8,128)(2,1)S(1)} %constant_dynamic-update-slice_fusion.2.near_ref.refs_3_, bf16[96,2048]{1,0:T(8,128)(2,1)S(1)} %collective-permute-done.28.far_ref, bf16[1,2048,4096]{2,1,0:T(8,128)(2,1)} %weight_ref.5, ...), custom_call_target="tpu_custom_call" | custom-call | flops 1 | bytes 1 | tf_op jit(solution)/shard_map/pallas_call | solution.py:221
  212.0 7.0 %shard_map.91 = (f32[64,4096]{1,0:T(8,128)S(1)}, bf16[64,4096]{1,0:T(8,128)(2,1)S(1)}) custom-call(s32[1]{0:T(128)} %bitcast.rank_ref, bf16[64,2048]{1,0:T(8,128)(2,1)S(1)} %get-tuple-element.153.near_ref, bf16[64,2048]{1,0:T(8,128)(2,1)S(1)} %get-tuple-element.154.far_ref, bf16[1,2048,4096]{2,1,0:T(8,128)(2,1)} %weight_ref.5, ...), custom_call_target="tpu_custom_call" | custom-call | flops 1 | bytes 1 | tf_op jit(solution)/shard_map/pallas_call | solution.py:221
  222.9 9.6 %collective-permute-done.36 = bf16[48,4096]{1,0:T(8,128)(2,1)S(1)} collective-permute-done((bf16[48,4096]{1,0:T(8,128)(2,1)S(1)}, bf16[48,4096]{1,0:T(8,128)(2,1)S(1)}, u32[]{:S(2)}, u32[]{:S(2)}) %collective-permute-start.36) | collective-permute-done | bytes 393248 | tf_op jit(solution)/shard_map/ppermute | solution.py:23
  232.7 5.0 %collective-permute-done.38 = bf16[32,4096]{1,0:T(8,128)(2,1)S(1)} collective-permute-done((bf16[32,4096]{1,0:T(8,128)(2,1)S(1)}, bf16[32,4096]{1,0:T(8,128)(2,1)S(1)}, u32[]{:S(2)}, u32[]{:S(2)}) %collective-permute-start.38) | collective-permute-done | bytes 262176 | tf_op jit(solution)/shard_map/ppermute | solution.py:23
  (151 shorter events, 65.2 us)
Async XLA Ops:
  31.3 11.0 %collective-permute-start.9 = (bf16[2,80,1024]{2,1,0:T(8,128)(2,1)S(1)}, bf16[2,80,1024]{2,1,0:T(8,128)(2,1)S(1)}, u32[]{:S(2)}, u32[]{:S(2)}) collective-permute-start(bf16[2,80,1024]{2,1,0:T(8,128)(2,1)S(1)} %pad_maximum_fusion.8), channel_id=1, source_target_pairs={{2,0},{0,2},{3,1},{1,3},{6,4},{4,6},{7,5},{5,7},{10,8},{8,10},{11,... | collective-permute-start | bytes 983048 | tf_op jit(solution)/shard_map/ppermute | solution.py:19
  39.4 18.5 %collective-permute-start.6 = (bf16[2,96,1792]{2,1,0:T(8,128)(2,1)S(1)}, bf16[2,96,1792]{2,1,0:T(8,128)(2,1)S(1)}, u32[]{:S(2)}, u32[]{:S(2)}) collective-permute-start(bf16[2,96,1792]{2,1,0:T(8,128)(2,1)S(1)} %get-tuple-element.73), channel_id=1, source_target_pairs={{0,2},{2,0},{1,3},{3,1},{4,6},{6,4},{5,7},{7,5},{8,10},{10,8},{9,1... | collective-permute-start | bytes 2064392 | tf_op jit(solution)/shard_map/ppermute | solution.py:23
  50.1 22.1 %collective-permute-start.14 = (bf16[2,2,80,1024]{3,2,1,0:T(8,128)(2,1)S(1)}, bf16[2,2,80,1024]{3,2,1,0:T(8,128)(2,1)S(1)}, u32[]{:S(2)}, u32[]{:S(2)}) collective-permute-start(bf16[2,2,80,1024]{3,2,1,0:T(8,128)(2,1)S(1)} %get-tuple-element.135), channel_id=1, source_target_pairs={{1,0},{0,1},{3,2},{2,3},{5,4},{4,5},{7,6},{6,7},{9,8},{8,9},{11,10... | collective-permute-start | bytes 1966088 | tf_op jit(solution)/shard_map/ppermute | solution.py:19
  50.1 20.3 %collective-permute-start.11 = (bf16[2,96,1792]{2,1,0:T(8,128)(2,1)S(1)}, bf16[2,96,1792]{2,1,0:T(8,128)(2,1)S(1)}, u32[]{:S(2)}, u32[]{:S(2)}) collective-permute-start(bf16[2,96,1792]{2,1,0:T(8,128)(2,1)S(1)} %get-tuple-element.79), channel_id=1, source_target_pairs={{0,2},{2,0},{1,3},{3,1},{4,6},{6,4},{5,7},{7,5},{8,10},{10,8},{9,1... | collective-permute-start | bytes 2064392 | tf_op jit(solution)/shard_map/ppermute | solution.py:23
  70.9 15.6 %collective-permute-start.13 = (bf16[96,3584]{1,0:T(8,128)(2,1)S(1)}, bf16[96,3584]{1,0:T(8,128)(2,1)S(1)}, u32[]{:S(2)}, u32[]{:S(2)}) collective-permute-start(bf16[96,3584]{1,0:T(8,128)(2,1)S(1)} %pad_maximum_fusion.refs_4_.refs_0_), channel_id=1, source_target_pairs={{2,0},{0,2},{3,1},{1,3},{6,4},{4,6},{7,5},{5,7},{10,8},{8,10},{11,... | collective-permute-start | bytes 2064392 | tf_op jit(solution)/shard_map/ppermute | solution.py:19
  85.6 30.1 %collective-permute-start.18 = (bf16[2,96,3584]{2,1,0:T(8,128)(2,1)S(1)}, bf16[2,96,3584]{2,1,0:T(8,128)(2,1)S(1)}, u32[]{:S(2)}, u32[]{:S(2)}) collective-permute-start(bf16[2,96,3584]{2,1,0:T(8,128)(2,1)S(1)} %get-tuple-element.90), channel_id=1, source_target_pairs={{0,2},{2,0},{1,3},{3,1},{4,6},{6,4},{5,7},{7,5},{8,10},{10,8},{9,1... | collective-permute-start | bytes 4128776 | tf_op jit(solution)/shard_map/ppermute | solution.py:23
  92.7 10.8 %collective-permute-start.15 = (bf16[96,2048]{1,0:T(8,128)(2,1)S(1)}, bf16[96,2048]{1,0:T(8,128)(2,1)S(1)}, u32[]{:S(2)}, u32[]{:S(2)}) collective-permute-start(bf16[96,2048]{1,0:T(8,128)(2,1)S(1)} %get-tuple-element.85), channel_id=1, source_target_pairs={{0,4},{4,0},{8,12},{12,8},{1,5},{5,1},{9,13},{13,9},{2,6},{6,2},{1... | collective-permute-start | bytes 1179656 | tf_op jit(solution)/shard_map/ppermute | solution.py:27
  116.4 20.1 %collective-permute-start.19 = (bf16[96,3584]{1,0:T(8,128)(2,1)S(1)}, bf16[96,3584]{1,0:T(8,128)(2,1)S(1)}, u32[]{:S(2)}, u32[]{:S(2)}) collective-permute-start(bf16[96,3584]{1,0:T(8,128)(2,1)S(1)} %fusion.1.refs_2_.refs_0_), channel_id=1, source_target_pairs={{2,0},{0,2},{3,1},{1,3},{6,4},{4,6},{7,5},{5,7},{10,8},{8,10},{11,... | collective-permute-start | bytes 2064392 | tf_op jit(solution)/shard_map/ppermute | solution.py:19
  117.9 18.6 %collective-permute-start.17 = (bf16[48,2048]{1,0:T(8,128)(2,1)S(1)}, bf16[48,2048]{1,0:T(8,128)(2,1)S(1)}, u32[]{:S(2)}, u32[]{:S(2)}) collective-permute-start(bf16[48,2048]{1,0:T(8,128)(2,1)S(1)} %add_convert_fusion.1.refs_3_), channel_id=1, source_target_pairs={{0,8},{4,12},{8,0},{12,4},{1,9},{5,13},{9,1},{13,5},{2,10},{6,14},... | collective-permute-start | bytes 589832 | tf_op jit(solution)/shard_map/ppermute | solution.py:27
  135.3 21.8 %collective-permute-start.22 = (bf16[2,64,3584]{2,1,0:T(8,128)(2,1)S(1)}, bf16[2,64,3584]{2,1,0:T(8,128)(2,1)S(1)}, u32[]{:S(2)}, u32[]{:S(2)}) collective-permute-start(bf16[2,64,3584]{2,1,0:T(8,128)(2,1)S(1)} %get-tuple-element.99), channel_id=1, source_target_pairs={{0,2},{2,0},{1,3},{3,1},{4,6},{6,4},{5,7},{7,5},{8,10},{10,8},{9,1... | collective-permute-start | bytes 2752520 | tf_op jit(solution)/shard_map/ppermute | solution.py:23
  136.5 10.6 %collective-permute-start.20 = (bf16[96,2048]{1,0:T(8,128)(2,1)S(1)}, bf16[96,2048]{1,0:T(8,128)(2,1)S(1)}, u32[]{:S(2)}, u32[]{:S(2)}) collective-permute-start(bf16[96,2048]{1,0:T(8,128)(2,1)S(1)} %constant_dynamic-update-slice_fusion.refs_4_.near_ref), channel_id=1, source_target_pairs={{0,4},{4,0},{8,12},{12,8},{1,5},{5,1},{9,13},{13,9},{2,6},{6,2},{1... | collective-permute-start | bytes 1179656 | tf_op jit(solution)/shard_map/ppermute | solution.py:27
  142.9 14.2 %collective-permute-start.24 = (bf16[96,2048]{1,0:T(8,128)(2,1)S(1)}, bf16[96,2048]{1,0:T(8,128)(2,1)S(1)}, u32[]{:S(2)}, u32[]{:S(2)}) collective-permute-start(bf16[96,2048]{1,0:T(8,128)(2,1)S(1)} %get-tuple-element.102), channel_id=1, source_target_pairs={{0,4},{4,0},{8,12},{12,8},{1,5},{5,1},{9,13},{13,9},{2,6},{6,2},{1... | collective-permute-start | bytes 1179656 | tf_op jit(solution)/shard_map/ppermute | solution.py:27
  157.7 11.8 %collective-permute-start.25 = (bf16[48,2048]{1,0:T(8,128)(2,1)S(1)}, bf16[48,2048]{1,0:T(8,128)(2,1)S(1)}, u32[]{:S(2)}, u32[]{:S(2)}) collective-permute-start(bf16[48,2048]{1,0:T(8,128)(2,1)S(1)} %slice.228.refs_5_), channel_id=1, source_target_pairs={{0,8},{4,12},{8,0},{12,4},{1,9},{5,13},{9,1},{13,5},{2,10},{6,14},... | collective-permute-start | bytes 589832 | tf_op jit(solution)/shard_map/ppermute | solution.py:27
  159.0 10.8 %collective-permute-start.23 = (bf16[64,3584]{1,0:T(8,128)(2,1)S(1)}, bf16[64,3584]{1,0:T(8,128)(2,1)S(1)}, u32[]{:S(2)}, u32[]{:S(2)}) collective-permute-start(bf16[64,3584]{1,0:T(8,128)(2,1)S(1)} %fusion.3.refs_0_.refs_4_), channel_id=1, source_target_pairs={{2,0},{0,2},{3,1},{1,3},{6,4},{4,6},{7,5},{5,7},{10,8},{8,10},{11,... | collective-permute-start | bytes 1376264 | tf_op jit(solution)/shard_map/ppermute | solution.py:19
  169.7 20.3 %collective-permute-start.21 = (bf16[96,4096]{1,0:T(8,128)(2,1)S(1)}, bf16[96,4096]{1,0:T(8,128)(2,1)S(1)}, u32[]{:S(2)}, u32[]{:S(2)}) collective-permute-start(bf16[96,4096]{1,0:T(8,128)(2,1)S(1)} %get-tuple-element.98), channel_id=1, source_target_pairs={{0,1},{1,0},{2,3},{3,2},{4,5},{5,4},{6,7},{7,6},{8,9},{9,8},{10,11... | collective-permute-start | bytes 2359304 | tf_op jit(solution)/shard_map/ppermute | solution.py:23
  176.2 10.4 %collective-permute-start.30 = (bf16[32,2048]{1,0:T(8,128)(2,1)S(1)}, bf16[32,2048]{1,0:T(8,128)(2,1)S(1)}, u32[]{:S(2)}, u32[]{:S(2)}) collective-permute-start(bf16[32,2048]{1,0:T(8,128)(2,1)S(1)} %slice.230), channel_id=1, source_target_pairs={{0,8},{4,12},{8,0},{12,4},{1,9},{5,13},{9,1},{13,5},{2,10},{6,14},... | collective-permute-start | bytes 393224 | tf_op jit(solution)/shard_map/ppermute | solution.py:27
  178.6 11.4 %collective-permute-start.31 = (bf16[32,2048]{1,0:T(8,128)(2,1)S(1)}, bf16[32,2048]{1,0:T(8,128)(2,1)S(1)}, u32[]{:S(2)}, u32[]{:S(2)}) collective-permute-start(bf16[32,2048]{1,0:T(8,128)(2,1)S(1)} %get-tuple-element.149), channel_id=1, source_target_pairs={{0,4},{4,0},{8,12},{12,8},{1,5},{5,1},{9,13},{13,9},{2,6},{6,2},{1... | collective-permute-start | bytes 393224 | tf_op jit(solution)/shard_map/ppermute | solution.py:27
  180.8 21.1 %collective-permute-start.28 = (bf16[96,2048]{1,0:T(8,128)(2,1)S(1)}, bf16[96,2048]{1,0:T(8,128)(2,1)S(1)}, u32[]{:S(2)}, u32[]{:S(2)}) collective-permute-start(bf16[96,2048]{1,0:T(8,128)(2,1)S(1)} %constant_dynamic-update-slice_fusion.2.near_ref.refs_3_), channel_id=1, source_target_pairs={{0,4},{4,0},{8,12},{12,8},{1,5},{5,1},{9,13},{13,9},{2,6},{6,2},{1... | collective-permute-start | bytes 1179656 | tf_op jit(solution)/shard_map/ppermute | solution.py:27
  190.2 21.7 %collective-permute-start.26 = (bf16[48,4096]{1,0:T(8,128)(2,1)S(1)}, bf16[48,4096]{1,0:T(8,128)(2,1)S(1)}, u32[]{:S(2)}, u32[]{:S(2)}) collective-permute-start(bf16[48,4096]{1,0:T(8,128)(2,1)S(1)} %slice.226.refs_1_), channel_id=1, source_target_pairs={{0,2},{2,0},{1,3},{3,1},{4,6},{6,4},{5,7},{7,5},{8,10},{10,8},{9,1... | collective-permute-start | bytes 1179656 | tf_op jit(solution)/shard_map/ppermute | solution.py:23
  191.7 20.0 %collective-permute-start.35 = (bf16[32,2048]{1,0:T(8,128)(2,1)S(1)}, bf16[32,2048]{1,0:T(8,128)(2,1)S(1)}, u32[]{:S(2)}, u32[]{:S(2)}) collective-permute-start(bf16[32,2048]{1,0:T(8,128)(2,1)S(1)} %add_convert_fusion.2.refs_2_), channel_id=1, source_target_pairs={{0,12},{4,8},{8,4},{12,0},{1,13},{5,9},{9,5},{13,1},{2,14},{6,10},... | collective-permute-start | bytes 393224 | tf_op jit(solution)/shard_map/ppermute | solution.py:27
  193.7 18.1 %collective-permute-start.34 = (bf16[32,2048]{1,0:T(8,128)(2,1)S(1)}, bf16[32,2048]{1,0:T(8,128)(2,1)S(1)}, u32[]{:S(2)}, u32[]{:S(2)}) collective-permute-start(bf16[32,2048]{1,0:T(8,128)(2,1)S(1)} %add_convert_fusion.2.refs_2_), channel_id=1, source_target_pairs={{0,8},{4,12},{8,0},{12,4},{1,9},{5,13},{9,1},{13,5},{2,10},{6,14},... | collective-permute-start | bytes 393224 | tf_op jit(solution)/shard_map/ppermute | solution.py:27
  194.6 17.2 %collective-permute-start.33 = (bf16[32,2048]{1,0:T(8,128)(2,1)S(1)}, bf16[32,2048]{1,0:T(8,128)(2,1)S(1)}, u32[]{:S(2)}, u32[]{:S(2)}) collective-permute-start(bf16[32,2048]{1,0:T(8,128)(2,1)S(1)} %add_convert_fusion.2.refs_2_), channel_id=1, source_target_pairs={{0,4},{4,0},{8,12},{12,8},{1,5},{5,1},{9,13},{13,9},{2,6},{6,2},{1... | collective-permute-start | bytes 393224 | tf_op jit(solution)/shard_map/ppermute | solution.py:27
  220.5 12.0 %collective-permute-start.36 = (bf16[48,4096]{1,0:T(8,128)(2,1)S(1)}, bf16[48,4096]{1,0:T(8,128)(2,1)S(1)}, u32[]{:S(2)}, u32[]{:S(2)}) collective-permute-start(bf16[48,4096]{1,0:T(8,128)(2,1)S(1)} %slice.225), channel_id=1, source_target_pairs={{0,2},{2,0},{1,3},{3,1},{4,6},{6,4},{5,7},{7,5},{8,10},{10,8},{9,1... | collective-permute-start | bytes 1179656 | tf_op jit(solution)/shard_map/ppermute | solution.py:23
  222.1 15.7 %collective-permute-start.38 = (bf16[32,4096]{1,0:T(8,128)(2,1)S(1)}, bf16[32,4096]{1,0:T(8,128)(2,1)S(1)}, u32[]{:S(2)}, u32[]{:S(2)}) collective-permute-start(bf16[32,4096]{1,0:T(8,128)(2,1)S(1)} %slice.227), channel_id=1, source_target_pairs={{0,2},{2,0},{1,3},{3,1},{4,6},{6,4},{5,7},{7,5},{8,10},{10,8},{9,1... | collective-permute-start | bytes 786440 | tf_op jit(solution)/shard_map/ppermute | solution.py:23
  (26 other events, 177.2 us)

commit v16 on v15

--- a/solution.py
+++ b/solution.py
@@ -216,7 +216,7 @@
     rows, depth = 2 * near.shape[0], near.shape[1]
     width = enc_weight.shape[2]
     rows_each = rows // members
-    tile = tile_of(width, 256)
+    tile = tile_of(width, 1024)
     tiles = width // tile
     return pl.pallas_call(
         functools.partial(encode_body, members, order, tiles),

time: 239 us -> 234 us (0.979)
  waiting for transfers between devices: 93.9 us -> 89 us
  Pallas kernels: 82.9 us -> 78.8 us
  starting transfers between devices: 50.3 us -> 54.3 us
    ppermute x18, waiting for transfers between devices: 52.1 us -> 45.9 us  [swap(): return lax.ppermute(value, axis, [(d, d ^ bit) for d in range(size)])]
    pallas_call x3, Pallas kernels: 26.9 us -> 22.8 us  [encode(): pl.pallas_call(functools.partial(encode_body, members, order, tiles), gri...]
    ppermute x10, starting transfers between devices: 9.77 us -> 13.1 us  [send(): lax.ppermute(value, axis, [(d, (d + hop) % size) for d in range(size)])]
  transfers between devices with their start and end apart: 39 -> 39, of which waited for: 21 -> 24; matrix products, arithmetic and copies ran while one was open for 2% -> 2% of each run, Pallas kernels for 35% -> 34%
where the time goes in v16:
time: 234 us
  waiting for transfers between devices  89 us (38%)
  Pallas kernels  78.8 us (34%)
  starting transfers between devices  54.3 us (23%)
  local copies, waits for them, and re-layouts  5.69 us (2%)
  other arithmetic  5.19 us (2%)
    ppermute x18, waiting for transfers between devices, swap(): return lax.ppermute(value, axis, [(d, d ^ bit) for d in range(size)])  45.9 us
    pallas_call x4, Pallas kernels, gate_up(): pl.pallas_call(functools.partial(gate_up_body, tiles, first), grid=(tiles...  37.5 us
    ppermute x18, starting transfers between devices, swap(): return lax.ppermute(value, axis, [(d, d ^ bit) for d in range(size)])  33.8 us
    ppermute x10, waiting for transfers between devices, send(): lax.ppermute(value, axis, [(d, (d + hop) % size) for d in range(size)])  29 us
    pallas_call x3, Pallas kernels, encode(): pl.pallas_call(functools.partial(encode_body, members, order, tiles), gri...  22.8 us
    pallas_call x3, Pallas kernels, down(): pl.pallas_call(functools.partial(down_body, owners, members, pieces, orde...  18.5 us
    ppermute x11, waiting for transfers between devices, shift(): lax.ppermute(value, axis, [((d + hop) % size, d) for d in range(size)])  14.1 us
    ppermute x10, starting transfers between devices, send(): lax.ppermute(value, axis, [(d, (d + hop) % size) for d in range(size)])  13.1 us
  transfers between devices with their start and end apart: 39, of which 24 were waited for; matrix products, arithmetic and copies ran while one was open for 2% of the time, Pallas kernels for 34%

profile of v16, /device:TPU:0, one launch (start us, length us, event | category | flops | bytes accessed | tf_op | source)
XLA Modules:
  0.0 233.6 jit_solution(6081159002158669115)
XLA Ops:
  1.1 4.1 %collective-permute-start = (bf16[1,48,1024]{2,1,0:T(8,128)(2,1)S(1)}, bf16[1,48,1024]{2,1,0:T(8,128)(2,1)S(1)}, u32[]{:S(2)}, u32[]{:S(2)}) collective-permute-start(bf16[1,48,1024]{2,1,0:T(8,128)(2,1)S(1)} %dynamic-slice_bitcast_fusion.1), channel_id=1, source_target_pairs={{0,8},{4,12},{8,0},{12,4},{1,9},{5,13},{9,1},{13,5},{2,10},{6,14},... | collective-permute-start | bytes 294920 | tf_op jit(solution)/shard_map/ppermute | solution.py:27
  5.2 4.9 %collective-permute-done = bf16[1,48,1024]{2,1,0:T(8,128)(2,1)S(1)} collective-permute-done((bf16[1,48,1024]{2,1,0:T(8,128)(2,1)S(1)}, bf16[1,48,1024]{2,1,0:T(8,128)(2,1)S(1)}, u32[]{:S(2)}, u32[]{:S(2)}) %collective-permute-start) | collective-permute-done | bytes 98336 | tf_op jit(solution)/shard_map/ppermute | solution.py:27
  15.0 5.1 %collective-permute-done.7 = bf16[1,80,1024]{2,1,0:T(8,128)(2,1)S(1)} collective-permute-done((bf16[1,80,1024]{2,1,0:T(8,128)(2,1)S(1)}, bf16[1,80,1024]{2,1,0:T(8,128)(2,1)S(1)}, u32[]{:S(2)}, u32[]{:S(2)}) %collective-permute-start.7) | collective-permute-done | bytes 163872 | tf_op jit(solution)/shard_map/ppermute | solution.py:27
  32.2 7.2 %shard_map.82 = (f32[2,96,1792]{2,1,0:T(8,128)S(1)}, bf16[2,96,1792]{2,1,0:T(8,128)(2,1)S(1)}) custom-call(bf16[2,2,2,48,1024]{4,3,2,1,0:T(8,128)(2,1)S(1)} %multiply_convert_fusion.1.x_ref, bf16[1,2048,3584]{2,1,0:T(8,128)(2,1)} %gate_ref.7, bf16[1,2048,3584]{2,1,0:T(8,128)(2,1)} %up_ref.7), custom_call_target="tpu_custom_call" | custom-call | flops 1 | bytes 1 | tf_op jit(solution)/shard_map/pallas_call | solution.py:127
  42.3 7.2 %shard_map.83 = (f32[2,96,1792]{2,1,0:T(8,128)S(1)}, bf16[2,96,1792]{2,1,0:T(8,128)(2,1)S(1)}) custom-call(bf16[2,2,2,48,1024]{4,3,2,1,0:T(8,128)(2,1)S(1)} %multiply_convert_fusion.1.x_ref, bf16[1,2048,3584]{2,1,0:T(8,128)(2,1)} %gate_ref.7, bf16[1,2048,3584]{2,1,0:T(8,128)(2,1)} %up_ref.7, f32[2,96,1792]{2,1,0:T(8,128)S(1)} %get-tuple-element.72.refs_0_, ...), custom_call_target="tpu_custom_call" | custom-call | flops 1 | bytes 1 | tf_op jit(solution)/shard_map/pallas_call | solution.py:127
  51.9 6.1 %collective-permute-done.12 = f32[2,80]{1,0:T(2,128)S(1)} collective-permute-done((f32[2,80]{1,0:T(2,128)S(1)}, f32[2,80]{1,0:T(2,128)S(1)}, u32[]{:S(2)}, u32[]{:S(2)}) %collective-permute-start.12) | collective-permute-done | bytes 672 | tf_op jit(solution)/shard_map/ppermute | solution.py:19
  58.3 12.2 %collective-permute-done.11 = bf16[2,96,1792]{2,1,0:T(8,128)(2,1)S(1)} collective-permute-done((bf16[2,96,1792]{2,1,0:T(8,128)(2,1)S(1)}, bf16[2,96,1792]{2,1,0:T(8,128)(2,1)S(1)}, u32[]{:S(2)}, u32[]{:S(2)}) %collective-permute-start.11) | collective-permute-done | bytes 688160 | tf_op jit(solution)/shard_map/ppermute | solution.py:23
  72.4 11.7 %shard_map.84 = (f32[2,96,3584]{2,1,0:T(8,128)S(1)}, bf16[2,96,3584]{2,1,0:T(8,128)(2,1)S(1)}) custom-call(bf16[2,2,2,48,1024]{4,3,2,1,0:T(8,128)(2,1)S(1)} %multiply_convert_fusion.x_ref, bf16[1,2048,3584]{2,1,0:T(8,128)(2,1)} %gate_ref.7, bf16[1,2048,3584]{2,1,0:T(8,128)(2,1)} %up_ref.7, f32[2,96,1792]{2,1,0:T(8,128)S(1)} %get-tuple-element.81.refs_0_, ...), custom_call_target="tpu_custom_call" | custom-call | flops 1 | bytes 1 | tf_op jit(solution)/shard_map/pallas_call | solution.py:127
  86.4 6.3 %shard_map.85 = (f32[96,2048]{1,0:T(8,128)S(1)}, bf16[96,2048]{1,0:T(8,128)(2,1)S(1)}) custom-call(s32[1]{0:T(128)} %bitcast.rank_ref, bf16[96,3584]{1,0:T(8,128)(2,1)S(1)} %pad_maximum_fusion.refs_4_.refs_0_, bf16[96,3584]{1,0:T(8,128)(2,1)S(1)} %collective-permute-done.13.refs_1_, bf16[1,3584,2048]{2,1,0:T(8,128)(2,1)} %refs_2_.5, f32[2,96,3584]{2,1,0:T(8,128)} %copy-done.2), custom_call_target="tpu_custom_call" | custom-call | flops 1 | bytes 1 | tf_op jit(solution)/shard_map/pallas_call | solution.py:175
  96.4 7.1 %collective-permute-done.15 = bf16[96,2048]{1,0:T(8,128)(2,1)S(1)} collective-permute-done((bf16[96,2048]{1,0:T(8,128)(2,1)S(1)}, bf16[96,2048]{1,0:T(8,128)(2,1)S(1)}, u32[]{:S(2)}, u32[]{:S(2)}) %collective-permute-start.15) | collective-permute-done | bytes 393248 | tf_op jit(solution)/shard_map/ppermute | solution.py:27
  103.7 4.6 %collective-permute-start.16 = (bf16[48,2048]{1,0:T(8,128)(2,1)S(1)}, bf16[48,2048]{1,0:T(8,128)(2,1)S(1)}, u32[]{:S(2)}, u32[]{:S(2)}) collective-permute-start(bf16[48,2048]{1,0:T(8,128)(2,1)S(1)} %slice.229.refs_1_), channel_id=1, source_target_pairs={{0,8},{4,12},{8,0},{12,4},{1,9},{5,13},{9,1},{13,5},{2,10},{6,14},... | collective-permute-start | bytes 589832 | tf_op jit(solution)/shard_map/ppermute | solution.py:27
  108.4 5.2 %collective-permute-done.16 = bf16[48,2048]{1,0:T(8,128)(2,1)S(1)} collective-permute-done((bf16[48,2048]{1,0:T(8,128)(2,1)S(1)}, bf16[48,2048]{1,0:T(8,128)(2,1)S(1)}, u32[]{:S(2)}, u32[]{:S(2)}) %collective-permute-start.16) | collective-permute-done | bytes 196640 | tf_op jit(solution)/shard_map/ppermute | solution.py:27
  117.9 4.6 %collective-permute-start.17 = (bf16[48,2048]{1,0:T(8,128)(2,1)S(1)}, bf16[48,2048]{1,0:T(8,128)(2,1)S(1)}, u32[]{:S(2)}, u32[]{:S(2)}) collective-permute-start(bf16[48,2048]{1,0:T(8,128)(2,1)S(1)} %add_convert_fusion.1.refs_3_), channel_id=1, source_target_pairs={{0,8},{4,12},{8,0},{12,4},{1,9},{5,13},{9,1},{13,5},{2,10},{6,14},... | collective-permute-start | bytes 589832 | tf_op jit(solution)/shard_map/ppermute | solution.py:27
  122.7 11.4 %shard_map.86 = (f32[2,64,3584]{2,1,0:T(8,128)S(1)}, bf16[2,64,3584]{2,1,0:T(8,128)(2,1)S(1)}) custom-call(bf16[2,2,2,32,1024]{4,3,2,1,0:T(8,128)(2,1)S(1)} %multiply_convert_fusion.2.x_ref, bf16[1,2048,3584]{2,1,0:T(8,128)(2,1)} %gate_ref.7, bf16[1,2048,3584]{2,1,0:T(8,128)(2,1)} %up_ref.7, f32[96,2048]{1,0:T(8,128)S(1)} %get-tuple-element.86.refs_0_, ...), custom_call_target="tpu_custom_call" | custom-call | flops 1 | bytes 1 | tf_op jit(solution)/shard_map/pallas_call | solution.py:127
  136.6 6.3 %shard_map.87 = (f32[96,2048]{1,0:T(8,128)S(1)}, bf16[96,2048]{1,0:T(8,128)(2,1)S(1)}) custom-call(s32[1]{0:T(128)} %bitcast.rank_ref, bf16[96,3584]{1,0:T(8,128)(2,1)S(1)} %fusion.1.refs_2_.refs_0_, bf16[96,3584]{1,0:T(8,128)(2,1)S(1)} %collective-permute-done.19.refs_1_, bf16[1,3584,2048]{2,1,0:T(8,128)(2,1)} %refs_2_.5, f32[2,64,3584]{2,1,0:T(8,128)} %copy-done.4, ...), custom_call_target="tpu_custom_call" | custom-call | flops 1 | bytes 1 | tf_op jit(solution)/shard_map/pallas_call | solution.py:175
  147.2 8.1 %shard_map.88 = (f32[96,4096]{1,0:T(8,128)}, bf16[96,4096]{1,0:T(8,128)(2,1)S(1)}) custom-call(s32[1]{0:T(128)} %bitcast.rank_ref, bf16[96,2048]{1,0:T(8,128)(2,1)S(1)} %constant_dynamic-update-slice_fusion.refs_4_.near_ref, bf16[96,2048]{1,0:T(8,128)(2,1)S(1)} %collective-permute-done.20.far_ref, bf16[1,2048,4096]{2,1,0:T(8,128)(2,1)} %weight_ref.5, ...), custom_call_target="tpu_custom_call" | custom-call | flops 1 | bytes 1 | tf_op jit(solution)/shard_map/pallas_call | solution.py:221
  158.6 8.1 %collective-permute-done.25 = bf16[48,2048]{1,0:T(8,128)(2,1)S(1)} collective-permute-done((bf16[48,2048]{1,0:T(8,128)(2,1)S(1)}, bf16[48,2048]{1,0:T(8,128)(2,1)S(1)}, u32[]{:S(2)}, u32[]{:S(2)}) %collective-permute-start.25) | collective-permute-done | bytes 196640 | tf_op jit(solution)/shard_map/ppermute | solution.py:27
  168.2 5.9 %shard_map.89 = (f32[64,2048]{1,0:T(8,128)S(1)}, bf16[64,2048]{1,0:T(8,128)(2,1)S(1)}) custom-call(s32[1]{0:T(128)} %bitcast.rank_ref, bf16[64,3584]{1,0:T(8,128)(2,1)S(1)} %fusion.3.refs_0_.refs_4_, bf16[64,3584]{1,0:T(8,128)(2,1)S(1)} %collective-permute-done.23.refs_1_, bf16[1,3584,2048]{2,1,0:T(8,128)(2,1)} %refs_2_.5, ...), custom_call_target="tpu_custom_call" | custom-call | flops 1 | bytes 1 | tf_op jit(solution)/shard_map/pallas_call | solution.py:175
  179.7 7.0 %collective-permute-done.30 = bf16[32,2048]{1,0:T(8,128)(2,1)S(1)} collective-permute-done((bf16[32,2048]{1,0:T(8,128)(2,1)S(1)}, bf16[32,2048]{1,0:T(8,128)(2,1)S(1)}, u32[]{:S(2)}, u32[]{:S(2)}) %collective-permute-start.30) | collective-permute-done | bytes 131104 | tf_op jit(solution)/shard_map/ppermute | solution.py:27
  194.9 8.0 %shard_map.90 = (f32[96,4096]{1,0:T(8,128)}, bf16[96,4096]{1,0:T(8,128)(2,1)S(1)}) custom-call(s32[1]{0:T(128)} %bitcast.rank_ref, bf16[96,2048]{1,0:T(8,128)(2,1)S(1)} %constant_dynamic-update-slice_fusion.2.near_ref.refs_3_, bf16[96,2048]{1,0:T(8,128)(2,1)S(1)} %collective-permute-done.28.far_ref, bf16[1,2048,4096]{2,1,0:T(8,128)(2,1)} %weight_ref.5, ...), custom_call_target="tpu_custom_call" | custom-call | flops 1 | bytes 1 | tf_op jit(solution)/shard_map/pallas_call | solution.py:221
  204.1 6.8 %shard_map.91 = (f32[64,4096]{1,0:T(8,128)S(1)}, bf16[64,4096]{1,0:T(8,128)(2,1)S(1)}) custom-call(s32[1]{0:T(128)} %bitcast.rank_ref, bf16[64,2048]{1,0:T(8,128)(2,1)S(1)} %get-tuple-element.153.near_ref, bf16[64,2048]{1,0:T(8,128)(2,1)S(1)} %get-tuple-element.154.far_ref, bf16[1,2048,4096]{2,1,0:T(8,128)(2,1)} %weight_ref.5, ...), custom_call_target="tpu_custom_call" | custom-call | flops 1 | bytes 1 | tf_op jit(solution)/shard_map/pallas_call | solution.py:221
  212.5 4.9 %collective-permute-start.36 = (bf16[48,4096]{1,0:T(8,128)(2,1)S(1)}, bf16[48,4096]{1,0:T(8,128)(2,1)S(1)}, u32[]{:S(2)}, u32[]{:S(2)}) collective-permute-start(bf16[48,4096]{1,0:T(8,128)(2,1)S(1)} %slice.225), channel_id=1, source_target_pairs={{0,2},{2,0},{1,3},{3,1},{4,6},{6,4},{5,7},{7,5},{8,10},{10,8},{9,1... | collective-permute-start | bytes 1179656 | tf_op jit(solution)/shard_map/ppermute | solution.py:23
  218.1 9.3 %collective-permute-done.36 = bf16[48,4096]{1,0:T(8,128)(2,1)S(1)} collective-permute-done((bf16[48,4096]{1,0:T(8,128)(2,1)S(1)}, bf16[48,4096]{1,0:T(8,128)(2,1)S(1)}, u32[]{:S(2)}, u32[]{:S(2)}) %collective-permute-start.36) | collective-permute-done | bytes 393248 | tf_op jit(solution)/shard_map/ppermute | solution.py:23
  227.6 5.2 %collective-permute-done.38 = bf16[32,4096]{1,0:T(8,128)(2,1)S(1)} collective-permute-done((bf16[32,4096]{1,0:T(8,128)(2,1)S(1)}, bf16[32,4096]{1,0:T(8,128)(2,1)S(1)}, u32[]{:S(2)}, u32[]{:S(2)}) %collective-permute-start.38) | collective-permute-done | bytes 262176 | tf_op jit(solution)/shard_map/ppermute | solution.py:23
  (151 shorter events, 66.0 us)
Async XLA Ops:
  31.3 11.0 %collective-permute-start.9 = (bf16[2,80,1024]{2,1,0:T(8,128)(2,1)S(1)}, bf16[2,80,1024]{2,1,0:T(8,128)(2,1)S(1)}, u32[]{:S(2)}, u32[]{:S(2)}) collective-permute-start(bf16[2,80,1024]{2,1,0:T(8,128)(2,1)S(1)} %pad_maximum_fusion.8), channel_id=1, source_target_pairs={{2,0},{0,2},{3,1},{1,3},{6,4},{4,6},{7,5},{5,7},{10,8},{8,10},{11,... | collective-permute-start | bytes 983048 | tf_op jit(solution)/shard_map/ppermute | solution.py:19
  39.4 18.5 %collective-permute-start.6 = (bf16[2,96,1792]{2,1,0:T(8,128)(2,1)S(1)}, bf16[2,96,1792]{2,1,0:T(8,128)(2,1)S(1)}, u32[]{:S(2)}, u32[]{:S(2)}) collective-permute-start(bf16[2,96,1792]{2,1,0:T(8,128)(2,1)S(1)} %get-tuple-element.73), channel_id=1, source_target_pairs={{0,2},{2,0},{1,3},{3,1},{4,6},{6,4},{5,7},{7,5},{8,10},{10,8},{9,1... | collective-permute-start | bytes 2064392 | tf_op jit(solution)/shard_map/ppermute | solution.py:23
  50.1 22.1 %collective-permute-start.14 = (bf16[2,2,80,1024]{3,2,1,0:T(8,128)(2,1)S(1)}, bf16[2,2,80,1024]{3,2,1,0:T(8,128)(2,1)S(1)}, u32[]{:S(2)}, u32[]{:S(2)}) collective-permute-start(bf16[2,2,80,1024]{3,2,1,0:T(8,128)(2,1)S(1)} %get-tuple-element.135), channel_id=1, source_target_pairs={{1,0},{0,1},{3,2},{2,3},{5,4},{4,5},{7,6},{6,7},{9,8},{8,9},{11,10... | collective-permute-start | bytes 1966088 | tf_op jit(solution)/shard_map/ppermute | solution.py:19
  50.1 20.3 %collective-permute-start.11 = (bf16[2,96,1792]{2,1,0:T(8,128)(2,1)S(1)}, bf16[2,96,1792]{2,1,0:T(8,128)(2,1)S(1)}, u32[]{:S(2)}, u32[]{:S(2)}) collective-permute-start(bf16[2,96,1792]{2,1,0:T(8,128)(2,1)S(1)} %get-tuple-element.79), channel_id=1, source_target_pairs={{0,2},{2,0},{1,3},{3,1},{4,6},{6,4},{5,7},{7,5},{8,10},{10,8},{9,1... | collective-permute-start | bytes 2064392 | tf_op jit(solution)/shard_map/ppermute | solution.py:23
  70.9 15.6 %collective-permute-start.13 = (bf16[96,3584]{1,0:T(8,128)(2,1)S(1)}, bf16[96,3584]{1,0:T(8,128)(2,1)S(1)}, u32[]{:S(2)}, u32[]{:S(2)}) collective-permute-start(bf16[96,3584]{1,0:T(8,128)(2,1)S(1)} %pad_maximum_fusion.refs_4_.refs_0_), channel_id=1, source_target_pairs={{2,0},{0,2},{3,1},{1,3},{6,4},{4,6},{7,5},{5,7},{10,8},{8,10},{11,... | collective-permute-start | bytes 2064392 | tf_op jit(solution)/shard_map/ppermute | solution.py:19
  85.6 30.1 %collective-permute-start.18 = (bf16[2,96,3584]{2,1,0:T(8,128)(2,1)S(1)}, bf16[2,96,3584]{2,1,0:T(8,128)(2,1)S(1)}, u32[]{:S(2)}, u32[]{:S(2)}) collective-permute-start(bf16[2,96,3584]{2,1,0:T(8,128)(2,1)S(1)} %get-tuple-element.90), channel_id=1, source_target_pairs={{0,2},{2,0},{1,3},{3,1},{4,6},{6,4},{5,7},{7,5},{8,10},{10,8},{9,1... | collective-permute-start | bytes 4128776 | tf_op jit(solution)/shard_map/ppermute | solution.py:23
  92.7 10.8 %collective-permute-start.15 = (bf16[96,2048]{1,0:T(8,128)(2,1)S(1)}, bf16[96,2048]{1,0:T(8,128)(2,1)S(1)}, u32[]{:S(2)}, u32[]{:S(2)}) collective-permute-start(bf16[96,2048]{1,0:T(8,128)(2,1)S(1)} %get-tuple-element.85), channel_id=1, source_target_pairs={{0,4},{4,0},{8,12},{12,8},{1,5},{5,1},{9,13},{13,9},{2,6},{6,2},{1... | collective-permute-start | bytes 1179656 | tf_op jit(solution)/shard_map/ppermute | solution.py:27
  116.4 20.1 %collective-permute-start.19 = (bf16[96,3584]{1,0:T(8,128)(2,1)S(1)}, bf16[96,3584]{1,0:T(8,128)(2,1)S(1)}, u32[]{:S(2)}, u32[]{:S(2)}) collective-permute-start(bf16[96,3584]{1,0:T(8,128)(2,1)S(1)} %fusion.1.refs_2_.refs_0_), channel_id=1, source_target_pairs={{2,0},{0,2},{3,1},{1,3},{6,4},{4,6},{7,5},{5,7},{10,8},{8,10},{11,... | collective-permute-start | bytes 2064392 | tf_op jit(solution)/shard_map/ppermute | solution.py:19
  117.9 18.6 %collective-permute-start.17 = (bf16[48,2048]{1,0:T(8,128)(2,1)S(1)}, bf16[48,2048]{1,0:T(8,128)(2,1)S(1)}, u32[]{:S(2)}, u32[]{:S(2)}) collective-permute-start(bf16[48,2048]{1,0:T(8,128)(2,1)S(1)} %add_convert_fusion.1.refs_3_), channel_id=1, source_target_pairs={{0,8},{4,12},{8,0},{12,4},{1,9},{5,13},{9,1},{13,5},{2,10},{6,14},... | collective-permute-start | bytes 589832 | tf_op jit(solution)/shard_map/ppermute | solution.py:27
  135.3 20.2 %collective-permute-start.22 = (bf16[2,64,3584]{2,1,0:T(8,128)(2,1)S(1)}, bf16[2,64,3584]{2,1,0:T(8,128)(2,1)S(1)}, u32[]{:S(2)}, u32[]{:S(2)}) collective-permute-start(bf16[2,64,3584]{2,1,0:T(8,128)(2,1)S(1)} %get-tuple-element.99), channel_id=1, source_target_pairs={{0,2},{2,0},{1,3},{3,1},{4,6},{6,4},{5,7},{7,5},{8,10},{10,8},{9,1... | collective-permute-start | bytes 2752520 | tf_op jit(solution)/shard_map/ppermute | solution.py:23
  136.5 10.6 %collective-permute-start.20 = (bf16[96,2048]{1,0:T(8,128)(2,1)S(1)}, bf16[96,2048]{1,0:T(8,128)(2,1)S(1)}, u32[]{:S(2)}, u32[]{:S(2)}) collective-permute-start(bf16[96,2048]{1,0:T(8,128)(2,1)S(1)} %constant_dynamic-update-slice_fusion.refs_4_.near_ref), channel_id=1, source_target_pairs={{0,4},{4,0},{8,12},{12,8},{1,5},{5,1},{9,13},{13,9},{2,6},{6,2},{1... | collective-permute-start | bytes 1179656 | tf_op jit(solution)/shard_map/ppermute | solution.py:27
  142.9 12.3 %collective-permute-start.24 = (bf16[96,2048]{1,0:T(8,128)(2,1)S(1)}, bf16[96,2048]{1,0:T(8,128)(2,1)S(1)}, u32[]{:S(2)}, u32[]{:S(2)}) collective-permute-start(bf16[96,2048]{1,0:T(8,128)(2,1)S(1)} %get-tuple-element.102), channel_id=1, source_target_pairs={{0,4},{4,0},{8,12},{12,8},{1,5},{5,1},{9,13},{13,9},{2,6},{6,2},{1... | collective-permute-start | bytes 1179656 | tf_op jit(solution)/shard_map/ppermute | solution.py:27
  156.0 10.6 %collective-permute-start.25 = (bf16[48,2048]{1,0:T(8,128)(2,1)S(1)}, bf16[48,2048]{1,0:T(8,128)(2,1)S(1)}, u32[]{:S(2)}, u32[]{:S(2)}) collective-permute-start(bf16[48,2048]{1,0:T(8,128)(2,1)S(1)} %slice.228.refs_5_), channel_id=1, source_target_pairs={{0,8},{4,12},{8,0},{12,4},{1,9},{5,13},{9,1},{13,5},{2,10},{6,14},... | collective-permute-start | bytes 589832 | tf_op jit(solution)/shard_map/ppermute | solution.py:27
  157.6 10.6 %collective-permute-start.23 = (bf16[64,3584]{1,0:T(8,128)(2,1)S(1)}, bf16[64,3584]{1,0:T(8,128)(2,1)S(1)}, u32[]{:S(2)}, u32[]{:S(2)}) collective-permute-start(bf16[64,3584]{1,0:T(8,128)(2,1)S(1)} %fusion.3.refs_0_.refs_4_), channel_id=1, source_target_pairs={{2,0},{0,2},{3,1},{1,3},{6,4},{4,6},{7,5},{5,7},{10,8},{8,10},{11,... | collective-permute-start | bytes 1376264 | tf_op jit(solution)/shard_map/ppermute | solution.py:19
  166.8 20.4 %collective-permute-start.21 = (bf16[96,4096]{1,0:T(8,128)(2,1)S(1)}, bf16[96,4096]{1,0:T(8,128)(2,1)S(1)}, u32[]{:S(2)}, u32[]{:S(2)}) collective-permute-start(bf16[96,4096]{1,0:T(8,128)(2,1)S(1)} %get-tuple-element.98), channel_id=1, source_target_pairs={{0,1},{1,0},{2,3},{3,2},{4,5},{5,4},{6,7},{7,6},{8,9},{9,8},{10,11... | collective-permute-start | bytes 2359304 | tf_op jit(solution)/shard_map/ppermute | solution.py:23
  175.1 11.6 %collective-permute-start.30 = (bf16[32,2048]{1,0:T(8,128)(2,1)S(1)}, bf16[32,2048]{1,0:T(8,128)(2,1)S(1)}, u32[]{:S(2)}, u32[]{:S(2)}) collective-permute-start(bf16[32,2048]{1,0:T(8,128)(2,1)S(1)} %slice.230), channel_id=1, source_target_pairs={{0,8},{4,12},{8,0},{12,4},{1,9},{5,13},{9,1},{13,5},{2,10},{6,14},... | collective-permute-start | bytes 393224 | tf_op jit(solution)/shard_map/ppermute | solution.py:27
  175.7 10.9 %collective-permute-start.31 = (bf16[32,2048]{1,0:T(8,128)(2,1)S(1)}, bf16[32,2048]{1,0:T(8,128)(2,1)S(1)}, u32[]{:S(2)}, u32[]{:S(2)}) collective-permute-start(bf16[32,2048]{1,0:T(8,128)(2,1)S(1)} %get-tuple-element.149), channel_id=1, source_target_pairs={{0,4},{4,0},{8,12},{12,8},{1,5},{5,1},{9,13},{13,9},{2,6},{6,2},{1... | collective-permute-start | bytes 393224 | tf_op jit(solution)/shard_map/ppermute | solution.py:27
  179.6 15.3 %collective-permute-start.28 = (bf16[96,2048]{1,0:T(8,128)(2,1)S(1)}, bf16[96,2048]{1,0:T(8,128)(2,1)S(1)}, u32[]{:S(2)}, u32[]{:S(2)}) collective-permute-start(bf16[96,2048]{1,0:T(8,128)(2,1)S(1)} %constant_dynamic-update-slice_fusion.2.near_ref.refs_3_), channel_id=1, source_target_pairs={{0,4},{4,0},{8,12},{12,8},{1,5},{5,1},{9,13},{13,9},{2,6},{6,2},{1... | collective-permute-start | bytes 1179656 | tf_op jit(solution)/shard_map/ppermute | solution.py:27
  187.4 16.6 %collective-permute-start.26 = (bf16[48,4096]{1,0:T(8,128)(2,1)S(1)}, bf16[48,4096]{1,0:T(8,128)(2,1)S(1)}, u32[]{:S(2)}, u32[]{:S(2)}) collective-permute-start(bf16[48,4096]{1,0:T(8,128)(2,1)S(1)} %slice.226.refs_1_), channel_id=1, source_target_pairs={{0,2},{2,0},{1,3},{3,1},{4,6},{6,4},{5,7},{7,5},{8,10},{10,8},{9,1... | collective-permute-start | bytes 1179656 | tf_op jit(solution)/shard_map/ppermute | solution.py:23
  189.1 13.8 %collective-permute-start.35 = (bf16[32,2048]{1,0:T(8,128)(2,1)S(1)}, bf16[32,2048]{1,0:T(8,128)(2,1)S(1)}, u32[]{:S(2)}, u32[]{:S(2)}) collective-permute-start(bf16[32,2048]{1,0:T(8,128)(2,1)S(1)} %add_convert_fusion.2.refs_2_), channel_id=1, source_target_pairs={{0,12},{4,8},{8,4},{12,0},{1,13},{5,9},{9,5},{13,1},{2,14},{6,10},... | collective-permute-start | bytes 393224 | tf_op jit(solution)/shard_map/ppermute | solution.py:27
  191.0 13.0 %collective-permute-start.34 = (bf16[32,2048]{1,0:T(8,128)(2,1)S(1)}, bf16[32,2048]{1,0:T(8,128)(2,1)S(1)}, u32[]{:S(2)}, u32[]{:S(2)}) collective-permute-start(bf16[32,2048]{1,0:T(8,128)(2,1)S(1)} %add_convert_fusion.2.refs_2_), channel_id=1, source_target_pairs={{0,8},{4,12},{8,0},{12,4},{1,9},{5,13},{9,1},{13,5},{2,10},{6,14},... | collective-permute-start | bytes 393224 | tf_op jit(solution)/shard_map/ppermute | solution.py:27
  192.5 11.5 %collective-permute-start.33 = (bf16[32,2048]{1,0:T(8,128)(2,1)S(1)}, bf16[32,2048]{1,0:T(8,128)(2,1)S(1)}, u32[]{:S(2)}, u32[]{:S(2)}) collective-permute-start(bf16[32,2048]{1,0:T(8,128)(2,1)S(1)} %add_convert_fusion.2.refs_2_), channel_id=1, source_target_pairs={{0,4},{4,0},{8,12},{12,8},{1,5},{5,1},{9,13},{13,9},{2,6},{6,2},{1... | collective-permute-start | bytes 393224 | tf_op jit(solution)/shard_map/ppermute | solution.py:27
  212.5 14.9 %collective-permute-start.36 = (bf16[48,4096]{1,0:T(8,128)(2,1)S(1)}, bf16[48,4096]{1,0:T(8,128)(2,1)S(1)}, u32[]{:S(2)}, u32[]{:S(2)}) collective-permute-start(bf16[48,4096]{1,0:T(8,128)(2,1)S(1)} %slice.225), channel_id=1, source_target_pairs={{0,2},{2,0},{1,3},{3,1},{4,6},{6,4},{5,7},{7,5},{8,10},{10,8},{9,1... | collective-permute-start | bytes 1179656 | tf_op jit(solution)/shard_map/ppermute | solution.py:23
  217.6 15.2 %collective-permute-start.38 = (bf16[32,4096]{1,0:T(8,128)(2,1)S(1)}, bf16[32,4096]{1,0:T(8,128)(2,1)S(1)}, u32[]{:S(2)}, u32[]{:S(2)}) collective-permute-start(bf16[32,4096]{1,0:T(8,128)(2,1)S(1)} %slice.227), channel_id=1, source_target_pairs={{0,2},{2,0},{1,3},{3,1},{4,6},{6,4},{5,7},{7,5},{8,10},{10,8},{9,1... | collective-permute-start | bytes 786440 | tf_op jit(solution)/shard_map/ppermute | solution.py:23
  (26 other events, 178.9 us)
